TPU v7x, 32 devices: a whole 2x2x4 slice. The times are simulated.
32 devices in a mesh: seq: 8 (over z, x), head: 4 (over y, core).
Axes of the slice: x: 2, y: 2, z: 4, core: 2. Of those that a mesh axis runs over, the one named last changes fastest.
Arguments:
- tokens: bfloat16 [4096, 4, 768], P(('seq', 'head')), may hold values from -6 to 6
- w_qkv: bfloat16 [768, 12, 3, 64], P(None, 'head'), may hold values from -0.21875 to 0.21875
- bias_qv: float32 [12, 2, 64], P('head'), may hold values from -1.8 to 1.8
- w_out: bfloat16 [12, 64, 768], P('head'), may hold values from -0.625 to 0.625
- bias_out: float32 [768], replicated, may hold values from -1.8 to 1.8
- gain_one: float32 [768], replicated, may hold values from 0.5 to 1.5
- bias_one: float32 [768], replicated, may hold values from -1.8 to 1.8
- up_weight: bfloat16 [768, 3072], P(None, 'head'), may hold values from -0.21875 to 0.21875
- up_bias_vector: bfloat16 [3072], P('head'), may hold values from -1.796875 to 1.796875
- down_weight: bfloat16 [3072, 768], P('head'), may hold values from -0.109375 to 0.109375
- down_bias_vector: float32 [768], replicated, may hold values from -1.8 to 1.8
- gain_two: float32 [768], replicated, may hold values from 0.5 to 1.5
- bias_two: float32 [768], replicated, may hold values from -1.8 to 1.8
- d_out: bfloat16 [4096, 4, 768], P(('seq', 'head')), may hold values from -6 to 6
- key_mask: int32 [4, 4096], replicated, may hold values from 0 to 1, as said below
- rand_idx: int32 [4, 64, 12, 3], replicated, may hold values from 1 to 62, as said below
Outputs:
- block_out: bfloat16 [4096, 4, 768], P(('seq', 'head'))
- d_tokens: bfloat16 [4096, 4, 768], P(('seq', 'head'))
- grad_w_qkv: float32 [768, 12, 3, 64], P(None, 'head')
- grad_bias_qv: float32 [12, 2, 64], P('head')
- grad_w_out: float32 [12, 64, 768], P('head')
- grad_bias_out: float32 [768], replicated
- grad_gain_one: float32 [768], replicated
- grad_bias_one: float32 [768], replicated
- grad_w_in: float32 [768, 3072], P(None, 'head')
- grad_bias_in: float32 [3072], P('head')
- grad_w_back: float32 [3072, 768], P('head')
- grad_bias_back: float32 [768], replicated
- grad_gain_two: float32 [768], replicated
- grad_bias_two: float32 [768], replicated
Inputs may be any that keep to these rules, and one draw needn't show every extreme that they name: key_mask[s, 0] is 1 for every sequence s. rand_idx[s, j, h] holds three different blocks, none of them 0, 63, j - 1, j or j + 1.
All inputs are finite; a program needn't handle non-finite values.
Results may differ from a plain program's by a relative error of at most 0.015.
Values may be sent and summed in bfloat16 or wider, within the bound.
No kernel may reach another device: no remote copies, remote signals or barrier semaphores. Data moves between devices by JAX's collectives and lax.ppermute only.
A program may use at most 320 MiB of HBM per device.

v0:
```python
import jax
import jax.numpy as jnp
from jax import lax
from jax.sharding import PartitionSpec as P

BLOCK = 64


NORM_EPS = 1e-12
MASK_FILL = -1000000000.0
MATMUL_ACCURACY = lax.Precision.HIGHEST


def norm_fwd(resid, gain, shift):
    row_mean = jnp.mean(resid, axis=-1, keepdims=True)
    centred = resid - row_mean
    inv_std = lax.rsqrt(jnp.mean(centred * centred, axis=-1, keepdims=True) + NORM_EPS)
    normed = centred * inv_std
    return (normed * gain + shift, normed, inv_std)


def norm_back(upstream, normed, inv_std, gain):
    d_normed = upstream * gain
    d_resid = inv_std * (
        d_normed
        - jnp.mean(d_normed, axis=-1, keepdims=True)
        - normed * jnp.mean(d_normed * normed, axis=-1, keepdims=True)
    )
    return (d_resid, jnp.sum(upstream * normed, axis=(0, 1)), jnp.sum(upstream, axis=(0, 1)))


def tanh_gelu(values):
    return jax.nn.gelu(values, approximate=True)


def gelu_back(preactivation_values, upstream):
    return jax.vjp(tanh_gelu, preactivation_values)[1](upstream)[0]


def per_device(
    tokens,
    w_qkv,
    bias_qv,
    w_out,
    bias_out,
    gain_one,
    bias_one,
    up_weight,
    up_bias_vector,
    down_weight,
    down_bias_vector,
    gain_two,
    bias_two,
    d_out,
    key_mask,
    rand_idx,
):
    seq_pos = lax.axis_index("seq")
    head_pos = lax.axis_index("head")
    model_width = tokens.shape[2]
    seq_count = tokens.shape[1]
    heads_dev = w_qkv.shape[1]
    head_dim = w_qkv.shape[3]
    score_scale = head_dim ** (-0.5)
    blocks_all = key_mask.shape[1] // BLOCK
    f32 = jnp.float32
    bf16 = jnp.bfloat16
    w_flat = w_qkv.reshape(model_width, heads_dev, 3 * head_dim)
    zero_bias = jnp.zeros((heads_dev, head_dim), f32)
    bias_full = jnp.stack([bias_qv[:, 0], zero_bias, bias_qv[:, 1]], axis=1).reshape(
        heads_dev, 3 * head_dim
    )
    shard_rows = lax.all_gather(tokens, "head", axis=0, tiled=True)
    projected = jnp.einsum("psd,dhc->pshc", shard_rows, w_flat, preferred_element_type=f32)
    x_rows = shard_rows
    qkv = (projected + bias_full).astype(bf16)
    span_rows = qkv.shape[0]
    per_dev = span_rows // BLOCK
    kv_all = lax.all_gather(qkv[..., head_dim:], "seq", axis=0, tiled=True)
    queries = qkv[..., :head_dim].reshape(per_dev, BLOCK, seq_count, heads_dev, head_dim)
    query_blocks = jnp.transpose(queries, (2, 0, 3, 1, 4))
    first_block = seq_pos * per_dev
    block_ids = first_block + jnp.arange(per_dev)
    glob_flag = (block_ids == 0) | (block_ids == blocks_all - 1)
    head_rand = lax.dynamic_slice_in_dim(rand_idx, head_pos * heads_dev, heads_dev, 2)
    chosen = lax.dynamic_slice_in_dim(head_rand, first_block, per_dev, 1)
    window = block_ids[:, None] + jnp.arange(-1, 2)[None, :]
    window_ok = (window >= 1) & (window <= blocks_all - 2)
    fixed_ids = jnp.concatenate(
        [
            jnp.clip(window, 0, blocks_all - 1),
            jnp.broadcast_to(jnp.array([0, blocks_all - 1], jnp.int32), (per_dev, 2)),
        ],
        axis=1,
    )
    fixed_ok = jnp.concatenate([window_ok, jnp.ones((per_dev, 2), bool)], axis=1)
    block_table = jnp.concatenate(
        [jnp.broadcast_to(fixed_ids[None, :, None, :], (seq_count, per_dev, heads_dev, 5)), chosen],
        axis=3,
    )
    table_ok = jnp.concatenate(
        [
            jnp.broadcast_to(fixed_ok[None, :, None, :], (seq_count, per_dev, heads_dev, 5)),
            jnp.ones((seq_count, per_dev, heads_dev, 3), bool),
        ],
        axis=3,
    )
    kv_blocks = kv_all.reshape(blocks_all, BLOCK, seq_count, heads_dev, 2 * head_dim)
    seq_index = jnp.arange(seq_count)[:, None, None, None]
    head_index = jnp.arange(heads_dev)[None, None, :, None]
    picked = kv_blocks[block_table, :, seq_index, head_index, :]
    keys_pick = picked[..., :head_dim].reshape(seq_count, per_dev, heads_dev, 8 * BLOCK, head_dim)
    values_pick = picked[..., head_dim:].reshape(seq_count, per_dev, heads_dev, 8 * BLOCK, head_dim)
    key_ok_all = key_mask == 1
    mask_pick = key_ok_all.reshape(seq_count, blocks_all, BLOCK)[seq_index, block_table]
    allowed = (mask_pick & table_ok[..., None]).reshape(seq_count, per_dev, heads_dev, 8 * BLOCK)
    scores = (
        jnp.einsum("sjhqd,sjhkd->sjhqk", query_blocks, keys_pick, preferred_element_type=f32)
        * score_scale
    )
    scores = jnp.where(allowed[:, :, :, None, :], scores, MASK_FILL)
    row_max = jnp.max(scores, axis=-1, keepdims=True)
    exp_scores = jnp.exp(scores - row_max)
    score_total = jnp.sum(exp_scores, axis=-1, keepdims=True)
    attn_prob = exp_scores / score_total
    prob_low = attn_prob.astype(bf16)
    out_sparse = jnp.einsum("sjhqk,sjhkd->sjhqd", prob_low, values_pick, preferred_element_type=f32)
    edge_block = jnp.where(seq_pos == 0, 0, per_dev - 1)
    q_edge = lax.dynamic_index_in_dim(query_blocks, edge_block, 1, keepdims=False)
    seq_group = 4
    group_starts = jnp.arange(0, seq_count, seq_group)

    def edge_scores_of():
        raw = (
            jnp.einsum(
                "shqd,lshd->shql", q_edge, kv_all[..., :head_dim], preferred_element_type=f32
            )
            * score_scale
        )
        return (jnp.where(key_ok_all[:, None, None, :], raw, MASK_FILL), kv_all)

    def edge_forward(first_seq):
        edge_sc, kv_group = edge_scores_of()
        edge_max = jnp.max(edge_sc, axis=-1, keepdims=True)
        edge_exp = jnp.exp(edge_sc - edge_max)
        edge_total = jnp.sum(edge_exp, axis=-1, keepdims=True)
        edge_low = (edge_exp / edge_total).astype(bf16)
        edge_res = jnp.einsum(
            "shql,lshd->shqd", edge_low, kv_group[..., head_dim:], preferred_element_type=f32
        )
        return (edge_res, edge_max + jnp.log(edge_total))

    edge_out, edge_lse = lax.map(edge_forward, group_starts)
    edge_out = edge_out.reshape(seq_count, heads_dev, BLOCK, head_dim)
    edge_lse = edge_lse.reshape(seq_count, heads_dev, BLOCK, 1)
    attn_blocks = jnp.where(glob_flag[None, :, None, None, None], edge_out[:, None], out_sparse)
    attn_low = (
        jnp.transpose(attn_blocks, (1, 3, 0, 2, 4))
        .reshape(span_rows, seq_count, heads_dev * head_dim)
        .astype(bf16)
    )
    w_out_flat = w_out.reshape(heads_dev * head_dim, model_width)
    row_slice = attn_low
    attn_sum = lax.psum_scatter(
        jnp.einsum("psc,cd->psd", row_slice, w_out_flat, preferred_element_type=f32),
        "head",
        scatter_dimension=0,
        tiled=True,
    )
    branch = attn_sum + bias_out
    first_residual_output, normed_one, inv_one = norm_fwd(
        tokens.astype(f32) + branch, gain_one, bias_one
    )
    y_one_low = first_residual_output.astype(bf16)
    shard_rows = lax.all_gather(y_one_low, "head", axis=0, tiled=True)
    y_rows = shard_rows
    preactivation_values = jnp.einsum(
        "psd,df->psf", shard_rows, up_weight, preferred_element_type=f32
    ) + up_bias_vector.astype(f32)
    hidden_activation = tanh_gelu(preactivation_values).astype(bf16)
    row_slice = hidden_activation
    ffn_sum = lax.psum_scatter(
        jnp.einsum("psf,fd->psd", row_slice, down_weight, preferred_element_type=f32),
        "head",
        scatter_dimension=0,
        tiled=True,
    )
    feedforward_output = ffn_sum + down_bias_vector
    result, normed_two, inv_two = norm_fwd(
        first_residual_output + feedforward_output, gain_two, bias_two
    )
    d_two, grad_gain_two, grad_bias_two = norm_back(
        d_out.astype(f32), normed_two, inv_two, gain_two
    )
    d_ffn = d_two.astype(bf16)
    grad_bias_back = jnp.sum(d_ffn.astype(f32), axis=(0, 1))
    shard_rows = lax.all_gather(d_ffn, "head", axis=0, tiled=True)
    d_ffn_rows = shard_rows
    d_hidden = jnp.einsum("psd,fd->psf", shard_rows, down_weight, preferred_element_type=f32)
    d_pre = gelu_back(preactivation_values, d_hidden).astype(bf16)
    row_slice = d_pre
    d_y_ffn = lax.psum_scatter(
        jnp.einsum("psf,df->psd", row_slice, up_weight, preferred_element_type=f32),
        "head",
        scatter_dimension=0,
        tiled=True,
    )
    grad_w_in = jnp.einsum("psd,psf->df", y_rows, d_pre, preferred_element_type=f32)
    grad_bias_in = jnp.sum(d_pre.astype(f32), axis=(0, 1))
    grad_w_back = jnp.einsum(
        "psf,psd->fd", hidden_activation, d_ffn_rows, preferred_element_type=f32
    )
    d_one, grad_gain_one, grad_bias_one = norm_back(d_two + d_y_ffn, normed_one, inv_one, gain_one)
    d_branch = d_one.astype(bf16)
    grad_bias_out = jnp.sum(d_branch.astype(f32), axis=(0, 1))
    shard_rows = lax.all_gather(d_branch, "head", axis=0, tiled=True)
    d_attn = jnp.einsum("psd,cd->psc", shard_rows, w_out_flat, preferred_element_type=f32)
    grad_w_out = jnp.einsum(
        "psc,psd->cd", attn_low, shard_rows, preferred_element_type=f32
    ).reshape(heads_dev, head_dim, model_width)
    d_attn_rows = d_attn.astype(bf16).reshape(span_rows, seq_count, heads_dev, head_dim)
    d_attn_low = jnp.transpose(
        d_attn_rows.reshape(per_dev, BLOCK, seq_count, heads_dev, head_dim), (2, 0, 3, 1, 4)
    )
    zero_attn = jnp.zeros_like(d_attn_low)
    d_sparse = jnp.where(glob_flag[None, :, None, None, None], zero_attn, d_attn_low)
    d_global = jnp.where(glob_flag[None, :, None, None, None], d_attn_low, zero_attn)
    d_edge = lax.dynamic_index_in_dim(d_global, edge_block, 1, keepdims=False)
    d_prob = jnp.einsum("sjhqd,sjhkd->sjhqk", d_sparse, values_pick, preferred_element_type=f32)
    row_dot = jnp.sum(d_prob * attn_prob, axis=-1, keepdims=True)
    d_scores = (attn_prob * (d_prob - row_dot)).astype(bf16)
    dq_sparse = (
        jnp.einsum("sjhqk,sjhkd->sjhqd", d_scores, keys_pick, preferred_element_type=f32)
        * score_scale
    )

    def edge_backward(first_seq):
        edge_sc, kv_group = edge_scores_of()
        edge_prob = jnp.exp(edge_sc - edge_lse)
        edge_dprob = jnp.einsum(
            "shqd,lshd->shql", d_edge, kv_group[..., head_dim:], preferred_element_type=f32
        )
        edge_dot = jnp.sum(edge_prob * edge_dprob, axis=-1, keepdims=True)
        edge_dscore = (edge_prob * (edge_dprob - edge_dot)).astype(bf16)
        edge_dq = (
            jnp.einsum(
                "shql,lshd->shqd", edge_dscore, kv_group[..., :head_dim], preferred_element_type=f32
            )
            * score_scale
        )
        return (edge_dq, edge_dot)

    dq_edge, edge_dot = lax.map(edge_backward, group_starts)
    dq_edge = dq_edge.reshape(seq_count, heads_dev, BLOCK, head_dim)
    edge_dot = edge_dot.reshape(seq_count, heads_dev, BLOCK, 1)
    dq_blocks = jnp.where(glob_flag[None, :, None, None, None], dq_edge[:, None], dq_sparse)
    d_query = jnp.transpose(dq_blocks, (1, 3, 0, 2, 4)).reshape(
        span_rows, seq_count, heads_dev, head_dim
    )
    key_grad = (
        jnp.einsum("sjhqk,sjhqd->sjhkd", d_scores, query_blocks, preferred_element_type=f32)
        * score_scale
    )
    value_grad = jnp.einsum("sjhqk,sjhqd->sjhkd", prob_low, d_sparse, preferred_element_type=f32)
    pick_grad = jnp.concatenate([key_grad, value_grad], axis=-1).reshape(
        seq_count, per_dev, heads_dev, 8, BLOCK, 2 * head_dim
    )
    block_count = lax.axis_size("seq") * span_rows // BLOCK
    range_ids = jnp.arange(block_count)
    onehot = (block_table[..., None] == range_ids).astype(f32)
    sparse_part = jnp.einsum(
        "sjhub,sjhutc->btshc", onehot, pick_grad, precision=MATMUL_ACCURACY
    ).reshape(lax.axis_size("seq") * span_rows, seq_count, heads_dev, 2 * head_dim)
    range_sc = (
        jnp.einsum("shqd,lshd->shql", q_edge, kv_all[..., :head_dim], preferred_element_type=f32)
        * score_scale
    )
    range_sc = jnp.where(key_ok_all[:, None, None, :], range_sc, MASK_FILL)
    range_prob = jnp.exp(range_sc - edge_lse)
    range_dprob = jnp.einsum(
        "shqd,lshd->shql", d_edge, kv_all[..., head_dim:], preferred_element_type=f32
    )
    range_dscore = (range_prob * (range_dprob - edge_dot)).astype(bf16)
    dense_key = (
        jnp.einsum("shql,shqd->lshd", range_dscore, q_edge, preferred_element_type=f32)
        * score_scale
    )
    dense_value = jnp.einsum(
        "shql,shqd->lshd", range_prob.astype(bf16), d_edge, preferred_element_type=f32
    )
    kv_grad = lax.psum_scatter(
        sparse_part + jnp.concatenate([dense_key, dense_value], axis=-1),
        "seq",
        scatter_dimension=0,
        tiled=True,
    )
    dqkv_low = jnp.concatenate([d_query, kv_grad], axis=-1).astype(bf16)
    grad_bias_qv = jnp.stack(
        [
            jnp.sum(dqkv_low[..., :head_dim].astype(f32), axis=(0, 1)),
            jnp.sum(dqkv_low[..., 2 * head_dim :].astype(f32), axis=(0, 1)),
        ],
        axis=1,
    )
    grad_w_qkv = jnp.einsum("psd,pshc->dhc", x_rows, dqkv_low, preferred_element_type=f32).reshape(
        model_width, heads_dev, 3, head_dim
    )
    row_slice = dqkv_low
    d_input = lax.psum_scatter(
        jnp.einsum("pshc,dhc->psd", row_slice, w_flat, preferred_element_type=f32).astype(
            jnp.bfloat16
        ),
        "head",
        scatter_dimension=0,
        tiled=True,
    ).astype(jnp.float32)
    d_tokens = (d_one + d_input).astype(bf16)
    grad_w_qkv, grad_bias_qv, grad_w_out, grad_w_in, grad_bias_in, grad_w_back = lax.psum(
        (grad_w_qkv, grad_bias_qv, grad_w_out, grad_w_in, grad_bias_in, grad_w_back), "seq"
    )
    grad_bias_out, grad_gain_one, grad_bias_one, grad_bias_back, grad_gain_two, grad_bias_two = (
        lax.psum(
            (
                grad_bias_out,
                grad_gain_one,
                grad_bias_one,
                grad_bias_back,
                grad_gain_two,
                grad_bias_two,
            ),
            ("seq", "head"),
        )
    )
    return (
        result.astype(bf16),
        d_tokens,
        grad_w_qkv,
        grad_bias_qv,
        grad_w_out,
        grad_bias_out,
        grad_gain_one,
        grad_bias_one,
        grad_w_in,
        grad_bias_in,
        grad_w_back,
        grad_bias_back,
        grad_gain_two,
        grad_bias_two,
    )


def solution(mesh):
    placed = (
        P(("seq", "head"), None, None),
        P(None, "head", None, None),
        P("head", None, None),
        P("head", None, None),
        P(),
        P(),
        P(),
        P(None, "head"),
        P("head"),
        P("head", None),
        P(),
        P(),
        P(),
        P(("seq", "head"), None, None),
        P(),
        P(),
    )
    return jax.shard_map(
        per_device,
        mesh=mesh,
        in_specs=placed,
        out_specs=(
            P(("seq", "head"), None, None),
            P(("seq", "head"), None, None),
            P(None, "head", None, None),
            P("head", None, None),
            P("head", None, None),
            P(),
            P(),
            P(),
            P(None, "head"),
            P("head"),
            P("head", None),
            P(),
            P(),
            P(),
        ),
        check_vma=False,
    )
```

profile of v0, /device:TPU:0, one launch (start us, length us, event | category | flops | bytes accessed | tf_op | source)
XLA Modules:
  0.0 1607.1 jit_solution(15258914525511534504)
XLA Ops:
  7.2 2.2 copy.51
  10.5 30.9 %all-gather.6.cloned.1.call-done = bf16[512,4,768]{2,0,1:T(8,128)(2,1)} async-done(((bf16[128,4,768]{2,0,1:T(8,128)(2,1)}), bf16[512,4,768]{2,0,1:T(8,128)(2,1)}) %all-gather.6.cloned.1.call-update) | async-done | bytes 3145744 | tf_op jit(solution)/shard_map/all_gather | solution.py:73
  41.4 4.1 add_convert_fusion
  50.8 4.2 gather_fusion
  59.6 165.5 %all-gather.8.cloned.1.call-done = bf16[4096,4,3,128]{0,3,2,1:T(8,128)(2,1)} async-done(((bf16[512,4,3,128]{0,3,2,1:T(8,128)(2,1)}), bf16[4096,4,3,128]{0,3,2,1:T(8,128)(2,1)}) %all-gather.8.cloned.1.call-update) | async-done | bytes 12582928 | tf_op jit(solution)/shard_map/all_gather | solution.py:79
  225.1 16.6 %copy.58 = bf16[4096,4,3,128]{3,0,2,1:T(8,128)(2,1)} copy(bf16[4096,4,3,128]{0,3,2,1:T(8,128)(2,1)} %all-gather.8.cloned.1.call-done) | data formatting | bytes 25165824 | tf_op jit(solution)/shard_map/all_gather | solution.py:79
  241.7 11.7 copy.59
  253.4 14.0 gather_fusion.1
  267.3 19.5 %fusion.107 = (bf16[4,8,3,8,64,64]{5,4,3,2,1,0:T(8,128)(2,1)}, bf16[4,8,3,8,64,64]{5,4,3,2,1,0:T(8,128)(2,1)}) fusion(bf16[4,8,3,8,64,128]{5,4,3,2,1,0:T(8,128)(2,1)} %bitcast.162), kind=kLoop, calls=%fused_computation.167 | loop fusion | bytes 25165824 | tf_op jit(solution)/shard_map/slice | solution.py:112
  286.8 4.5 fusion.109
  291.4 1.9 fusion.3
  293.3 2.9 copy-done.2
  296.1 13.5 fusion.53
  309.7 14.9 fusion.110
  324.6 8.7 fusion.61
  333.3 11.5 fusion.35
  344.9 2.0 copy.62
  346.9 11.8 convert_element_type.89
  358.7 4.8 fusion.111
  363.7 56.7 %reduce-scatter.6.cloned.1.call-done = f32[128,4,768]{2,0,1:T(8,128)} async-done(((f32[512,4,768]{2,0,1:T(8,128)}), f32[128,4,768]{2,0,1:T(8,128)}) %reduce-scatter.6.cloned.1.call-update) | async-done | bytes 1572880 | tf_op jit(solution)/shard_map/reduce_scatter | solution.py:164
  424.3 28.0 %all-gather.10.cloned.1.call-done = bf16[512,4,768]{2,0,1:T(8,128)(2,1)} async-done(((bf16[128,4,768]{2,0,1:T(8,128)(2,1)}), bf16[512,4,768]{2,0,1:T(8,128)(2,1)}) %all-gather.10.cloned.1.call-update) | async-done | bytes 3145744 | tf_op jit(solution)/shard_map/all_gather | solution.py:175
  452.3 4.8 fusion.75
  457.2 2.6 copy-done.75
  459.7 5.8 fusion.71
  465.6 58.4 %reduce-scatter.8.cloned.1.call-done = f32[128,4,768]{2,0,1:T(8,128)} async-done(((f32[512,4,768]{2,0,1:T(8,128)}), f32[128,4,768]{2,0,1:T(8,128)}) %reduce-scatter.8.cloned.1.call-update) | async-done | bytes 1572880 | tf_op jit(solution)/shard_map/reduce_scatter | solution.py:182
  524.0 1.9 fusion.105
  526.4 2.1 fusion.48
  528.4 2.7 convert_reduce_fusion.2
  531.2 28.6 %all-gather.12.cloned.1.call-done = bf16[512,4,768]{2,0,1:T(8,128)(2,1)} async-done(((bf16[128,4,768]{2,0,1:T(8,128)(2,1)}), bf16[512,4,768]{2,0,1:T(8,128)(2,1)}) %all-gather.12.cloned.1.call-update) | async-done | bytes 3145744 | tf_op jit(solution)/shard_map/all_gather | solution.py:197
  559.9 10.9 convert_reduce_fusion
  572.5 4.5 fusion.73
  577.1 58.4 %reduce-scatter.10.cloned.1.call-done = f32[128,4,768]{2,0,1:T(8,128)} async-done(((f32[512,4,768]{2,0,1:T(8,128)}), f32[128,4,768]{2,0,1:T(8,128)}) %reduce-scatter.10.cloned.1.call-update) | async-done | bytes 1572880 | tf_op jit(solution)/shard_map/reduce_scatter | solution.py:202
  635.5 4.1 multiply_reduce_fusion.2
  639.7 2.0 convert_reduce_fusion.3
  643.5 26.9 %all-gather.14.cloned.1.call-done = bf16[512,4,768]{2,0,1:T(8,128)(2,1)} async-done(((bf16[128,4,768]{2,0,1:T(8,128)(2,1)}), bf16[512,4,768]{2,0,1:T(8,128)(2,1)}) %all-gather.14.cloned.1.call-update) | async-done | bytes 3145744 | tf_op jit(solution)/shard_map/all_gather | solution.py:216
  670.5 3.1 convolution_convert_fusion
  676.6 14.7 multiply_reduce_fusion
  691.3 8.5 fusion.36
  699.9 12.2 convolution_bitcast_fusion
  712.1 12.3 multiply_reduce_fusion.1
  724.4 6.9 multiply_convert_fusion.1
  731.4 6.4 multiply_bitcast_fusion
  737.8 9.4 multiply_convert_fusion
  749.8 14.5 pad_maximum_fusion
  764.3 24.7 %copy.69 = f32[4,8,3,512,128]{4,3,2,1,0:T(8,128)} copy(f32[4,8,3,512,128]{3,4,2,1,0:T(8,128)} %pad_maximum_fusion) | data formatting | bytes 50331648 | tf_op jit(solution)/shard_map/concatenate | solution.py:265
  789.0 37.1 %fusion.6 = f32[64,64,4,3,128]{4,0,1,3,2:T(8,128)} fusion(f32[4,8,3,8,64,128]{5,4,3,2,1,0:T(8,128)} %bitcast.165, s32[4,8,3,8]{3,1,2,0:T(8,128)S(1)} %pad_add_fusion), kind=kOutput, calls=%fused_computation.23 | convolution fusion | flops 4831887360 | bytes 50334720 | tf_op jit(solution)/shard_map/sjhub,sjhutc->btshc/dot_general | solution.py:271
  826.1 25.1 %copy.72 = f32[64,64,4,3,128]{4,1,0,3,2:T(8,128)} copy(f32[64,64,4,3,128]{4,0,1,3,2:T(8,128)} %fusion.6) | data formatting | bytes 50331648 | tf_op jit(solution)/shard_map/sjhub,sjhutc->btshc/transpose | solution.py:271
  851.2 24.7 %copy.75 = f32[4096,4,3,128]{0,3,2,1:T(8,128)} copy(f32[4096,4,3,128]{3,0,2,1:T(8,128)} %bitcast.166) | data formatting | bytes 50331648 | tf_op jit(solution)/shard_map/reshape | solution.py:273
  876.0 25.5 %maximum_add_fusion = f32[4096,4,3,128]{0,3,2,1:T(8,128)} fusion(f32[4096,4,3,128]{0,3,2,1:T(8,128)} %copy.75, f32[4096,4,3,64]{0,3,2,1:T(8,128)} %convolution_bitcast_fusion, f32[4096,4,3,64]{0,3,2,1:T(8,128)} %multiply_bitcast_fusion), kind=kLoop, calls=%fused_computation.4 | loop fusion | flops 12582912 | bytes 75497472 | tf_op jit(solution)/shard_map/add | solution.py:292
  901.6 6.4 fusion.67
  907.9 11.1 fusion.34
  919.0 2.1 copy.66
  922.1 384.0 %reduce-scatter.12.cloned.1.call-done = f32[512,4,3,128]{0,3,2,1:T(8,128)} async-done(((f32[4096,4,3,128]{0,3,2,1:T(8,128)}), f32[512,4,3,128]{0,3,2,1:T(8,128)}) %reduce-scatter.12.cloned.1.call-update) | async-done | bytes 3145744 | tf_op jit(solution)/shard_map/reduce_scatter | solution.py:291
  1306.1 2.1 convert.8
  1308.2 4.1 bitcast_convert_fusion
  1312.7 7.1 convolution_bitcast_fusion.2
  1319.7 8.2 convolution_bitcast_fusion.1
  1329.6 3.2 fusion.30
  1335.5 42.5 %all-reduce.2 = (f32[768]{0:T(1024)}, f32[768]{0:T(1024)}, f32[768]{0:T(1024)}, f32[768]{0:T(1024)}, f32[768]{0:T(1024)}, /*index=5*/f32[768]{0:T(1024)}) all-reduce(f32[768]{0:T(1024)S(1)} %copy-done.61, f32[768]{0:T(1024)S(1)} %copy-done.55, f32[768]{0:T(1024)S(1)} %copy-done.56, ...), channel_id=1, replica_groups=mesh['seq'=8,'head'=4] {'seq','head'}, use_global_device_ids=true, to_apply=%region_25.26 | all-reduce | flops 4608 | bytes 36864 | tf_op jit(solution)/shard_map/psum | solution.py:322
  1379.5 23.4 %all-reduce.3 = (f32[3,2,64]{2,0,1:T(4,128)S(1)}, f32[768]{0:T(1024)}) all-reduce(f32[3,2,64]{2,0,1:T(4,128)S(1)} %pad_maximum_fusion.5, f32[768]{0:T(1024)S(1)} %copy-done.68), channel_id=1, replica_groups=mesh['seq'=8,'head'=4] {'seq'}, use_global_device_ids=true, to_apply=%region_22.23 | all-reduce | flops 1152 | bytes 9216 | tf_op jit(solution)/shard_map/psum | solution.py:318
  1403.6 2.3 add_convert_fusion.1
  1407.3 185.0 %all-reduce.7.cloned.1.call-done = (f32[768,3,3,64]{0,3,2,1:T(8,128)}, f32[3,64,768]{2,1,0:T(8,128)}, f32[768,768]{1,0:T(8,128)}, f32[768,768]{1,0:T(8,128)}) async-done(((f32[768,3,3,64]{0,3,2,1:T(8,128)}, f32[3,64,768]{2,1,0:T(8,128)}, f32[768,768]{1,0:T(8,128)}, f32[768,768]{1,0:T(8,128)}), (f32[768,3,3,64]{0,3,2,1:T(8,128)}, f32[3,64,768]{2,1,0:T(8,128)}, f32[768,768]{1,0:T(8,128)}, ...) | async-done | bytes 7077904 | tf_op jit(solution)/shard_map/psum | solution.py:318
  1592.3 2.9 copy.124
  1595.3 2.0 copy.125
  (244 shorter events, 36.3 us)
Async XLA Ops:
  7.2 452.6 %copy-start = (bf16[768,768]{1,0:T(8,128)(2,1)S(1)}, bf16[768,768]{1,0:T(8,128)(2,1)}, u32[]{:S(2)}) copy-start(bf16[768,768]{1,0:T(8,128)(2,1)} %param.26) | copy-start | bytes 3538948
  7.2 34.2 %all-gather.6.cloned.1.call-start = ((), (), s32[]{:S(2)}) async-start(), calls=%async_computation.5 | async-start | bytes 3932160 | tf_op jit(solution)/shard_map/all_gather | solution.py:73
  9.4 215.6 %all-gather.8.cloned.1.call-start = ((), (), s32[]{:S(2)}) async-start(), calls=%async_computation.6 | async-start | bytes 14155776 | tf_op jit(solution)/shard_map/all_gather | solution.py:79
  48.3 7.8 slice-start.3
  48.3 372.0 %reduce-scatter.6.cloned.1.call-start = ((), (), s32[]{:S(2)}) async-start(), calls=%async_computation.7 | async-start | bytes 7864320 | tf_op jit(solution)/shard_map/reduce_scatter | solution.py:164
  56.1 277.2 %copy-start.62 = (pred[8]{0:T(512)(128)(4,1)}, pred[8]{0:T(512)(128)(4,1)S(1)}, u32[]{:S(2)}) copy-start(pred[8]{0:T(512)(128)(4,1)S(1)} %compare_or_fusion) | copy-start | bytes 28
  57.0 184.7 %copy-start.8 = (bf16[8,64,4,3,64]{1,0,4,3,2:T(8,128)(2,1)}, bf16[8,64,4,3,64]{1,0,4,3,2:T(8,128)(2,1)S(1)}, u32[]{:S(2)}) copy-start(bf16[8,64,4,3,64]{1,0,4,3,2:T(8,128)(2,1)S(1)} %reshape.245) | copy-start | bytes 2359300
  59.6 227.2 %copy-start.23 = (bf16[1,64,4,3,64]{4,1,3,2,0:T(8,128)(2,1)}, bf16[1,64,4,3,64]{4,1,3,2,0:T(8,128)(2,1)S(1)}, u32[]{:S(2)}) copy-start(bf16[1,64,4,3,64]{4,1,3,2,0:T(8,128)(2,1)S(1)} %copy.98) | copy-start | bytes 294916
  267.3 19.5 %copy-start.26 = (pred[4,4096]{1,0:T(4,128)(4,1)S(1)}, pred[4,4096]{1,0:T(4,128)(4,1)}, u32[]{:S(2)}) copy-start(pred[4,4096]{1,0:T(4,128)(4,1)} %copy-done.25) | copy-start | bytes 49156
  291.4 33.2 %copy-start.34 = (f32[4,3,64]{2,1,0:T(4,128)}, f32[4,3,64]{2,1,0:T(4,128)S(1)}, u32[]{:S(2)}) copy-start(f32[4,3,64]{2,1,0:T(4,128)S(1)} %get-tuple-element.120) | copy-start | bytes 9220
  296.1 28.5 %copy-start.45 = (f32[4,3,64]{2,1,0:T(4,128)}, f32[4,3,64]{2,1,0:T(4,128)S(1)}, u32[]{:S(2)}) copy-start(f32[4,3,64]{2,1,0:T(4,128)S(1)} %fusion.3) | copy-start | bytes 9220
  296.1 13.5 copy-start.39
  324.6 8.7 copy-start.36
  363.6 56.8 %copy-start.18 = (bf16[128,4,768]{2,1,0:T(4,128)(2,1)S(1)}, bf16[128,4,768]{2,1,0:T(4,128)(2,1)}, u32[]{:S(2)}) copy-start(bf16[128,4,768]{2,1,0:T(4,128)(2,1)} %param.17) | copy-start | bytes 2359300
  363.6 56.8 %copy-start.69 = (f32[768]{0:T(1024)S(1)}, f32[768]{0:T(1024)}, u32[]{:S(2)}) copy-start(f32[768]{0:T(1024)} %param.21) | copy-start | bytes 9220
  363.6 58.8 %copy-start.28 = (f32[768]{0:T(1024)S(1)}, f32[768]{0:T(1024)}, u32[]{:S(2)}) copy-start(f32[768]{0:T(1024)} %param.22) | copy-start | bytes 9220
  363.6 58.8 %copy-start.60 = (f32[768]{0:T(1024)S(1)}, f32[768]{0:T(1024)}, u32[]{:S(2)}) copy-start(f32[768]{0:T(1024)} %param.23) | copy-start | bytes 9220
  363.6 88.7 %all-gather.10.cloned.1.call-start = ((), (), s32[]{:S(2)}) async-start(), calls=%async_computation.8 | async-start | bytes 3932160 | tf_op jit(solution)/shard_map/all_gather | solution.py:175
  422.0 217.7 %copy-start.3 = (f32[128,4,768]{2,0,1:T(8,128)}, f32[128,4,768]{2,0,1:T(8,128)S(1)}, u32[]{:S(2)}) copy-start(f32[128,4,768]{2,0,1:T(8,128)S(1)} %get-tuple-element.112) | copy-start | bytes 4718596
  422.0 217.7 %copy-start.30 = (f32[128,4]{0,1:T(4,128)}, f32[128,4]{0,1:T(4,128)S(1)}, u32[]{:S(2)}) copy-start(f32[128,4]{0,1:T(4,128)S(1)} %broadcast_multiply_fusion.6) | copy-start | bytes 6148
  422.4 217.4 %copy-start.32 = (f32[128,4]{0,1:T(4,128)}, f32[128,4]{0,1:T(4,128)S(1)}, u32[]{:S(2)}) copy-start(f32[128,4]{0,1:T(4,128)S(1)} %add_rsqrt_fusion.1) | copy-start | bytes 6148
  423.6 100.5 %reduce-scatter.8.cloned.1.call-start = ((), (), s32[]{:S(2)}) async-start(), calls=%async_computation.9 | async-start | bytes 7864320 | tf_op jit(solution)/shard_map/reduce_scatter | solution.py:182
  424.3 32.8 %copy-start.66 = (f32[768]{0:T(1024)}, f32[768]{0:T(1024)S(1)}, u32[]{:S(2)}) copy-start(f32[768]{0:T(1024)S(1)} %convert_element_type.91) | copy-start | bytes 9220
  465.5 60.8 %copy-start.11 = (bf16[128,4,768]{2,1,0:T(4,128)(2,1)S(1)}, bf16[128,4,768]{2,1,0:T(4,128)(2,1)}, u32[]{:S(2)}) copy-start(bf16[128,4,768]{2,1,0:T(4,128)(2,1)} %param.30) | copy-start | bytes 2359300
  465.6 94.3 %all-gather.12.cloned.1.call-start = ((), (), s32[]{:S(2)}) async-start(), calls=%async_computation.10 | async-start | bytes 3932160 | tf_op jit(solution)/shard_map/all_gather | solution.py:197
  531.2 104.3 %reduce-scatter.10.cloned.1.call-start = ((), (), s32[]{:S(2)}) async-start(), calls=%async_computation.11 | async-start | bytes 7864320 | tf_op jit(solution)/shard_map/reduce_scatter | solution.py:202
  559.9 12.6 copy-start.72
  577.0 58.6 %copy-start.40 = (f32[768]{0:T(1024)S(1)}, f32[768]{0:T(1024)}, u32[]{:S(2)}) copy-start(f32[768]{0:T(1024)} %param.28) | copy-start | bytes 9220
  577.0 58.6 %copy-start.44 = (f32[128,4]{0,1:T(4,128)S(1)}, f32[128,4]{0,1:T(4,128)}, u32[]{:S(2)}) copy-start(f32[128,4]{0,1:T(4,128)} %copy-done.43) | copy-start | bytes 6148
  577.0 58.6 %copy-start.52 = (f32[128,4]{0,1:T(4,128)S(1)}, f32[128,4]{0,1:T(4,128)}, u32[]{:S(2)}) copy-start(f32[128,4]{0,1:T(4,128)} %copy-done.51) | copy-start | bytes 6148
  577.0 58.6 %copy-start.54 = (f32[128,4]{0,1:T(4,128)S(1)}, f32[128,4]{0,1:T(4,128)}, u32[]{:S(2)}) copy-start(f32[128,4]{0,1:T(4,128)} %copy-done.53) | copy-start | bytes 6148
  577.0 58.6 %copy-start.65 = (f32[768]{0:T(1024)S(1)}, f32[768]{0:T(1024)}, u32[]{:S(2)}) copy-start(f32[768]{0:T(1024)} %param.29) | copy-start | bytes 9220
  577.0 64.8 %copy-start.63 = (pred[8]{0:T(512)(128)(4,1)S(1)}, pred[8]{0:T(512)(128)(4,1)}, u32[]{:S(2)}) copy-start(pred[8]{0:T(512)(128)(4,1)} %copy-done.62) | copy-start | bytes 28
  577.0 66.4 %copy-start.42 = (s32[8,5]{1,0:T(8,128)S(1)}, s32[8,5]{1,0:T(8,128)}, u32[]{:S(2)}) copy-start(s32[8,5]{1,0:T(8,128)} %copy-done.41) | copy-start | bytes 484
  577.0 66.4 %copy-start.35 = (f32[4,3,64]{2,1,0:T(4,128)S(1)}, f32[4,3,64]{2,1,0:T(4,128)}, u32[]{:S(2)}) copy-start(f32[4,3,64]{2,1,0:T(4,128)} %copy-done.34) | copy-start | bytes 9220
  577.0 66.4 %copy-start.46 = (f32[4,3,64]{2,1,0:T(4,128)S(1)}, f32[4,3,64]{2,1,0:T(4,128)}, u32[]{:S(2)}) copy-start(f32[4,3,64]{2,1,0:T(4,128)} %copy-done.45) | copy-start | bytes 9220
  577.1 93.4 %copy-start.27 = (bf16[3,64,768]{2,1,0:T(8,128)(2,1)S(1)}, bf16[3,64,768]{2,1,0:T(8,128)(2,1)}, u32[]{:S(2)}) copy-start(bf16[3,64,768]{2,1,0:T(8,128)(2,1)} %param.20) | copy-start | bytes 884740
  577.1 93.4 %all-gather.14.cloned.1.call-start = ((), (), s32[]{:S(2)}) async-start(), calls=%async_computation.12 | async-start | bytes 3932160 | tf_op jit(solution)/shard_map/all_gather | solution.py:216
  641.8 664.3 %reduce-scatter.12.cloned.1.call-start = ((), (), s32[]{:S(2)}) async-start(), calls=%async_computation.13 | async-start | bytes 28311552 | tf_op jit(solution)/shard_map/reduce_scatter | solution.py:291
  643.5 33.1 %copy-start.37 = (f32[4,8,3,64]{3,2,1,0:T(4,128)S(1)}, f32[4,8,3,64]{3,2,1,0:T(4,128)}, u32[]{:S(2)}) copy-start(f32[4,8,3,64]{3,2,1,0:T(4,128)} %copy-done.36) | copy-start | bytes 73732
  643.5 33.1 %copy-start.64 = (pred[8]{0:T(512)(128)(4,1)S(1)}, pred[8]{0:T(512)(128)(4,1)}, u32[]{:S(2)}) copy-start(pred[8]{0:T(512)(128)(4,1)} %copy-done.62) | copy-start | bytes 28
  676.6 14.7 copy-start.20
  699.9 24.5 %slice-start = ((s8[12582912]{0:T(1024)(128)(4,1)}), s8[4194304]{0:T(1024)(128)(4,1)S(1)}, s32[]{:S(2)}) async-start(s8[12582912]{0:T(1024)(128)(4,1)} %bitcast.160), calls=%async_computation.16 | async-start | bytes 8388608
  699.9 24.5 %slice-start.1 = ((s8[12582912]{0:T(1024)(128)(4,1)}), s8[4194304]{0:T(1024)(128)(4,1)S(1)}, s32[]{:S(2)}) async-start(s8[12582912]{0:T(1024)(128)(4,1)} %bitcast.160), calls=%async_computation.17 | async-start | bytes 8388608
  712.0 12.3 slice-start.2
  724.4 6.9 copy-start.24
  731.3 6.5 copy-start.7
  737.8 9.4 copy-start.9
  901.5 502.0 %reduce-scatter.14.cloned.1.call-start = ((), (), s32[]{:S(2)}) async-start(), calls=%async_computation.14 | async-start | bytes 3932160 | tf_op jit(solution)/shard_map/reduce_scatter | solution.py:309
  919.0 389.2 %copy-start.73 = (bf16[768,3,3,64]{0,3,2,1:T(8,128)(2,1)S(1)}, bf16[768,3,3,64]{0,3,2,1:T(8,128)(2,1)}, u32[]{:S(2)}) copy-start(bf16[768,3,3,64]{0,3,2,1:T(8,128)(2,1)} %param.18) | copy-start | bytes 2654212
  1308.2 21.4 %copy-start.15 = (bf16[512,4,3,128]{0,3,2,1:T(8,128)(2,1)}, bf16[512,4,3,128]{0,3,2,1:T(8,128)(2,1)S(1)}, u32[]{:S(2)}) copy-start(bf16[512,4,3,128]{0,3,2,1:T(8,128)(2,1)S(1)} %convert.8) | copy-start | bytes 4718596
  1312.3 7.4 copy-start.67
  1312.3 280.0 %all-reduce.7.cloned.1.call-start = ((), (), s32[]{:S(2)}) async-start(), calls=%async_computation.15 | async-start | bytes 14155776 | tf_op jit(solution)/shard_map/psum | solution.py:318
  1312.6 7.1 copy-start.71
  1319.7 8.3 copy-start.13
  1319.7 8.3 copy-start.17
  1319.7 9.9 copy-start.70
  1332.8 46.6 %copy-start.68 = (f32[768]{0:T(1024)S(1)}, f32[768]{0:T(1024)}, u32[]{:S(2)}) copy-start(f32[768]{0:T(1024)} %get-tuple-element.128) | copy-start | bytes 9220
  1332.9 70.7 %copy-start.4 = (f32[128,4,768]{2,0,1:T(8,128)S(1)}, f32[128,4,768]{2,0,1:T(8,128)}, u32[]{:S(2)}) copy-start(f32[128,4,768]{2,0,1:T(8,128)} %copy-done.3) | copy-start | bytes 4718596
  1332.9 70.7 %copy-start.29 = (f32[768]{0:T(1024)S(1)}, f32[768]{0:T(1024)}, u32[]{:S(2)}) copy-start(f32[768]{0:T(1024)} %param.22) | copy-start | bytes 9220
  1332.9 70.6 %copy-start.31 = (f32[128,4]{0,1:T(4,128)S(1)}, f32[128,4]{0,1:T(4,128)}, u32[]{:S(2)}) copy-start(f32[128,4]{0,1:T(4,128)} %copy-done.30) | copy-start | bytes 6148
  1332.9 70.6 %copy-start.33 = (f32[128,4]{0,1:T(4,128)S(1)}, f32[128,4]{0,1:T(4,128)}, u32[]{:S(2)}) copy-start(f32[128,4]{0,1:T(4,128)} %copy-done.32) | copy-start | bytes 6148
  1332.9 70.6 %copy-start.48 = (f32[128,4]{0,1:T(4,128)S(1)}, f32[128,4]{0,1:T(4,128)}, u32[]{:S(2)}) copy-start(f32[128,4]{0,1:T(4,128)} %copy-done.47) | copy-start | bytes 6148
  1332.9 70.6 %copy-start.50 = (f32[128,4]{0,1:T(4,128)S(1)}, f32[128,4]{0,1:T(4,128)}, u32[]{:S(2)}) copy-start(f32[128,4]{0,1:T(4,128)} %copy-done.49) | copy-start | bytes 6148
  (27 other events, 84.3 us)
Sparse Core Ops, SparseCore 0:
  10.2 31.2 all-gather.5
  48.5 176.5 all-gather.7
  363.7 56.5 reduce-scatter.5
  423.7 28.5 all-gather.9
  465.7 58.3 reduce-scatter.7
  531.3 28.5 all-gather.11
  577.1 58.3 reduce-scatter.9
  641.9 28.5 all-gather.13
  901.6 404.4 reduce-scatter.11
  1312.5 37.5 reduce-scatter.13
  1355.6 236.6 all-reduce.6
where the time goes:
time: 1620 us; the launch traced here: 1610 us
  waiting for transfers between devices  1020 us (63%)
  matrix products  211 us (13%)
  local copies, waits for them, and re-layouts  195 us (12%)
  other arithmetic  96.7 us (6%)
  blocking collectives  65.9 us (4%)
    reduce_scatter x1, waiting for transfers between devices, per_device(): lax.psum_scatter(sparse_part + jnp.concatenate([dense_key, dense_value],...  384 us
    psum x1, waiting for transfers between devices, per_device(): lax.psum((grad_w_qkv, grad_bias_qv, grad_w_out, grad_w_in, grad_bias_in,...  185 us
    all_gather x1, waiting for transfers between devices, per_device(): kv_all = lax.all_gather(qkv[..., head_dim:], 'seq', axis=0, tiled=True)  165 us
    reduce_scatter x1, waiting for transfers between devices, per_device(): lax.psum_scatter(jnp.einsum('psf,fd->psd', row_slice, down_weight, prefer...  58.4 us
    reduce_scatter x1, waiting for transfers between devices, per_device(): lax.psum_scatter(jnp.einsum('psf,df->psd', row_slice, up_weight, preferre...  58.4 us
    reduce_scatter x1, waiting for transfers between devices, per_device(): lax.psum_scatter(jnp.einsum('psc,cd->psd', row_slice, w_out_flat, preferr...  56.7 us
    psum x1, blocking collectives, per_device(): lax.psum((grad_bias_out, grad_gain_one, grad_bias_one, grad_bias_back, gr...  42.5 us
    dot_general x1, matrix products, per_device(): jnp.einsum('sjhub,sjhutc->btshc', onehot, pick_grad, precision=MATMUL_ACC...  37.1 us
  transfers between devices with their start and end apart: 11, of which 10 were waited for; matrix products, arithmetic and copies ran while one was open for 4% of the time, Pallas kernels for 0%

commit v1 on v0

v1 whole, which is shorter than its diff:
```python
import functools

import jax
import jax.numpy as jnp
import numpy as np
from jax import lax
from jax.experimental import pallas as pl
from jax.experimental.pallas import tpu as pltpu
from jax.sharding import Mesh
from jax.sharding import PartitionSpec as P

BLOCK = 64
PICKS = 8
CHUNK = 512
NORM_EPS = 1e-12
MASK_FILL = -1000000000.0

f32 = jnp.float32
bf16 = jnp.bfloat16

PLANE = ("part", "hy", "hc")
HEAD = ("hy", "hc")
SEQ = ("sq", "part")


def norm_fwd(resid, gain, shift):
    row_mean = jnp.mean(resid, axis=-1, keepdims=True)
    centred = resid - row_mean
    inv_std = lax.rsqrt(jnp.mean(centred * centred, axis=-1, keepdims=True) + NORM_EPS)
    normed = centred * inv_std
    return (normed * gain + shift, normed, inv_std)


def norm_back(upstream, normed, inv_std, gain):
    d_normed = upstream * gain
    d_resid = inv_std * (
        d_normed
        - jnp.mean(d_normed, axis=-1, keepdims=True)
        - normed * jnp.mean(d_normed * normed, axis=-1, keepdims=True)
    )
    return (d_resid, jnp.sum(upstream * normed, axis=0), jnp.sum(upstream, axis=0))


def tanh_gelu(values):
    return jax.nn.gelu(values, approximate=True)


def gelu_back(preactivation_values, upstream):
    return jax.vjp(tanh_gelu, preactivation_values)[1](upstream)[0]


def dot_nt(a, b):
    return lax.dot_general(a, b, (((1,), (1,)), ((), ())), preferred_element_type=f32)


def dot_nn(a, b):
    return lax.dot_general(a, b, (((1,), (0,)), ((), ())), preferred_element_type=f32)


def dot_tn(a, b):
    return lax.dot_general(a, b, (((0,), (0,)), ((), ())), preferred_element_type=f32)


def gathered(kv_ref, table_ref, base, cols):
    return jnp.concatenate(
        [
            kv_ref[pl.ds(pl.multiple_of(table_ref[base + u] * BLOCK, BLOCK), BLOCK), cols]
            for u in range(PICKS)
        ],
        axis=0,
    )


def lane_pick(values, lane):
    lanes = lax.broadcasted_iota(jnp.int32, values.shape, 1)
    return jnp.sum(jnp.where(lanes == lane, values, 0.0), axis=1, keepdims=True)


def attn_fwd_kernel(heads, hd, table_ref, edge_ref, q_ref, kv_ref, bias_ref, mask_ref, o_ref, lse_ref, s_ref):
    wide = 2 * hd
    blocks = q_ref.shape[0] // BLOCK
    chunks = kv_ref.shape[0] // CHUNK
    lanes = lax.broadcasted_iota(jnp.int32, (BLOCK, 128), 1)

    def one(jl, carry):
        rows = pl.ds(pl.multiple_of(jl * BLOCK, BLOCK), BLOCK)
        outs = []
        lse_tile = jnp.zeros((BLOCK, 128), f32)
        for h in range(heads):
            cols = slice(h * wide, (h + 1) * wide)
            kvg = gathered(kv_ref, table_ref, (jl * heads + h) * PICKS, cols)
            s = dot_nt(q_ref[rows, cols], kvg) + bias_ref[jl, h : h + 1, :]
            top = jnp.max(s, axis=1, keepdims=True)
            p = jnp.exp(s - top)
            total = jnp.sum(p, axis=1, keepdims=True)
            low = (p * (1.0 / total)).astype(bf16)
            outs.append(dot_nn(low, kvg)[:, hd:])
            lse_tile = jnp.where(lanes == h, top + jnp.log(total), lse_tile)
        o_ref[rows, :] = jnp.concatenate(outs, axis=1).astype(bf16)
        lse_ref[rows, :] = lse_tile
        return carry

    lax.fori_loop(0, blocks, one, 0)

    def edge(jl):
        rows = slice(jl * BLOCK, (jl + 1) * BLOCK)
        outs = []
        lse_tile = jnp.zeros((BLOCK, 128), f32)
        for h in range(heads):
            cols = slice(h * wide, (h + 1) * wide)
            q = q_ref[rows, cols]

            def score(c, top):
                part = pl.ds(pl.multiple_of(c * CHUNK, CHUNK), CHUNK)
                s = dot_nt(q, kv_ref[part, cols]) + mask_ref[:, part]
                s_ref[:, part] = s
                return jnp.maximum(top, jnp.max(s, axis=1, keepdims=True))

            top = lax.fori_loop(0, chunks, score, jnp.full((BLOCK, 1), -3e38, f32))

            def add(c, total):
                part = pl.ds(pl.multiple_of(c * CHUNK, CHUNK), CHUNK)
                return total + jnp.sum(jnp.exp(s_ref[:, part] - top), axis=1, keepdims=True)

            total = lax.fori_loop(0, chunks, add, jnp.zeros((BLOCK, 1), f32))
            inv = 1.0 / total

            def out(c, acc):
                part = pl.ds(pl.multiple_of(c * CHUNK, CHUNK), CHUNK)
                low = (jnp.exp(s_ref[:, part] - top) * inv).astype(bf16)
                return acc + dot_nn(low, kv_ref[part, cols])

            acc = lax.fori_loop(0, chunks, out, jnp.zeros((BLOCK, wide), f32))
            outs.append(acc[:, hd:])
            lse_tile = jnp.where(lanes == h, top + jnp.log(total), lse_tile)
        o_ref[rows, :] = jnp.concatenate(outs, axis=1).astype(bf16)
        lse_ref[rows, :] = lse_tile

    @pl.when(edge_ref[0] == 1)
    def _():
        edge(0)

    @pl.when(edge_ref[1] == 1)
    def _():
        edge(blocks - 1)


def attn_bwd_kernel(
    heads, hd, scale, table_ref, edge_ref, qd_ref, kv_ref, bias_ref, mask_ref, lse_ref, dq_ref, dkv_ref, acc_ref, p_ref, dp_ref
):
    wide = 2 * hd
    blocks = qd_ref.shape[0] // BLOCK
    chunks = kv_ref.shape[0] // CHUNK
    left = lax.broadcasted_iota(jnp.int32, (BLOCK, wide), 1) < hd
    nil = jnp.zeros((BLOCK, wide), bf16)

    def clear(c, carry):
        part = pl.ds(pl.multiple_of(c * CHUNK, CHUNK), CHUNK)
        acc_ref[part, :] = jnp.zeros((CHUNK, heads * wide), f32)
        return carry

    lax.fori_loop(0, chunks, clear, 0)

    def stacked(qd):
        return jnp.concatenate([jnp.where(left, qd, nil), jnp.where(left, nil, qd)], axis=0)

    def one(jl, carry):
        rows = pl.ds(pl.multiple_of(jl * BLOCK, BLOCK), BLOCK)
        lse_tile = lse_ref[rows, :]
        outs = []
        for h in range(heads):
            cols = slice(h * wide, (h + 1) * wide)
            base = (jl * heads + h) * PICKS
            kvg = gathered(kv_ref, table_ref, base, cols)
            both = stacked(qd_ref[rows, cols])
            prod = dot_nt(both, kvg)
            p = jnp.exp(prod[:BLOCK] + bias_ref[jl, h : h + 1, :] - lane_pick(lse_tile, h))
            dp = prod[BLOCK:]
            dot_row = jnp.sum(p * dp, axis=1, keepdims=True)
            ds = (p * (dp - dot_row)).astype(bf16)
            outs.append(dot_nn(ds, kvg)[:, :hd])
            dkv = dot_tn(jnp.concatenate([ds, p.astype(bf16)], axis=0), both)
            for u in range(PICKS):
                place = pl.ds(pl.multiple_of(table_ref[base + u] * BLOCK, BLOCK), BLOCK)
                acc_ref[place, cols] += dkv[u * BLOCK : (u + 1) * BLOCK]
        dq_ref[rows, :] = (jnp.concatenate(outs, axis=1) * scale).astype(bf16)
        return carry

    lax.fori_loop(edge_ref[0], blocks - edge_ref[1], one, 0)

    def edge(jl):
        rows = slice(jl * BLOCK, (jl + 1) * BLOCK)
        lse_tile = lse_ref[rows, :]
        outs = []
        for h in range(heads):
            cols = slice(h * wide, (h + 1) * wide)
            both = stacked(qd_ref[rows, cols])
            lse = lane_pick(lse_tile, h)

            def first(c, total):
                part = pl.ds(pl.multiple_of(c * CHUNK, CHUNK), CHUNK)
                prod = dot_nt(both, kv_ref[part, cols])
                p = jnp.exp(prod[:BLOCK] + mask_ref[:, part] - lse)
                dp = prod[BLOCK:]
                p_ref[:, part] = p
                dp_ref[:, part] = dp
                return total + jnp.sum(p * dp, axis=1, keepdims=True)

            dot_row = lax.fori_loop(0, chunks, first, jnp.zeros((BLOCK, 1), f32))

            def second(c, dq):
                part = pl.ds(pl.multiple_of(c * CHUNK, CHUNK), CHUNK)
                p = p_ref[:, part]
                ds = (p * (dp_ref[:, part] - dot_row)).astype(bf16)
                acc_ref[part, cols] += dot_tn(jnp.concatenate([ds, p.astype(bf16)], axis=0), both)
                return dq + dot_nn(ds, kv_ref[part, cols])

            dq = lax.fori_loop(0, chunks, second, jnp.zeros((BLOCK, wide), f32))
            outs.append(dq[:, :hd])
        dq_ref[rows, :] = (jnp.concatenate(outs, axis=1) * scale).astype(bf16)

    @pl.when(edge_ref[0] == 1)
    def _():
        edge(0)

    @pl.when(edge_ref[1] == 1)
    def _():
        edge(blocks - 1)

    def put(c, carry):
        part = pl.ds(pl.multiple_of(c * CHUNK, CHUNK), CHUNK)
        dkv_ref[part, :] = acc_ref[part, :].astype(bf16)
        return carry

    lax.fori_loop(0, chunks, put, 0)


SMEM_SPEC = pl.BlockSpec(memory_space=pltpu.SMEM)
VMEM_SPEC = pl.BlockSpec(memory_space=pltpu.VMEM)
VMEM_LIMIT = 48 * 1024 * 1024


def attn_forward(heads, hd, table, edges, q, kv, bias, mask):
    rows, keys = q.shape[0], kv.shape[0]
    return pl.pallas_call(
        functools.partial(attn_fwd_kernel, heads, hd),
        out_shape=(
            jax.ShapeDtypeStruct((rows, heads * hd), bf16),
            jax.ShapeDtypeStruct((rows, 128), f32),
        ),
        in_specs=[SMEM_SPEC] * 2 + [VMEM_SPEC] * 4,
        out_specs=(VMEM_SPEC, VMEM_SPEC),
        scratch_shapes=[pltpu.VMEM((BLOCK, keys), f32)],
        compiler_params=pltpu.CompilerParams(vmem_limit_bytes=VMEM_LIMIT),
        cost_estimate=pl.CostEstimate(
            flops=4 * rows * heads * CHUNK * 2 * hd, bytes_accessed=8 << 20, transcendentals=rows * heads * CHUNK
        ),
        name="attn_forward",
    )(table, edges, q, kv, bias, mask)


def attn_backward(heads, hd, scale, table, edges, qd, kv, bias, mask, lse):
    rows, keys = qd.shape[0], kv.shape[0]
    return pl.pallas_call(
        functools.partial(attn_bwd_kernel, heads, hd, scale),
        out_shape=(
            jax.ShapeDtypeStruct((rows, heads * hd), bf16),
            jax.ShapeDtypeStruct((keys, heads * 2 * hd), bf16),
        ),
        in_specs=[SMEM_SPEC] * 2 + [VMEM_SPEC] * 5,
        out_specs=(VMEM_SPEC, VMEM_SPEC),
        scratch_shapes=[
            pltpu.VMEM((keys, heads * 2 * hd), f32),
            pltpu.VMEM((BLOCK, keys), f32),
            pltpu.VMEM((BLOCK, keys), f32),
        ],
        compiler_params=pltpu.CompilerParams(vmem_limit_bytes=VMEM_LIMIT),
        cost_estimate=pl.CostEstimate(
            flops=10 * rows * heads * CHUNK * 2 * hd, bytes_accessed=12 << 20, transcendentals=rows * heads * CHUNK
        ),
        name="attn_backward",
    )(table, edges, qd, kv, bias, mask, lse)


def per_device(
    tokens,
    w_qkv,
    bias_qv,
    w_out,
    bias_out,
    gain_one,
    bias_one,
    up_weight,
    up_bias_vector,
    down_weight,
    down_bias_vector,
    gain_two,
    bias_two,
    d_out,
    key_mask,
    rand_idx,
):
    sq = lax.axis_index("sq")
    part = lax.axis_index("part")
    head = lax.axis_index(HEAD)
    parts = lax.axis_size("part")
    groups = lax.axis_size(HEAD)
    span, seqs, width = tokens.shape
    heads, hd = w_qkv.shape[1], w_qkv.shape[3]
    scale = hd ** (-0.5)
    length = key_mask.shape[1]
    blocks_all = length // BLOCK
    per_chunk = groups * span // BLOCK
    mine = seqs * per_chunk

    tok = lax.all_to_all(jnp.transpose(tokens, (1, 0, 2)), "sq", 0, 0, tiled=True)
    x_all = lax.all_gather(tok, PLANE, axis=0, tiled=False)
    d_res = lax.all_to_all(jnp.transpose(d_out, (1, 0, 2)), "sq", 0, 0, tiled=True)

    w_out_full = lax.all_gather(w_out.reshape(heads * hd, width), HEAD, axis=0, tiled=False)
    up_full = lax.all_gather(up_weight, HEAD, axis=0, tiled=False)
    down_full = lax.all_gather(down_weight, HEAD, axis=0, tiled=False)
    up_bias_full = lax.all_gather(up_bias_vector.astype(f32), HEAD, axis=0, tiled=False)

    chunk_ids = jnp.arange(seqs) * parts + part
    block_ids = (chunk_ids[:, None] * per_chunk + jnp.arange(per_chunk)[None, :]).reshape(mine)
    rand_seq = lax.dynamic_index_in_dim(rand_idx, sq, 0, keepdims=False)
    rand_head = lax.dynamic_slice_in_dim(rand_seq, head * heads, heads, 1)
    chosen = jnp.take(rand_head, block_ids, axis=0)
    window = block_ids[:, None] + jnp.arange(-1, 2)[None, :]
    window_ok = (window >= 1) & (window <= blocks_all - 2)
    fixed_ids = jnp.concatenate(
        [
            jnp.clip(window, 0, blocks_all - 1),
            jnp.broadcast_to(jnp.array([0, blocks_all - 1], jnp.int32), (mine, 2)),
        ],
        axis=1,
    )
    fixed_ok = jnp.concatenate([window_ok, jnp.ones((mine, 2), bool)], axis=1)
    table = jnp.concatenate(
        [jnp.broadcast_to(fixed_ids[:, None, :], (mine, heads, 5)), chosen], axis=2
    )
    table_ok = jnp.concatenate(
        [
            jnp.broadcast_to(fixed_ok[:, None, :], (mine, heads, 5)),
            jnp.ones((mine, heads, PICKS - 5), bool),
        ],
        axis=2,
    )
    mask_seq = lax.dynamic_index_in_dim(key_mask, sq, 0, keepdims=False)
    mask_blocks = (mask_seq == 1).reshape(blocks_all, BLOCK).astype(bf16)
    onehot = (table[..., None] == jnp.arange(blocks_all)).astype(bf16) * table_ok[..., None].astype(bf16)
    allowed = jnp.einsum("jhub,bk->jhuk", onehot, mask_blocks, preferred_element_type=f32)
    bias_rows = ((1.0 - allowed) * MASK_FILL).reshape(mine, heads, PICKS * BLOCK)
    mask_row = jnp.where(mask_seq == 1, 0.0, MASK_FILL).astype(f32).reshape(1, length)
    edges = jnp.stack([part == 0, part == parts - 1]).astype(jnp.int32)
    table = table.reshape(-1).astype(jnp.int32)

    w_kv = w_qkv[:, :, 1:].reshape(width, heads * 2 * hd)
    bias_kv = jnp.stack([jnp.zeros((heads, hd), f32), bias_qv[:, 1]], axis=1).reshape(heads * 2 * hd)
    w_q = w_qkv[:, :, 0].reshape(width, heads * hd)
    bias_q = bias_qv[:, 0].reshape(heads * hd)
    x_rows = x_all.reshape(parts, groups, seqs, span, width)
    x_mine = lax.dynamic_index_in_dim(x_rows, part, 0, keepdims=False)
    kv_rows = (jnp.einsum("pgzsd,dc->pgzsc", x_rows, w_kv, preferred_element_type=f32) + bias_kv).astype(bf16)
    kv = jnp.transpose(kv_rows, (2, 0, 1, 3, 4)).reshape(length, heads * 2 * hd)
    q_rows = (jnp.einsum("gzsd,dc->gzsc", x_mine, w_q, preferred_element_type=f32) + bias_q).astype(bf16)
    q_low = jnp.transpose(q_rows, (1, 0, 2, 3)).reshape(mine * BLOCK, heads, hd) * bf16(scale)
    q_pad = jnp.concatenate([q_low, jnp.zeros_like(q_low)], axis=-1).reshape(mine * BLOCK, heads * 2 * hd)

    attn_mine, lse = attn_forward(heads, hd, table, edges, q_pad, kv, bias_rows, mask_row)
    attn_send = jnp.transpose(attn_mine.reshape(seqs, groups, span, heads * hd), (1, 0, 2, 3))
    attn = lax.all_to_all(attn_send, HEAD, 0, 0, tiled=True).reshape(groups, seqs * span, heads * hd)

    rows = seqs * span
    tok_rows = tok.reshape(rows, width)
    branch = jnp.einsum("grc,gcd->rd", attn, w_out_full, preferred_element_type=f32) + bias_out
    y_one, normed_one, inv_one = norm_fwd(tok_rows.astype(f32) + branch, gain_one, bias_one)
    y_low = y_one.astype(bf16)
    pre = jnp.einsum("rd,gdf->grf", y_low, up_full, preferred_element_type=f32) + up_bias_full[:, None, :]
    hidden = tanh_gelu(pre).astype(bf16)
    ffn = jnp.einsum("grf,gfd->rd", hidden, down_full, preferred_element_type=f32) + down_bias_vector
    result, normed_two, inv_two = norm_fwd(y_one + ffn, gain_two, bias_two)
    result = lax.all_to_all(result.astype(bf16).reshape(seqs, span, width), "sq", 0, 0, tiled=True)
    d_two, grad_gain_two, grad_bias_two = norm_back(
        d_res.reshape(rows, width).astype(f32), normed_two, inv_two, gain_two
    )
    d_ffn = d_two.astype(bf16)
    grad_bias_back = jnp.sum(d_ffn.astype(f32), axis=0)
    d_hidden = jnp.einsum("rd,gfd->grf", d_ffn, down_full, preferred_element_type=f32)
    d_pre = gelu_back(pre, d_hidden).astype(bf16)
    d_y_ffn = jnp.einsum("grf,gdf->rd", d_pre, up_full, preferred_element_type=f32)
    grad_w_in = jnp.einsum("rd,grf->gdf", y_low, d_pre, preferred_element_type=f32).astype(bf16)
    grad_bias_in = jnp.sum(d_pre.astype(f32), axis=1)
    grad_w_back = jnp.einsum("grf,rd->gfd", hidden, d_ffn, preferred_element_type=f32).astype(bf16)
    d_one, grad_gain_one, grad_bias_one = norm_back(d_two + d_y_ffn, normed_one, inv_one, gain_one)
    d_branch = d_one.astype(bf16)
    grad_bias_out = jnp.sum(d_branch.astype(f32), axis=0)
    d_attn = jnp.einsum("rd,gcd->grc", d_branch, w_out_full, preferred_element_type=f32).astype(bf16)
    grad_w_out = jnp.einsum("grc,rd->gcd", attn, d_branch, preferred_element_type=f32).astype(bf16)

    d_attn_mine = lax.all_to_all(d_attn.reshape(groups, seqs, span, heads * hd), HEAD, 0, 0, tiled=True)
    d_attn_nat = jnp.transpose(d_attn_mine, (1, 0, 2, 3)).reshape(mine * BLOCK, heads, hd)
    qd = jnp.concatenate([q_low, d_attn_nat], axis=-1).reshape(mine * BLOCK, heads * 2 * hd)

    wide_part = jnp.concatenate([grad_w_in, grad_w_back, grad_w_out], axis=1)
    wide_sum = lax.psum_scatter(wide_part, HEAD, scatter_dimension=0, tiled=True)[0]
    wide_sum = lax.psum(wide_sum, SEQ)

    dq, dkv = attn_backward(heads, hd, scale, table, edges, qd, kv, bias_rows, mask_row, lse)
    dkv_rows = jnp.transpose(
        dkv.reshape(seqs, parts, groups, span, heads * 2 * hd), (1, 2, 0, 3, 4)
    )
    dq_rows = jnp.transpose(dq.reshape(seqs, groups, span, heads * hd), (1, 0, 2, 3))
    dq_all = lax.dynamic_update_index_in_dim(
        jnp.zeros((parts, groups, seqs, span, heads * hd), bf16), dq_rows, part, 0
    )
    d_x = jnp.einsum("pgzsc,dc->pgzsd", dkv_rows, w_kv, preferred_element_type=f32) + jnp.einsum(
        "pgzsc,dc->pgzsd", dq_all, w_q, preferred_element_type=f32
    )
    d_x = lax.psum_scatter(
        d_x.astype(bf16).reshape(parts * groups, seqs, span, width), PLANE, scatter_dimension=0, tiled=True
    )
    d_tok = (d_one + d_x.reshape(rows, width).astype(f32)).astype(bf16)
    d_tok = lax.all_to_all(d_tok.reshape(seqs, span, width), "sq", 0, 0, tiled=True)

    grad_kv = jnp.einsum("pgzsd,pgzsc->dc", x_rows, dkv_rows, preferred_element_type=f32)
    grad_q = jnp.einsum("gzsd,gzsc->dc", x_mine, dq_rows, preferred_element_type=f32)
    grad_w_qkv = jnp.concatenate(
        [grad_q.reshape(width, heads, 1, hd), grad_kv.reshape(width, heads, 2, hd)], axis=2
    )
    bias_q_sum = jnp.sum(dq_rows.astype(f32), axis=(0, 1, 2)).reshape(heads, 1, hd)
    bias_v_sum = jnp.sum(dkv_rows.astype(f32), axis=(0, 1, 2, 3)).reshape(heads, 2, hd)[:, 1:]
    grad_bias_qv = jnp.concatenate([bias_q_sum, bias_v_sum], axis=1)
    grad_w_qkv = lax.psum(grad_w_qkv.astype(bf16), SEQ).astype(f32)

    small = jnp.stack(
        [grad_bias_out, grad_gain_one, grad_bias_one, grad_bias_back, grad_gain_two, grad_bias_two]
    )
    all_bias_in = grad_bias_in
    bias_qv_all = lax.dynamic_update_index_in_dim(
        jnp.zeros((groups, heads * 2 * hd), f32), grad_bias_qv.reshape(-1), head, 0
    )
    packed = jnp.concatenate([small.reshape(-1), all_bias_in.reshape(-1), bias_qv_all.reshape(-1)])
    packed = lax.psum(packed, ("sq", "part", "hy", "hc"))
    n_small = 6 * width
    small = packed[:n_small].reshape(6, width)
    n_in = n_small + all_bias_in.size
    hidden_dev = up_weight.shape[1]
    grad_bias_in = lax.dynamic_slice_in_dim(packed[n_small:n_in], head * hidden_dev, hidden_dev, 0)
    grad_bias_qv = lax.dynamic_slice_in_dim(
        packed[n_in:], head * heads * 2 * hd, heads * 2 * hd, 0
    ).reshape(heads, 2, hd)

    wide_sum = wide_sum.astype(f32)
    grad_w_in = wide_sum[:width]
    grad_w_back = wide_sum[width : width + hidden_dev]
    grad_w_out = wide_sum[width + hidden_dev :].reshape(heads, hd, width)
    return (
        jnp.transpose(result, (1, 0, 2)),
        jnp.transpose(d_tok, (1, 0, 2)),
        grad_w_qkv,
        grad_bias_qv,
        grad_w_out,
        small[0],
        small[1],
        small[2],
        grad_w_in,
        grad_bias_in,
        grad_w_back,
        small[3],
        small[4],
        small[5],
    )


def solution(mesh):
    seq_size, head_size = mesh.shape["seq"], mesh.shape["head"]

    def run(*args):
        seqs = args[0].shape[1]
        fine = Mesh(
            np.asarray(mesh.devices).reshape(seqs, seq_size // seqs, head_size // 2, 2),
            ("sq", "part", "hy", "hc"),
        )
        rows = P(("sq", "part", "hy", "hc"), None, None)
        placed = (
            rows,
            P(None, HEAD, None, None),
            P(HEAD, None, None),
            P(HEAD, None, None),
            P(),
            P(),
            P(),
            P(None, HEAD),
            P(HEAD),
            P(HEAD, None),
            P(),
            P(),
            P(),
            rows,
            P(),
            P(),
        )
        return jax.shard_map(
            per_device,
            mesh=fine,
            in_specs=placed,
            out_specs=(
                rows,
                rows,
                P(None, HEAD, None, None),
                P(HEAD, None, None),
                P(HEAD, None, None),
                P(),
                P(),
                P(),
                P(None, HEAD),
                P(HEAD),
                P(HEAD, None),
                P(),
                P(),
                P(),
            ),
            check_vma=False,
        )(*args)

    return run
```

time: 1620 us -> 564 us (0.35)
  waiting for transfers between devices: 1020 us -> 166 us
  local copies, waits for them, and re-layouts: 195 us -> 36.3 us
  matrix products: 211 us -> 65.3 us
  Pallas kernels: 0 us -> 108 us
  other arithmetic: 96.7 us -> 27.5 us
  blocking collectives: 65.9 us -> 119 us
  starting transfers between devices: 0.71 us -> 17 us
    reduce_scatter x5 -> x2, waiting for transfers between devices: 558 us -> 44.8 us  [the longest x1 44.8 us: per_device(): lax.psum_scatter(d_x.astype(bf16).reshape(parts * groups, seqs, span, wid...]
    all_gather x5 -> x4, waiting for transfers between devices: 280 us -> 33.3 us  [the longest x1 33.3 us: per_device(): x_all = lax.all_gather(tok, PLANE, axis=0, tiled=False)]
    dot_general x25 -> x16, matrix products: 211 us -> 65.3 us  [the longest x1 7.79 us: per_device(): jnp.einsum('grf,gfd->rd', hidden, down_full, preferred_element_type=f32)]
    pallas_call x0 -> x2, Pallas kernels: none -> 108 us  [the longest x1 54.8 us: attn_backward(): pl.pallas_call(functools.partial(attn_bwd_kernel, heads, hd, scale), out_...]
    psum x1, waiting for transfers between devices: 185 us -> 85.9 us  [per_device(): wide_sum = lax.psum(wide_sum, SEQ)]
    all_to_all x0 -> x2, blocking collectives: none -> 40.7 us  [the longest x1 26.5 us: per_device(): lax.all_to_all(jnp.transpose(tokens, (1, 0, 2)), 'sq', 0, 0, tiled=True)]
    reshape x6 -> x16, local copies, waits for them, and re-layouts: 40.2 us -> 10.3 us  [the longest x1 2.96 us: per_device(): dkv.reshape(seqs, parts, groups, span, heads * 2 * hd)]
    concatenate x7 -> x3, local copies, waits for them, and re-layouts: 25.9 us -> 0.26 us  [the longest x1 0.17 us: per_device(): jnp.concatenate([q_low, jnp.zeros_like(q_low)], axis=-1)]
  transfers between devices with their start and end apart: 11 -> 11, of which waited for: 10 -> 3; matrix products, arithmetic and copies ran while one was open for 4% -> 13% of each run, Pallas kernels for 0% -> 20%
where the time goes in v1:
time: 564 us; the launch traced here: 555 us
  waiting for transfers between devices  166 us (29%)
  blocking collectives  119 us (21%)
  Pallas kernels  108 us (19%)
  matrix products  65.3 us (12%)
  local copies, waits for them, and re-layouts  36.3 us (6%)
  other arithmetic  27.5 us (5%)
  starting transfers between devices  17 us (3%)
  between operations  15.1 us (3%)
    psum x1, waiting for transfers between devices, per_device(): wide_sum = lax.psum(wide_sum, SEQ)  85.9 us
    psum x1, blocking collectives, per_device(): packed = lax.psum(packed, ('sq', 'part', 'hy', 'hc'))  57.2 us
    pallas_call x1, Pallas kernels, attn_backward(): pl.pallas_call(functools.partial(attn_bwd_kernel, heads, hd, scale), out_...  54.8 us
    pallas_call x1, Pallas kernels, attn_forward(): pl.pallas_call(functools.partial(attn_fwd_kernel, heads, hd), out_shape=(...  53.7 us
    reduce_scatter x1, waiting for transfers between devices, per_device(): lax.psum_scatter(d_x.astype(bf16).reshape(parts * groups, seqs, span, wid...  44.8 us
    all_gather x1, waiting for transfers between devices, per_device(): x_all = lax.all_gather(tok, PLANE, axis=0, tiled=False)  33.3 us
    all_to_all x1, blocking collectives, per_device(): lax.all_to_all(jnp.transpose(tokens, (1, 0, 2)), 'sq', 0, 0, tiled=True)  26.5 us
    all_gather x1, blocking collectives, per_device(): lax.all_gather(up_bias_vector.astype(f32), HEAD, axis=0, tiled=False)  21.3 us
  transfers between devices with their start and end apart: 11, of which 3 were waited for; matrix products, arithmetic and copies ran while one was open for 13% of the time, Pallas kernels for 20%

profile of v1, /device:TPU:0, one launch (start us, length us, event | category | flops | bytes accessed | tf_op | source)
XLA Modules:
  0.0 554.8 jit_solution(9782258547132844518)
XLA Ops:
  7.2 1.2 copy.239
  8.5 26.5 %all_to_all.30 = bf16[4,128,768]{2,1,0:T(8,128)(2,1)} all-to-all(bf16[4,128,768]{2,1,0:T(8,128)(2,1)S(1)} %bitcast.251), channel_id=1, replica_groups=mesh['sq'=4,'part'=2,'hy'=2,'hc'=2] {'sq'}, dimensions={0} | all-to-all | bytes 1572864 | tf_op jit(solution)/shard_map/all_to_all | solution.py:316
  35.0 0.7 all-gather.10.cloned.1.call-update
  35.8 0.7 all-gather.14.cloned.1.call-update
  37.0 1.0 copy.238
  38.0 4.3 all-to-all-start.3
  43.1 0.6 gather_fusion
  44.2 0.9 slice.63
  46.5 33.3 %all-gather.12.cloned.1.call-done = bf16[32,128,768]{2,1,0:T(8,128)(2,1)} async-done(((bf16[4,128,768]{2,1,0:T(8,128)(2,1)}), bf16[32,128,768]{2,1,0:T(8,128)(2,1)}) %all-gather.12.cloned.1.call-update) | async-done | bytes 6291472 | tf_op jit(solution)/shard_map/all_gather | solution.py:317
  79.8 3.1 fusion.48
  82.8 0.6 copy.168
  83.5 0.6 mul.204
  84.2 0.7 copy-done.8
  84.9 0.9 copy.173.q_ref
  85.8 6.6 %fusion.13 = bf16[4,2,4,128,384]{4,3,0,2,1:T(8,128)(2,1)S(1)} fusion(f32[384]{0:T(512)S(1)} %add.258, bf16[2,4,4,128,768]{4,3,2,1,0:T(8,128)(2,1)} %bitcast.265, bf16[768,384,1,1,1]{0,1,4,3,2:T(8,128)(2,1)} %bitcast.253), kind=kOutput, calls=%fused_computation.25 | convolution fusion | flops 2419064832 | bytes 10028544 | tf_op jit(solution)/shard_map/pgzsd,dc->pgzsc/dot_general | solution.py:365
  92.4 2.0 copy.170
  94.4 53.7 %attn_forward.1 = (bf16[2048,192]{1,0:T(8,128)(2,1)S(1)}, f32[2048,128]{1,0:T(8,128)S(1)}) custom-call(s32[768]{0:T(1024)S(1)} %reshape.266.table_ref, s32[2]{0:T(128)S(1)} %add_convert_fusion.4.edge_ref, bf16[2048,384]{1,0:T(8,128)(2,1)S(1)} %copy.173.q_ref, bf16[4096,384]{1,0:T(8,128)(2,1)} %bitcast.245, f32[32,3,512]{2,1,0:T(4,128)S(1)} %reshape.327.bias_ref, ...), custom_call_target="tpu_custom_call" | custom-call | flops 1610612736 | bytes 8388608 | tf_op jit(solution)/shard_map/attn_forward/pallas_call | solution.py:245
  148.1 1.0 copy-done.2
  149.0 1.3 copy.175
  150.3 3.5 all-to-all-start.1
  153.9 21.3 %all-gather.4 = f32[4,1,768]{2,1,0:T(1,128)S(1)} all-gather(f32[1,1,768]{2,1,0:T(1,128)S(1)} %reshape.308), channel_id=4, replica_groups=mesh['sq'=4,'part'=2,'hy'=2,'hc'=2] {'hy','hc'}, dimensions={0}, use_global_device_ids=true | all-gather | bytes 15360 | tf_op jit(solution)/shard_map/all_gather | solution.py:323
  175.2 1.5 convert_reduce_fusion.2
  176.8 2.5 fusion.95
  179.7 7.3 %fusion.87 = f32[512,4,768]{2,0,1:T(8,128)} fusion(bf16[4,768,768]{2,1,0:T(8,128)(2,1)} %bitcast.268, f32[512,768]{1,0:T(8,128)S(1)} %get-tuple-element.104, f32[768]{0:T(1024)S(1)} %copy-done.28, f32[768]{0:T(1024)S(1)} %copy-done.21, f32[512]{0:T(512)S(1)} %add_rsqrt_fusion.1, f32[512]{0:T(512)S(1)} %broadcast_multiply_fusion.4), kind=kOutput, calls=%fused_computation.141 | convolution fusion | flops 2417885184 | bytes 12593152 | tf_op jit(solution)/shard_map/rd,gdf->grf/dot_general | solution.py:380
  187.0 7.8 %fusion.96 = (f32[512]{0:T(512)S(1)}, f32[512,768]{1,0:T(8,128)S(1)}) fusion(f32[768]{0:T(1024)S(1)} %copy-done.27, bf16[4,768,768]{2,1,0:T(8,128)(2,1)} %bitcast.272, f32[512,4,768]{2,0,1:T(8,128)} %fusion.87, f32[4,768]{1,0:T(4,128)S(1)} %bitcast.261, f32[768]{0:T(1024)S(1)} %copy-done.28, f32[768]{0:T(1024)S(1)} %copy-done.21, ...), kind=kOutput, calls=%fused_computation.146 | convolution fusion | flops 2434399744 | bytes 14183424 | tf_op jit(solution)/shard_map/grf,gfd->rd/dot_general | solution.py:382
  195.2 2.0 fusion.30
  197.2 2.8 convert_reduce_fusion.4
  200.0 6.6 %convert_reduce_fusion.1 = (f32[4,768]{1,0:T(4,128)S(1)}, bf16[4,512,768]{2,1,0:T(8,128)(2,1)S(1)}) fusion(f32[512,4,768]{2,0,1:T(8,128)S(1)} %copy-done.29, f32[4,768]{1,0:T(4,128)S(1)} %bitcast.262, bf16[4,768,768]{2,1,0:T(8,128)(2,1)S(1)} %bitcast.273, f32[512,768]{1,0:T(8,128)S(1)} %get-tuple-element.89), kind=kOutput, calls=%fused_computation.22 | convolution fusion | flops 2452485120 | bytes 15753216 | tf_op jit(solution)/shard_map/rd,gfd->grf/dot_general | solution.py:390
  206.6 3.1 multiply_reduce_fusion
  209.7 3.2 convert_bitcast_fusion
  212.9 4.6 convolution_convert_fusion
  218.6 0.8 convolution_convert_fusion.1
  219.4 10.9 %pad_maximum_fusion = bf16[4,1728,768]{2,1,0:T(8,128)(2,1)} fusion(bf16[4,192,768]{2,1,0:T(8,128)(2,1)S(1)} %convolution_convert_fusion.1, bf16[4,768,768]{2,1,0:T(8,128)(2,1)S(1)} %convolution_convert_fusion, bf16[4,768,768]{2,1,0:T(8,128)(2,1)S(1)} %convert_bitcast_fusion), kind=kLoop, calls=%fused_computation.2 | loop fusion | flops 31850496 | bytes 21233664 | tf_op jit(solution)/shard_map/concatenate | solution.py:406
  230.4 2.1 fusion.51
  232.7 14.2 %all_to_all.31 = bf16[4,4,128,192]{2,1,3,0:T(4,128)(2,1)S(1)} all-to-all(bf16[4,4,128,192]{2,1,3,0:T(4,128)(2,1)S(1)} %reshape.275), channel_id=1, replica_groups=mesh['sq'=4,'part'=2,'hy'=2,'hc'=2] {'hy','hc'}, dimensions={0} | all-to-all | bytes 1572864 | tf_op jit(solution)/shard_map/all_to_all | solution.py:402
  246.9 1.0 copy.180
  247.9 0.6 reshape.276
  248.5 1.2 pad_maximum_fusion.1
  249.8 1.9 copy.181.qd_ref
  251.7 1.2 copy-done.3
  252.9 54.8 %attn_backward.1 = (bf16[2048,192]{1,0:T(8,128)(2,1)S(1)}, bf16[4096,384]{1,0:T(8,128)(2,1)}) custom-call(s32[768]{0:T(1024)S(1)} %reshape.266.table_ref, s32[2]{0:T(128)S(1)} %add_convert_fusion.4.edge_ref, bf16[2048,384]{1,0:T(8,128)(2,1)S(1)} %copy.181.qd_ref, bf16[4096,384]{1,0:T(8,128)(2,1)} %bitcast.246, f32[32,3,512]{2,1,0:T(4,128)S(1)} %reshape.327.bias_ref, ...), custom_call_target="tpu_custom_call" | custom-call | flops 4026531840 | bytes 12582912 | tf_op jit(solution)/shard_map/attn_backward/pallas_call | solution.py:264
  307.7 1.2 copy.186
  309.3 1.5 bitcast_dynamic-update-slice_fusion
  311.2 4.6 fusion.16
  315.7 4.5 add_convert_fusion
  320.4 3.0 copy.183
  323.3 3.0 fusion.59
  326.9 5.3 fusion.40
  332.2 1.0 pad_maximum_fusion.2
  333.2 4.2 all-to-all-start.2
  337.3 44.8 %reduce-scatter.3.cloned.1.call-done = bf16[1,4,128,768]{3,2,1,0:T(8,128)(2,1)} async-done(((bf16[8,4,128,768]{3,2,1,0:T(8,128)(2,1)}), bf16[1,4,128,768]{3,2,1,0:T(8,128)(2,1)}) %reduce-scatter.3.cloned.1.call-update) | async-done | bytes 786448 | tf_op jit(solution)/shard_map/reduce_scatter | solution.py:421
  382.2 2.2 fusion.23
  384.4 4.7 all-to-all-start.5
  389.2 2.4 convert_reduce_fusion
  392.2 57.2 %psum.22 = f32[9216]{0:T(1024)S(1)} all-reduce(f32[9216]{0:T(1024)S(1)} %pad_maximum_fusion.3), channel_id=1, replica_groups=mesh['sq'=4,'part'=2,'hy'=2,'hc'=2] {'sq','part','hy','hc'}, use_global_device_ids=true, to_apply=%region_19.20 | all-reduce | flops 9216 | bytes 73728 | tf_op jit(solution)/shard_map/psum | solution.py:445
  449.5 0.7 reshape.289
  450.1 0.7 dynamic_slice.26
  450.8 0.6 fusion.93
  451.4 1.5 copy.193
  452.9 1.5 copy.194
  454.4 85.9 %all-reduce.7.cloned.1.call-done = (bf16[1728,768]{1,0:T(8,128)(2,1)}, bf16[768,3,3,64]{0,3,2,1:T(8,128)(2,1)}) async-done(((bf16[1728,768]{1,0:T(8,128)(2,1)}, bf16[768,3,3,64]{0,3,2,1:T(8,128)(2,1)}), (bf16[1728,768]{1,0:T(8,128)(2,1)}, bf16[768,3,3,64]{0,3,2,1:T(8,128)(2,1)})) %all-reduce.7.cloned.1.call-update) | async-done | bytes 3538960 | tf_op jit(solution)/shard_map/psum | solution.py:408
  540.3 4.3 fusion.92
  544.6 1.8 slice.81
  546.4 1.4 convert_element_type.130
  (155 shorter events, 7.6 us)
Async XLA Ops:
  7.2 35.4 %copy-start = (s32[4,64,12,3]{1,0,3,2:T(4,128)S(1)}, s32[4,64,12,3]{1,0,3,2:T(4,128)}, u32[]{:S(2)}) copy-start(s32[4,64,12,3]{1,0,3,2:T(4,128)} %param.32) | copy-start | bytes 110596
  7.2 72.6 %all-gather.12.cloned.1.call-start = ((), (), s32[]{:S(2)}) async-start(), calls=%async_computation.11 | async-start | bytes 7077888 | tf_op jit(solution)/shard_map/all_gather | solution.py:317
  8.5 28.6 %copy-start.18 = (bf16[128,4,768]{2,1,0:T(4,128)(2,1)S(1)}, bf16[128,4,768]{2,1,0:T(4,128)(2,1)}, u32[]{:S(2)}) copy-start(bf16[128,4,768]{2,1,0:T(4,128)(2,1)} %param.30) | copy-start | bytes 2359300
  35.0 141.8 %all-gather.10.cloned.1.call-start = ((), (), s32[]{:S(2)}) async-start(), calls=%async_computation.8 | async-start | bytes 1474560 | tf_op jit(solution)/shard_map/all_gather | solution.py:320
  35.7 143.9 %all-gather.14.cloned.1.call-start = ((), (), s32[]{:S(2)}) async-start(), calls=%async_computation.12 | async-start | bytes 5898240 | tf_op jit(solution)/shard_map/all_gather | solution.py:321
  36.4 7.7 %copy-start.16 = (bf16[768,3,3,64]{0,3,2,1:T(8,128)(2,1)S(1)}, bf16[768,3,3,64]{0,3,2,1:T(8,128)(2,1)}, u32[]{:S(2)}) copy-start(bf16[768,3,3,64]{0,3,2,1:T(8,128)(2,1)} %param.18) | copy-start | bytes 2654212
  36.5 150.6 %all-gather.16.cloned.1.call-start = ((), (), s32[]{:S(2)}) async-start(), calls=%async_computation.13 | async-start | bytes 5898240 | tf_op jit(solution)/shard_map/all_gather | solution.py:322
  38.0 7.1 %copy-start.20 = (s32[4,4096]{1,0:T(4,128)S(1)}, s32[4,4096]{1,0:T(4,128)}, u32[]{:S(2)}) copy-start(s32[4,4096]{1,0:T(4,128)} %param.31) | copy-start | bytes 196612
  38.0 112.3 %all-to-all-start.3 = ((bf16[4,128,768]{2,1,0:T(8,128)(2,1)}), bf16[4,128,768]{2,1,0:T(8,128)(2,1)}, u32[]{:S(2)}, u32[]{:S(2)}) async-start(bf16[4,128,768]{2,1,0:T(8,128)(2,1)} %bitcast.234), calls=%async_computation.3 | async-start | bytes 1572864 | tf_op jit(solution)/shard_map/all_to_all | solution.py:318
  43.1 3.1 copy-start.23
  44.2 38.6 %copy-start.14 = (bf16[768,3,1,64]{0,3,2,1:T(8,128)(2,1)}, bf16[768,3,1,64]{0,3,2,1:T(8,128)(2,1)S(1)}, u32[]{:S(2)}) copy-start(bf16[768,3,1,64]{0,3,2,1:T(8,128)(2,1)S(1)} %slice.61) | copy-start | bytes 884740
  84.1 0.9 copy-start.8
  148.0 1.0 copy-start.2
  149.0 4.8 copy-start.24
  149.0 26.2 %copy-start.19 = (f32[768]{0:T(1024)S(1)}, f32[768]{0:T(1024)}, u32[]{:S(2)}) copy-start(f32[768]{0:T(1024)} %param.28) | copy-start | bytes 9220
  149.0 27.7 %copy-start.13 = (bf16[4,128,768]{2,1,0:T(8,128)(2,1)S(1)}, bf16[4,128,768]{2,1,0:T(8,128)(2,1)}, u32[]{:S(2)}) copy-start(bf16[4,128,768]{2,1,0:T(8,128)(2,1)} %all_to_all.30) | copy-start | bytes 2359300
  149.0 27.7 %copy-start.26 = (f32[768]{0:T(1024)S(1)}, f32[768]{0:T(1024)}, u32[]{:S(2)}) copy-start(f32[768]{0:T(1024)} %param.21) | copy-start | bytes 9220
  150.3 26.4 %all-to-all-start.1 = ((bf16[4,4,128,192]{2,3,1,0:T(8,128)(2,1)}), bf16[4,4,128,192]{2,3,1,0:T(8,128)(2,1)S(1)}, u32[]{:S(2)}, u32[]{:S(2)}) async-start(bf16[4,4,128,192]{2,3,1,0:T(8,128)(2,1)} %bitcast.19), calls=%async_computation.1 | async-start | bytes 1572864 | tf_op jit(solution)/shard_map/all_to_all | solution.py:373
  153.8 179.4 %reduce-scatter.5.cloned.1.call-start = ((), (), s32[]{:S(2)}) async-start(), calls=%async_computation.10 | async-start | bytes 13271040 | tf_op jit(solution)/shard_map/reduce_scatter | solution.py:407
  176.7 2.6 copy-start.11
  176.8 2.9 copy-start.21
  176.8 2.9 copy-start.28
  179.7 7.4 %copy-start.27 = (f32[768]{0:T(1024)S(1)}, f32[768]{0:T(1024)}, u32[]{:S(2)}) copy-start(f32[768]{0:T(1024)} %param.27) | copy-start | bytes 9220
  187.0 13.0 %copy-start.29 = (f32[512,4,768]{2,0,1:T(8,128)S(1)}, f32[512,4,768]{2,0,1:T(8,128)}, u32[]{:S(2)}) copy-start(f32[512,4,768]{2,0,1:T(8,128)} %fusion.87) | copy-start | bytes 18874372
  194.8 2.3 copy-start.22
  195.2 4.8 copy-start.25
  197.2 9.4 %slice-start = ((s8[4718592]{0:T(1024)(128)(4,1)}), s8[4194304]{0:T(1024)(128)(4,1)S(1)}, s32[]{:S(2)}) async-start(s8[4718592]{0:T(1024)(128)(4,1)} %bitcast.269), calls=%async_computation.15 | async-start | bytes 8388608
  200.0 6.6 %slice-start.1 = ((s8[4718592]{0:T(1024)(128)(4,1)}), s8[524288]{0:T(1024)(128)(4,1)S(1)}, s32[]{:S(2)}) async-start(s8[4718592]{0:T(1024)(128)(4,1)} %bitcast.269), calls=%async_computation.16 | async-start | bytes 1048576
  217.5 1.1 copy-start.12
  218.0 12.4 %copy-start.5 = (f32[512,768]{1,0:T(8,128)}, f32[512,768]{1,0:T(8,128)S(1)}, u32[]{:S(2)}) copy-start(f32[512,768]{1,0:T(8,128)S(1)} %get-tuple-element.91) | copy-start | bytes 4718596
  230.4 151.8 %reduce-scatter.3.cloned.1.call-start = ((), (), s32[]{:S(2)}) async-start(), calls=%async_computation.9 | async-start | bytes 7077888 | tf_op jit(solution)/shard_map/reduce_scatter | solution.py:421
  232.7 15.8 %copy-start.9 = (bf16[2048,3,64]{0,2,1:T(8,128)(2,1)S(1)}, bf16[2048,3,64]{0,2,1:T(8,128)(2,1)}, u32[]{:S(2)}) copy-start(bf16[2048,3,64]{0,2,1:T(8,128)(2,1)} %copy-done.8) | copy-start | bytes 2359300
  251.7 1.2 copy-start.3
  308.9 2.2 copy-start.4
  311.2 4.6 copy-start.15
  320.3 220.0 %all-reduce.7.cloned.1.call-start = ((), (), s32[]{:S(2)}) async-start(), calls=%async_computation.14 | async-start | bytes 7077888 | tf_op jit(solution)/shard_map/psum | solution.py:408
  323.3 3.6 copy-start.7
  333.1 49.0 %copy-start.6 = (f32[512,768]{1,0:T(8,128)S(1)}, f32[512,768]{1,0:T(8,128)}, u32[]{:S(2)}) copy-start(f32[512,768]{1,0:T(8,128)} %copy-done.5) | copy-start | bytes 4718596
  333.2 51.2 %all-to-all-start.2 = ((bf16[4,128,768]{2,1,0:T(8,128)(2,1)}), bf16[4,128,768]{2,1,0:T(8,128)(2,1)S(1)}, u32[]{:S(2)}, u32[]{:S(2)}) async-start(bf16[4,128,768]{2,1,0:T(8,128)(2,1)} %bitcast.27), calls=%async_computation.2 | async-start | bytes 1572864 | tf_op jit(solution)/shard_map/all_to_all | solution.py:384
  384.4 7.3 %copy-start.10 = (bf16[4,4,128,192]{2,3,0,1:T(8,128)(2,1)S(1)}, bf16[4,4,128,192]{2,3,0,1:T(8,128)(2,1)}, u32[]{:S(2)}) copy-start(bf16[4,4,128,192]{2,3,0,1:T(8,128)(2,1)} %copy.186) | copy-start | bytes 2359300
  384.4 68.5 %all-to-all-start.5 = ((bf16[4,128,768]{2,1,0:T(8,128)(2,1)}), bf16[4,128,768]{2,1,0:T(8,128)(2,1)S(1)}, u32[]{:S(2)}, u32[]{:S(2)}) async-start(bf16[4,128,768]{2,1,0:T(8,128)(2,1)} %bitcast.50), calls=%async_computation.6 | async-start | bytes 1572864 | tf_op jit(solution)/shard_map/all_to_all | solution.py:425
  540.3 6.1 %copy-start.17 = (bf16[768,3,3,64]{0,3,2,1:T(8,128)(2,1)S(1)}, bf16[768,3,3,64]{0,3,2,1:T(8,128)(2,1)}, u32[]{:S(2)}) copy-start(bf16[768,3,3,64]{0,3,2,1:T(8,128)(2,1)} %get-tuple-element.87) | copy-start | bytes 2654212
  540.3 7.4 %copy-start.1 = (s32[4,64,12,3]{1,0,3,2:T(4,128)S(1)}, s32[4,64,12,3]{1,0,3,2:T(4,128)}, u32[]{:S(2)}) copy-start(s32[4,64,12,3]{1,0,3,2:T(4,128)} %param.32) | copy-start | bytes 110596
Sparse Core Ops, SparseCore 0:
  35.1 44.6 all-gather.11
  81.3 17.4 all-gather.9
  100.4 37.7 all-gather.13
  139.6 45.9 all-gather.15
  230.5 86.1 reduce-scatter.4
  320.4 61.7 reduce-scatter.2
  386.8 153.4 all-reduce.6

commit v2 on v1

--- a/solution.py
+++ b/solution.py
@@ -282,7 +282,7 @@
     )(table, edges, qd, kv, bias, mask, lse)
 
 
-def per_device(
+def general_layer(
     tokens,
     w_qkv,
     bias_qv,
@@ -474,6 +474,1235 @@
     )
 
 
+def swap(value, axis, step=1, name="swap"):
+    size = lax.axis_size(axis)
+    with jax.named_scope(name + "_" + axis + str(step)):
+        return lax.ppermute(value, axis, [(i, i ^ step) for i in range(size)])
+
+
+def flipped(value, bit, axis):
+    return jnp.where(bit == 1, jnp.flip(value, axis), value)
+
+
+def relative(value, place):
+    shape = value.shape
+    value = value.reshape((2, 2) + shape[1:])
+    value = flipped(flipped(value, place // 2, 0), place % 2, 1)
+    return value.reshape(shape)
+
+
+ANY_SPEC = pl.BlockSpec(memory_space=pl.ANY)
+
+
+def after(value, *orders):
+    return pl.pallas_call(
+        lambda *refs: None,
+        out_shape=jax.ShapeDtypeStruct(value.shape, value.dtype),
+        in_specs=[ANY_SPEC] * (1 + len(orders)),
+        out_specs=ANY_SPEC,
+        input_output_aliases={0: 0},
+        name="after",
+    )(value, *orders)
+
+
+def params(limit_mb):
+    return pltpu.CompilerParams(vmem_limit_bytes=limit_mb * 1024 * 1024)
+
+
+def fill_tables(coord_ref, rand_ref, place_ref, nat_ref, heads, span):
+    per_span = span // BLOCK
+
+    def one(b, carry):
+        own = b // per_span
+        kz = (own // 8) ^ coord_ref[0]
+        kx = (own // 4 % 2) ^ coord_ref[1]
+        ky = (own // 2 % 2) ^ coord_ref[2]
+        kc = (own % 2) ^ coord_ref[3]
+        odd = kz % 2
+        one, two = jnp.where(odd == 0, kx, ky), jnp.where(odd == 0, ky, kx)
+        spot = ((((odd * 2 + kc) * 2 + two) * 2 + one) * 2 + kz // 2) * per_span + b % per_span
+        place_ref[b] = spot
+        nat_ref[spot] = b
+        return carry
+
+    lax.fori_loop(0, place_ref.shape[0], one, 0)
+
+
+def natural_block(coord_ref, jl, per_span):
+    kz = (jl // per_span % 2 * 2 + jl // (per_span * 2) % 2) ^ coord_ref[0]
+    kc = jl // (per_span * 4) % 2 ^ coord_ref[3]
+    ky = jl // (per_span * 8) ^ coord_ref[2]
+    return (((kz * 2 + coord_ref[1]) * 2 + ky) * 2 + kc) * per_span + jl % per_span
+
+
+def edge_of(coord_ref, blocks, per_span):
+    last = coord_ref[1]
+    kz = (last * 3) ^ coord_ref[0]
+    ky = last ^ coord_ref[2]
+    kc = last ^ coord_ref[3]
+    return ((ky * 2 + kc) * 4 + kz % 2 * 2 + kz // 2) * per_span + last * (per_span - 1)
+
+
+def picks_of(coord_ref, rand_ref, jl, h, heads, per_span, blocks_all):
+    b = natural_block(coord_ref, jl, per_span)
+    inner = (b > 0) & (b < blocks_all - 1)
+    ids, rows = [], []
+    for u in range(3):
+        key = b + u - 1
+        ids.append(jnp.clip(key, 0, blocks_all - 1))
+        rows.append(jnp.where(inner & (key >= 1) & (key <= blocks_all - 2), key, blocks_all))
+    for key in (0, blocks_all - 1):
+        ids.append(key)
+        rows.append(jnp.where(inner, key, blocks_all))
+    for u in range(3):
+        key = rand_ref[(b * heads + h) * 3 + u]
+        ids.append(key)
+        rows.append(jnp.where(inner, key, blocks_all))
+    return ids, rows
+
+
+def mask_of(mask_ref, rows, left):
+    pairs = []
+    for u in range(0, len(rows), 2):
+        a, b = mask_ref[pl.ds(rows[u], 1), :], mask_ref[pl.ds(rows[u + 1], 1), :]
+        pairs.append(jnp.where(left, a, b))
+    return jnp.concatenate(pairs, axis=1)
+
+
+def blocks_of(kv_ref, place_ref, ids, cols):
+    return jnp.concatenate(
+        [kv_ref[pl.ds(pl.multiple_of(place_ref[b] * BLOCK, BLOCK), BLOCK), cols] for b in ids], axis=0
+    )
+
+
+def query_pieces(pair):
+    out = []
+    for ky in range(2):
+        for kc in range(2):
+            at = (ky * 2 + kc) * 2 * pair
+            out.append((at, kc * 2 + ky, 0))
+            out.append((at + pair, 4 + kc * 2, ky * pair))
+    return out
+
+
+def project_and_attend_kernel(heads, hd, span, n_orders, coord_ref, rand_ref, *refs):
+    x_refs = refs[:8]
+    w_kv_ref, w_q_ref, b_kv_ref, b_q_ref, mask_ref = refs[8:13]
+    refs = refs[13 + n_orders :]
+    o_refs, (lse_ref, kv_ref, q_ref, s_ref, place_ref, nat_ref) = refs[:2], refs[2:]
+    near = o_refs[0].shape[0] // BLOCK
+    wide = 2 * hd
+    piece, pair = 4 * span, 2 * span
+    per_span = span // BLOCK
+    blocks = q_ref.shape[0] // BLOCK
+    blocks_all = kv_ref.shape[0] // BLOCK
+    chunks = kv_ref.shape[0] // CHUNK
+    lanes = lax.broadcasted_iota(jnp.int32, (BLOCK, 128), 1)
+    left = lax.broadcasted_iota(jnp.int32, (1, 128), 1) < BLOCK
+    fill_tables(coord_ref, rand_ref, place_ref, nat_ref, heads, span)
+
+    for n, x_ref in enumerate(x_refs):
+        kv_ref[n * piece : (n + 1) * piece, :] = (dot_nn(x_ref[...], w_kv_ref[...]) + b_kv_ref[...]).astype(bf16)
+    for at, n, src in query_pieces(pair):
+        x = x_refs[n][src : src + pair, :]
+        q_ref[at : at + pair, :] = (dot_nn(x, w_q_ref[...]) + b_q_ref[...]).astype(bf16) * bf16(hd**-0.5)
+
+    def finish(jl, accs, tops, totals):
+        lse_tile = jnp.zeros((BLOCK, 128), f32)
+        for h in range(heads):
+            lse_tile = jnp.where(lanes == h, tops[h] + jnp.log(totals[h]), lse_tile)
+        lse_ref[pl.ds(pl.multiple_of(jl * BLOCK, BLOCK), BLOCK), :] = lse_tile
+        return jnp.concatenate([accs[h][:, hd:] * (1.0 / totals[h]) for h in range(heads)], axis=1).astype(bf16)
+
+    def put(o_ref, jl, value):
+        o_ref[pl.ds(pl.multiple_of(jl * BLOCK, BLOCK), BLOCK), :] = value
+
+    unroll = 4
+
+    def some(half, it, carry):
+        items = [(half * near + it * unroll + u, h) for u in range(unroll) for h in range(heads)]
+        scores, kvs = [], []
+        for jl, h in items:
+            rows = pl.ds(pl.multiple_of(jl * BLOCK, BLOCK), BLOCK)
+            cols = slice(h * wide, (h + 1) * wide)
+            ids, mask_rows = picks_of(coord_ref, rand_ref, jl, h, heads, per_span, blocks_all)
+            kvg = blocks_of(kv_ref, place_ref, ids, cols)
+            scores.append(dot_nt(q_ref[rows, cols], kvg) + mask_of(mask_ref, mask_rows, left))
+            kvs.append(kvg)
+        lows, tops, totals = [], [], []
+        for s in scores:
+            top = jnp.max(s, axis=1, keepdims=True)
+            p = jnp.exp(s - top)
+            totals.append(jnp.sum(p, axis=1, keepdims=True))
+            tops.append(top)
+            lows.append(p.astype(bf16))
+        accs = [dot_nn(p, kvg) for p, kvg in zip(lows, kvs)]
+        for u in range(unroll):
+            of = slice(u * heads, (u + 1) * heads)
+            jl = it * unroll + u
+            put(o_refs[half], jl, finish(half * near + jl, accs[of], tops[of], totals[of]))
+        return carry
+
+    for half in range(2):
+        lax.fori_loop(0, near // unroll, functools.partial(some, half), 0)
+
+    edge = edge_of(coord_ref, blocks, per_span)
+    rows = pl.ds(pl.multiple_of(edge * BLOCK, BLOCK), BLOCK)
+    head_cols = [slice(h * wide, (h + 1) * wide) for h in range(heads)]
+    qs = [q_ref[rows, cols] for cols in head_cols]
+
+    def score(c, tops):
+        part = pl.ds(pl.multiple_of(c * CHUNK, CHUNK), CHUNK)
+        mask = mask_of(mask_ref, [nat_ref[c * PICKS + u] for u in range(PICKS)], left)
+        ss = [dot_nt(qs[h], kv_ref[part, head_cols[h]]) + mask for h in range(heads)]
+        for h in range(heads):
+            s_ref[h, :, part] = ss[h]
+        return tuple(jnp.maximum(tops[h], ss[h]) for h in range(heads))
+
+    tops = lax.fori_loop(0, chunks, score, tuple(jnp.full((BLOCK, CHUNK), -3e38, f32) for _ in range(heads)))
+    tops = [jnp.max(t, axis=1, keepdims=True) for t in tops]
+
+    def out(c, carry):
+        accs, sums = carry
+        part = pl.ds(pl.multiple_of(c * CHUNK, CHUNK), CHUNK)
+        ps = [jnp.exp(s_ref[h, :, part] - tops[h]) for h in range(heads)]
+        accs = tuple(accs[h] + dot_nn(ps[h].astype(bf16), kv_ref[part, head_cols[h]]) for h in range(heads))
+        sums = tuple(sums[h] + ps[h] for h in range(heads))
+        return accs, sums
+
+    accs, sums = lax.fori_loop(
+        0,
+        chunks,
+        out,
+        (
+            tuple(jnp.zeros((BLOCK, wide), f32) for _ in range(heads)),
+            tuple(jnp.zeros((BLOCK, CHUNK), f32) for _ in range(heads)),
+        ),
+    )
+    value = finish(edge, accs, tops, [jnp.sum(t, axis=1, keepdims=True) for t in sums])
+
+    @pl.when(edge < near)
+    def _():
+        put(o_refs[0], edge, value)
+
+    @pl.when(edge >= near)
+    def _():
+        put(o_refs[1], edge - near, value)
+
+
+def project_and_attend(heads, hd, span, coords, rand, xs, w_kv, w_q, b_kv, b_q, mask, orders):
+    keys = 8 * xs[0].shape[0]
+    rows = keys // 2
+    cols = heads * 2 * hd
+    return pl.pallas_call(
+        functools.partial(project_and_attend_kernel, heads, hd, span, len(orders)),
+        out_shape=(
+            jax.ShapeDtypeStruct((rows // 2, heads * hd), bf16),
+            jax.ShapeDtypeStruct((rows // 2, heads * hd), bf16),
+            jax.ShapeDtypeStruct((rows, 128), f32),
+            jax.ShapeDtypeStruct((keys, cols), bf16),
+            jax.ShapeDtypeStruct((rows, cols), bf16),
+        ),
+        in_specs=[SMEM_SPEC] * 2 + [VMEM_SPEC] * 13 + [ANY_SPEC] * len(orders),
+        out_specs=(VMEM_SPEC,) * 5,
+        scratch_shapes=[
+            pltpu.VMEM((heads, BLOCK, keys), f32),
+            pltpu.SMEM((keys // BLOCK,), jnp.int32),
+            pltpu.SMEM((keys // BLOCK,), jnp.int32),
+        ],
+        compiler_params=params(58),
+        cost_estimate=pl.CostEstimate(
+            flops=40 << 30, bytes_accessed=16 << 20, transcendentals=rows * heads * CHUNK
+        ),
+        name="project_and_attend",
+    )(coords, rand, *xs, w_kv, w_q, b_kv, b_q, mask, *orders)
+
+
+def attend_back_kernel(heads, hd, span, n_orders, coord_ref, rand_ref, q_ref, *refs):
+    do_parts, o_parts = refs[:4], refs[4:6]
+    kv_ref, mask_ref, lse_ref, w_kv_ref, w_q_ref = refs[6:11]
+    dq_ref, dkv_ref, near_ref, far_ref, acc_ref, do_ref, o_ref, place_ref, nat_ref = refs[11 + n_orders :]
+    own = do_parts[0].shape[0]
+    for k, ref in enumerate(do_parts):
+        do_ref[k * own : (k + 1) * own, :] = ref[0] if len(ref.shape) == 3 else ref[...]
+    for k, ref in enumerate(o_parts):
+        o_ref[k * 2 * own : (k + 1) * 2 * own, :] = ref[...]
+    wide = 2 * hd
+    piece = 4 * span
+    per_span = span // BLOCK
+    scale = hd**-0.5
+    blocks = q_ref.shape[0] // BLOCK
+    blocks_all = kv_ref.shape[0] // BLOCK
+    chunks = kv_ref.shape[0] // CHUNK
+    head_cols = [slice(h * wide, (h + 1) * wide) for h in range(heads)]
+    nil = jnp.zeros((BLOCK, hd), bf16)
+    left = lax.broadcasted_iota(jnp.int32, (1, 128), 1) < BLOCK
+    fill_tables(coord_ref, rand_ref, place_ref, nat_ref, heads, span)
+
+    def clear(c, carry):
+        part = pl.ds(pl.multiple_of(c * CHUNK, CHUNK), CHUNK)
+        acc_ref[part, :] = jnp.zeros((CHUNK, heads * wide), f32)
+        return carry
+
+    lax.fori_loop(0, chunks, clear, 0)
+
+    def of_rows(rows):
+        d_o = do_ref[rows, :]
+        prod = d_o.astype(f32) * o_ref[rows, :].astype(f32)
+        lse = lse_ref[rows, :]
+        boths, dots, lses = [], [], []
+        for h in range(heads):
+            low = jnp.concatenate([nil, d_o[:, h * hd : (h + 1) * hd]], axis=1)
+            boths.append(jnp.concatenate([q_ref[rows, head_cols[h]], low], axis=0))
+            dots.append(jnp.sum(prod[:, h * hd : (h + 1) * hd], axis=1, keepdims=True))
+            lses.append(lse[:, h : h + 1])
+        return boths, dots, lses
+
+    unroll = 2
+
+    def some(it, carry):
+        items, boths, dots, lses = [], [], [], []
+        for u in range(unroll):
+            jl = it * unroll + u
+            rows = pl.ds(pl.multiple_of(jl * BLOCK, BLOCK), BLOCK)
+            b, d, e = of_rows(rows)
+            boths, dots, lses = boths + b, dots + d, lses + e
+            items += [(jl, h) for h in range(heads)]
+        kvs, prods, picks, masks = [], [], [], []
+        for i, (jl, h) in enumerate(items):
+            ids, mask_rows = picks_of(coord_ref, rand_ref, jl, h, heads, per_span, blocks_all)
+            kvg = blocks_of(kv_ref, place_ref, ids, head_cols[h])
+            prods.append(dot_nt(boths[i], kvg))
+            masks.append(mask_of(mask_ref, mask_rows, left))
+            kvs.append(kvg)
+            picks.append(ids)
+        dss, lows = [], []
+        for i, (jl, h) in enumerate(items):
+            p = jnp.exp(prods[i][:BLOCK] + masks[i] - lses[i])
+            dss.append((p * (prods[i][BLOCK:] - dots[i])).astype(bf16))
+            lows.append(p.astype(bf16))
+        dqs = [dot_nn(ds, kvg)[:, :hd] for ds, kvg in zip(dss, kvs)]
+        dkvs = [dot_tn(jnp.concatenate([ds, p], axis=0), both) for ds, p, both in zip(dss, lows, boths)]
+        for i, (jl, h) in enumerate(items):
+            for u in range(PICKS):
+                place = pl.ds(pl.multiple_of(place_ref[picks[i][u]] * BLOCK, BLOCK), BLOCK)
+                acc_ref[place, head_cols[h]] += dkvs[i][u * BLOCK : (u + 1) * BLOCK]
+        for u in range(unroll):
+            rows = pl.ds(pl.multiple_of((it * unroll + u) * BLOCK, BLOCK), BLOCK)
+            dq_ref[rows, :] = (jnp.concatenate(dqs[u * heads : (u + 1) * heads], axis=1) * scale).astype(bf16)
+        return carry
+
+    lax.fori_loop(0, blocks // unroll, some, 0)
+
+    rows = pl.ds(pl.multiple_of(edge_of(coord_ref, blocks, per_span) * BLOCK, BLOCK), BLOCK)
+    boths, dots, lses = of_rows(rows)
+
+    def edge(c, dqs):
+        part = pl.ds(pl.multiple_of(c * CHUNK, CHUNK), CHUNK)
+        mask = mask_of(mask_ref, [nat_ref[c * PICKS + u] for u in range(PICKS)], left)
+        kvs = [kv_ref[part, cols] for cols in head_cols]
+        prods = [dot_nt(boths[h], kvs[h]) for h in range(heads)]
+        dss, lows = [], []
+        for h in range(heads):
+            p = jnp.exp(prods[h][:BLOCK] + mask - lses[h])
+            dss.append((p * (prods[h][BLOCK:] - dots[h])).astype(bf16))
+            lows.append(p.astype(bf16))
+        new = tuple(dqs[h] + dot_nn(dss[h], kvs[h]) for h in range(heads))
+        dkvs = [dot_tn(jnp.concatenate([dss[h], lows[h]], axis=0), boths[h]) for h in range(heads)]
+        for h in range(heads):
+            acc_ref[part, head_cols[h]] += dkvs[h]
+        return new
+
+    dqs = lax.fori_loop(0, chunks, edge, tuple(jnp.zeros((BLOCK, wide), f32) for _ in range(heads)))
+    dq_ref[rows, :] = (jnp.concatenate([dq[:, :hd] for dq in dqs], axis=1) * scale).astype(bf16)
+
+    pair = 2 * span
+    mine = {(n, src): at for at, n, src in query_pieces(pair)}
+    for n in range(8):
+        kc = n // 2 % 2
+        to = n % 2 * piece
+        of = slice(n * piece, (n + 1) * piece)
+        dkv = acc_ref[of, :].astype(bf16)
+        dkv_ref[of, :] = dkv
+        dx = dot_nt(dkv, w_kv_ref[...])
+        for src in (0, pair):
+            part = dx[src : src + pair]
+            if (n, src) in mine:
+                at = mine[n, src]
+                part = part + dot_nt(dq_ref[at : at + pair, :], w_q_ref[...])
+            (far_ref if kc else near_ref)[n // 4, to + src : to + src + pair, :] = part.astype(bf16)
+
+
+def attend_back(heads, hd, span, coords, rand, q, d_os, os, kv, mask, lse, w_kv, w_q, orders):
+    rows, keys = q.shape[0], kv.shape[0]
+    width = w_kv.shape[0]
+    piece = 4 * span
+    return pl.pallas_call(
+        functools.partial(attend_back_kernel, heads, hd, span, len(orders)),
+        out_shape=(
+            jax.ShapeDtypeStruct((rows, heads * hd), bf16),
+            jax.ShapeDtypeStruct((keys, heads * 2 * hd), bf16),
+        )
+        + (jax.ShapeDtypeStruct((2, 2 * piece, width), bf16),) * 2,
+        in_specs=[SMEM_SPEC] * 2 + [VMEM_SPEC] * 12 + [ANY_SPEC] * len(orders),
+        out_specs=(VMEM_SPEC,) * 4,
+        scratch_shapes=[
+            pltpu.VMEM((keys, heads * 2 * hd), f32),
+            pltpu.VMEM((rows, heads * hd), bf16),
+            pltpu.VMEM((rows, heads * hd), bf16),
+            pltpu.SMEM((keys // BLOCK,), jnp.int32),
+            pltpu.SMEM((keys // BLOCK,), jnp.int32),
+        ],
+        compiler_params=params(58),
+        cost_estimate=pl.CostEstimate(
+            flops=60 << 30, bytes_accessed=24 << 20, transcendentals=rows * heads * CHUNK
+        ),
+        name="attend_back",
+    )(coords, rand, q, *d_os, *os, kv, mask, lse, w_kv, w_q, *orders)
+
+
+def split_low(value):
+    top = value.astype(bf16)
+    return jnp.concatenate([top, (value - top.astype(f32)).astype(bf16)], axis=0)
+
+
+def joined(low):
+    return low[:8].astype(f32) + low[8:16].astype(f32)
+
+
+def qkv_grad_kernel(span, spot_ref, dq_ref, dkv_ref, keep_ref, got_ref, small_ref, *refs):
+    x_refs, out_ref = refs[:8], refs[-1]
+    piece = 4 * span
+    n_kv = dkv_ref.shape[1]
+    n_q = dq_ref.shape[1]
+    rows, width = out_ref.shape[1], x_refs[0].shape[1]
+    acc = jnp.zeros((n_kv, width), f32)
+    acc_q = jnp.zeros((n_q, width), f32)
+    for n, x_ref in enumerate(x_refs):
+        acc = acc + dot_tn(dkv_ref[n * piece : (n + 1) * piece, :], x_ref[...])
+    pair = 2 * span
+    for at, n, src in query_pieces(pair):
+        acc_q = acc_q + dot_tn(dq_ref[at : at + pair, :], x_refs[n][src : src + pair, :])
+    out_ref[...] = jnp.zeros_like(out_ref)
+    both = jnp.concatenate([acc, acc_q], axis=0)
+    octets = [both[o * rows : (o + 1) * rows] for o in range(6)]
+    w_out = keep_ref[keep_ref.shape[0] - 1].astype(f32) + got_ref[got_ref.shape[0] - 1].astype(f32)
+    octets += [w_out[:, :width], w_out[:, width:]]
+    sums = jnp.concatenate(
+        [
+            jnp.sum(dq_ref[...].astype(f32), axis=0, keepdims=True),
+            jnp.sum(dkv_ref[...].astype(f32), axis=0, keepdims=True),
+            jnp.zeros((1, 1024 - n_q - n_kv), f32),
+        ],
+        axis=1,
+    )
+    sums = jnp.concatenate([sums[:, i * 128 : (i + 1) * 128] for i in range(8)], axis=0)
+    for o in range(8):
+        spot = spot_ref[o]
+        out_ref[spot, :, :width] = octets[o].astype(bf16)
+        out_ref[spot, :16, width:] = split_low(small_ref[o] if o < 7 else sums)
+
+
+def qkv_grad(span, spots, dq, dkv, keep, got, small, xs, orders):
+    width = xs[0].shape[1]
+    rows = (dq.shape[1] + dkv.shape[1]) // 6
+    return pl.pallas_call(
+        functools.partial(qkv_grad_kernel, span),
+        out_shape=jax.ShapeDtypeStruct((8, rows, width + 128), bf16),
+        in_specs=[SMEM_SPEC] + [VMEM_SPEC] * 13 + [ANY_SPEC] * len(orders),
+        out_specs=VMEM_SPEC,
+        compiler_params=params(48),
+        cost_estimate=pl.CostEstimate(
+            flops=14 << 30, bytes_accessed=12 << 20, transcendentals=0
+        ),
+        name="qkv_grad",
+    )(spots, dq, dkv, keep, got, small, *xs, *orders)
+
+
+def wide_sum_kernel(order_ref, keep_ref, y_ref, x_ref, out_ref):
+    out_ref[...] = (keep_ref[...].astype(f32) + y_ref[...].astype(f32) + x_ref[...].astype(f32)).astype(bf16)
+
+
+def wide_sum(order, keep, y_got, x_got):
+    _, rows, cols = keep.shape
+    octet = pl.BlockSpec((1, rows, cols), lambda i, order_ref: (i, 0, 0))
+    return pl.pallas_call(
+        wide_sum_kernel,
+        grid_spec=pltpu.PrefetchScalarGridSpec(
+            num_scalar_prefetch=1,
+            grid=(4,),
+            in_specs=[octet] * 3,
+            out_specs=pl.BlockSpec((1, rows, cols), lambda i, order_ref: (order_ref[i], 0, 0)),
+        ),
+        out_shape=jax.ShapeDtypeStruct((4, rows, cols), bf16),
+        compiler_params=params(58),
+        cost_estimate=pl.CostEstimate(flops=1 << 28, bytes_accessed=6 << 20, transcendentals=0),
+        name="wide_sum",
+    )(order, keep, y_got, x_got)
+
+
+def tail_sum_kernel(n_orders, tail_ref, got_ref, *refs):
+    out_refs = refs[n_orders:]
+    thin = tail_ref.shape[2] - 128
+    for k in range(4):
+        out_refs[k][:, :thin] = (tail_ref[k, :, :thin].astype(f32) + got_ref[k, :, :thin].astype(f32)).astype(bf16)
+        out_refs[k][:, thin:] = jnp.zeros((tail_ref.shape[1], 128), bf16)
+        out_refs[k][:16, thin:] = split_low(joined(tail_ref[k, :16, thin:]) + joined(got_ref[k, :16, thin:]))
+
+
+def tail_sum(tail, tail_got, orders):
+    _, rows, cols = tail.shape
+    return pl.pallas_call(
+        functools.partial(tail_sum_kernel, len(orders)),
+        out_shape=(jax.ShapeDtypeStruct((rows, cols), bf16),) * 4,
+        in_specs=[VMEM_SPEC] * 2 + [ANY_SPEC] * len(orders),
+        out_specs=(VMEM_SPEC,) * 4,
+        compiler_params=params(58),
+        cost_estimate=pl.CostEstimate(flops=1 << 28, bytes_accessed=2 << 20, transcendentals=0),
+        name="tail_sum",
+    )(tail, tail_got, *orders)
+
+
+def wide_end_kernel(wide_ref, top_ref, low_ref, out_ref):
+    half = top_ref.shape[0]
+    for i, more_ref in enumerate((top_ref, low_ref)):
+        of = slice(i * half, (i + 1) * half)
+        out_ref[of, :] = (wide_ref[of, :].astype(f32) + more_ref[...].astype(f32)).astype(bf16)
+
+
+def wide_end(wide, top, low):
+    return pl.pallas_call(
+        wide_end_kernel,
+        out_shape=jax.ShapeDtypeStruct(wide.shape, bf16),
+        in_specs=[VMEM_SPEC] * 3,
+        out_specs=VMEM_SPEC,
+        compiler_params=params(58),
+        cost_estimate=pl.CostEstimate(flops=1 << 28, bytes_accessed=3 << 20, transcendentals=0),
+        name="wide_end",
+    )(wide, top, low)
+
+
+def tail_end_kernel(*refs):
+    thin_refs, out_ref = refs[:4], refs[-1]
+    thin = out_ref.shape[1] - 128
+    out_ref[:, :thin] = sum(r[:, :thin].astype(f32) for r in thin_refs).astype(bf16)
+    out_ref[:, thin:] = jnp.zeros((out_ref.shape[0], 128), bf16)
+    out_ref[:16, thin:] = split_low(sum(joined(r[:16, thin:]) for r in thin_refs))
+
+
+def tail_end(thins, orders):
+    return pl.pallas_call(
+        tail_end_kernel,
+        out_shape=jax.ShapeDtypeStruct(thins[0].shape, bf16),
+        in_specs=[VMEM_SPEC] * 4 + [ANY_SPEC] * len(orders),
+        out_specs=VMEM_SPEC,
+        compiler_params=params(58),
+        cost_estimate=pl.CostEstimate(flops=1 << 28, bytes_accessed=3 << 20, transcendentals=0),
+        name="tail_end",
+    )(*thins, *orders)
+
+
+def tail_place_kernel(spot_ref, *refs):
+    ins, out_ref, small_ref = refs[:8], refs[8], refs[9]
+    rows = ins[0].shape[0]
+    cols = out_ref.shape[1]
+    for n in range(8):
+        spot = spot_ref[n]
+        out_ref[pl.ds(pl.multiple_of(spot * rows, 16), rows), :] = ins[n][:, :cols]
+        small_ref[spot] = joined(ins[n][:16, cols:])
+
+
+def tail_place(spots, parts):
+    rows, cols = parts[0].shape
+    return pl.pallas_call(
+        tail_place_kernel,
+        out_shape=(
+            jax.ShapeDtypeStruct((8 * rows, cols - 128), bf16),
+            jax.ShapeDtypeStruct((8, 8, 128), f32),
+        ),
+        in_specs=[SMEM_SPEC] + [VMEM_SPEC] * 8,
+        out_specs=(VMEM_SPEC,) * 2,
+        compiler_params=params(58),
+        cost_estimate=pl.CostEstimate(flops=1 << 28, bytes_accessed=3 << 20, transcendentals=0),
+        name="tail_place",
+    )(spots, *parts)
+
+
+def across_sum_kernel(a_ref, b_ref, c_ref, d_ref, top_ref, low_ref):
+    half = top_ref.shape[0]
+    for i, out in enumerate((top_ref, low_ref)):
+        of = slice(i * half, (i + 1) * half)
+        out[...] = sum(r[of, :].astype(f32) for r in (a_ref, b_ref, c_ref, d_ref)).astype(bf16)
+
+
+def across_sum(parts):
+    rows, cols = parts[0].shape
+    return pl.pallas_call(
+        across_sum_kernel,
+        out_shape=(jax.ShapeDtypeStruct((rows // 2, cols), bf16),) * 2,
+        in_specs=[VMEM_SPEC] * 4,
+        out_specs=(VMEM_SPEC,) * 2,
+        compiler_params=params(58),
+        cost_estimate=pl.CostEstimate(flops=1 << 24, bytes_accessed=1 << 20, transcendentals=0),
+        name="across_sum",
+    )(*parts)
+
+
+def split_kernel(n_orders, coord_ref, rows_ref, *refs):
+    value = rows_ref[...].astype(f32)
+    pieces = [value[:, s, :] for s in range(4)]
+    z = coord_ref[0]
+    for k, out in enumerate(refs[n_orders:]):
+        low = jnp.where((z ^ k) % 2 == 0, pieces[0], pieces[1])
+        high = jnp.where((z ^ k) % 2 == 0, pieces[2], pieces[3])
+        out[...] = jnp.where((z ^ k) // 2 == 0, low, high).astype(bf16)
+
+
+def split(coords, rows, orders=()):
+    span, seqs, width = rows.shape
+    return pl.pallas_call(
+        functools.partial(split_kernel, len(orders)),
+        out_shape=(jax.ShapeDtypeStruct((span, width), bf16),) * seqs,
+        in_specs=[SMEM_SPEC, VMEM_SPEC] + [ANY_SPEC] * len(orders),
+        out_specs=(VMEM_SPEC,) * seqs,
+        compiler_params=params(32),
+        cost_estimate=pl.CostEstimate(flops=1 << 20, bytes_accessed=1 << 20, transcendentals=0),
+        name="split",
+    )(coords, rows, *orders)
+
+
+def qkv_weights_kernel(n_orders, w_ref, b_ref, *refs):
+    kv_ref, q_pad_ref, q_ref, b_kv_ref, b_q_ref = refs[n_orders:]
+    width, heads, _, hd = w_ref.shape
+    wide = 2 * hd
+    value = w_ref[...].astype(f32)
+    nil = jnp.zeros((width, hd), f32)
+    qs = []
+    for h in range(heads):
+        q, k, v = [value[:, h, c, :] for c in range(3)]
+        cols = slice(h * wide, (h + 1) * wide)
+        kv_ref[:, cols] = jnp.concatenate([k, v], axis=1).astype(bf16)
+        q_pad_ref[:, cols] = jnp.concatenate([q, nil], axis=1).astype(bf16)
+        b_kv_ref[:, cols] = jnp.concatenate([nil[:1], b_ref[h, 1:2, :]], axis=1)
+        b_q_ref[:, cols] = jnp.concatenate([b_ref[h, 0:1, :], nil[:1]], axis=1)
+        qs.append(q)
+    q_ref[...] = jnp.concatenate(qs, axis=1).astype(bf16)
+
+
+def qkv_weights(w_qkv, bias_qv, orders):
+    width, heads, _, hd = w_qkv.shape
+    cols = heads * 2 * hd
+    return pl.pallas_call(
+        functools.partial(qkv_weights_kernel, len(orders)),
+        out_shape=(
+            jax.ShapeDtypeStruct((width, cols), bf16),
+            jax.ShapeDtypeStruct((width, cols), bf16),
+            jax.ShapeDtypeStruct((width, heads * hd), bf16),
+            jax.ShapeDtypeStruct((1, cols), f32),
+            jax.ShapeDtypeStruct((1, cols), f32),
+        ),
+        in_specs=[VMEM_SPEC] * 2 + [ANY_SPEC] * len(orders),
+        out_specs=(VMEM_SPEC,) * 5,
+        compiler_params=params(40),
+        cost_estimate=pl.CostEstimate(flops=1 << 20, bytes_accessed=1 << 20, transcendentals=0),
+        name="qkv_weights",
+    )(w_qkv, bias_qv, *orders)
+
+
+def pack_kernel(heads_rows, order_ref, up_ref, down_ref, out_ref_in, bias_ref, pack_ref, first_ref, up_rows_ref):
+    width = up_ref.shape[0]
+    eighth = down_ref.shape[0] // 8
+    half = heads_rows // 2
+    for i in range(0, down_ref.shape[0], 256):
+        up_rows_ref[i : i + 256, :] = up_ref[:, i : i + 256].astype(f32).T.astype(bf16)
+    pack_ref[:half, :width] = out_ref_in[:half, :]
+    pack_ref[:half, width:] = out_ref_in[half:, :]
+    pack_ref[half : half + 16, :width] = bias_ref[...]
+    pack_ref[half : half + 16, width:] = jnp.zeros((16, width), bf16)
+    for n in range(8):
+        src = pl.ds(pl.multiple_of(order_ref[n] * eighth, 16), eighth)
+        for ref, at in ((pack_ref, half + 16), (first_ref, 0))[: 2 if n < 2 else 1]:
+            to = slice(at + n * eighth, at + (n + 1) * eighth)
+            ref[to, :width] = up_rows_ref[src, :]
+            ref[to, width:] = down_ref[src, :]
+
+
+def pack(order, up, down, w_out, bias):
+    hidden, width = down.shape
+    rows = w_out.shape[0] // 2 + 16
+    return pl.pallas_call(
+        functools.partial(pack_kernel, w_out.shape[0]),
+        out_shape=(
+            jax.ShapeDtypeStruct((rows + hidden, 2 * width), bf16),
+            jax.ShapeDtypeStruct((hidden // 4, 2 * width), bf16),
+        ),
+        in_specs=[SMEM_SPEC] + [VMEM_SPEC] * 4,
+        out_specs=(VMEM_SPEC,) * 2,
+        scratch_shapes=[pltpu.VMEM((hidden, width), bf16)],
+        compiler_params=params(32),
+        cost_estimate=pl.CostEstimate(flops=1 << 20, bytes_accessed=1 << 20, transcendentals=0),
+        name="pack",
+    )(order, up, down, w_out, bias)
+
+
+def copies_kernel(n_orders, *refs):
+    n = (len(refs) - n_orders) // 2
+    for ref, out in zip(refs[:n], refs[n + n_orders :]):
+        out[...] = ref[: out.shape[0], :]
+
+
+def copies(values, rows, orders):
+    return pl.pallas_call(
+        functools.partial(copies_kernel, len(orders)),
+        out_shape=tuple(jax.ShapeDtypeStruct((n, a.shape[1]), a.dtype) for a, n in zip(values, rows)),
+        grid=(1,),
+        in_specs=[pl.BlockSpec((n, a.shape[1]), lambda i: (0, 0)) for a, n in zip(values, rows)]
+        + [ANY_SPEC] * len(orders),
+        out_specs=tuple(pl.BlockSpec((n, a.shape[1]), lambda i: (0, 0)) for a, n in zip(values, rows)),
+        compiler_params=params(58),
+        cost_estimate=pl.CostEstimate(flops=1 << 20, bytes_accessed=1 << 20, transcendentals=0),
+        name="copies",
+    )(*values, *orders)
+
+
+def rows_kernel(width, n_out, tile_rows, *refs):
+    attn_refs, pack_refs = refs[:4], refs[4 : 4 + len(tile_rows)]
+    refs = refs[4 + len(tile_rows) :]
+    tok_refs, dres_refs, vec_ref = refs[:2], refs[2:6], refs[6]
+    result_refs = refs[7:11]
+    done_ref, hid_ref, dpre_ref, ylow_ref, dffn_ref, dbr_ref = refs[11:17]
+    dattn_refs = refs[17:20]
+    small_ref, bin_ref = refs[20:22]
+    slope_ref = refs[22]
+    bias_out, gain_one, bias_one, down_bias, gain_two, bias_two = [vec_ref[i : i + 1, :] for i in range(6)]
+    step = pl.program_id(0)
+    half = n_out // 2
+    tiles, wos, biases = [], [], []
+    for ref, first in zip(pack_refs, tile_rows):
+        if first:
+            wos.append(jnp.concatenate([ref[:half, :width], ref[:half, width:]], axis=0))
+            biases.append(ref[half : half + 1, :width].astype(f32))
+        left = ref.shape[0] - first
+        if left == 0:
+            continue
+        size = min(left, width // 2)
+        tiles += [ref.at[first + i * size : first + (i + 1) * size] for i in range(left // size)]
+    up_bias = jnp.concatenate(biases, axis=1)
+
+    def by_step(ones, twos):
+        pairs = [jnp.where(step == 0, a[...].astype(f32), b[...].astype(f32)) for a, b in zip(ones, twos)]
+        return pairs[0] if len(pairs) == 1 else jnp.concatenate(pairs, axis=0)
+
+    @pl.when(pl.program_id(0) == 0)
+    def _():
+        small_ref[...] = jnp.zeros_like(small_ref)
+        bin_ref[...] = jnp.zeros_like(bin_ref)
+
+    branch = bias_out
+    for k in range(4):
+        branch = branch + dot_nn(attn_refs[k][...], wos[k])
+    y_one, normed_one, inv_one = norm_fwd(by_step(tok_refs[:1], tok_refs[1:]) + branch, gain_one, bias_one)
+    y_low = y_one.astype(bf16)
+    ylow_ref[...] = y_low
+    ffn = down_bias
+    at = 0
+    spans = []
+    for tile in tiles:
+        spans.append(slice(at, at + tile.shape[0]))
+        at += tile.shape[0]
+    for cols, tile in zip(spans, tiles):
+        v = dot_nt(y_low, tile[:, :width]) + up_bias[:, cols]
+        sq = v * v
+        th = jnp.tanh(0.7978845608028654 * v * (1.0 + 0.044715 * sq))
+        half = 0.5 * (1.0 + th)
+        slope_ref[:, cols] = half + 0.5 * v * (1.0 - th * th) * (
+            0.7978845608028654 * (1.0 + 3.0 * 0.044715 * sq)
+        )
+        hid = (v * half).astype(bf16)
+        hid_ref[:, cols] = hid
+        ffn = ffn + dot_nn(hid, tile[:, width:])
+    result, normed_two, inv_two = norm_fwd(y_one + ffn, gain_two, bias_two)
+    for s in range(2):
+
+        @pl.when(step == s)
+        def _(s=s):
+            for k in range(2):
+                ref = result_refs[s + 2 * k]
+                ref[...] = result[k * ref.shape[0] : (k + 1) * ref.shape[0]].astype(bf16)
+
+    d_two, g_gain_two, g_bias_two = norm_back(by_step(dres_refs[::2], dres_refs[1::2]), normed_two, inv_two, gain_two)
+    d_ffn = d_two.astype(bf16)
+    dffn_ref[...] = d_ffn
+    g_bias_back = jnp.sum(d_ffn.astype(f32), axis=0)
+    d_y = d_two
+    for cols, tile in zip(spans, tiles):
+        d_pre = (dot_nt(d_ffn, tile[:, width:]) * slope_ref[:, cols]).astype(bf16)
+        dpre_ref[:, cols] = d_pre
+        bin_ref[:, cols] += jnp.sum(d_pre.astype(f32), axis=0, keepdims=True)
+        d_y = d_y + dot_nn(d_pre, tile[:, :width])
+    d_one, g_gain_one, g_bias_one = norm_back(d_y, normed_one, inv_one, gain_one)
+    done_ref[...] = d_one
+    d_branch = d_one.astype(bf16)
+    dbr_ref[...] = d_branch
+    g_bias_out = jnp.sum(d_branch.astype(f32), axis=0)
+    for k in range(4):
+        d_attn = dot_nt(d_branch, wos[k]).astype(bf16)
+        if k < 2:
+            dattn_refs[k][...] = d_attn
+        else:
+            dattn_refs[2][k - 2] = d_attn
+    sums = [g_bias_out, g_gain_one, g_bias_one, g_bias_back, g_gain_two, g_bias_two]
+    for i, one in enumerate(sums):
+        small_ref[i : i + 1, :] += one[None, :]
+
+
+def rows_work(attns, packs, first_rows, toks, d_res, vecs):
+    span, width = d_res[0].shape
+    rows = 4 * span
+    cols = attns[0].shape[1]
+    hidden = sum(a.shape[0] - n for a, n in zip(packs, first_rows))
+    tile = rows // 2
+
+    def by_rows(n):
+        return pl.BlockSpec((tile, n), lambda i: (i, 0))
+
+    def whole(a):
+        return pl.BlockSpec(a.shape, lambda i, nd=a.ndim: (0,) * nd, pipeline_mode=pl.Buffered(1))
+
+    def fixed(shape):
+        return pl.BlockSpec(shape, lambda i: (0, 0))
+
+    low = functools.partial(jax.ShapeDtypeStruct, dtype=bf16)
+    return pl.pallas_call(
+        functools.partial(rows_kernel, width, cols, first_rows),
+        grid=(rows // tile,),
+        out_shape=(low((span, width)),) * 4
+        + (
+            jax.ShapeDtypeStruct((rows, width), f32),
+            low((rows, hidden)),
+            low((rows, hidden)),
+            low((rows, width)),
+            low((rows, width)),
+            low((rows, width)),
+            low((rows, cols)),
+            low((rows, cols)),
+            low((2, rows, cols)),
+            jax.ShapeDtypeStruct((8, width), f32),
+            jax.ShapeDtypeStruct((1, hidden), f32),
+        ),
+        in_specs=[by_rows(cols)] * 4 + [whole(a) for a in (*packs, *toks, *d_res, vecs)],
+        out_specs=(fixed((span, width)),) * 4
+        + (
+            by_rows(width),
+            by_rows(hidden),
+            by_rows(hidden),
+            by_rows(width),
+            by_rows(width),
+            by_rows(width),
+            by_rows(cols),
+            by_rows(cols),
+            pl.BlockSpec((2, tile, cols), lambda i: (0, i, 0)),
+            fixed((8, width)),
+            fixed((1, hidden)),
+        ),
+        scratch_shapes=[pltpu.VMEM((tile, hidden), f32)],
+        compiler_params=params(58),
+        cost_estimate=pl.CostEstimate(flops=50 << 30, bytes_accessed=30 << 20, transcendentals=rows * hidden),
+        name="rows_work",
+    )(*attns, *packs, *toks, *d_res, vecs)
+
+
+def tile_grads(ylow_ref, dpre_ref, hid_ref, dffn_ref):
+    return dot_tn(dpre_ref[...], ylow_ref[...]), dot_tn(hid_ref[...], dffn_ref[...])
+
+
+def far_grad_kernel(ylow_ref, dpre_ref, hid_ref, dffn_ref, dbr_ref, attn0_ref, attn1_ref, out_ref):
+    width = ylow_ref.shape[1]
+    eighth = out_ref.shape[1]
+
+    @pl.when(pl.program_id(0) < 4)
+    def _():
+        g_in, g_back = tile_grads(ylow_ref, dpre_ref, hid_ref, dffn_ref)
+        for n in range(4):
+            out_ref[n, :, :width] = g_in[n * eighth : (n + 1) * eighth].astype(bf16)
+            out_ref[n, :, width:] = g_back[n * eighth : (n + 1) * eighth].astype(bf16)
+
+    @pl.when(pl.program_id(0) == 4)
+    def _():
+        for k, attn_ref in enumerate((attn0_ref, attn1_ref)):
+            g_out = dot_tn(attn_ref[...], dbr_ref[...]).astype(bf16)
+            out_ref[k, :, :width] = g_out[:eighth]
+            out_ref[k, :, width:] = g_out[eighth:]
+            out_ref[2 + k] = jnp.zeros_like(out_ref[2 + k])
+
+
+def near_grad_kernel(
+    n_orders, ylow_ref, dpre_ref, hid_ref, dffn_ref, dbr_ref, attn0_ref, attn1_ref, got_ref, *refs
+):
+    keep_ref, y_ref, x_ref, *across_refs, held_ref, sems = refs[n_orders:]
+    width = ylow_ref.shape[1]
+    eighth = got_ref.shape[1]
+    step = pl.program_id(0)
+
+    def moves(n):
+        if n == 0:
+            pairs = [(held_ref.at[0], keep_ref.at[0:4])]
+        elif n == 1:
+            pairs = [(held_ref.at[1], x_ref.at[0:4])]
+        elif n == 2:
+            pairs = [(held_ref.at[0], y_ref.at[0:4])]
+        elif n == 3:
+            pairs = [(held_ref.at[1, k], across_refs[k]) for k in range(4)]
+        else:
+            pairs = [(held_ref.at[0, 0], keep_ref.at[4]), (held_ref.at[0, 1], y_ref.at[4])]
+        return [pltpu.make_async_copy(a, b, sems.at[n, i]) for i, (a, b) in enumerate(pairs)]
+
+    for n in range(5):
+
+        @pl.when(step == n)
+        def _(n=n):
+            if n >= 2:
+                for copy in moves(n - 2):
+                    copy.wait()
+            if n < 4:
+                g_in, g_back = tile_grads(ylow_ref, dpre_ref, hid_ref, dffn_ref)
+                for k in range(4):
+                    rows = slice(k * eighth, (k + 1) * eighth)
+                    held_ref[n % 2, k, :, :width] = (g_in[rows] + got_ref[k, :, :width].astype(f32)).astype(bf16)
+                    held_ref[n % 2, k, :, width:] = (g_back[rows] + got_ref[k, :, width:].astype(f32)).astype(bf16)
+            else:
+                for k, attn_ref in enumerate((attn0_ref, attn1_ref)):
+                    g_out = dot_tn(attn_ref[...], dbr_ref[...])
+                    held_ref[0, k, :, :width] = (g_out[:eighth] + got_ref[k, :, :width].astype(f32)).astype(bf16)
+                    held_ref[0, k, :, width:] = (g_out[eighth:] + got_ref[k, :, width:].astype(f32)).astype(bf16)
+            for copy in moves(n):
+                copy.start()
+            if n == 4:
+                for copy in moves(3) + moves(4):
+                    copy.wait()
+
+
+def rows_grad(kc, y_low, d_pre, hidden, d_ffn, d_branch, attn0, attn1, got=None, orders=()):
+    rows, width = y_low.shape
+    part = hidden.shape[1] // 8
+    eighth = part // 4
+    block = (4, eighth, 2 * width)
+
+    def fixed(n):
+        return pl.BlockSpec((rows, n), lambda i: (0, 0), pipeline_mode=pl.Buffered(1))
+
+    def tile_of(i):
+        i = jnp.minimum(i, 3)
+        return (0, (i // 2) * 4 + kc * 2 + i % 2)
+
+    tile = pl.BlockSpec((rows, part), tile_of)
+    in_specs = [fixed(width), tile, tile, fixed(width), fixed(width), fixed(attn0.shape[1]), fixed(attn1.shape[1])]
+    octets = pl.BlockSpec(block, lambda i: (i, 0, 0))
+    cost = pl.CostEstimate(flops=8 << 30, bytes_accessed=16 << 20, transcendentals=0)
+    operands = (y_low, d_pre, hidden, d_ffn, d_branch, attn0, attn1)
+    if kc == 1:
+        return pl.pallas_call(
+            far_grad_kernel,
+            grid=(5,),
+            out_shape=jax.ShapeDtypeStruct((20,) + block[1:], bf16),
+            in_specs=in_specs,
+            out_specs=octets,
+            compiler_params=params(58),
+            cost_estimate=cost,
+            name="far_grad",
+        )(*operands)
+    return pl.pallas_call(
+        functools.partial(near_grad_kernel, len(orders)),
+        grid=(5,),
+        out_shape=tuple(jax.ShapeDtypeStruct((n,) + block[1:], bf16) for n in (5, 5, 4))
+        + (jax.ShapeDtypeStruct(block[1:], bf16),) * 4,
+        in_specs=in_specs + [octets] + [ANY_SPEC] * len(orders),
+        out_specs=(ANY_SPEC,) * 7,
+        scratch_shapes=[pltpu.VMEM((2,) + block, bf16), pltpu.SemaphoreType.DMA((5, 4))],
+        compiler_params=params(58),
+        cost_estimate=cost,
+        name="near_grad",
+    )(*operands, got, *orders)
+
+
+def row_sum_one_kernel(near_ref, got_ref, *refs):
+    for i, out in enumerate(refs[-2:]):
+
+        @pl.when(pl.program_id(0) == i)
+        def _(out=out):
+            out[...] = (near_ref[0].astype(f32) + got_ref[0].astype(f32)).astype(bf16)
+
+
+def row_sum_one(near, got, orders):
+    _, rows, width = near.shape
+    far = pl.BlockSpec((1, rows // 2, width), lambda i: (i, 1, 0))
+    return pl.pallas_call(
+        row_sum_one_kernel,
+        grid=(2,),
+        out_shape=(jax.ShapeDtypeStruct((rows // 2, width), bf16),) * 2,
+        in_specs=[far] * 2 + [ANY_SPEC] * len(orders),
+        out_specs=(pl.BlockSpec((rows // 2, width), lambda i: (0, 0)),) * 2,
+        compiler_params=params(58),
+        cost_estimate=pl.CostEstimate(flops=1 << 28, bytes_accessed=6 << 20, transcendentals=0),
+        name="row_sum_one",
+    )(near, got, *orders)
+
+
+def row_sum_two_kernel(near_ref, got_ref, even_ref, odd_ref, *refs):
+    for i, (src, out) in enumerate(zip((even_ref, odd_ref), refs[-2:])):
+
+        @pl.when(pl.program_id(0) == i)
+        def _(src=src, out=out):
+            out[...] = (near_ref[0].astype(f32) + got_ref[0].astype(f32) + src[...].astype(f32)).astype(bf16)
+
+
+def row_sum_two(near, got, even, odd, orders):
+    quarter, width = near.shape[1] // 4, near.shape[2]
+    part = pl.BlockSpec((1, quarter, width), lambda i: (i, 1, 0))
+    return pl.pallas_call(
+        row_sum_two_kernel,
+        grid=(2,),
+        out_shape=(jax.ShapeDtypeStruct((quarter, width), bf16),) * 2,
+        in_specs=[part] * 2 + [pl.BlockSpec((quarter, width), lambda i: (1, 0))] * 2 + [ANY_SPEC] * len(orders),
+        out_specs=(pl.BlockSpec((quarter, width), lambda i: (0, 0)),) * 2,
+        compiler_params=params(58),
+        cost_estimate=pl.CostEstimate(flops=1 << 28, bytes_accessed=4 << 20, transcendentals=0),
+        name="row_sum_two",
+    )(near, got, even, odd, *orders)
+
+
+def row_sum_three_kernel(near_ref, got_ref, even_ref, odd_ref, even_got, odd_got, done_ref, *out_refs):
+    rows = near_ref.shape[1]
+    for i, (one, two) in enumerate(((even_ref, even_got), (odd_ref, odd_got))):
+
+        @pl.when(pl.program_id(0) == i)
+        def _(i=i, one=one, two=two):
+            total = (
+                near_ref[0].astype(f32)
+                + got_ref[0].astype(f32)
+                + one[:rows, :].astype(f32)
+                + two[:rows, :].astype(f32)
+                + done_ref[...]
+            ).astype(bf16)
+            out_refs[i][...] = total[: rows // 2]
+            out_refs[i + 2][...] = total[rows // 2 :]
+
+
+def row_sum_three(near, got, even, odd, even_got, odd_got, d_one):
+    quarter, width = near.shape[1] // 4, near.shape[2]
+    part = pl.BlockSpec((1, quarter, width), lambda i: (i, 0, 0))
+    first = pl.BlockSpec((quarter, width), lambda i: (0, 0))
+    out = pl.BlockSpec((quarter // 2, width), lambda i: (0, 0))
+    return pl.pallas_call(
+        row_sum_three_kernel,
+        grid=(2,),
+        out_shape=(jax.ShapeDtypeStruct((quarter // 2, width), bf16),) * 4,
+        in_specs=[part] * 2 + [first] * 4 + [pl.BlockSpec((quarter, width), lambda i: (i, 0))],
+        out_specs=(out,) * 4,
+        compiler_params=params(58),
+        cost_estimate=pl.CostEstimate(flops=1 << 28, bytes_accessed=4 << 20, transcendentals=0),
+        name="row_sum_three",
+    )(near, got, even, odd, even_got, odd_got, d_one)
+
+
+def plane_layer(
+    tokens,
+    w_qkv,
+    bias_qv,
+    w_out,
+    bias_out,
+    gain_one,
+    bias_one,
+    up_weight,
+    up_bias_vector,
+    down_weight,
+    down_bias_vector,
+    gain_two,
+    bias_two,
+    d_out,
+    key_mask,
+    rand_idx,
+):
+    z = lax.axis_index("sq")
+    px = lax.axis_index("part")
+    hy = lax.axis_index("hy")
+    hc = lax.axis_index("hc")
+    head = hy * 2 + hc
+    span, seqs, width = tokens.shape
+    heads, hd = w_qkv.shape[1], w_qkv.shape[3]
+    n_o, n_kv = heads * hd, heads * 2 * hd
+    hidden_dev = up_weight.shape[1]
+    eighth = hidden_dev // 8
+    length = key_mask.shape[1]
+    blocks_all = length // BLOCK
+    rows = seqs * span
+    coords = jnp.stack([z, px, hy, hc]).astype(jnp.int32)
+    octet = jnp.arange(8)
+
+    def turn_octets(value):
+        shape = value.shape
+        value = flipped(value.reshape((2, 2, 2) + shape[1:]), z // 2, 0)
+        return flipped(flipped(value, z % 2, 1), px, 2).reshape(shape)
+
+    held_zd = octet // 2 % 2 + octet % 2 * 2
+    held_order = ((held_zd ^ z) * 2 + ((octet // 4) ^ px)).astype(jnp.int32)
+    bias_row = jnp.moveaxis(turn_octets(up_bias_vector.reshape(8, eighth)).reshape(2, 2, 2, eighth), (0, 2), (2, 0))
+    bias_row = jnp.pad(bias_row.reshape(1, hidden_dev), ((0, 15), (0, 0)))
+    wf, wf_first = pack(held_order, up_weight, down_weight, w_out.reshape(n_o, width), bias_row)
+    n_wo = n_o // 2 + 16
+    quarter = swap(wf_first, "hy", name="weight")
+
+    raw = split(coords, tokens, [wf])
+    tok = [raw[0]] + [swap(raw[k], "sq", k, name="tok") for k in range(1, 4)]
+    w_kv, w_q_pad, w_q, b_kv, b_q = qkv_weights(w_qkv, bias_qv, raw)
+    even = after(jnp.concatenate([tok[0], tok[2]], axis=0), *tok, w_kv, quarter)
+    odd = after(jnp.concatenate([tok[1], tok[3]], axis=0), *tok, w_kv, quarter)
+    even_x = swap(even, "part", name="tok")
+    odd_y = swap(odd, "hy", name="tok")
+    units = copies([quarter], [2 * eighth], [even, odd])[0]
+    wf_z = swap(units, "sq", 1, name="weight")
+    even_near = after(jnp.concatenate([even, even_x], axis=0), units)
+    odd_near = after(jnp.concatenate([odd, odd_y], axis=0), units)
+    even_far = swap(even_near, "hy", name="tok")
+    odd_far = swap(odd_near, "part", name="tok")
+    xs = [even_near, even_far, swap(even_near, "hc", name="tok"), swap(even_far, "hc", name="tok")]
+    xs += [odd_near, odd_far, swap(odd_near, "hc", name="tok"), swap(odd_far, "hc", name="tok")]
+    dres_raw = split(coords, d_out, [even_near, odd_near])
+    dres = [dres_raw[0]] + [swap(dres_raw[k], "sq", k, name="dres") for k in range(1, 4)]
+
+    mask_seq = lax.dynamic_index_in_dim(key_mask, z, 0, keepdims=False).reshape(blocks_all, BLOCK)
+    mask = jnp.where(mask_seq == 1, 0.0, MASK_FILL).astype(f32)
+    mask = jnp.pad(jnp.concatenate([mask, mask], axis=1), ((0, 8), (0, 0)), constant_values=MASK_FILL)
+    rand = lax.dynamic_slice(rand_idx, (z, 0, head * heads, 0), (1, blocks_all, heads, 3)).reshape(-1)
+    vecs = jnp.stack([bias_out, gain_one, bias_one, down_bias_vector, gain_two, bias_two])
+    vecs = jnp.pad(vecs, ((0, 2), (0, 0)))
+
+    wf_c = swap(wf, "hc", name="weight")
+    quarter_c = swap(quarter, "hc", name="weight")
+    wf_zc = swap(wf_z, "hc", name="weight")
+    units, units_z, wo = copies([quarter, wf_z, wf], [2 * eighth, 2 * eighth, n_wo], xs)
+    wo_y = swap(wo, "hy", name="weight")
+    wf_x = swap(units, "part", name="weight")
+    wf_zx = swap(units_z, "part", name="weight")
+
+    o_near, o_far, lse, kv, q = project_and_attend(
+        heads, hd, span, coords, rand, xs, w_kv, w_q_pad, b_kv, b_q, mask, [wf_c, quarter_c, wf_zc, units, *dres_raw]
+    )
+    o_far = after(o_far, *dres[1:])
+    wo_y, wf_x, wf_zx = after(wo_y, o_near), after(wf_x, o_near), after(wf_zx, o_near)
+    wo_yc = swap(wo_y, "hc", name="weight")
+    wf_xc = swap(wf_x, "hc", name="weight")
+    wf_zxc = swap(wf_zx, "hc", name="weight")
+    attn_y = swap(o_far, "hy", name="attn")
+    attn_c = swap(o_near[rows:], "hc", name="attn")
+    attn_yc = swap(attn_y[rows:], "hc", name="attn")
+
+    packs = [wf, wf_c, wo_y, quarter, wf_z, wf_x, wf_zx, wo_yc, quarter_c, wf_zc, wf_xc, wf_zxc]
+    first_rows = (n_wo, n_wo, n_wo, 0, 0, 0, 0, n_wo, 0, 0, 0, 0)
+    out = rows_work([o_near, attn_c, attn_y, attn_yc], packs, first_rows, [even, odd], dres, vecs)
+    result, (d_one, hidden, d_pre, y_low, d_ffn, d_branch, d_00, d_01, d_far, small, bin_sum) = out[:4], out[4:]
+
+    d_y = swap(d_far, "hy", name="dattn")
+    d_c = swap(d_01, "hc", name="dattn")
+    d_yc = swap(d_y[1], "hc", name="dattn")
+
+    other = rows_grad(1, y_low, d_pre, hidden, d_ffn, d_branch, attn_c, attn_yc)
+    wide_got = swap(other, "hc", name="wide")
+    res = [result[0]] + [swap(result[k], "sq", k, name="result") for k in range(1, 4)]
+    keep, to_y, to_x, *across = rows_grad(0, y_low, d_pre, hidden, d_ffn, d_branch, o_near, attn_y, wide_got, [d_y, d_c])
+    y_got = swap(to_y, "hy", name="wide")
+    x_got = swap(to_x, "part", name="wide")
+    across_got = [swap(across[p], "sq", k, name="wide") for p, k in ((2, 1), (1, 2), (3, 3))]
+
+    dq, dkv, dx, dx_far = attend_back(
+        heads,
+        hd,
+        span,
+        coords,
+        rand,
+        q,
+        [d_00, d_c, d_y, d_yc],
+        [o_near, o_far],
+        kv,
+        mask,
+        lse,
+        w_kv,
+        w_q,
+        [to_y, to_x, *across, *res[1:]],
+    )
+    dx_far = after(dx_far, y_got, x_got, *across_got)
+
+    b_in = bin_sum.reshape(4, hidden_dev)
+    flat = small[:6].reshape(-1)
+    n_flat = flat.size
+    got = swap(after(jnp.concatenate([flat, b_in[1], b_in[3]]), dq), "hc", name="small")
+    flat = flat + got[:n_flat]
+    b_in = jnp.stack([b_in[0], b_in[2]]) + got[n_flat:].reshape(2, hidden_dev)
+    got = swap(jnp.concatenate([flat, b_in[1]]), "hy", name="small")
+    flat = flat + got[:n_flat]
+    b_in = (b_in[0] + got[n_flat:]).reshape(2, 2, 2, eighth)
+    b_in = turn_octets(jnp.moveaxis(b_in, (2, 0), (0, 2)).reshape(8, eighth)).reshape(1, hidden_dev)
+    small = jnp.concatenate([flat.reshape(6, width), b_in, jnp.zeros((1, width), f32)], axis=0)
+    small = jnp.pad(small.reshape(8, width // 128, 128), ((0, 0), (0, 8 - width // 128), (0, 0)))
+
+    dx_got = swap(dx_far, "hc", name="dtok")
+    octets = octet[:4]
+    wide = wide_sum(((octets // 2 + octets % 2 * 2) ^ z).astype(jnp.int32), keep, y_got, x_got)
+    top, low = across_sum([across[0]] + across_got)
+    sent = row_sum_one(dx, dx_got, [wide, top, low])
+    wide = lax.psum_scatter(wide, "sq", scatter_dimension=0, tiled=True)[0]
+    top, low = swap(top, "part", name="across"), swap(low, "hy", name="across")
+    even_got, odd_got = swap(sent[0], "hy", name="dtok"), swap(sent[1], "part", name="dtok")
+
+    zq, xq = octet // 2, octet % 2
+    zd = zq ^ z
+    spots = ((xq ^ px) * 4 + (zd % 2) * 2 + zd // 2).astype(jnp.int32)
+    tail = qkv_grad(span, spots, dq, dkv, keep, y_got, small, xs, [*sent, top, low])
+    top, low = swap(top, "hy", name="across"), swap(low, "part", name="across")
+    tail_got = swap(tail[4:], "part", name="tail")
+    wide = wide_end(wide, top, low)
+    sent_two = row_sum_two(dx, dx_got, even_got, odd_got, [wide])
+    wide = lax.all_gather(wide, SEQ, axis=0, tiled=True)
+    even_got2, odd_got2 = swap(sent_two[0], "part", name="dtok"), swap(sent_two[1], "hy", name="dtok")
+    thins = tail_sum(tail, tail_got, [*sent_two])
+    thins = [thins[0]] + [swap(thins[p], "sq", k, name="tail") for p, k in ((2, 1), (1, 2), (3, 3))]
+    back_sent = row_sum_three(dx, dx_got, even_got, odd_got, even_got2, odd_got2, d_one)
+    back = [back_sent[0]] + [swap(back_sent[k], "sq", k, name="dtok") for k in range(1, 4)]
+
+    back_spots = (((octet % 4) ^ z) * 2 + ((octet // 4) ^ px)).astype(jnp.int32)
+    thin_held = tail_end(thins, [*back_sent])
+    thin_held = [thin_held] + [swap(thin_held, "sq", k, name="tail") for k in range(1, 4)]
+    thin_held += [swap(a, "part", name="tail") for a in thin_held]
+    grad_w_in = jnp.transpose(wide[:, :width]).astype(f32)
+    grad_w_back = wide[:, width:].astype(f32)
+    thin, small = tail_place(back_spots, thin_held)
+    g_kv = jnp.transpose(thin[:n_kv]).reshape(width, heads, 2, hd)
+    g_q = jnp.transpose(thin[n_kv : n_kv + n_o]).reshape(width, heads, 1, hd)
+    grad_w_qkv = jnp.concatenate([g_q, g_kv], axis=2).astype(f32)
+    grad_w_out = thin[n_kv + n_o :].reshape(heads, hd, width).astype(f32)
+    small = small.reshape(8, 1024)
+    grad_bias_qv = jnp.stack(
+        [small[7, :n_o].reshape(heads, hd), small[7, n_o : n_o + n_kv].reshape(heads, 2, hd)[:, 1]], axis=1
+    )
+    small = small[:, :width]
+    return (
+        jnp.transpose(relative(jnp.stack(res), z), (1, 0, 2)),
+        jnp.transpose(relative(jnp.stack(back), z), (1, 0, 2)),
+        grad_w_qkv,
+        grad_bias_qv,
+        grad_w_out,
+        small[0],
+        small[1],
+        small[2],
+        grad_w_in,
+        small[6],
+        grad_w_back,
+        small[3],
+        small[4],
+        small[5],
+    )
+
+
 def solution(mesh):
     seq_size, head_size = mesh.shape["seq"], mesh.shape["head"]
 
@@ -484,6 +1713,9 @@
             ("sq", "part", "hy", "hc"),
         )
         rows = P(("sq", "part", "hy", "hc"), None, None)
+        span = args[0].shape[0] // (seq_size * head_size)
+        fits = seqs == 4 and seq_size == 8 and head_size == 4 and span % BLOCK == 0
+        layer = plane_layer if fits else general_layer
         placed = (
             rows,
             P(None, HEAD, None, None),
@@ -503,7 +1735,7 @@
             P(),
         )
         return jax.shard_map(
-            per_device,
+            layer,
             mesh=fine,
             in_specs=placed,
             out_specs=(

time: 564 us -> 436 us (0.77)
  blocking collectives: 119 us -> 0 us
  matrix products: 65.3 us -> 0 us
  Pallas kernels: 108 us -> 165 us
  starting transfers between devices: 17 us -> 68.3 us
  waiting for transfers between devices: 166 us -> 128 us
  other arithmetic: 27.5 us -> 16.1 us
    ppermute x0 -> x65, waiting for transfers between devices: none -> 121 us  [swap(): return lax.ppermute(value, axis, [(i, i ^ step) for i in range(size)])]
    psum x1 -> x0, waiting for transfers between devices: 85.9 us -> none  [per_device(): wide_sum = lax.psum(wide_sum, SEQ)]
    ppermute x0 -> x65, starting transfers between devices: none -> 68.2 us  [swap(): return lax.ppermute(value, axis, [(i, i ^ step) for i in range(size)])]
    dot_general x16 -> x0, matrix products: 65.3 us -> none  [the longest x1 7.79 us: per_device(): jnp.einsum('grf,gfd->rd', hidden, down_full, preferred_element_type=f32)]
    psum x1 -> x0, blocking collectives: 57.2 us -> none  [per_device(): packed = lax.psum(packed, ('sq', 'part', 'hy', 'hc'))]
    pallas_call x2 -> x31, Pallas kernels: 108 us -> 165 us  [the longest x1 35.6 us: attend_back(): pl.pallas_call(functools.partial(attend_back_kernel, heads, hd, span, len...]
    all_to_all x2 -> x0, blocking collectives: 40.7 us -> none  [the longest x1 26.5 us: per_device(): lax.all_to_all(jnp.transpose(tokens, (1, 0, 2)), 'sq', 0, 0, tiled=True)]
    reduce_scatter x2 -> x1, waiting for transfers between devices: 44.8 us -> 7.62 us  [plane_layer(): wide = lax.psum_scatter(wide, 'sq', scatter_dimension=0, tiled=True)[0]]
  transfers between devices with their start and end apart: 11 -> 67, of which waited for: 3 -> 23; matrix products, arithmetic and copies ran while one was open for 13% -> 6% of each run, Pallas kernels for 20% -> 28%
where the time goes in v2:
time: 436 us; the launch traced here: 431 us
  Pallas kernels  165 us (38%)
  waiting for transfers between devices  128 us (29%)
  starting transfers between devices  68.3 us (16%)
  local copies, waits for them, and re-layouts  38.3 us (9%)
  other arithmetic  16.1 us (4%)
  between operations  15.4 us (4%)
    ppermute x65, waiting for transfers between devices, swap(): return lax.ppermute(value, axis, [(i, i ^ step) for i in range(size)])  121 us
    ppermute x65, starting transfers between devices, swap(): return lax.ppermute(value, axis, [(i, i ^ step) for i in range(size)])  68.2 us
    pallas_call x1, Pallas kernels, attend_back(): pl.pallas_call(functools.partial(attend_back_kernel, heads, hd, span, len...  35.6 us
    pallas_call x1, Pallas kernels, rows_work(): pl.pallas_call(functools.partial(rows_kernel, width, cols, first_rows), g...  34.3 us
    unnamed x187, local copies, waits for them, and re-layouts  28 us
    pallas_call x1, Pallas kernels, project_and_attend(): pl.pallas_call(functools.partial(project_and_attend_kernel, heads, hd, sp...  26.6 us
    pallas_call x1, Pallas kernels, rows_grad(): pl.pallas_call(functools.partial(near_grad_kernel, len(orders)), grid=(5,...  9.75 us
  transfers between devices with their start and end apart: 67, of which 23 were waited for; matrix products, arithmetic and copies ran while one was open for 6% of the time, Pallas kernels for 28%

profile of v2, /device:TPU:0, one launch (start us, length us, event | category | flops | bytes accessed | tf_op | source)
XLA Modules:
  0.0 431.2 jit_solution(1124622429312586626)
XLA Ops:
  11.7 2.7 pack.1
  14.5 3.0 collective-permute-start.3
  17.5 3.3 split.2
  20.8 1.6 collective-permute-start.1
  22.5 2.5 collective-permute-start.2
  25.1 4.0 copy.57.w_ref
  29.0 2.9 qkv_weights.1
  35.0 1.7 pad_maximum_fusion.5.refs_0_
  36.7 6.4 %collective-permute-done.refs_3_ = bf16[128,768]{1,0:T(8,128)(2,1)} collective-permute-done((bf16[128,768]{1,0:T(8,128)(2,1)S(1)}, bf16[128,768]{1,0:T(8,128)(2,1)}, u32[]{:S(2)}, u32[]{:S(2)}) %collective-permute-start) | collective-permute-done | bytes 196640 | tf_op jit(solution)/shard_map/tok_sq2/ppermute | solution.py:480
  43.7 1.7 pad_maximum_fusion.4.refs_0_
  46.9 1.9 copies.2.refs_1_
  48.8 5.3 %collective-permute-done.8 = bf16[256,768]{1,0:T(8,128)(2,1)S(1)} collective-permute-done((bf16[256,768]{1,0:T(8,128)(2,1)}, bf16[256,768]{1,0:T(8,128)(2,1)S(1)}, u32[]{:S(2)}, u32[]{:S(2)}) %collective-permute-start.8) | collective-permute-done | bytes 393248 | tf_op jit(solution)/shard_map/tok_hy1/ppermute | solution.py:480
  56.6 1.9 pad_maximum_fusion.refs_0_
  59.9 3.7 collective-permute-done.14.refs_1_.refs_8_
  63.6 10.1 %collective-permute-done.9.refs_8_.refs_5_ = bf16[512,768]{1,0:T(8,128)(2,1)S(1)} collective-permute-done((bf16[512,768]{1,0:T(8,128)(2,1)}, bf16[512,768]{1,0:T(8,128)(2,1)S(1)}, u32[]{:S(2)}, u32[]{:S(2)}) %collective-permute-start.9) | collective-permute-done | bytes 786464 | tf_op jit(solution)/shard_map/tok_part1/ppermute | solution.py:480
  73.7 3.1 collective-permute-done.5.refs_4_.refs_1_
  79.4 3.3 split.3
  86.7 2.5 collective-permute-start.18
  89.3 2.5 copies.3
  91.8 1.9 collective-permute-start.19
  96.7 26.6 %project_and_attend.1 = (bf16[1024,192]{1,0:T(8,128)(2,1)}, bf16[1024,192]{1,0:T(8,128)(2,1)}, f32[2048,128]{1,0:T(8,128)}, bf16[4096,384]{1,0:T(8,128)(2,1)}, bf16[2048,384]{1,0:T(8,128)(2,1)}) custom-call(s32[4]{0:T(128)} %copy-done.20, s32[576]{0:T(1024)} %reshape.119.rand_ref, bf16[512,768]{1,0:T(8,128)(2,1)} %after.12.refs_3_.refs_0_, ...), custom_call_target="tpu_custom_call" | custom-call | flops 42949672960 | bytes 16777216 | tf_op jit(solution)/shard_map/project_and_attend/pallas_call | solution.py:697
  128.8 8.2 %collective-permute-done.20.refs_2_.attn1_ref = bf16[1024,192]{1,0:T(8,128)(2,1)S(1)} collective-permute-done((bf16[1024,192]{1,0:T(8,128)(2,1)}, bf16[1024,192]{1,0:T(8,128)(2,1)S(1)}, u32[]{:S(2)}, u32[]{:S(2)}) %collective-permute-start.20) | collective-permute-done | bytes 393248 | tf_op jit(solution)/shard_map/attn_hy1/ppermute | solution.py:480
  140.3 34.3 %rows_work.1 = (bf16[128,768]{1,0:T(8,128)(2,1)}, bf16[128,768]{1,0:T(8,128)(2,1)}, bf16[128,768]{1,0:T(8,128)(2,1)}, bf16[128,768]{1,0:T(8,128)(2,1)}, f32[512,...) custom-call(bf16[1024,192]{1,0:T(8,128)(2,1)} %get-tuple-element.94., ...), custom_call_target="tpu_custom_call" | custom-call | flops 53687091200 | bytes 31457280 | tf_op jit(solution)/shard_map/rows_work/pallas_call | solution.py:1276
  174.7 7.9 %far_grad.1 = bf16[20,96,1536]{2,1,0:T(8,128)(2,1)} custom-call(bf16[512,768]{1,0:T(8,128)(2,1)} %get-tuple-element.109.ylow_ref, bf16[512,3072]{1,0:T(8,128)(2,1)} %get-tuple-element.110.dpre_ref, bf16[512,3072]{1,0:T(8,128)(2,1)} %get-tuple-element.111.hid_ref, bf16[512,768]{1,0:T(8,128)(2,1)} %get-tuple-element.112.dffn_ref, ...), custom_call_target="tpu_custom_call" | custom-call | flops 8589934592 | bytes 16777216 | tf_op jit(solution)/shard_map/far_grad/pallas_call | solution.py:1404
  183.9 2.5 collective-permute-start.29
  186.4 10.6 %collective-permute-done.32.refs_0_.refs_2_ = bf16[2,512,192]{2,1,0:T(8,128)(2,1)S(1)} collective-permute-done((bf16[2,512,192]{2,1,0:T(8,128)(2,1)S(1)}, bf16[2,512,192]{2,1,0:T(8,128)(2,1)S(1)}, u32[]{:S(2)}, u32[]{:S(2)}) %collective-permute-start.32) | collective-permute-done | bytes 393248 | tf_op jit(solution)/shard_map/dattn_hy1/ppermute | solution.py:480
  196.9 2.0 collective-permute-start.30
  199.7 9.8 %near_grad.1 = (bf16[5,96,1536]{2,1,0:T(8,128)(2,1)}, bf16[5,96,1536]{2,1,0:T(8,128)(2,1)}, bf16[4,96,1536]{2,1,0:T(8,128)(2,1)}, bf16[96,1536]{1,0:T(8,128)(2,1...) custom-call(bf16[512,768]{1,0:T(8,128)(2,1)} %get-tuple-element.109.ylow_ref, ...), custom_call_target="tpu_custom_call" | custom-call | flops 8589934592 | bytes 16777216 | tf_op jit(solution)/shard_map/near_grad/pallas_call | solution.py:1414
  209.5 2.4 collective-permute-start.38
  211.9 2.0 collective-permute-start.39
  215.9 35.6 %attend_back.1 = (bf16[2048,192]{1,0:T(8,128)(2,1)}, bf16[4096,384]{1,0:T(8,128)(2,1)}, bf16[2,1024,768]{2,1,0:T(8,128)(2,1)}, bf16[2,1024,768]{2,1,0:T(8,128)(2,1)}) custom-call(s32[4]{0:T(128)} %copy-done.20, s32[576]{0:T(1024)} %reshape.119.rand_ref, bf16[2048,384]{1,0:T(8,128)(2,1)} %get-tuple-element.102.q_ref, ...), custom_call_target="tpu_custom_call" | custom-call | flops 64424509440 | bytes 25165824 | tf_op jit(solution)/shard_map/attend_back/pallas_call | solution.py:840
  254.0 4.8 %wide_sum.1.refs_0_ = bf16[4,96,1536]{2,1,0:T(8,128)(2,1)} custom-call(s32[4]{0:T(128)} %fusion.14.order_ref, bf16[5,96,1536]{2,1,0:T(8,128)(2,1)} %get-tuple-element.122.keep_ref, bf16[5,96,1536]{2,1,0:T(8,128)(2,1)} %copy-done.32, bf16[4,96,1536]{2,1,0:T(8,128)(2,1)} %copy-done.33), custom_call_target="tpu_custom_call" | custom-call | flops 268435456 | bytes 6291456 | tf_op jit(solution)/shard_map/wide_sum/pallas_call | solution.py:929
  261.2 1.6 collective-permute-start.53
  263.0 2.1 collective-permute-done.53
  265.3 2.0 across_sum.1
  269.7 3.1 collective-permute-done.43.refs_10_
  275.0 2.8 collective-permute-done.44.top_ref
  277.9 1.5 collective-permute-done.46.low_ref
  279.4 7.6 %reduce-scatter.2.cloned.1.call-done = bf16[1,96,1536]{2,1,0:T(8,128)(2,1)} async-done(((bf16[4,96,1536]{2,1,0:T(8,128)(2,1)}), bf16[1,96,1536]{2,1,0:T(8,128)(2,1)}) %reduce-scatter.2.cloned.1.call-update) | async-done | bytes 294928 | tf_op jit(solution)/shard_map/reduce_scatter | solution.py:1653
  287.0 1.9 wide_end.1.refs_0_
  289.0 3.6 row_sum_one.1
  295.6 8.7 %qkv_grad.1.tail_ref = bf16[8,96,896]{2,1,0:T(8,128)(2,1)} custom-call(s32[8]{0:T(128)S(1)} %fusion.12.spot_ref, bf16[2048,192]{1,0:T(8,128)(2,1)} %get-tuple-element.134.refs_1_.dq_ref, bf16[4096,384]{1,0:T(8,128)(2,1)} %get-tuple-element.135.dkv_ref, bf16[5,96,1536]{2,1,0:T(8,128)(2,1)} %get-tuple-element.122.keep_ref, bf16[5,96,1536]{2,1,0:T(8,128)(2,1)} %copy-done.32, ...), custom_call_target="tpu_custom_call" | custom-call | flops 15032385536 | bytes 12582912 | tf_op jit(solution)/shard_map/qkv_grad/pallas_call | solution.py:909
  306.2 5.8 %collective-permute-done.41.even_ref = bf16[512,768]{1,0:T(8,128)(2,1)S(1)} collective-permute-done((bf16[512,768]{1,0:T(8,128)(2,1)}, bf16[512,768]{1,0:T(8,128)(2,1)S(1)}, u32[]{:S(2)}, u32[]{:S(2)}) %collective-permute-start.41) | collective-permute-done | bytes 786464 | tf_op jit(solution)/shard_map/dtok_hy1/ppermute | solution.py:480
  311.9 6.0 %collective-permute-done.42.odd_ref = bf16[512,768]{1,0:T(8,128)(2,1)S(1)} collective-permute-done((bf16[512,768]{1,0:T(8,128)(2,1)}, bf16[512,768]{1,0:T(8,128)(2,1)S(1)}, u32[]{:S(2)}, u32[]{:S(2)}) %collective-permute-start.42) | collective-permute-done | bytes 786464 | tf_op jit(solution)/shard_map/dtok_part1/ppermute | solution.py:480
  318.8 2.6 row_sum_two.1
  323.6 21.6 %collective-permute-done.54.got_ref = bf16[4,96,896]{2,1,0:T(8,128)(2,1)S(1)} collective-permute-done((bf16[4,96,896]{2,1,0:T(8,128)(2,1)S(1)}, bf16[4,96,896]{2,1,0:T(8,128)(2,1)S(1)}, u32[]{:S(2)}, u32[]{:S(2)}) %collective-permute-start.54) | collective-permute-done | bytes 688160 | tf_op jit(solution)/shard_map/tail_part1/ppermute | solution.py:480
  346.0 2.5 tail_sum.1
  348.6 4.4 %collective-permute-start.57 = (bf16[96,896]{1,0:T(8,128)(2,1)}, bf16[96,896]{1,0:T(8,128)(2,1)S(1)}, u32[]{:S(2)}, u32[]{:S(2)}) collective-permute-start(bf16[96,896]{1,0:T(8,128)(2,1)} %get-tuple-element.141), channel_id=1, source_target_pairs={{0,24},{8,16},{16,8},{24,0},{1,25},{9,17},{17,9},{25,1},{2,26},{10... | collective-permute-start | bytes 516104 | tf_op jit(solution)/shard_map/tail_sq3/ppermute | solution.py:480
  353.8 3.4 row_sum_three.1
  357.3 2.0 collective-permute-done.55.refs_1_
  359.2 6.5 %collective-permute-done.56.refs_2_ = bf16[96,896]{1,0:T(8,128)(2,1)S(1)} collective-permute-done((bf16[96,896]{1,0:T(8,128)(2,1)}, bf16[96,896]{1,0:T(8,128)(2,1)S(1)}, u32[]{:S(2)}, u32[]{:S(2)}) %collective-permute-start.56) | collective-permute-done | bytes 172064 | tf_op jit(solution)/shard_map/tail_sq2/ppermute | solution.py:480
  366.5 1.9 tail_end.1.refs_0_
  368.4 2.5 collective-permute-start.58
  370.9 2.4 collective-permute-start.60
  375.3 3.5 collective-permute-done.58.refs_1_
  378.8 1.9 collective-permute-start.51
  381.4 4.9 %collective-permute-done.59.refs_2_ = bf16[96,896]{1,0:T(8,128)(2,1)S(1)} collective-permute-done((bf16[96,896]{1,0:T(8,128)(2,1)}, bf16[96,896]{1,0:T(8,128)(2,1)S(1)}, u32[]{:S(2)}, u32[]{:S(2)}) %collective-permute-start.59) | collective-permute-done | bytes 172064 | tf_op jit(solution)/shard_map/tail_sq2/ppermute | solution.py:480
  386.3 2.5 collective-permute-start.61
  388.9 1.9 collective-permute-start.63
  390.9 10.0 %collective-permute-done.50 = bf16[128,768]{1,0:T(8,128)(2,1)S(1)} collective-permute-done((bf16[128,768]{1,0:T(8,128)(2,1)}, bf16[128,768]{1,0:T(8,128)(2,1)S(1)}, u32[]{:S(2)}, u32[]{:S(2)}) %collective-permute-start.50) | collective-permute-done | bytes 196640 | tf_op jit(solution)/shard_map/dtok_sq2/ppermute | solution.py:480
  400.9 3.5 collective-permute-start.64
  409.6 2.5 tail_place.1
  418.8 3.4 slice_convert_fusion
  422.2 1.9 copy.65
  (371 shorter events, 70.4 us)
Async XLA Ops:
  7.2 279.8 %reduce-scatter.2.cloned.1.call-start = ((), (), s32[]{:S(2)}) async-start(), calls=%async_computation.1 | async-start | bytes 1474560 | tf_op jit(solution)/shard_map/reduce_scatter | solution.py:1653
  14.5 28.6 %collective-permute-start.3 = (bf16[192,1536]{1,0:T(8,128)(2,1)}, bf16[192,1536]{1,0:T(8,128)(2,1)}, u32[]{:S(2)}, u32[]{:S(2)}) collective-permute-start(bf16[192,1536]{1,0:T(8,128)(2,1)} %get-tuple-element.85), channel_id=1, source_target_pairs={{0,2},{2,0},{1,3},{3,1},{4,6},{6,4},{5,7},{7,5},{8,10},{10,8},{9,1... | collective-permute-start | bytes 1769480 | tf_op jit(solution)/shard_map/weight_hy1/ppermute | solution.py:480
  17.5 78.2 %collective-permute-start.12 = (bf16[880,1536]{1,0:T(8,128)(2,1)}, bf16[880,1536]{1,0:T(8,128)(2,1)}, u32[]{:S(2)}, u32[]{:S(2)}) collective-permute-start(bf16[880,1536]{1,0:T(8,128)(2,1)} %get-tuple-element.79.refs_0_.refs_2_.refs_4_), channel_id=1, source_target_pairs={{0,1},{1,0},{2,3},{3,2},{4,5},{5,4},{6,7},{7,6},{8,9},{9,8},{10,11... | collective-permute-start | bytes 8110088 | tf_op jit(solution)/shard_map/weight_hc1/ppermute | solution.py:480
  20.8 12.7 %collective-permute-start.1 = (bf16[128,768]{1,0:T(8,128)(2,1)S(1)}, bf16[128,768]{1,0:T(8,128)(2,1)S(1)}, u32[]{:S(2)}, u32[]{:S(2)}) collective-permute-start(bf16[128,768]{1,0:T(8,128)(2,1)S(1)} %get-tuple-element.82.refs_1_), channel_id=1, source_target_pairs={{0,8},{8,0},{16,24},{24,16},{1,9},{9,1},{17,25},{25,17},{2,10},{10... | collective-permute-start | bytes 589832 | tf_op jit(solution)/shard_map/tok_sq1/ppermute | solution.py:480
  22.5 12.6 %collective-permute-start.2 = (bf16[128,768]{1,0:T(8,128)(2,1)S(1)}, bf16[128,768]{1,0:T(8,128)(2,1)}, u32[]{:S(2)}, u32[]{:S(2)}) collective-permute-start(bf16[128,768]{1,0:T(8,128)(2,1)S(1)} %get-tuple-element.83.refs_3_), channel_id=1, source_target_pairs={{0,24},{8,16},{16,8},{24,0},{1,25},{9,17},{17,9},{25,1},{2,26},{10... | collective-permute-start | bytes 589832 | tf_op jit(solution)/shard_map/tok_sq3/ppermute | solution.py:480
  25.0 18.1 %collective-permute-start = (bf16[128,768]{1,0:T(8,128)(2,1)S(1)}, bf16[128,768]{1,0:T(8,128)(2,1)}, u32[]{:S(2)}, u32[]{:S(2)}) collective-permute-start(bf16[128,768]{1,0:T(8,128)(2,1)S(1)} %get-tuple-element.81.refs_2_), channel_id=1, source_target_pairs={{0,16},{8,24},{16,0},{24,8},{1,17},{9,25},{17,1},{25,9},{2,18},{10... | collective-permute-start | bytes 589832 | tf_op jit(solution)/shard_map/tok_sq2/ppermute | solution.py:480
  43.1 11.0 %collective-permute-start.8 = (bf16[256,768]{1,0:T(8,128)(2,1)}, bf16[256,768]{1,0:T(8,128)(2,1)S(1)}, u32[]{:S(2)}, u32[]{:S(2)}) collective-permute-start(bf16[256,768]{1,0:T(8,128)(2,1)} %after.11.refs_2_.refs_17_), channel_id=1, source_target_pairs={{0,2},{2,0},{1,3},{3,1},{4,6},{6,4},{5,7},{7,5},{8,10},{10,8},{9,1... | collective-permute-start | bytes 1179656 | tf_op jit(solution)/shard_map/tok_hy1/ppermute | solution.py:480
  45.4 11.2 %collective-permute-start.4 = (bf16[256,768]{1,0:T(8,128)(2,1)}, bf16[256,768]{1,0:T(8,128)(2,1)}, u32[]{:S(2)}, u32[]{:S(2)}) collective-permute-start(bf16[256,768]{1,0:T(8,128)(2,1)} %after.10.refs_1_.refs_16_), channel_id=1, source_target_pairs={{0,4},{4,0},{1,5},{5,1},{2,6},{6,2},{3,7},{7,3},{8,12},{12,8},{9,1... | collective-permute-start | bytes 1179656 | tf_op jit(solution)/shard_map/tok_part1/ppermute | solution.py:480
  48.8 14.7 %collective-permute-start.14 = (bf16[192,1536]{1,0:T(8,128)(2,1)}, bf16[192,1536]{1,0:T(8,128)(2,1)}, u32[]{:S(2)}, u32[]{:S(2)}) collective-permute-start(bf16[192,1536]{1,0:T(8,128)(2,1)} %copies.2.refs_1_), channel_id=1, source_target_pairs={{0,8},{8,0},{16,24},{24,16},{1,9},{9,1},{17,25},{25,17},{2,10},{10... | collective-permute-start | bytes 1769480 | tf_op jit(solution)/shard_map/weight_sq1/ppermute | solution.py:480
  55.1 18.6 %collective-permute-start.9 = (bf16[512,768]{1,0:T(8,128)(2,1)}, bf16[512,768]{1,0:T(8,128)(2,1)S(1)}, u32[]{:S(2)}, u32[]{:S(2)}) collective-permute-start(bf16[512,768]{1,0:T(8,128)(2,1)} %after.13.refs_7_.refs_1_.refs_4_), channel_id=1, source_target_pairs={{0,4},{4,0},{1,5},{5,1},{2,6},{6,2},{3,7},{7,3},{8,12},{12,8},{9,1... | collective-permute-start | bytes 2359304 | tf_op jit(solution)/shard_map/tok_part1/ppermute | solution.py:480
  58.5 18.3 %collective-permute-start.5 = (bf16[512,768]{1,0:T(8,128)(2,1)}, bf16[512,768]{1,0:T(8,128)(2,1)S(1)}, u32[]{:S(2)}, u32[]{:S(2)}) collective-permute-start(bf16[512,768]{1,0:T(8,128)(2,1)} %after.12.refs_3_.refs_0_), channel_id=1, source_target_pairs={{0,2},{2,0},{1,3},{3,1},{4,6},{6,4},{5,7},{7,5},{8,10},{10,8},{9,1... | collective-permute-start | bytes 2359304 | tf_op jit(solution)/shard_map/tok_hy1/ppermute | solution.py:480
  59.9 17.0 %collective-permute-start.10 = (bf16[512,768]{1,0:T(8,128)(2,1)S(1)}, bf16[512,768]{1,0:T(8,128)(2,1)S(1)}, u32[]{:S(2)}, u32[]{:S(2)}) collective-permute-start(bf16[512,768]{1,0:T(8,128)(2,1)S(1)} %copy-done.2), channel_id=1, source_target_pairs={{0,1},{1,0},{2,3},{3,2},{4,5},{5,4},{6,7},{7,6},{8,9},{9,8},{10,11... | collective-permute-start | bytes 2359304 | tf_op jit(solution)/shard_map/tok_hc1/ppermute | solution.py:480
  63.5 14.7 %collective-permute-start.6 = (bf16[512,768]{1,0:T(8,128)(2,1)}, bf16[512,768]{1,0:T(8,128)(2,1)}, u32[]{:S(2)}, u32[]{:S(2)}) collective-permute-start(bf16[512,768]{1,0:T(8,128)(2,1)} %after.12.refs_3_.refs_0_), channel_id=1, source_target_pairs={{0,1},{1,0},{2,3},{3,2},{4,5},{5,4},{6,7},{7,6},{8,9},{9,8},{10,11... | collective-permute-start | bytes 2359304 | tf_op jit(solution)/shard_map/tok_hc1/ppermute | solution.py:480
  73.7 10.4 %collective-permute-start.11 = (bf16[512,768]{1,0:T(8,128)(2,1)S(1)}, bf16[512,768]{1,0:T(8,128)(2,1)}, u32[]{:S(2)}, u32[]{:S(2)}) collective-permute-start(bf16[512,768]{1,0:T(8,128)(2,1)S(1)} %collective-permute-done.9.refs_8_.refs_5_), channel_id=1, source_target_pairs={{0,1},{1,0},{2,3},{3,2},{4,5},{5,4},{6,7},{7,6},{8,9},{9,8},{10,11... | collective-permute-start | bytes 2359304 | tf_op jit(solution)/shard_map/tok_hc1/ppermute | solution.py:480
  76.8 9.9 %collective-permute-start.7 = (bf16[512,768]{1,0:T(8,128)(2,1)S(1)}, bf16[512,768]{1,0:T(8,128)(2,1)}, u32[]{:S(2)}, u32[]{:S(2)}) collective-permute-start(bf16[512,768]{1,0:T(8,128)(2,1)S(1)} %collective-permute-done.5.refs_4_.refs_1_), channel_id=1, source_target_pairs={{0,1},{1,0},{2,3},{3,2},{4,5},{5,4},{6,7},{7,6},{8,9},{9,8},{10,11... | collective-permute-start | bytes 2359304 | tf_op jit(solution)/shard_map/tok_hc1/ppermute | solution.py:480
  77.8 14.0 %collective-permute-start.13 = (bf16[192,1536]{1,0:T(8,128)(2,1)}, bf16[192,1536]{1,0:T(8,128)(2,1)}, u32[]{:S(2)}, u32[]{:S(2)}) collective-permute-start(bf16[192,1536]{1,0:T(8,128)(2,1)} %collective-permute-done.3.refs_6_.refs_0_.refs_7_), channel_id=1, source_target_pairs={{0,1},{1,0},{2,3},{3,2},{4,5},{5,4},{6,7},{7,6},{8,9},{9,8},{10,11... | collective-permute-start | bytes 1769480 | tf_op jit(solution)/shard_map/weight_hc1/ppermute | solution.py:480
  78.2 16.4 %collective-permute-start.15 = (bf16[192,1536]{1,0:T(8,128)(2,1)}, bf16[192,1536]{1,0:T(8,128)(2,1)}, u32[]{:S(2)}, u32[]{:S(2)}) collective-permute-start(bf16[192,1536]{1,0:T(8,128)(2,1)} %collective-permute-done.14.refs_1_.refs_8_), channel_id=1, source_target_pairs={{0,1},{1,0},{2,3},{3,2},{4,5},{5,4},{6,7},{7,6},{8,9},{9,8},{10,11... | collective-permute-start | bytes 1769480 | tf_op jit(solution)/shard_map/weight_hc1/ppermute | solution.py:480
  84.1 9.6 %collective-permute-start.17 = (bf16[128,768]{1,0:T(8,128)(2,1)}, bf16[128,768]{1,0:T(8,128)(2,1)S(1)}, u32[]{:S(2)}, u32[]{:S(2)}) collective-permute-start(bf16[128,768]{1,0:T(8,128)(2,1)} %get-tuple-element.91.refs_18_), channel_id=1, source_target_pairs={{0,8},{8,0},{16,24},{24,16},{1,9},{9,1},{17,25},{25,17},{2,10},{10... | collective-permute-start | bytes 589832 | tf_op jit(solution)/shard_map/dres_sq1/ppermute | solution.py:480
  86.7 36.6 %collective-permute-start.18 = (bf16[128,768]{1,0:T(8,128)(2,1)}, bf16[128,768]{1,0:T(8,128)(2,1)S(1)}, u32[]{:S(2)}, u32[]{:S(2)}) collective-permute-start(bf16[128,768]{1,0:T(8,128)(2,1)} %copy-done.26), channel_id=1, source_target_pairs={{0,16},{8,24},{16,0},{24,8},{1,17},{9,25},{17,1},{25,9},{2,18},{10... | collective-permute-start | bytes 589832 | tf_op jit(solution)/shard_map/dres_sq2/ppermute | solution.py:480
  91.8 31.6 %collective-permute-start.19 = (bf16[128,768]{1,0:T(8,128)(2,1)S(1)}, bf16[128,768]{1,0:T(8,128)(2,1)S(1)}, u32[]{:S(2)}, u32[]{:S(2)}) collective-permute-start(bf16[128,768]{1,0:T(8,128)(2,1)S(1)} %get-tuple-element.93.refs_20_), channel_id=1, source_target_pairs={{0,24},{8,16},{16,8},{24,0},{1,25},{9,17},{17,9},{25,1},{2,26},{10... | collective-permute-start | bytes 589832 | tf_op jit(solution)/shard_map/dres_sq3/ppermute | solution.py:480
  93.6 31.5 %collective-permute-start.24 = (bf16[192,1536]{1,0:T(8,128)(2,1)}, bf16[192,1536]{1,0:T(8,128)(2,1)S(1)}, u32[]{:S(2)}, u32[]{:S(2)}) collective-permute-start(bf16[192,1536]{1,0:T(8,128)(2,1)} %get-tuple-element.97), channel_id=1, source_target_pairs={{0,4},{4,0},{1,5},{5,1},{2,6},{6,2},{3,7},{7,3},{8,12},{12,8},{9,1... | collective-permute-start | bytes 1769480 | tf_op jit(solution)/shard_map/weight_part1/ppermute | solution.py:480
  94.6 31.5 %collective-permute-start.23 = (bf16[192,1536]{1,0:T(8,128)(2,1)}, bf16[192,1536]{1,0:T(8,128)(2,1)S(1)}, u32[]{:S(2)}, u32[]{:S(2)}) collective-permute-start(bf16[192,1536]{1,0:T(8,128)(2,1)} %get-tuple-element.89.refs_16_), channel_id=1, source_target_pairs={{0,4},{4,0},{1,5},{5,1},{2,6},{6,2},{3,7},{7,3},{8,12},{12,8},{9,1... | collective-permute-start | bytes 1769480 | tf_op jit(solution)/shard_map/weight_part1/ppermute | solution.py:480
  95.7 31.8 %collective-permute-start.22 = (bf16[112,1536]{1,0:T(8,128)(2,1)}, bf16[112,1536]{1,0:T(8,128)(2,1)S(1)}, u32[]{:S(2)}, u32[]{:S(2)}) collective-permute-start(bf16[112,1536]{1,0:T(8,128)(2,1)} %get-tuple-element.96), channel_id=1, source_target_pairs={{0,2},{2,0},{1,3},{3,1},{4,6},{6,4},{5,7},{7,5},{8,10},{10,8},{9,1... | collective-permute-start | bytes 1032200 | tf_op jit(solution)/shard_map/weight_hy1/ppermute | solution.py:480
  124.1 12.8 %collective-permute-start.20 = (bf16[1024,192]{1,0:T(8,128)(2,1)}, bf16[1024,192]{1,0:T(8,128)(2,1)S(1)}, u32[]{:S(2)}, u32[]{:S(2)}) collective-permute-start(bf16[1024,192]{1,0:T(8,128)(2,1)} %after.14.refs_5_), channel_id=1, source_target_pairs={{0,2},{2,0},{1,3},{3,1},{4,6},{6,4},{5,7},{7,5},{8,10},{10,8},{9,1... | collective-permute-start | bytes 1179656 | tf_op jit(solution)/shard_map/attn_hy1/ppermute | solution.py:480
  126.0 12.5 %collective-permute-start.27 = (bf16[192,1536]{1,0:T(8,128)(2,1)}, bf16[192,1536]{1,0:T(8,128)(2,1)S(1)}, u32[]{:S(2)}, u32[]{:S(2)}) collective-permute-start(bf16[192,1536]{1,0:T(8,128)(2,1)} %after.17.refs_10_), channel_id=1, source_target_pairs={{0,1},{1,0},{2,3},{3,2},{4,5},{5,4},{6,7},{7,6},{8,9},{9,8},{10,11... | collective-permute-start | bytes 1769480 | tf_op jit(solution)/shard_map/weight_hc1/ppermute | solution.py:480
  127.0 11.6 %collective-permute-start.26 = (bf16[192,1536]{1,0:T(8,128)(2,1)}, bf16[192,1536]{1,0:T(8,128)(2,1)S(1)}, u32[]{:S(2)}, u32[]{:S(2)}) collective-permute-start(bf16[192,1536]{1,0:T(8,128)(2,1)} %after.16.refs_9_), channel_id=1, source_target_pairs={{0,1},{1,0},{2,3},{3,2},{4,5},{5,4},{6,7},{7,6},{8,9},{9,8},{10,11... | collective-permute-start | bytes 1769480 | tf_op jit(solution)/shard_map/weight_hc1/ppermute | solution.py:480
  128.2 9.7 %collective-permute-start.25 = (bf16[112,1536]{1,0:T(8,128)(2,1)}, bf16[112,1536]{1,0:T(8,128)(2,1)S(1)}, u32[]{:S(2)}, u32[]{:S(2)}) collective-permute-start(bf16[112,1536]{1,0:T(8,128)(2,1)} %after.15.refs_6_), channel_id=1, source_target_pairs={{0,1},{1,0},{2,3},{3,2},{4,5},{5,4},{6,7},{7,6},{8,9},{9,8},{10,11... | collective-permute-start | bytes 1032200 | tf_op jit(solution)/shard_map/weight_hc1/ppermute | solution.py:480
  128.2 9.6 %collective-permute-start.16 = (bf16[512,192]{1,0:T(8,128)(2,1)S(1)}, bf16[512,192]{1,0:T(8,128)(2,1)S(1)}, u32[]{:S(2)}, u32[]{:S(2)}) collective-permute-start(bf16[512,192]{1,0:T(8,128)(2,1)S(1)} %slice.145), channel_id=1, source_target_pairs={{0,1},{1,0},{2,3},{3,2},{4,5},{5,4},{6,7},{7,6},{8,9},{9,8},{10,11... | collective-permute-start | bytes 589832 | tf_op jit(solution)/shard_map/attn_hc1/ppermute | solution.py:480
  182.6 16.5 %collective-permute-start.34 = (bf16[20,96,1536]{2,1,0:T(8,128)(2,1)}, bf16[20,96,1536]{2,1,0:T(8,128)(2,1)}, u32[]{:S(2)}, u32[]{:S(2)}) collective-permute-start(bf16[20,96,1536]{2,1,0:T(8,128)(2,1)} %far_grad.1), channel_id=1, source_target_pairs={{0,1},{1,0},{2,3},{3,2},{4,5},{5,4},{6,7},{7,6},{8,9},{9,8},{10,11... | collective-permute-start | bytes 17694728 | tf_op jit(solution)/shard_map/wide_hc1/ppermute | solution.py:480
  182.7 14.2 %collective-permute-start.32 = (bf16[2,512,192]{2,1,0:T(8,128)(2,1)S(1)}, bf16[2,512,192]{2,1,0:T(8,128)(2,1)S(1)}, u32[]{:S(2)}, u32[]{:S(2)}) collective-permute-start(bf16[2,512,192]{2,1,0:T(8,128)(2,1)S(1)} %copy-done.79), channel_id=1, source_target_pairs={{0,2},{2,0},{1,3},{3,1},{4,6},{6,4},{5,7},{7,5},{8,10},{10,8},{9,1... | collective-permute-start | bytes 1179656 | tf_op jit(solution)/shard_map/dattn_hy1/ppermute | solution.py:480
  183.8 15.2 %collective-permute-start.31 = (bf16[512,192]{1,0:T(8,128)(2,1)S(1)}, bf16[512,192]{1,0:T(8,128)(2,1)S(1)}, u32[]{:S(2)}, u32[]{:S(2)}) collective-permute-start(bf16[512,192]{1,0:T(8,128)(2,1)S(1)} %copy-done.85), channel_id=1, source_target_pairs={{0,1},{1,0},{2,3},{3,2},{4,5},{5,4},{6,7},{7,6},{8,9},{9,8},{10,11... | collective-permute-start | bytes 589832 | tf_op jit(solution)/shard_map/dattn_hc1/ppermute | solution.py:480
  183.9 25.7 %collective-permute-start.28 = (bf16[128,768]{1,0:T(8,128)(2,1)S(1)}, bf16[128,768]{1,0:T(8,128)(2,1)S(1)}, u32[]{:S(2)}, u32[]{:S(2)}) collective-permute-start(bf16[128,768]{1,0:T(8,128)(2,1)S(1)} %copy-done.88), channel_id=1, source_target_pairs={{0,8},{8,0},{16,24},{24,16},{1,9},{9,1},{17,25},{25,17},{2,10},{10... | collective-permute-start | bytes 589832 | tf_op jit(solution)/shard_map/result_sq1/ppermute | solution.py:480
  183.9 28.0 %collective-permute-start.29 = (bf16[128,768]{1,0:T(8,128)(2,1)S(1)}, bf16[128,768]{1,0:T(8,128)(2,1)S(1)}, u32[]{:S(2)}, u32[]{:S(2)}) collective-permute-start(bf16[128,768]{1,0:T(8,128)(2,1)S(1)} %copy-done.87), channel_id=1, source_target_pairs={{0,16},{8,24},{16,0},{24,8},{1,17},{9,25},{17,1},{25,9},{2,18},{10... | collective-permute-start | bytes 589832 | tf_op jit(solution)/shard_map/result_sq2/ppermute | solution.py:480
  196.9 17.0 %collective-permute-start.30 = (bf16[128,768]{1,0:T(8,128)(2,1)S(1)}, bf16[128,768]{1,0:T(8,128)(2,1)S(1)}, u32[]{:S(2)}, u32[]{:S(2)}) collective-permute-start(bf16[128,768]{1,0:T(8,128)(2,1)S(1)} %copy-done.86), channel_id=1, source_target_pairs={{0,24},{8,16},{16,8},{24,0},{1,25},{9,17},{17,9},{25,1},{2,26},{10... | collective-permute-start | bytes 589832 | tf_op jit(solution)/shard_map/result_sq3/ppermute | solution.py:480
  199.0 15.9 %collective-permute-start.33 = (bf16[512,192]{1,0:T(8,128)(2,1)S(1)}, bf16[512,192]{1,0:T(8,128)(2,1)S(1)}, u32[]{:S(2)}, u32[]{:S(2)}) collective-permute-start(bf16[512,192]{1,0:T(8,128)(2,1)S(1)} %slice_bitcast_fusion), channel_id=1, source_target_pairs={{0,1},{1,0},{2,3},{3,2},{4,5},{5,4},{6,7},{7,6},{8,9},{9,8},{10,11... | collective-permute-start | bytes 589832 | tf_op jit(solution)/shard_map/dattn_hc1/ppermute | solution.py:480
  209.4 42.1 %collective-permute-start.37 = (bf16[96,1536]{1,0:T(8,128)(2,1)}, bf16[96,1536]{1,0:T(8,128)(2,1)S(1)}, u32[]{:S(2)}, u32[]{:S(2)}) collective-permute-start(bf16[96,1536]{1,0:T(8,128)(2,1)} %get-tuple-element.118.refs_15_), channel_id=1, source_target_pairs={{0,8},{8,0},{16,24},{24,16},{1,9},{9,1},{17,25},{25,17},{2,10},{10... | collective-permute-start | bytes 884744 | tf_op jit(solution)/shard_map/wide_sq1/ppermute | solution.py:480
  209.5 42.0 %collective-permute-start.38 = (bf16[96,1536]{1,0:T(8,128)(2,1)}, bf16[96,1536]{1,0:T(8,128)(2,1)S(1)}, u32[]{:S(2)}, u32[]{:S(2)}) collective-permute-start(bf16[96,1536]{1,0:T(8,128)(2,1)} %get-tuple-element.117.refs_14_), channel_id=1, source_target_pairs={{0,16},{8,24},{16,0},{24,8},{1,17},{9,25},{17,1},{25,9},{2,18},{10... | collective-permute-start | bytes 884744 | tf_op jit(solution)/shard_map/wide_sq2/ppermute | solution.py:480
  211.9 39.7 %collective-permute-start.39 = (bf16[96,1536]{1,0:T(8,128)(2,1)}, bf16[96,1536]{1,0:T(8,128)(2,1)S(1)}, u32[]{:S(2)}, u32[]{:S(2)}) collective-permute-start(bf16[96,1536]{1,0:T(8,128)(2,1)} %get-tuple-element.119.refs_16_), channel_id=1, source_target_pairs={{0,24},{8,16},{16,8},{24,0},{1,25},{9,17},{17,9},{25,1},{2,26},{10... | collective-permute-start | bytes 884744 | tf_op jit(solution)/shard_map/wide_sq3/ppermute | solution.py:480
  213.9 37.7 %collective-permute-start.35 = (bf16[5,96,1536]{2,1,0:T(8,128)(2,1)}, bf16[5,96,1536]{2,1,0:T(8,128)(2,1)S(1)}, u32[]{:S(2)}, u32[]{:S(2)}) collective-permute-start(bf16[5,96,1536]{2,1,0:T(8,128)(2,1)} %get-tuple-element.114.refs_11_), channel_id=1, source_target_pairs={{0,2},{2,0},{1,3},{3,1},{4,6},{6,4},{5,7},{7,5},{8,10},{10,8},{9,1... | collective-permute-start | bytes 4423688 | tf_op jit(solution)/shard_map/wide_hy1/ppermute | solution.py:480
  214.9 36.7 %collective-permute-start.36 = (bf16[4,96,1536]{2,1,0:T(8,128)(2,1)}, bf16[4,96,1536]{2,1,0:T(8,128)(2,1)S(1)}, u32[]{:S(2)}, u32[]{:S(2)}) collective-permute-start(bf16[4,96,1536]{2,1,0:T(8,128)(2,1)} %get-tuple-element.115.refs_12_), channel_id=1, source_target_pairs={{0,4},{4,0},{1,5},{5,1},{2,6},{6,2},{3,7},{7,3},{8,12},{12,8},{9,1... | collective-permute-start | bytes 3538952 | tf_op jit(solution)/shard_map/wide_part1/ppermute | solution.py:480
  253.5 35.4 %collective-permute-start.40 = (bf16[2,1024,768]{2,1,0:T(8,128)(2,1)}, bf16[2,1024,768]{2,1,0:T(8,128)(2,1)}, u32[]{:S(2)}, u32[]{:S(2)}) collective-permute-start(bf16[2,1024,768]{2,1,0:T(8,128)(2,1)} %after.18), channel_id=1, source_target_pairs={{0,1},{1,0},{2,3},{3,2},{4,5},{5,4},{6,7},{7,6},{8,9},{9,8},{10,11... | collective-permute-start | bytes 9437192 | tf_op jit(solution)/shard_map/dtok_hc1/ppermute | solution.py:480
  258.9 159.9 %all-gather.2.cloned.1.call-start = ((), (), s32[]{:S(2)}) async-start(), calls=%async_computation.2 | async-start | bytes 2654208 | tf_op jit(solution)/shard_map/all_gather | solution.py:1665
  267.4 5.4 %collective-permute-start.43 = (bf16[48,1536]{1,0:T(8,128)(2,1)}, bf16[48,1536]{1,0:T(8,128)(2,1)S(1)}, u32[]{:S(2)}, u32[]{:S(2)}) collective-permute-start(bf16[48,1536]{1,0:T(8,128)(2,1)} %get-tuple-element.123.refs_1_), channel_id=1, source_target_pairs={{0,4},{4,0},{1,5},{5,1},{2,6},{6,2},{3,7},{7,3},{8,12},{12,8},{9,1... | collective-permute-start | bytes 442376 | tf_op jit(solution)/shard_map/across_part1/ppermute | solution.py:480
  268.4 5.8 %collective-permute-start.45 = (bf16[48,1536]{1,0:T(8,128)(2,1)}, bf16[48,1536]{1,0:T(8,128)(2,1)S(1)}, u32[]{:S(2)}, u32[]{:S(2)}) collective-permute-start(bf16[48,1536]{1,0:T(8,128)(2,1)} %get-tuple-element.124.refs_2_), channel_id=1, source_target_pairs={{0,2},{2,0},{1,3},{3,1},{4,6},{6,4},{5,7},{7,5},{8,10},{10,8},{9,1... | collective-permute-start | bytes 442376 | tf_op jit(solution)/shard_map/across_hy1/ppermute | solution.py:480
  272.7 5.1 %collective-permute-start.44 = (bf16[48,1536]{1,0:T(8,128)(2,1)S(1)}, bf16[48,1536]{1,0:T(8,128)(2,1)S(1)}, u32[]{:S(2)}, u32[]{:S(2)}) collective-permute-start(bf16[48,1536]{1,0:T(8,128)(2,1)S(1)} %collective-permute-done.43.refs_10_), channel_id=1, source_target_pairs={{0,2},{2,0},{1,3},{3,1},{4,6},{6,4},{5,7},{7,5},{8,10},{10,8},{9,1... | collective-permute-start | bytes 442376 | tf_op jit(solution)/shard_map/across_hy1/ppermute | solution.py:480
  274.2 5.1 %collective-permute-start.46 = (bf16[48,1536]{1,0:T(8,128)(2,1)S(1)}, bf16[48,1536]{1,0:T(8,128)(2,1)S(1)}, u32[]{:S(2)}, u32[]{:S(2)}) collective-permute-start(bf16[48,1536]{1,0:T(8,128)(2,1)S(1)} %collective-permute-done.45.refs_11_), channel_id=1, source_target_pairs={{0,4},{4,0},{1,5},{5,1},{2,6},{6,2},{3,7},{7,3},{8,12},{12,8},{9,1... | collective-permute-start | bytes 442376 | tf_op jit(solution)/shard_map/across_part1/ppermute | solution.py:480
  292.6 19.3 %collective-permute-start.41 = (bf16[512,768]{1,0:T(8,128)(2,1)}, bf16[512,768]{1,0:T(8,128)(2,1)S(1)}, u32[]{:S(2)}, u32[]{:S(2)}) collective-permute-start(bf16[512,768]{1,0:T(8,128)(2,1)} %get-tuple-element.125.refs_8_), channel_id=1, source_target_pairs={{0,2},{2,0},{1,3},{3,1},{4,6},{6,4},{5,7},{7,5},{8,10},{10,8},{9,1... | collective-permute-start | bytes 2359304 | tf_op jit(solution)/shard_map/dtok_hy1/ppermute | solution.py:480
  294.1 23.8 %collective-permute-start.42 = (bf16[512,768]{1,0:T(8,128)(2,1)}, bf16[512,768]{1,0:T(8,128)(2,1)S(1)}, u32[]{:S(2)}, u32[]{:S(2)}) collective-permute-start(bf16[512,768]{1,0:T(8,128)(2,1)} %get-tuple-element.126.refs_9_), channel_id=1, source_target_pairs={{0,4},{4,0},{1,5},{5,1},{2,6},{6,2},{3,7},{7,3},{8,12},{12,8},{9,1... | collective-permute-start | bytes 2359304 | tf_op jit(solution)/shard_map/dtok_part1/ppermute | solution.py:480
  305.4 39.8 %collective-permute-start.54 = (bf16[4,96,896]{2,1,0:T(8,128)(2,1)S(1)}, bf16[4,96,896]{2,1,0:T(8,128)(2,1)S(1)}, u32[]{:S(2)}, u32[]{:S(2)}) collective-permute-start(bf16[4,96,896]{2,1,0:T(8,128)(2,1)S(1)} %slice.188), channel_id=1, source_target_pairs={{0,4},{4,0},{1,5},{5,1},{2,6},{6,2},{3,7},{7,3},{8,12},{12,8},{9,1... | collective-permute-start | bytes 2064392 | tf_op jit(solution)/shard_map/tail_part1/ppermute | solution.py:480
  321.4 31.5 %collective-permute-start.47 = (bf16[256,768]{1,0:T(8,128)(2,1)}, bf16[256,768]{1,0:T(8,128)(2,1)S(1)}, u32[]{:S(2)}, u32[]{:S(2)}) collective-permute-start(bf16[256,768]{1,0:T(8,128)(2,1)} %get-tuple-element.127.refs_0_), channel_id=1, source_target_pairs={{0,4},{4,0},{1,5},{5,1},{2,6},{6,2},{3,7},{7,3},{8,12},{12,8},{9,1... | collective-permute-start | bytes 1179656 | tf_op jit(solution)/shard_map/dtok_part1/ppermute | solution.py:480
  322.5 30.5 %collective-permute-start.48 = (bf16[256,768]{1,0:T(8,128)(2,1)}, bf16[256,768]{1,0:T(8,128)(2,1)S(1)}, u32[]{:S(2)}, u32[]{:S(2)}) collective-permute-start(bf16[256,768]{1,0:T(8,128)(2,1)} %get-tuple-element.128.refs_1_), channel_id=1, source_target_pairs={{0,2},{2,0},{1,3},{3,1},{4,6},{6,4},{5,7},{7,5},{8,10},{10,8},{9,1... | collective-permute-start | bytes 1179656 | tf_op jit(solution)/shard_map/dtok_hy1/ppermute | solution.py:480
  348.5 10.7 %collective-permute-start.55 = (bf16[96,896]{1,0:T(8,128)(2,1)}, bf16[96,896]{1,0:T(8,128)(2,1)S(1)}, u32[]{:S(2)}, u32[]{:S(2)}) collective-permute-start(bf16[96,896]{1,0:T(8,128)(2,1)} %get-tuple-element.139), channel_id=1, source_target_pairs={{0,8},{8,0},{16,24},{24,16},{1,9},{9,1},{17,25},{25,17},{2,10},{10... | collective-permute-start | bytes 516104 | tf_op jit(solution)/shard_map/tail_sq1/ppermute | solution.py:480
  348.5 17.2 %collective-permute-start.56 = (bf16[96,896]{1,0:T(8,128)(2,1)}, bf16[96,896]{1,0:T(8,128)(2,1)S(1)}, u32[]{:S(2)}, u32[]{:S(2)}) collective-permute-start(bf16[96,896]{1,0:T(8,128)(2,1)} %get-tuple-element.140), channel_id=1, source_target_pairs={{0,16},{8,24},{16,0},{24,8},{1,17},{9,25},{17,1},{25,9},{2,18},{10... | collective-permute-start | bytes 516104 | tf_op jit(solution)/shard_map/tail_sq2/ppermute | solution.py:480
  348.6 17.2 %collective-permute-start.57 = (bf16[96,896]{1,0:T(8,128)(2,1)}, bf16[96,896]{1,0:T(8,128)(2,1)S(1)}, u32[]{:S(2)}, u32[]{:S(2)}) collective-permute-start(bf16[96,896]{1,0:T(8,128)(2,1)} %get-tuple-element.141), channel_id=1, source_target_pairs={{0,24},{8,16},{16,8},{24,0},{1,25},{9,17},{17,9},{25,1},{2,26},{10... | collective-permute-start | bytes 516104 | tf_op jit(solution)/shard_map/tail_sq3/ppermute | solution.py:480
  368.4 10.4 %collective-permute-start.58 = (bf16[96,896]{1,0:T(8,128)(2,1)}, bf16[96,896]{1,0:T(8,128)(2,1)S(1)}, u32[]{:S(2)}, u32[]{:S(2)}) collective-permute-start(bf16[96,896]{1,0:T(8,128)(2,1)} %tail_end.1.refs_0_), channel_id=1, source_target_pairs={{0,8},{8,0},{16,24},{24,16},{1,9},{9,1},{17,25},{25,17},{2,10},{10... | collective-permute-start | bytes 516104 | tf_op jit(solution)/shard_map/tail_sq1/ppermute | solution.py:480
  370.9 15.4 %collective-permute-start.59 = (bf16[96,896]{1,0:T(8,128)(2,1)}, bf16[96,896]{1,0:T(8,128)(2,1)S(1)}, u32[]{:S(2)}, u32[]{:S(2)}) collective-permute-start(bf16[96,896]{1,0:T(8,128)(2,1)} %tail_end.1.refs_0_), channel_id=1, source_target_pairs={{0,16},{8,24},{16,0},{24,8},{1,17},{9,25},{17,1},{25,9},{2,18},{10... | collective-permute-start | bytes 516104 | tf_op jit(solution)/shard_map/tail_sq2/ppermute | solution.py:480
  370.9 18.0 %collective-permute-start.60 = (bf16[96,896]{1,0:T(8,128)(2,1)}, bf16[96,896]{1,0:T(8,128)(2,1)S(1)}, u32[]{:S(2)}, u32[]{:S(2)}) collective-permute-start(bf16[96,896]{1,0:T(8,128)(2,1)} %tail_end.1.refs_0_), channel_id=1, source_target_pairs={{0,24},{8,16},{16,8},{24,0},{1,25},{9,17},{17,9},{25,1},{2,26},{10... | collective-permute-start | bytes 516104 | tf_op jit(solution)/shard_map/tail_sq3/ppermute | solution.py:480
  373.3 15.7 %collective-permute-start.49 = (bf16[128,768]{1,0:T(8,128)(2,1)}, bf16[128,768]{1,0:T(8,128)(2,1)S(1)}, u32[]{:S(2)}, u32[]{:S(2)}) collective-permute-start(bf16[128,768]{1,0:T(8,128)(2,1)} %get-tuple-element.131.refs_5_), channel_id=1, source_target_pairs={{0,8},{8,0},{16,24},{24,16},{1,9},{9,1},{17,25},{25,17},{2,10},{10... | collective-permute-start | bytes 589832 | tf_op jit(solution)/shard_map/dtok_sq1/ppermute | solution.py:480
  374.4 26.5 %collective-permute-start.50 = (bf16[128,768]{1,0:T(8,128)(2,1)}, bf16[128,768]{1,0:T(8,128)(2,1)S(1)}, u32[]{:S(2)}, u32[]{:S(2)}) collective-permute-start(bf16[128,768]{1,0:T(8,128)(2,1)} %get-tuple-element.132.refs_6_), channel_id=1, source_target_pairs={{0,16},{8,24},{16,0},{24,8},{1,17},{9,25},{17,1},{25,9},{2,18},{10... | collective-permute-start | bytes 589832 | tf_op jit(solution)/shard_map/dtok_sq2/ppermute | solution.py:480
  378.8 25.6 %collective-permute-start.51 = (bf16[128,768]{1,0:T(8,128)(2,1)}, bf16[128,768]{1,0:T(8,128)(2,1)S(1)}, u32[]{:S(2)}, u32[]{:S(2)}) collective-permute-start(bf16[128,768]{1,0:T(8,128)(2,1)} %get-tuple-element.133.refs_7_), channel_id=1, source_target_pairs={{0,24},{8,16},{16,8},{24,0},{1,25},{9,17},{17,9},{25,1},{2,26},{10... | collective-permute-start | bytes 589832 | tf_op jit(solution)/shard_map/dtok_sq3/ppermute | solution.py:480
  386.3 21.8 %collective-permute-start.61 = (bf16[96,896]{1,0:T(8,128)(2,1)}, bf16[96,896]{1,0:T(8,128)(2,1)S(1)}, u32[]{:S(2)}, u32[]{:S(2)}) collective-permute-start(bf16[96,896]{1,0:T(8,128)(2,1)} %tail_end.1.refs_0_), channel_id=1, source_target_pairs={{0,4},{4,0},{1,5},{5,1},{2,6},{6,2},{3,7},{7,3},{8,12},{12,8},{9,1... | collective-permute-start | bytes 516104 | tf_op jit(solution)/shard_map/tail_part1/ppermute | solution.py:480
  388.8 19.3 %collective-permute-start.62 = (bf16[96,896]{1,0:T(8,128)(2,1)S(1)}, bf16[96,896]{1,0:T(8,128)(2,1)S(1)}, u32[]{:S(2)}, u32[]{:S(2)}) collective-permute-start(bf16[96,896]{1,0:T(8,128)(2,1)S(1)} %collective-permute-done.58.refs_1_), channel_id=1, source_target_pairs={{0,4},{4,0},{1,5},{5,1},{2,6},{6,2},{3,7},{7,3},{8,12},{12,8},{9,1... | collective-permute-start | bytes 516104 | tf_op jit(solution)/shard_map/tail_part1/ppermute | solution.py:480
  388.9 19.2 %collective-permute-start.63 = (bf16[96,896]{1,0:T(8,128)(2,1)S(1)}, bf16[96,896]{1,0:T(8,128)(2,1)S(1)}, u32[]{:S(2)}, u32[]{:S(2)}) collective-permute-start(bf16[96,896]{1,0:T(8,128)(2,1)S(1)} %collective-permute-done.59.refs_2_), channel_id=1, source_target_pairs={{0,4},{4,0},{1,5},{5,1},{2,6},{6,2},{3,7},{7,3},{8,12},{12,8},{9,1... | collective-permute-start | bytes 516104 | tf_op jit(solution)/shard_map/tail_part1/ppermute | solution.py:480
  400.9 7.2 %collective-permute-start.64 = (bf16[96,896]{1,0:T(8,128)(2,1)S(1)}, bf16[96,896]{1,0:T(8,128)(2,1)S(1)}, u32[]{:S(2)}, u32[]{:S(2)}) collective-permute-start(bf16[96,896]{1,0:T(8,128)(2,1)S(1)} %collective-permute-done.60.refs_3_), channel_id=1, source_target_pairs={{0,4},{4,0},{1,5},{5,1},{2,6},{6,2},{3,7},{7,3},{8,12},{12,8},{9,1... | collective-permute-start | bytes 516104 | tf_op jit(solution)/shard_map/tail_part1/ppermute | solution.py:480
  (94 other events, 779.5 us)
Sparse Core Ops, SparseCore 0:
  259.0 27.9 reduce-scatter.1
  289.2 75.6 all-gather.1

commit v3 on v2

--- a/solution.py
+++ b/solution.py
@@ -586,10 +586,24 @@
 
 
 def project_and_attend_kernel(heads, hd, span, n_orders, coord_ref, rand_ref, *refs):
-    x_refs = refs[:8]
-    w_kv_ref, w_q_ref, b_kv_ref, b_q_ref, mask_ref = refs[8:13]
+    x_from = refs[:8]
+    w_from, (b_kv_ref, b_q_ref, mask_ref) = refs[8:10], refs[10:13]
     refs = refs[13 + n_orders :]
-    o_refs, (lse_ref, kv_ref, q_ref, s_ref, place_ref, nat_ref) = refs[:2], refs[2:]
+    outs, refs = refs[:5], refs[5:]
+    x_refs, (w_kv_ref, w_q_ref), o_refs = refs[:8], refs[8:10], refs[10:12]
+    lse_ref, kv_ref, q_ref, s_ref, place_ref, nat_ref, in_sems, out_sems = refs[12:]
+    arriving = [
+        pltpu.make_async_copy(a, b, in_sems.at[i])
+        for i, (a, b) in enumerate(zip((*w_from, *x_from), (w_kv_ref, w_q_ref, *x_refs)))
+    ]
+    for copy in arriving:
+        copy.start()
+    leaving = []
+
+    def leave(src, dst):
+        leaving.append(pltpu.make_async_copy(src, dst, out_sems.at[len(leaving)]))
+        leaving[-1].start()
+
     near = o_refs[0].shape[0] // BLOCK
     wide = 2 * hd
     piece, pair = 4 * span, 2 * span
@@ -601,11 +615,17 @@
     left = lax.broadcasted_iota(jnp.int32, (1, 128), 1) < BLOCK
     fill_tables(coord_ref, rand_ref, place_ref, nat_ref, heads, span)
 
+    arriving[0].wait()
+    arriving[1].wait()
     for n, x_ref in enumerate(x_refs):
-        kv_ref[n * piece : (n + 1) * piece, :] = (dot_nn(x_ref[...], w_kv_ref[...]) + b_kv_ref[...]).astype(bf16)
+        arriving[2 + n].wait()
+        of = slice(n * piece, (n + 1) * piece)
+        kv_ref[of, :] = (dot_nn(x_ref[...], w_kv_ref[...]) + b_kv_ref[...]).astype(bf16)
+        leave(kv_ref.at[of], outs[3].at[of])
     for at, n, src in query_pieces(pair):
         x = x_refs[n][src : src + pair, :]
         q_ref[at : at + pair, :] = (dot_nn(x, w_q_ref[...]) + b_q_ref[...]).astype(bf16) * bf16(hd**-0.5)
+    leave(q_ref, outs[4])
 
     def finish(jl, accs, tops, totals):
         lse_tile = jnp.zeros((BLOCK, 128), f32)
@@ -652,27 +672,35 @@
     qs = [q_ref[rows, cols] for cols in head_cols]
 
     def score(c, tops):
-        part = pl.ds(pl.multiple_of(c * CHUNK, CHUNK), CHUNK)
-        mask = mask_of(mask_ref, [nat_ref[c * PICKS + u] for u in range(PICKS)], left)
-        ss = [dot_nt(qs[h], kv_ref[part, head_cols[h]]) + mask for h in range(heads)]
-        for h in range(heads):
-            s_ref[h, :, part] = ss[h]
-        return tuple(jnp.maximum(tops[h], ss[h]) for h in range(heads))
-
-    tops = lax.fori_loop(0, chunks, score, tuple(jnp.full((BLOCK, CHUNK), -3e38, f32) for _ in range(heads)))
+        parts = [pl.ds(pl.multiple_of((c * 2 + i) * CHUNK, CHUNK), CHUNK) for i in range(2)]
+        masks = [
+            mask_of(mask_ref, [nat_ref[(c * 2 + i) * PICKS + u] for u in range(PICKS)], left) for i in range(2)
+        ]
+        ss = [
+            [dot_nt(qs[h], kv_ref[parts[i], head_cols[h]]) + masks[i] for h in range(heads)] for i in range(2)
+        ]
+        for i in range(2):
+            for h in range(heads):
+                s_ref[h, :, parts[i]] = ss[i][h]
+        return tuple(jnp.maximum(tops[h], jnp.maximum(ss[0][h], ss[1][h])) for h in range(heads))
+
+    tops = lax.fori_loop(0, chunks // 2, score, tuple(jnp.full((BLOCK, CHUNK), -3e38, f32) for _ in range(heads)))
     tops = [jnp.max(t, axis=1, keepdims=True) for t in tops]
 
     def out(c, carry):
         accs, sums = carry
-        part = pl.ds(pl.multiple_of(c * CHUNK, CHUNK), CHUNK)
-        ps = [jnp.exp(s_ref[h, :, part] - tops[h]) for h in range(heads)]
-        accs = tuple(accs[h] + dot_nn(ps[h].astype(bf16), kv_ref[part, head_cols[h]]) for h in range(heads))
-        sums = tuple(sums[h] + ps[h] for h in range(heads))
+        parts = [pl.ds(pl.multiple_of((c * 2 + i) * CHUNK, CHUNK), CHUNK) for i in range(2)]
+        ps = [[jnp.exp(s_ref[h, :, part] - tops[h]) for h in range(heads)] for part in parts]
+        adds = [
+            [dot_nn(ps[i][h].astype(bf16), kv_ref[parts[i], head_cols[h]]) for h in range(heads)] for i in range(2)
+        ]
+        accs = tuple(accs[h] + (adds[0][h] + adds[1][h]) for h in range(heads))
+        sums = tuple(sums[h] + (ps[0][h] + ps[1][h]) for h in range(heads))
         return accs, sums
 
     accs, sums = lax.fori_loop(
         0,
-        chunks,
+        chunks // 2,
         out,
         (
             tuple(jnp.zeros((BLOCK, wide), f32) for _ in range(heads)),
@@ -688,6 +716,11 @@
     @pl.when(edge >= near)
     def _():
         put(o_refs[1], edge - near, value)
+
+    for src, dst in zip((*o_refs, lse_ref), outs):
+        leave(src, dst)
+    for copy in leaving:
+        copy.wait()
 
 
 def project_and_attend(heads, hd, span, coords, rand, xs, w_kv, w_q, b_kv, b_q, mask, orders):
@@ -703,14 +736,21 @@
             jax.ShapeDtypeStruct((keys, cols), bf16),
             jax.ShapeDtypeStruct((rows, cols), bf16),
         ),
-        in_specs=[SMEM_SPEC] * 2 + [VMEM_SPEC] * 13 + [ANY_SPEC] * len(orders),
-        out_specs=(VMEM_SPEC,) * 5,
-        scratch_shapes=[
+        in_specs=[SMEM_SPEC] * 2 + [ANY_SPEC] * 10 + [VMEM_SPEC] * 3 + [ANY_SPEC] * len(orders),
+        out_specs=(ANY_SPEC,) * 5,
+        scratch_shapes=[pltpu.VMEM(a.shape, bf16) for a in (*xs, w_kv, w_q)]
+        + [pltpu.VMEM((rows // 2, heads * hd), bf16)] * 2
+        + [
+            pltpu.VMEM((rows, 128), f32),
+            pltpu.VMEM((keys, cols), bf16),
+            pltpu.VMEM((rows, cols), bf16),
             pltpu.VMEM((heads, BLOCK, keys), f32),
             pltpu.SMEM((keys // BLOCK,), jnp.int32),
             pltpu.SMEM((keys // BLOCK,), jnp.int32),
+            pltpu.SemaphoreType.DMA((10,)),
+            pltpu.SemaphoreType.DMA((12,)),
         ],
-        compiler_params=params(58),
+        compiler_params=params(60),
         cost_estimate=pl.CostEstimate(
             flops=40 << 30, bytes_accessed=16 << 20, transcendentals=rows * heads * CHUNK
         ),
@@ -718,15 +758,21 @@
     )(coords, rand, *xs, w_kv, w_q, b_kv, b_q, mask, *orders)
 
 
-def attend_back_kernel(heads, hd, span, n_orders, coord_ref, rand_ref, q_ref, *refs):
-    do_parts, o_parts = refs[:4], refs[4:6]
-    kv_ref, mask_ref, lse_ref, w_kv_ref, w_q_ref = refs[6:11]
-    dq_ref, dkv_ref, near_ref, far_ref, acc_ref, do_ref, o_ref, place_ref, nat_ref = refs[11 + n_orders :]
+def attend_back_kernel(heads, hd, span, n_orders, coord_ref, rand_ref, q_from, *refs):
+    do_parts, o_parts, (kv_from, lse_from, w_kv_from, w_q_from, mask_ref) = refs[:4], refs[4:6], refs[6:11]
+    refs = refs[11 + n_orders :]
+    dq_out, dkv_out, near_out, far_out, acc_ref, do_ref, o_ref, place_ref, nat_ref = refs[:9]
+    q_ref, kv_ref, lse_ref, w_kv_ref, w_q_ref, dq_ref, dkv_ref, dx_ref, in_sems, out_sems = refs[9:]
     own = do_parts[0].shape[0]
+    pairs = [(q_from, q_ref), (kv_from, kv_ref), (lse_from, lse_ref)]
     for k, ref in enumerate(do_parts):
-        do_ref[k * own : (k + 1) * own, :] = ref[0] if len(ref.shape) == 3 else ref[...]
+        pairs.append((ref.at[0] if len(ref.shape) == 3 else ref, do_ref.at[k * own : (k + 1) * own]))
     for k, ref in enumerate(o_parts):
-        o_ref[k * 2 * own : (k + 1) * 2 * own, :] = ref[...]
+        pairs.append((ref, o_ref.at[k * 2 * own : (k + 1) * 2 * own]))
+    pairs += [(w_kv_from, w_kv_ref), (w_q_from, w_q_ref)]
+    arriving = [pltpu.make_async_copy(a, b, in_sems.at[i]) for i, (a, b) in enumerate(pairs)]
+    for copy in arriving:
+        copy.start()
     wide = 2 * hd
     piece = 4 * span
     per_span = span // BLOCK
@@ -745,6 +791,8 @@
         return carry
 
     lax.fori_loop(0, chunks, clear, 0)
+    for copy in arriving[:-2]:
+        copy.wait()
 
     def of_rows(rows):
         d_o = do_ref[rows, :]
@@ -758,7 +806,7 @@
             lses.append(lse[:, h : h + 1])
         return boths, dots, lses
 
-    unroll = 2
+    unroll = 4
 
     def some(it, carry):
         items, boths, dots, lses = [], [], [], []
@@ -798,39 +846,62 @@
     boths, dots, lses = of_rows(rows)
 
     def edge(c, dqs):
-        part = pl.ds(pl.multiple_of(c * CHUNK, CHUNK), CHUNK)
-        mask = mask_of(mask_ref, [nat_ref[c * PICKS + u] for u in range(PICKS)], left)
-        kvs = [kv_ref[part, cols] for cols in head_cols]
-        prods = [dot_nt(boths[h], kvs[h]) for h in range(heads)]
+        items = [(i, h) for i in range(2) for h in range(heads)]
+        parts = [pl.ds(pl.multiple_of((c * 2 + i) * CHUNK, CHUNK), CHUNK) for i in range(2)]
+        masks = [
+            mask_of(mask_ref, [nat_ref[(c * 2 + i) * PICKS + u] for u in range(PICKS)], left) for i in range(2)
+        ]
+        kvs = [kv_ref[parts[i], head_cols[h]] for i, h in items]
+        prods = [dot_nt(boths[h], kvg) for (i, h), kvg in zip(items, kvs)]
         dss, lows = [], []
-        for h in range(heads):
-            p = jnp.exp(prods[h][:BLOCK] + mask - lses[h])
-            dss.append((p * (prods[h][BLOCK:] - dots[h])).astype(bf16))
+        for (i, h), prod in zip(items, prods):
+            p = jnp.exp(prod[:BLOCK] + masks[i] - lses[h])
+            dss.append((p * (prod[BLOCK:] - dots[h])).astype(bf16))
             lows.append(p.astype(bf16))
-        new = tuple(dqs[h] + dot_nn(dss[h], kvs[h]) for h in range(heads))
-        dkvs = [dot_tn(jnp.concatenate([dss[h], lows[h]], axis=0), boths[h]) for h in range(heads)]
-        for h in range(heads):
-            acc_ref[part, head_cols[h]] += dkvs[h]
-        return new
-
-    dqs = lax.fori_loop(0, chunks, edge, tuple(jnp.zeros((BLOCK, wide), f32) for _ in range(heads)))
+        adds = [dot_nn(ds, kvg) for ds, kvg in zip(dss, kvs)]
+        dkvs = [dot_tn(jnp.concatenate([ds, p], axis=0), boths[h]) for (i, h), ds, p in zip(items, dss, lows)]
+        for (i, h), dkv in zip(items, dkvs):
+            acc_ref[parts[i], head_cols[h]] += dkv
+        return tuple(dqs[h] + (adds[h] + adds[heads + h]) for h in range(heads))
+
+    dqs = lax.fori_loop(0, chunks // 2, edge, tuple(jnp.zeros((BLOCK, wide), f32) for _ in range(heads)))
     dq_ref[rows, :] = (jnp.concatenate([dq[:, :hd] for dq in dqs], axis=1) * scale).astype(bf16)
 
     pair = 2 * span
     mine = {(n, src): at for at, n, src in query_pieces(pair)}
-    for n in range(8):
+    leaving = [pltpu.make_async_copy(dq_ref, dq_out, out_sems.at[0])]
+    leaving[0].start()
+    arriving[-2].wait()
+    arriving[-1].wait()
+    moves = []
+    for i, n in enumerate((2, 3, 6, 7, 0, 1, 4, 5)):
         kc = n // 2 % 2
         to = n % 2 * piece
         of = slice(n * piece, (n + 1) * piece)
+        slot = i % 2
+        if i >= 2:
+            for copy in moves[i - 2]:
+                copy.wait()
         dkv = acc_ref[of, :].astype(bf16)
-        dkv_ref[of, :] = dkv
+        dkv_ref[slot] = dkv
         dx = dot_nt(dkv, w_kv_ref[...])
         for src in (0, pair):
             part = dx[src : src + pair]
             if (n, src) in mine:
                 at = mine[n, src]
                 part = part + dot_nt(dq_ref[at : at + pair, :], w_q_ref[...])
-            (far_ref if kc else near_ref)[n // 4, to + src : to + src + pair, :] = part.astype(bf16)
+            dx_ref[slot, src : src + pair, :] = part.astype(bf16)
+        dx_out = (far_out if kc else near_out).at[n // 4, to : to + piece]
+        moves.append(
+            [
+                pltpu.make_async_copy(dkv_ref.at[slot], dkv_out.at[of], out_sems.at[1 + 2 * i]),
+                pltpu.make_async_copy(dx_ref.at[slot], dx_out, out_sems.at[2 + 2 * i]),
+            ]
+        )
+        for copy in moves[-1]:
+            copy.start()
+    for copy in (*leaving, *moves[-2], *moves[-1]):
+        copy.wait()
 
 
 def attend_back(heads, hd, span, coords, rand, q, d_os, os, kv, mask, lse, w_kv, w_q, orders):
@@ -844,21 +915,31 @@
             jax.ShapeDtypeStruct((keys, heads * 2 * hd), bf16),
         )
         + (jax.ShapeDtypeStruct((2, 2 * piece, width), bf16),) * 2,
-        in_specs=[SMEM_SPEC] * 2 + [VMEM_SPEC] * 12 + [ANY_SPEC] * len(orders),
-        out_specs=(VMEM_SPEC,) * 4,
+        in_specs=[SMEM_SPEC] * 2 + [ANY_SPEC] * 11 + [VMEM_SPEC] + [ANY_SPEC] * len(orders),
+        out_specs=(ANY_SPEC,) * 4,
         scratch_shapes=[
             pltpu.VMEM((keys, heads * 2 * hd), f32),
             pltpu.VMEM((rows, heads * hd), bf16),
             pltpu.VMEM((rows, heads * hd), bf16),
             pltpu.SMEM((keys // BLOCK,), jnp.int32),
             pltpu.SMEM((keys // BLOCK,), jnp.int32),
+            pltpu.VMEM(q.shape, bf16),
+            pltpu.VMEM(kv.shape, bf16),
+            pltpu.VMEM(lse.shape, f32),
+            pltpu.VMEM(w_kv.shape, bf16),
+            pltpu.VMEM(w_q.shape, bf16),
+            pltpu.VMEM((rows, heads * hd), bf16),
+            pltpu.VMEM((2, piece, heads * 2 * hd), bf16),
+            pltpu.VMEM((2, piece, width), bf16),
+            pltpu.SemaphoreType.DMA((11,)),
+            pltpu.SemaphoreType.DMA((17,)),
         ],
-        compiler_params=params(58),
+        compiler_params=params(60),
         cost_estimate=pl.CostEstimate(
             flops=60 << 30, bytes_accessed=24 << 20, transcendentals=rows * heads * CHUNK
         ),
         name="attend_back",
-    )(coords, rand, q, *d_os, *os, kv, mask, lse, w_kv, w_q, *orders)
+    )(coords, rand, q, *d_os, *os, kv, lse, w_kv, w_q, mask, *orders)
 
 
 def split_low(value):
@@ -870,7 +951,7 @@
     return low[:8].astype(f32) + low[8:16].astype(f32)
 
 
-def qkv_grad_kernel(span, spot_ref, dq_ref, dkv_ref, keep_ref, got_ref, small_ref, *refs):
+def qkv_grad_kernel(span, spot_ref, coord_ref, dq_ref, dkv_ref, keep_ref, got_ref, small_ref, *refs):
     x_refs, out_ref = refs[:8], refs[-1]
     piece = 4 * span
     n_kv = dkv_ref.shape[1]
@@ -886,7 +967,7 @@
     out_ref[...] = jnp.zeros_like(out_ref)
     both = jnp.concatenate([acc, acc_q], axis=0)
     octets = [both[o * rows : (o + 1) * rows] for o in range(6)]
-    w_out = keep_ref[keep_ref.shape[0] - 1].astype(f32) + got_ref[got_ref.shape[0] - 1].astype(f32)
+    w_out = keep_ref[4].astype(f32) + got_ref[4 * rows : 5 * rows, :].astype(f32)
     octets += [w_out[:, :width], w_out[:, width:]]
     sums = jnp.concatenate(
         [
@@ -897,48 +978,75 @@
         axis=1,
     )
     sums = jnp.concatenate([sums[:, i * 128 : (i + 1) * 128] for i in range(8)], axis=0)
+
+    others = joined(got_ref[5 * rows :, :width])
+    own = joined(split_low(small_ref[...]))
+    small = own + others
+    held = split_low(own + pltpu.roll(others, 7, 0))
+    unit = lax.broadcasted_iota(jnp.int32, (width, width), 0)
+    octet = unit // rows
+    zq = (octet // 2 % 2 + octet % 2 * 2) ^ coord_ref[0]
+    own_unit = (zq * 2 + (octet // 4 ^ coord_ref[1])) * rows + unit % rows
+    turn = jnp.where(own_unit == lax.broadcasted_iota(jnp.int32, (width, width), 1), 1.0, 0.0).astype(bf16)
+    b_in = joined(dot_nn(held, turn))[6:7]
+
+    def lanes_down(row):
+        parts = [row[:, i * 128 : (i + 1) * 128] for i in range(width // 128)]
+        return jnp.concatenate(parts + [jnp.zeros((8 - width // 128, 128), f32)], axis=0)
+
+    vectors = [lanes_down(small[i : i + 1]) for i in range(6)] + [lanes_down(b_in), sums]
     for o in range(8):
         spot = spot_ref[o]
         out_ref[spot, :, :width] = octets[o].astype(bf16)
-        out_ref[spot, :16, width:] = split_low(small_ref[o] if o < 7 else sums)
-
-
-def qkv_grad(span, spots, dq, dkv, keep, got, small, xs, orders):
+        out_ref[spot, :16, width:] = split_low(vectors[o])
+
+
+def qkv_grad(span, spots, coords, dq, dkv, keep, got, small, xs, orders):
     width = xs[0].shape[1]
     rows = (dq.shape[1] + dkv.shape[1]) // 6
     return pl.pallas_call(
         functools.partial(qkv_grad_kernel, span),
         out_shape=jax.ShapeDtypeStruct((8, rows, width + 128), bf16),
-        in_specs=[SMEM_SPEC] + [VMEM_SPEC] * 13 + [ANY_SPEC] * len(orders),
+        in_specs=[SMEM_SPEC] * 2 + [VMEM_SPEC] * 13 + [ANY_SPEC] * len(orders),
         out_specs=VMEM_SPEC,
-        compiler_params=params(48),
+        compiler_params=params(60),
         cost_estimate=pl.CostEstimate(
             flops=14 << 30, bytes_accessed=12 << 20, transcendentals=0
         ),
         name="qkv_grad",
-    )(spots, dq, dkv, keep, got, small, *xs, *orders)
-
-
-def wide_sum_kernel(order_ref, keep_ref, y_ref, x_ref, out_ref):
-    out_ref[...] = (keep_ref[...].astype(f32) + y_ref[...].astype(f32) + x_ref[...].astype(f32)).astype(bf16)
-
-
-def wide_sum(order, keep, y_got, x_got):
+    )(spots, coords, dq, dkv, keep, got, small, *xs, *orders)
+
+
+def wide_sum_kernel(order_ref, keep_ref, y_ref, x_ref, a_ref, b_ref, c_ref, d_ref, out_ref, top_ref, low_ref):
+    rows = keep_ref.shape[1]
+    half = rows // 2
+    for i, out in enumerate((top_ref, low_ref)):
+        of = slice(i * half, (i + 1) * half)
+        out[...] = sum(r[of, :].astype(f32) for r in (a_ref, b_ref, c_ref, d_ref)).astype(bf16)
+    for k in range(4):
+        of = slice(k * rows, (k + 1) * rows)
+        out_ref[order_ref[k]] = (keep_ref[k].astype(f32) + y_ref[of, :].astype(f32) + x_ref[k].astype(f32)).astype(bf16)
+
+
+def wide_sum(order, keep, y_got, x_got, across):
     _, rows, cols = keep.shape
-    octet = pl.BlockSpec((1, rows, cols), lambda i, order_ref: (i, 0, 0))
+    four = pl.BlockSpec((4, rows, cols), lambda i: (0, 0, 0))
+    octet = pl.BlockSpec((rows, cols), lambda i: (0, 0))
+    half = pl.BlockSpec((rows // 2, cols), lambda i: (0, 0))
     return pl.pallas_call(
         wide_sum_kernel,
-        grid_spec=pltpu.PrefetchScalarGridSpec(
-            num_scalar_prefetch=1,
-            grid=(4,),
-            in_specs=[octet] * 3,
-            out_specs=pl.BlockSpec((1, rows, cols), lambda i, order_ref: (order_ref[i], 0, 0)),
+        grid=(1,),
+        in_specs=[SMEM_SPEC, four, pl.BlockSpec((4 * rows, cols), lambda i: (0, 0)), four] + [octet] * 4,
+        out_specs=(four, half, half),
+        out_shape=(
+            jax.ShapeDtypeStruct((4, rows, cols), bf16),
+            jax.ShapeDtypeStruct((rows // 2, cols), bf16),
+            jax.ShapeDtypeStruct((rows // 2, cols), bf16),
         ),
-        out_shape=jax.ShapeDtypeStruct((4, rows, cols), bf16),
-        compiler_params=params(58),
+        compiler_params=params(60),
         cost_estimate=pl.CostEstimate(flops=1 << 28, bytes_accessed=6 << 20, transcendentals=0),
         name="wide_sum",
-    )(order, keep, y_got, x_got)
+    )(order, keep, y_got, x_got, *across)
 
 
 def tail_sum_kernel(n_orders, tail_ref, got_ref, *refs):
@@ -957,29 +1065,30 @@
         out_shape=(jax.ShapeDtypeStruct((rows, cols), bf16),) * 4,
         in_specs=[VMEM_SPEC] * 2 + [ANY_SPEC] * len(orders),
         out_specs=(VMEM_SPEC,) * 4,
-        compiler_params=params(58),
+        compiler_params=params(60),
         cost_estimate=pl.CostEstimate(flops=1 << 28, bytes_accessed=2 << 20, transcendentals=0),
         name="tail_sum",
     )(tail, tail_got, *orders)
 
 
-def wide_end_kernel(wide_ref, top_ref, low_ref, out_ref):
+def wide_end_kernel(wide_ref, top_ref, low_ref, *refs):
+    out_ref = refs[-1]
     half = top_ref.shape[0]
     for i, more_ref in enumerate((top_ref, low_ref)):
         of = slice(i * half, (i + 1) * half)
         out_ref[of, :] = (wide_ref[of, :].astype(f32) + more_ref[...].astype(f32)).astype(bf16)
 
 
-def wide_end(wide, top, low):
+def wide_end(wide, top, low, orders):
     return pl.pallas_call(
         wide_end_kernel,
         out_shape=jax.ShapeDtypeStruct(wide.shape, bf16),
-        in_specs=[VMEM_SPEC] * 3,
+        in_specs=[VMEM_SPEC] * 3 + [ANY_SPEC] * len(orders),
         out_specs=VMEM_SPEC,
-        compiler_params=params(58),
+        compiler_params=params(60),
         cost_estimate=pl.CostEstimate(flops=1 << 28, bytes_accessed=3 << 20, transcendentals=0),
         name="wide_end",
-    )(wide, top, low)
+    )(wide, top, low, *orders)
 
 
 def tail_end_kernel(*refs):
@@ -996,56 +1105,46 @@
         out_shape=jax.ShapeDtypeStruct(thins[0].shape, bf16),
         in_specs=[VMEM_SPEC] * 4 + [ANY_SPEC] * len(orders),
         out_specs=VMEM_SPEC,
-        compiler_params=params(58),
+        compiler_params=params(60),
         cost_estimate=pl.CostEstimate(flops=1 << 28, bytes_accessed=3 << 20, transcendentals=0),
         name="tail_end",
     )(*thins, *orders)
 
 
-def tail_place_kernel(spot_ref, *refs):
-    ins, out_ref, small_ref = refs[:8], refs[8], refs[9]
+def tail_place_kernel(n_qkv, heads, spot_ref, *refs):
+    ins, (qkv_ref, w_out_ref, small_ref, held_ref) = refs[:8], refs[-4:]
     rows = ins[0].shape[0]
-    cols = out_ref.shape[1]
+    cols = held_ref.shape[1]
     for n in range(8):
         spot = spot_ref[n]
-        out_ref[pl.ds(pl.multiple_of(spot * rows, 16), rows), :] = ins[n][:, :cols]
+        held_ref[pl.ds(pl.multiple_of(spot * rows, 16), rows), :] = ins[n][:, :cols].astype(f32)
         small_ref[spot] = joined(ins[n][:16, cols:])
-
-
-def tail_place(spots, parts):
+    w_out_ref[...] = held_ref[n_qkv:, :]
+    hd = n_qkv // 3 // heads
+    parts = []
+    for h in range(heads):
+        q_at, kv_at = 2 * heads * hd + h * hd, 2 * h * hd
+        parts += [held_ref[q_at : q_at + hd, :], held_ref[kv_at : kv_at + 2 * hd, :]]
+    qkv_ref[...] = jnp.concatenate(parts, axis=0).T
+
+
+def tail_place(spots, parts, n_qkv, heads, orders):
     rows, cols = parts[0].shape
+    width = cols - 128
     return pl.pallas_call(
-        tail_place_kernel,
+        functools.partial(tail_place_kernel, n_qkv, heads),
         out_shape=(
-            jax.ShapeDtypeStruct((8 * rows, cols - 128), bf16),
+            jax.ShapeDtypeStruct((width, n_qkv), f32),
+            jax.ShapeDtypeStruct((8 * rows - n_qkv, width), f32),
             jax.ShapeDtypeStruct((8, 8, 128), f32),
         ),
-        in_specs=[SMEM_SPEC] + [VMEM_SPEC] * 8,
-        out_specs=(VMEM_SPEC,) * 2,
-        compiler_params=params(58),
+        in_specs=[SMEM_SPEC] + [VMEM_SPEC] * 8 + [ANY_SPEC] * len(orders),
+        out_specs=(VMEM_SPEC,) * 3,
+        scratch_shapes=[pltpu.VMEM((8 * rows, width), f32)],
+        compiler_params=params(60),
         cost_estimate=pl.CostEstimate(flops=1 << 28, bytes_accessed=3 << 20, transcendentals=0),
         name="tail_place",
-    )(spots, *parts)
-
-
-def across_sum_kernel(a_ref, b_ref, c_ref, d_ref, top_ref, low_ref):
-    half = top_ref.shape[0]
-    for i, out in enumerate((top_ref, low_ref)):
-        of = slice(i * half, (i + 1) * half)
-        out[...] = sum(r[of, :].astype(f32) for r in (a_ref, b_ref, c_ref, d_ref)).astype(bf16)
-
-
-def across_sum(parts):
-    rows, cols = parts[0].shape
-    return pl.pallas_call(
-        across_sum_kernel,
-        out_shape=(jax.ShapeDtypeStruct((rows // 2, cols), bf16),) * 2,
-        in_specs=[VMEM_SPEC] * 4,
-        out_specs=(VMEM_SPEC,) * 2,
-        compiler_params=params(58),
-        cost_estimate=pl.CostEstimate(flops=1 << 24, bytes_accessed=1 << 20, transcendentals=0),
-        name="across_sum",
-    )(*parts)
+    )(spots, *parts, *orders)
 
 
 def split_kernel(n_orders, coord_ref, rows_ref, *refs):
@@ -1109,60 +1208,43 @@
     )(w_qkv, bias_qv, *orders)
 
 
-def pack_kernel(heads_rows, order_ref, up_ref, down_ref, out_ref_in, bias_ref, pack_ref, first_ref, up_rows_ref):
+def pack_kernel(n_orders, order_ref, up_ref, down_ref, w_out_ref, bias_ref, *refs):
+    pack_ref, first_ref, out_ref, up_rows_ref = refs[n_orders:]
     width = up_ref.shape[0]
     eighth = down_ref.shape[0] // 8
-    half = heads_rows // 2
+    half = w_out_ref.shape[0] // 2
     for i in range(0, down_ref.shape[0], 256):
         up_rows_ref[i : i + 256, :] = up_ref[:, i : i + 256].astype(f32).T.astype(bf16)
-    pack_ref[:half, :width] = out_ref_in[:half, :]
-    pack_ref[:half, width:] = out_ref_in[half:, :]
-    pack_ref[half : half + 16, :width] = bias_ref[...]
-    pack_ref[half : half + 16, width:] = jnp.zeros((16, width), bf16)
+    for ref in (pack_ref, out_ref):
+        ref[:half, :width] = w_out_ref[:half, :]
+        ref[:half, width:] = w_out_ref[half:, :]
+        ref[half : half + 16, :width] = bias_ref[...]
+        ref[half : half + 16, width:] = jnp.zeros((16, width), bf16)
     for n in range(8):
         src = pl.ds(pl.multiple_of(order_ref[n] * eighth, 16), eighth)
-        for ref, at in ((pack_ref, half + 16), (first_ref, 0))[: 2 if n < 2 else 1]:
+        for ref, at in ((pack_ref, half + 16), (first_ref, 0))[: 2 if n < 4 else 1]:
             to = slice(at + n * eighth, at + (n + 1) * eighth)
             ref[to, :width] = up_rows_ref[src, :]
             ref[to, width:] = down_ref[src, :]
 
 
-def pack(order, up, down, w_out, bias):
+def pack(order, up, down, w_out, bias, orders):
     hidden, width = down.shape
     rows = w_out.shape[0] // 2 + 16
     return pl.pallas_call(
-        functools.partial(pack_kernel, w_out.shape[0]),
+        functools.partial(pack_kernel, len(orders)),
         out_shape=(
             jax.ShapeDtypeStruct((rows + hidden, 2 * width), bf16),
-            jax.ShapeDtypeStruct((hidden // 4, 2 * width), bf16),
+            jax.ShapeDtypeStruct((hidden // 2, 2 * width), bf16),
+            jax.ShapeDtypeStruct((rows, 2 * width), bf16),
         ),
-        in_specs=[SMEM_SPEC] + [VMEM_SPEC] * 4,
-        out_specs=(VMEM_SPEC,) * 2,
+        in_specs=[SMEM_SPEC] + [VMEM_SPEC] * 4 + [ANY_SPEC] * len(orders),
+        out_specs=(VMEM_SPEC,) * 3,
         scratch_shapes=[pltpu.VMEM((hidden, width), bf16)],
         compiler_params=params(32),
         cost_estimate=pl.CostEstimate(flops=1 << 20, bytes_accessed=1 << 20, transcendentals=0),
         name="pack",
-    )(order, up, down, w_out, bias)
-
-
-def copies_kernel(n_orders, *refs):
-    n = (len(refs) - n_orders) // 2
-    for ref, out in zip(refs[:n], refs[n + n_orders :]):
-        out[...] = ref[: out.shape[0], :]
-
-
-def copies(values, rows, orders):
-    return pl.pallas_call(
-        functools.partial(copies_kernel, len(orders)),
-        out_shape=tuple(jax.ShapeDtypeStruct((n, a.shape[1]), a.dtype) for a, n in zip(values, rows)),
-        grid=(1,),
-        in_specs=[pl.BlockSpec((n, a.shape[1]), lambda i: (0, 0)) for a, n in zip(values, rows)]
-        + [ANY_SPEC] * len(orders),
-        out_specs=tuple(pl.BlockSpec((n, a.shape[1]), lambda i: (0, 0)) for a, n in zip(values, rows)),
-        compiler_params=params(58),
-        cost_estimate=pl.CostEstimate(flops=1 << 20, bytes_accessed=1 << 20, transcendentals=0),
-        name="copies",
-    )(*values, *orders)
+    )(order, up, down, w_out, bias, *orders)
 
 
 def rows_kernel(width, n_out, tile_rows, *refs):
@@ -1178,8 +1260,8 @@
     step = pl.program_id(0)
     half = n_out // 2
     tiles, wos, biases = [], [], []
-    for ref, first in zip(pack_refs, tile_rows):
-        if first:
+    for ref, (first, whole) in zip(pack_refs, tile_rows):
+        if whole:
             wos.append(jnp.concatenate([ref[:half, :width], ref[:half, width:]], axis=0))
             biases.append(ref[half : half + 1, :width].astype(f32))
         left = ref.shape[0] - first
@@ -1260,7 +1342,7 @@
     span, width = d_res[0].shape
     rows = 4 * span
     cols = attns[0].shape[1]
-    hidden = sum(a.shape[0] - n for a, n in zip(packs, first_rows))
+    hidden = sum(a.shape[0] - n for a, (n, _) in zip(packs, first_rows))
     tile = rows // 2
 
     def by_rows(n):
@@ -1306,123 +1388,155 @@
             fixed((1, hidden)),
         ),
         scratch_shapes=[pltpu.VMEM((tile, hidden), f32)],
-        compiler_params=params(58),
+        compiler_params=params(60),
         cost_estimate=pl.CostEstimate(flops=50 << 30, bytes_accessed=30 << 20, transcendentals=rows * hidden),
         name="rows_work",
     )(*attns, *packs, *toks, *d_res, vecs)
 
 
-def tile_grads(ylow_ref, dpre_ref, hid_ref, dffn_ref):
-    return dot_tn(dpre_ref[...], ylow_ref[...]), dot_tn(hid_ref[...], dffn_ref[...])
-
-
-def far_grad_kernel(ylow_ref, dpre_ref, hid_ref, dffn_ref, dbr_ref, attn0_ref, attn1_ref, out_ref):
+def small_rows(kc, small_ref, bin_ref):
+    width = small_ref.shape[1]
+    ends = [bin_ref[:, (ky * 2 + kc) * width : (ky * 2 + kc + 1) * width] for ky in range(2)]
+    return jnp.concatenate([small_ref[:6, :]] + ends, axis=0)
+
+
+def rows_grad_kernel(kc, n_orders, *refs):
+    *sources, small_ref, bin_ref = refs[:9]
+    refs = refs[9:]
+    got_from = refs[0] if kc == 0 else None
+    refs = refs[(1 if kc == 0 else 0) + n_orders :]
+    n_outs = 1 if kc else 8
+    outs, (ylow_ref, dpre_ref, hid_ref, dffn_ref, dbr_ref, attn0_ref, attn1_ref, held_ref, got_ref, low_ref) = (
+        refs[:n_outs],
+        refs[n_outs : n_outs + 10],
+    )
+    in_sems, got_sems, out_sems = refs[n_outs + 10 :]
     width = ylow_ref.shape[1]
-    eighth = out_ref.shape[1]
-
-    @pl.when(pl.program_id(0) < 4)
-    def _():
-        g_in, g_back = tile_grads(ylow_ref, dpre_ref, hid_ref, dffn_ref)
-        for n in range(4):
-            out_ref[n, :, :width] = g_in[n * eighth : (n + 1) * eighth].astype(bf16)
-            out_ref[n, :, width:] = g_back[n * eighth : (n + 1) * eighth].astype(bf16)
-
-    @pl.when(pl.program_id(0) == 4)
-    def _():
-        for k, attn_ref in enumerate((attn0_ref, attn1_ref)):
-            g_out = dot_tn(attn_ref[...], dbr_ref[...]).astype(bf16)
-            out_ref[k, :, :width] = g_out[:eighth]
-            out_ref[k, :, width:] = g_out[eighth:]
-            out_ref[2 + k] = jnp.zeros_like(out_ref[2 + k])
-
-
-def near_grad_kernel(
-    n_orders, ylow_ref, dpre_ref, hid_ref, dffn_ref, dbr_ref, attn0_ref, attn1_ref, got_ref, *refs
-):
-    keep_ref, y_ref, x_ref, *across_refs, held_ref, sems = refs[n_orders:]
-    width = ylow_ref.shape[1]
-    eighth = got_ref.shape[1]
-    step = pl.program_id(0)
-
-    def moves(n):
-        if n == 0:
-            pairs = [(held_ref.at[0], keep_ref.at[0:4])]
-        elif n == 1:
-            pairs = [(held_ref.at[1], x_ref.at[0:4])]
+    rows = ylow_ref.shape[0]
+    part = width // 2
+    eighth = held_ref.shape[1]
+
+    def cols_of(n):
+        at = ((n // 2) * 4 + kc * 2 + n % 2) * part
+        return slice(at, at + part)
+
+    pairs = [(sources[0], ylow_ref), (sources[3], dffn_ref)]
+    for n in range(4):
+        pairs.append((sources[1].at[:, cols_of(n)], dpre_ref.at[n]))
+        pairs.append((sources[2].at[:, cols_of(n)], hid_ref.at[n]))
+    pairs += [(sources[4], dbr_ref)]
+    pairs += [(source.at[0:rows], ref) for source, ref in zip(sources[5:], (attn0_ref, attn1_ref))]
+    arriving = [pltpu.make_async_copy(a, b, in_sems.at[i]) for i, (a, b) in enumerate(pairs)]
+    gots = []
+    if kc == 0:
+        gots = [
+            pltpu.make_async_copy(got_from.at[4 * n : 4 * n + 4], got_ref.at[4 * n : 4 * n + 4], got_sems.at[n])
+            for n in range(5)
+        ]
+    for i, copy in enumerate(arriving):
+        copy.start()
+        if gots and i in (3, 5, 7, 9):
+            gots[(i - 3) // 2].start()
+    if gots:
+        gots[4].start()
+    arriving[0].wait()
+    arriving[1].wait()
+    leaving = []
+
+    def leave(src, dst):
+        leaving.append(pltpu.make_async_copy(src, dst, out_sems.at[len(leaving)]))
+        leaving[-1].start()
+
+    def put(at, k, lanes, value):
+        if gots:
+            value = value + got_ref[at + k, :, lanes].astype(f32)
+        held_ref[at + k, :, lanes] = value.astype(bf16)
+
+    left, right = slice(0, width), slice(width, 2 * width)
+    for n in range(4):
+        arriving[2 + 2 * n].wait()
+        arriving[3 + 2 * n].wait()
+        g_in = dot_tn(dpre_ref[n], ylow_ref[...])
+        g_back = dot_tn(hid_ref[n], dffn_ref[...])
+        if gots:
+            gots[n].wait()
+        for k in range(4):
+            put(4 * n, k, left, g_in[k * eighth : (k + 1) * eighth])
+            put(4 * n, k, right, g_back[k * eighth : (k + 1) * eighth])
+        if kc:
+            leave(held_ref.at[4 * n : 4 * n + 4], outs[0].at[4 * n : 4 * n + 4])
+        elif n < 2:
+            leave(held_ref.at[4 * n : 4 * n + 4], outs[2 * n].at[0:4])
         elif n == 2:
-            pairs = [(held_ref.at[0], y_ref.at[0:4])]
-        elif n == 3:
-            pairs = [(held_ref.at[1, k], across_refs[k]) for k in range(4)]
+            for k in range(4):
+                leave(held_ref.at[8 + k], outs[1].at[k * eighth : (k + 1) * eighth])
         else:
-            pairs = [(held_ref.at[0, 0], keep_ref.at[4]), (held_ref.at[0, 1], y_ref.at[4])]
-        return [pltpu.make_async_copy(a, b, sems.at[n, i]) for i, (a, b) in enumerate(pairs)]
-
-    for n in range(5):
-
-        @pl.when(step == n)
-        def _(n=n):
-            if n >= 2:
-                for copy in moves(n - 2):
-                    copy.wait()
-            if n < 4:
-                g_in, g_back = tile_grads(ylow_ref, dpre_ref, hid_ref, dffn_ref)
-                for k in range(4):
-                    rows = slice(k * eighth, (k + 1) * eighth)
-                    held_ref[n % 2, k, :, :width] = (g_in[rows] + got_ref[k, :, :width].astype(f32)).astype(bf16)
-                    held_ref[n % 2, k, :, width:] = (g_back[rows] + got_ref[k, :, width:].astype(f32)).astype(bf16)
-            else:
-                for k, attn_ref in enumerate((attn0_ref, attn1_ref)):
-                    g_out = dot_tn(attn_ref[...], dbr_ref[...])
-                    held_ref[0, k, :, :width] = (g_out[:eighth] + got_ref[k, :, :width].astype(f32)).astype(bf16)
-                    held_ref[0, k, :, width:] = (g_out[eighth:] + got_ref[k, :, width:].astype(f32)).astype(bf16)
-            for copy in moves(n):
-                copy.start()
-            if n == 4:
-                for copy in moves(3) + moves(4):
-                    copy.wait()
-
-
-def rows_grad(kc, y_low, d_pre, hidden, d_ffn, d_branch, attn0, attn1, got=None, orders=()):
+            for k in range(4):
+                leave(held_ref.at[12 + k], outs[3 + k])
+    for copy in arriving[10:]:
+        copy.wait()
+    if gots:
+        gots[4].wait()
+    for ky, attn_ref in enumerate((attn0_ref, attn1_ref)):
+        g_out = dot_tn(attn_ref[...], dbr_ref[...])
+        put(16, ky, left, g_out[:eighth])
+        put(16, ky, right, g_out[eighth:])
+    low_ref[...] = jnp.zeros_like(low_ref)
+    if kc:
+        low_ref[:16, :width] = split_low(small_rows(1, small_ref, bin_ref))
+        leave(held_ref.at[16:18], outs[0].at[16:18])
+        leave(low_ref, outs[0].at[18])
+        leave(low_ref, outs[0].at[19])
+    else:
+        sums = joined(split_low(small_rows(0, small_ref, bin_ref))) + joined(got_ref[18, :16, :width])
+        outs[7][...] = sums
+        low_ref[:16, :width] = split_low(sums)
+        leave(held_ref.at[16], outs[0].at[4])
+        leave(held_ref.at[17], outs[1].at[4 * eighth : 5 * eighth])
+        leave(low_ref.at[0:16], outs[1].at[5 * eighth : 5 * eighth + 16])
+    for copy in leaving:
+        copy.wait()
+
+
+def rows_grad(kc, y_low, d_pre, hidden, d_ffn, d_branch, attn0, attn1, small, bin_sum, got=None, orders=()):
     rows, width = y_low.shape
     part = hidden.shape[1] // 8
     eighth = part // 4
-    block = (4, eighth, 2 * width)
-
-    def fixed(n):
-        return pl.BlockSpec((rows, n), lambda i: (0, 0), pipeline_mode=pl.Buffered(1))
-
-    def tile_of(i):
-        i = jnp.minimum(i, 3)
-        return (0, (i // 2) * 4 + kc * 2 + i % 2)
-
-    tile = pl.BlockSpec((rows, part), tile_of)
-    in_specs = [fixed(width), tile, tile, fixed(width), fixed(width), fixed(attn0.shape[1]), fixed(attn1.shape[1])]
-    octets = pl.BlockSpec(block, lambda i: (i, 0, 0))
-    cost = pl.CostEstimate(flops=8 << 30, bytes_accessed=16 << 20, transcendentals=0)
-    operands = (y_low, d_pre, hidden, d_ffn, d_branch, attn0, attn1)
+    octet = (eighth, 2 * width)
+    low = functools.partial(jax.ShapeDtypeStruct, dtype=bf16)
     if kc == 1:
-        return pl.pallas_call(
-            far_grad_kernel,
-            grid=(5,),
-            out_shape=jax.ShapeDtypeStruct((20,) + block[1:], bf16),
-            in_specs=in_specs,
-            out_specs=octets,
-            compiler_params=params(58),
-            cost_estimate=cost,
-            name="far_grad",
-        )(*operands)
-    return pl.pallas_call(
-        functools.partial(near_grad_kernel, len(orders)),
-        grid=(5,),
-        out_shape=tuple(jax.ShapeDtypeStruct((n,) + block[1:], bf16) for n in (5, 5, 4))
-        + (jax.ShapeDtypeStruct(block[1:], bf16),) * 4,
-        in_specs=in_specs + [octets] + [ANY_SPEC] * len(orders),
-        out_specs=(ANY_SPEC,) * 7,
-        scratch_shapes=[pltpu.VMEM((2,) + block, bf16), pltpu.SemaphoreType.DMA((5, 4))],
-        compiler_params=params(58),
-        cost_estimate=cost,
-        name="near_grad",
-    )(*operands, got, *orders)
+        out_shape = (low((20,) + octet),)
+        out_specs = (ANY_SPEC,)
+    else:
+        out_shape = (low((5,) + octet), low((5 * eighth + 16, 2 * width)), low((4,) + octet)) + (low(octet),) * 4
+        out_shape += (jax.ShapeDtypeStruct((8, width), f32),)
+        out_specs = (ANY_SPEC,) * 7 + (VMEM_SPEC,)
+    extra = () if got is None else (got,)
+    out = pl.pallas_call(
+        functools.partial(rows_grad_kernel, kc, len(orders)),
+        out_shape=out_shape,
+        in_specs=[ANY_SPEC] * 7 + [VMEM_SPEC] * 2 + [ANY_SPEC] * (len(extra) + len(orders)),
+        out_specs=out_specs,
+        scratch_shapes=[
+            pltpu.VMEM((rows, width), bf16),
+            pltpu.VMEM((4, rows, part), bf16),
+            pltpu.VMEM((4, rows, part), bf16),
+            pltpu.VMEM((rows, width), bf16),
+            pltpu.VMEM((rows, width), bf16),
+            pltpu.VMEM((rows, attn0.shape[1]), bf16),
+            pltpu.VMEM((rows, attn1.shape[1]), bf16),
+            pltpu.VMEM((18,) + octet, bf16),
+            pltpu.VMEM((20,) + octet, bf16),
+            pltpu.VMEM(octet, bf16),
+            pltpu.SemaphoreType.DMA((13,)),
+            pltpu.SemaphoreType.DMA((5,)),
+            pltpu.SemaphoreType.DMA((16,)),
+        ],
+        compiler_params=params(60),
+        cost_estimate=pl.CostEstimate(flops=8 << 30, bytes_accessed=16 << 20, transcendentals=0),
+        name="far_grad" if kc else "near_grad",
+    )(y_low, d_pre, hidden, d_ffn, d_branch, attn0, attn1, small, bin_sum, *extra, *orders)
+    return out[0] if kc else out
 
 
 def row_sum_one_kernel(near_ref, got_ref, *refs):
@@ -1442,7 +1556,7 @@
         out_shape=(jax.ShapeDtypeStruct((rows // 2, width), bf16),) * 2,
         in_specs=[far] * 2 + [ANY_SPEC] * len(orders),
         out_specs=(pl.BlockSpec((rows // 2, width), lambda i: (0, 0)),) * 2,
-        compiler_params=params(58),
+        compiler_params=params(60),
         cost_estimate=pl.CostEstimate(flops=1 << 28, bytes_accessed=6 << 20, transcendentals=0),
         name="row_sum_one",
     )(near, got, *orders)
@@ -1465,7 +1579,7 @@
         out_shape=(jax.ShapeDtypeStruct((quarter, width), bf16),) * 2,
         in_specs=[part] * 2 + [pl.BlockSpec((quarter, width), lambda i: (1, 0))] * 2 + [ANY_SPEC] * len(orders),
         out_specs=(pl.BlockSpec((quarter, width), lambda i: (0, 0)),) * 2,
-        compiler_params=params(58),
+        compiler_params=params(60),
         cost_estimate=pl.CostEstimate(flops=1 << 28, bytes_accessed=4 << 20, transcendentals=0),
         name="row_sum_two",
     )(near, got, even, odd, *orders)
@@ -1499,7 +1613,7 @@
         out_shape=(jax.ShapeDtypeStruct((quarter // 2, width), bf16),) * 4,
         in_specs=[part] * 2 + [first] * 4 + [pl.BlockSpec((quarter, width), lambda i: (i, 0))],
         out_specs=(out,) * 4,
-        compiler_params=params(58),
+        compiler_params=params(60),
         cost_estimate=pl.CostEstimate(flops=1 << 28, bytes_accessed=4 << 20, transcendentals=0),
         name="row_sum_three",
     )(near, got, even, odd, even_got, odd_got, d_one)
@@ -1548,57 +1662,50 @@
     held_order = ((held_zd ^ z) * 2 + ((octet // 4) ^ px)).astype(jnp.int32)
     bias_row = jnp.moveaxis(turn_octets(up_bias_vector.reshape(8, eighth)).reshape(2, 2, 2, eighth), (0, 2), (2, 0))
     bias_row = jnp.pad(bias_row.reshape(1, hidden_dev), ((0, 15), (0, 0)))
-    wf, wf_first = pack(held_order, up_weight, down_weight, w_out.reshape(n_o, width), bias_row)
     n_wo = n_o // 2 + 16
-    quarter = swap(wf_first, "hy", name="weight")
+    wf, wf_first, wo = pack(held_order, up_weight, down_weight, w_out.reshape(n_o, width), bias_row, [])
+    wf_y = swap(wf_first, "hy", name="weight")
+    wf_c = swap(wf, "hc", name="weight")
 
     raw = split(coords, tokens, [wf])
     tok = [raw[0]] + [swap(raw[k], "sq", k, name="tok") for k in range(1, 4)]
     w_kv, w_q_pad, w_q, b_kv, b_q = qkv_weights(w_qkv, bias_qv, raw)
-    even = after(jnp.concatenate([tok[0], tok[2]], axis=0), *tok, w_kv, quarter)
-    odd = after(jnp.concatenate([tok[1], tok[3]], axis=0), *tok, w_kv, quarter)
+    dres_raw = split(coords, d_out, raw)
+    dres = [dres_raw[0]] + [swap(dres_raw[k], "sq", k, name="dres") for k in range(1, 4)]
+    odd = after(jnp.concatenate([tok[1], tok[3]], axis=0), *tok, w_kv, wf_y, wf_c, *dres_raw)
+    even = after(jnp.concatenate([tok[0], tok[2]], axis=0), *tok, w_kv, wf_y, wf_c, *dres_raw)
     even_x = swap(even, "part", name="tok")
     odd_y = swap(odd, "hy", name="tok")
-    units = copies([quarter], [2 * eighth], [even, odd])[0]
-    wf_z = swap(units, "sq", 1, name="weight")
-    even_near = after(jnp.concatenate([even, even_x], axis=0), units)
-    odd_near = after(jnp.concatenate([odd, odd_y], axis=0), units)
+    wo_y = swap(after(wo, odd), "hy", name="weight")
+    even_near = after(jnp.concatenate([even, even_x], axis=0), odd_y, wo_y)
+    odd_near = after(jnp.concatenate([odd, odd_y], axis=0), even_x)
     even_far = swap(even_near, "hy", name="tok")
     odd_far = swap(odd_near, "part", name="tok")
-    xs = [even_near, even_far, swap(even_near, "hc", name="tok"), swap(even_far, "hc", name="tok")]
-    xs += [odd_near, odd_far, swap(odd_near, "hc", name="tok"), swap(odd_far, "hc", name="tok")]
-    dres_raw = split(coords, d_out, [even_near, odd_near])
-    dres = [dres_raw[0]] + [swap(dres_raw[k], "sq", k, name="dres") for k in range(1, 4)]
-
     mask_seq = lax.dynamic_index_in_dim(key_mask, z, 0, keepdims=False).reshape(blocks_all, BLOCK)
     mask = jnp.where(mask_seq == 1, 0.0, MASK_FILL).astype(f32)
     mask = jnp.pad(jnp.concatenate([mask, mask], axis=1), ((0, 8), (0, 0)), constant_values=MASK_FILL)
     rand = lax.dynamic_slice(rand_idx, (z, 0, head * heads, 0), (1, blocks_all, heads, 3)).reshape(-1)
+    even_far = after(even_far, mask, rand, *dres[1:])
+    xs = [even_near, even_far, swap(even_near, "hc", name="tok"), swap(even_far, "hc", name="tok")]
+    xs += [odd_near, odd_far, swap(odd_near, "hc", name="tok"), swap(odd_far, "hc", name="tok")]
     vecs = jnp.stack([bias_out, gain_one, bias_one, down_bias_vector, gain_two, bias_two])
     vecs = jnp.pad(vecs, ((0, 2), (0, 0)))
 
-    wf_c = swap(wf, "hc", name="weight")
-    quarter_c = swap(quarter, "hc", name="weight")
-    wf_zc = swap(wf_z, "hc", name="weight")
-    units, units_z, wo = copies([quarter, wf_z, wf], [2 * eighth, 2 * eighth, n_wo], xs)
-    wo_y = swap(wo, "hy", name="weight")
-    wf_x = swap(units, "part", name="weight")
-    wf_zx = swap(units_z, "part", name="weight")
+    wf_yc = swap(wf_y, "hc", name="weight")
+    wf_x = swap(wf_y, "part", name="weight")
+    wo_yc = swap(wo_y, "hc", name="weight")
 
     o_near, o_far, lse, kv, q = project_and_attend(
-        heads, hd, span, coords, rand, xs, w_kv, w_q_pad, b_kv, b_q, mask, [wf_c, quarter_c, wf_zc, units, *dres_raw]
-    )
-    o_far = after(o_far, *dres[1:])
-    wo_y, wf_x, wf_zx = after(wo_y, o_near), after(wf_x, o_near), after(wf_zx, o_near)
-    wo_yc = swap(wo_y, "hc", name="weight")
-    wf_xc = swap(wf_x, "hc", name="weight")
-    wf_zxc = swap(wf_zx, "hc", name="weight")
+        heads, hd, span, coords, rand, xs, w_kv, w_q_pad, b_kv, b_q, mask, []
+    )
     attn_y = swap(o_far, "hy", name="attn")
     attn_c = swap(o_near[rows:], "hc", name="attn")
     attn_yc = swap(attn_y[rows:], "hc", name="attn")
-
-    packs = [wf, wf_c, wo_y, quarter, wf_z, wf_x, wf_zx, wo_yc, quarter_c, wf_zc, wf_xc, wf_zxc]
-    first_rows = (n_wo, n_wo, n_wo, 0, 0, 0, 0, n_wo, 0, 0, 0, 0)
+    wf_x = after(wf_x, attn_c)
+    wf_xc = swap(wf_x, "hc", name="weight")
+
+    packs = [wf, wf_c, wo_y, wf_y, wf_x, wo_yc, wf_yc, wf_xc]
+    first_rows = tuple((n, n > 0) for n in (n_wo, n_wo, n_wo, 0, 0, n_wo, 0, 0))
     out = rows_work([o_near, attn_c, attn_y, attn_yc], packs, first_rows, [even, odd], dres, vecs)
     result, (d_one, hidden, d_pre, y_low, d_ffn, d_branch, d_00, d_01, d_far, small, bin_sum) = out[:4], out[4:]
 
@@ -1606,10 +1713,12 @@
     d_c = swap(d_01, "hc", name="dattn")
     d_yc = swap(d_y[1], "hc", name="dattn")
 
-    other = rows_grad(1, y_low, d_pre, hidden, d_ffn, d_branch, attn_c, attn_yc)
+    other = rows_grad(1, y_low, d_pre, hidden, d_ffn, d_branch, attn_c, attn_yc, small, bin_sum)
     wide_got = swap(other, "hc", name="wide")
     res = [result[0]] + [swap(result[k], "sq", k, name="result") for k in range(1, 4)]
-    keep, to_y, to_x, *across = rows_grad(0, y_low, d_pre, hidden, d_ffn, d_branch, o_near, attn_y, wide_got, [d_y, d_c])
+    keep, to_y, to_x, *across, small = rows_grad(
+        0, y_low, d_pre, hidden, d_ffn, d_branch, o_near, attn_y, small, bin_sum, wide_got, [d_y, d_c]
+    )
     y_got = swap(to_y, "hy", name="wide")
     x_got = swap(to_x, "part", name="wide")
     across_got = [swap(across[p], "sq", k, name="wide") for p, k in ((2, 1), (1, 2), (3, 3))]
@@ -1632,23 +1741,11 @@
     )
     dx_far = after(dx_far, y_got, x_got, *across_got)
 
-    b_in = bin_sum.reshape(4, hidden_dev)
-    flat = small[:6].reshape(-1)
-    n_flat = flat.size
-    got = swap(after(jnp.concatenate([flat, b_in[1], b_in[3]]), dq), "hc", name="small")
-    flat = flat + got[:n_flat]
-    b_in = jnp.stack([b_in[0], b_in[2]]) + got[n_flat:].reshape(2, hidden_dev)
-    got = swap(jnp.concatenate([flat, b_in[1]]), "hy", name="small")
-    flat = flat + got[:n_flat]
-    b_in = (b_in[0] + got[n_flat:]).reshape(2, 2, 2, eighth)
-    b_in = turn_octets(jnp.moveaxis(b_in, (2, 0), (0, 2)).reshape(8, eighth)).reshape(1, hidden_dev)
-    small = jnp.concatenate([flat.reshape(6, width), b_in, jnp.zeros((1, width), f32)], axis=0)
-    small = jnp.pad(small.reshape(8, width // 128, 128), ((0, 0), (0, 8 - width // 128), (0, 0)))
-
     dx_got = swap(dx_far, "hc", name="dtok")
     octets = octet[:4]
-    wide = wide_sum(((octets // 2 + octets % 2 * 2) ^ z).astype(jnp.int32), keep, y_got, x_got)
-    top, low = across_sum([across[0]] + across_got)
+    wide, top, low = wide_sum(
+        ((octets // 2 + octets % 2 * 2) ^ z).astype(jnp.int32), keep, y_got, x_got, [across[0]] + across_got
+    )
     sent = row_sum_one(dx, dx_got, [wide, top, low])
     wide = lax.psum_scatter(wide, "sq", scatter_dimension=0, tiled=True)[0]
     top, low = swap(top, "part", name="across"), swap(low, "hy", name="across")
@@ -1657,11 +1754,12 @@
     zq, xq = octet // 2, octet % 2
     zd = zq ^ z
     spots = ((xq ^ px) * 4 + (zd % 2) * 2 + zd // 2).astype(jnp.int32)
-    tail = qkv_grad(span, spots, dq, dkv, keep, y_got, small, xs, [*sent, top, low])
+    tail = qkv_grad(span, spots, coords, dq, dkv, keep, y_got, small, xs, [*sent])
+    top, low = after(top, tail), after(low, tail)
     top, low = swap(top, "hy", name="across"), swap(low, "part", name="across")
     tail_got = swap(tail[4:], "part", name="tail")
-    wide = wide_end(wide, top, low)
-    sent_two = row_sum_two(dx, dx_got, even_got, odd_got, [wide])
+    wide = wide_end(wide, top, low, [tail, even_got, odd_got])
+    sent_two = row_sum_two(dx, dx_got, even_got, odd_got, [tail])
     wide = lax.all_gather(wide, SEQ, axis=0, tiled=True)
     even_got2, odd_got2 = swap(sent_two[0], "part", name="dtok"), swap(sent_two[1], "hy", name="dtok")
     thins = tail_sum(tail, tail_got, [*sent_two])
@@ -1675,11 +1773,11 @@
     thin_held += [swap(a, "part", name="tail") for a in thin_held]
     grad_w_in = jnp.transpose(wide[:, :width]).astype(f32)
     grad_w_back = wide[:, width:].astype(f32)
-    thin, small = tail_place(back_spots, thin_held)
-    g_kv = jnp.transpose(thin[:n_kv]).reshape(width, heads, 2, hd)
-    g_q = jnp.transpose(thin[n_kv : n_kv + n_o]).reshape(width, heads, 1, hd)
-    grad_w_qkv = jnp.concatenate([g_q, g_kv], axis=2).astype(f32)
-    grad_w_out = thin[n_kv + n_o :].reshape(heads, hd, width).astype(f32)
+    thin, grad_w_out, small = tail_place(
+        back_spots, thin_held, n_o + n_kv, heads, [grad_w_in, grad_w_back]
+    )
+    grad_w_out = grad_w_out.reshape(heads, hd, width)
+    grad_w_qkv = thin.reshape(width, heads, 3, hd)
     small = small.reshape(8, 1024)
     grad_bias_qv = jnp.stack(
         [small[7, :n_o].reshape(heads, hd), small[7, n_o : n_o + n_kv].reshape(heads, 2, hd)[:, 1]], axis=1

time: 436 us -> 397 us (0.911)
  waiting for transfers between devices: 128 us -> 99.1 us
  Pallas kernels: 165 us -> 148 us
  starting transfers between devices: 68.3 us -> 73.3 us
  local copies, waits for them, and re-layouts: 38.3 us -> 42.8 us
    ppermute x65 -> x59, waiting for transfers between devices: 121 us -> 95.8 us  [swap(): return lax.ppermute(value, axis, [(i, i ^ step) for i in range(size)])]
    pallas_call x8 -> x5, Pallas kernels: 34.2 us -> 26.6 us  [the longest x2 16.2 us: rows_grad(): pl.pallas_call(functools.partial(rows_grad_kernel, kc, len(orders)), out_...]
    ppermute x65 -> x59, starting transfers between devices: 68.2 us -> 73.2 us  [swap(): return lax.ppermute(value, axis, [(i, i ^ step) for i in range(size)])]
    pallas_call x1, Pallas kernels: 34.3 us -> 29.5 us  [rows_work(): pl.pallas_call(functools.partial(rows_kernel, width, cols, first_rows), g...]
    unnamed x187 -> x186, local copies, waits for them, and re-layouts: 28 us -> 30.4 us
  transfers between devices with their start and end apart: 67 -> 61, of which waited for: 23 -> 20; matrix products, arithmetic and copies ran while one was open for 6% -> 7% of each run, Pallas kernels for 28% -> 26%
where the time goes in v3:
time: 397 us; the launch traced here: 392 us
  Pallas kernels  148 us (37%)
  waiting for transfers between devices  99.1 us (25%)
  starting transfers between devices  73.3 us (18%)
  local copies, waits for them, and re-layouts  42.8 us (11%)
  between operations  15.2 us (4%)
  other arithmetic  14.1 us (4%)
    ppermute x59, waiting for transfers between devices, swap(): return lax.ppermute(value, axis, [(i, i ^ step) for i in range(size)])  95.8 us
    ppermute x59, starting transfers between devices, swap(): return lax.ppermute(value, axis, [(i, i ^ step) for i in range(size)])  73.2 us
    pallas_call x1, Pallas kernels, attend_back(): pl.pallas_call(functools.partial(attend_back_kernel, heads, hd, span, len...  32.5 us
    unnamed x186, local copies, waits for them, and re-layouts  30.4 us
    pallas_call x1, Pallas kernels, rows_work(): pl.pallas_call(functools.partial(rows_kernel, width, cols, first_rows), g...  29.5 us
    pallas_call x1, Pallas kernels, project_and_attend(): pl.pallas_call(functools.partial(project_and_attend_kernel, heads, hd, sp...  23.2 us
    pallas_call x2, Pallas kernels, rows_grad(): pl.pallas_call(functools.partial(rows_grad_kernel, kc, len(orders)), out_...  16.2 us
    pallas_call x1, Pallas kernels, qkv_grad(): pl.pallas_call(functools.partial(qkv_grad_kernel, span), out_shape=jax.Sh...  10.8 us
  transfers between devices with their start and end apart: 61, of which 20 were waited for; matrix products, arithmetic and copies ran while one was open for 7% of the time, Pallas kernels for 26%

profile of v3, /device:TPU:0, one launch (start us, length us, event | category | flops | bytes accessed | tf_op | source)
XLA Modules:
  0.0 392.3 jit_solution(16744637296853916967)
XLA Ops:
  11.7 3.0 pack.1
  15.9 2.5 collective-permute-start.3
  18.5 3.3 split.2
  21.8 1.6 collective-permute-start.1
  23.4 2.5 collective-permute-start.2
  26.0 4.2 %copy.57.w_ref = bf16[768,3,3,64]{3,2,1,0:T(4,128)(2,1)S(1)} copy(bf16[768,3,3,64]{0,3,2,1:T(8,128)(2,1)} %param.17) | data formatting | bytes 1769472 | tf_op args[1]
  30.2 3.3 split.3
  36.2 2.9 qkv_weights.1
  40.7 2.0 pad_maximum_fusion.5.refs_0_
  45.4 1.8 collective-permute-start.6
  47.2 1.7 pad_maximum_fusion.4.refs_0_
  48.9 1.5 collective-permute-start.5
  51.3 6.4 %collective-permute-done.6.refs_1_ = bf16[256,768]{1,0:T(8,128)(2,1)S(1)} collective-permute-done((bf16[256,768]{1,0:T(8,128)(2,1)}, bf16[256,768]{1,0:T(8,128)(2,1)S(1)}, u32[]{:S(2)}, u32[]{:S(2)}) %collective-permute-start.6) | collective-permute-done | bytes 393248 | tf_op jit(solution)/shard_map/tok_hy1/ppermute | solution.py:480
  60.4 1.6 collective-permute-start.14
  61.9 1.9 pad_maximum_fusion.refs_0_
  64.7 1.5 collective-permute-start.8
  66.3 2.6 collective-permute-start.10
  73.1 9.0 %collective-permute-done.10.refs_4_.refs_16_ = bf16[128,768]{1,0:T(8,128)(2,1)S(1)} collective-permute-done((bf16[128,768]{1,0:T(8,128)(2,1)S(1)}, bf16[128,768]{1,0:T(8,128)(2,1)S(1)}, u32[]{:S(2)}, u32[]{:S(2)}) %collective-permute-start.10) | collective-permute-done | bytes 196640 | tf_op jit(solution)/shard_map/dres_sq2/ppermute | solution.py:480
  84.8 1.5 collective-permute-start.20
  86.3 1.9 collective-permute-done.16.refs_7_
  89.1 23.2 %project_and_attend.1 = (bf16[1024,192]{1,0:T(8,128)(2,1)}, bf16[1024,192]{1,0:T(8,128)(2,1)}, f32[2048,128]{1,0:T(8,128)}, bf16[4096,384]{1,0:T(8,128)(2,1)}, bf16[2048,384]{1,0:T(8,128)(2,1)}) custom-call(s32[4]{0:T(128)} %copy-done.18, s32[576]{0:T(1024)} %reshape.65.refs_2_.rand_ref, bf16[512,768]{1,0:T(8,128)(2,1)} %after.13.refs_0_, ...), custom_call_target="tpu_custom_call" | custom-call | flops 42949672960 | bytes 16777216 | tf_op jit(solution)/shard_map/project_and_attend/pallas_call | solution.py:730
  116.3 13.7 %collective-permute-done.18.refs_2_.refs_6_ = bf16[1024,192]{1,0:T(8,128)(2,1)S(1)} collective-permute-done((bf16[1024,192]{1,0:T(8,128)(2,1)S(1)}, bf16[1024,192]{1,0:T(8,128)(2,1)S(1)}, u32[]{:S(2)}, u32[]{:S(2)}) %collective-permute-start.18) | collective-permute-done | bytes 393248 | tf_op jit(solution)/shard_map/attn_hy1/ppermute | solution.py:480
  133.4 29.5 %rows_work.1 = (bf16[128,768]{1,0:T(8,128)(2,1)}, bf16[128,768]{1,0:T(8,128)(2,1)}, bf16[128,768]{1,0:T(8,128)(2,1)}, bf16[128,768]{1,0:T(8,128)(2,1)}, f32[512,...) custom-call(bf16[1024,192]{1,0:T(8,128)(2,1)} %get-tuple-element.95., ...), custom_call_target="tpu_custom_call" | custom-call | flops 53687091200 | bytes 31457280 | tf_op jit(solution)/shard_map/rows_work/pallas_call | solution.py:1358
  162.9 7.5 %far_grad.1 = bf16[20,96,1536]{2,1,0:T(8,128)(2,1)} custom-call(bf16[512,768]{1,0:T(8,128)(2,1)} %get-tuple-element.108.refs_0_, bf16[512,3072]{1,0:T(8,128)(2,1)} %get-tuple-element.109.refs_1_, bf16[512,3072]{1,0:T(8,128)(2,1)} %get-tuple-element.110.refs_2_, bf16[512,768]{1,0:T(8,128)(2,1)} %get-tuple-element.111.refs_3_, ...), custom_call_target="tpu_custom_call" | custom-call | flops 8589934592 | bytes 16777216 | tf_op jit(solution)/shard_map/far_grad/pallas_call | solution.py:1515
  171.1 2.8 collective-permute-start.24
  173.9 1.9 collective-permute-start.25
  175.8 9.0 %collective-permute-done.28.refs_10_.refs_2_ = bf16[2,512,192]{2,1,0:T(8,128)(2,1)S(1)} collective-permute-done((bf16[2,512,192]{2,1,0:T(8,128)(2,1)S(1)}, bf16[2,512,192]{2,1,0:T(8,128)(2,1)S(1)}, u32[]{:S(2)}, u32[]{:S(2)}) %collective-permute-start.28) | collective-permute-done | bytes 393248 | tf_op jit(solution)/shard_map/dattn_hy1/ppermute | solution.py:480
  184.8 2.4 collective-permute-start.26
  187.9 8.6 %near_grad.1 = (bf16[5,96,1536]{2,1,0:T(8,128)(2,1)}, bf16[496,1536]{1,0:T(8,128)(2,1)}, bf16[4,96,1536]{2,1,0:T(8,128)(2,1)}, bf16[96,1536]{1,0:T(8,128)(2,1)},...) custom-call(bf16[512,768]{1,0:T(8,128)(2,1)} %get-tuple-element.108.refs_0_, ...), custom_call_target="tpu_custom_call" | custom-call | flops 8589934592 | bytes 16777216 | tf_op jit(solution)/shard_map/near_grad/pallas_call | solution.py:1515
  196.6 1.6 collective-permute-start.31
  198.2 1.5 collective-permute-start.32
  199.7 1.6 collective-permute-start.33
  202.3 2.8 collective-permute-start.35
  205.0 32.5 %attend_back.1 = (bf16[2048,192]{1,0:T(8,128)(2,1)}, bf16[4096,384]{1,0:T(8,128)(2,1)}, bf16[2,1024,768]{2,1,0:T(8,128)(2,1)}, bf16[2,1024,768]{2,1,0:T(8,128)(2,1)}) custom-call(s32[4]{0:T(128)} %copy-done.18, s32[576]{0:T(1024)} %reshape.65.refs_2_.rand_ref, bf16[2048,384]{1,0:T(8,128)(2,1)} %get-tuple-element.101.q_from, ...), custom_call_target="tpu_custom_call" | custom-call | flops 64424509440 | bytes 25165824 | tf_op jit(solution)/shard_map/attend_back/pallas_call | solution.py:911
  240.1 3.9 wide_sum.1
  244.6 1.6 collective-permute-start.57
  246.7 1.7 copy-done.25
  248.4 3.3 row_sum_one.1
  252.4 1.4 collective-permute-start.38
  253.8 10.8 %qkv_grad.1.refs_0_.tail_ref.refs_1_ = bf16[8,96,896]{2,1,0:T(8,128)(2,1)} custom-call(s32[8]{0:T(128)} %fusion.11.spot_ref, s32[4]{0:T(128)} %copy-done.18, bf16[2048,192]{1,0:T(8,128)(2,1)} %get-tuple-element.129.dq_ref, bf16[4096,384]{1,0:T(8,128)(2,1)} %get-tuple-element.130.dkv_ref, bf16[5,96,1536]{2,1,0:T(8,128)(2,1)} %get-tuple-element.123.keep_ref, ...), custom_call_target="tpu_custom_call" | custom-call | flops 15032385536 | bytes 12582912 | tf_op jit(solution)/shard_map/qkv_grad/pallas_call | solution.py:1007
  268.0 3.3 reduce-scatter.2.cloned.1.call-done
  271.3 3.6 collective-permute-done.58.low_ref
  276.1 2.0 wide_end.1
  278.2 1.5 collective-permute-start.44
  279.7 2.6 row_sum_two.1
  284.3 15.5 %collective-permute-done.44.got_ref = bf16[4,96,896]{2,1,0:T(8,128)(2,1)S(1)} collective-permute-done((bf16[4,96,896]{2,1,0:T(8,128)(2,1)S(1)}, bf16[4,96,896]{2,1,0:T(8,128)(2,1)S(1)}, u32[]{:S(2)}, u32[]{:S(2)}) %collective-permute-start.44) | collective-permute-done | bytes 688160 | tf_op jit(solution)/shard_map/tail_part1/ppermute | solution.py:480
  300.7 2.4 tail_sum.1
  304.5 3.0 collective-permute-start.47
  308.4 3.4 row_sum_three.1
  311.8 2.1 collective-permute-done.45.refs_1_
  313.9 10.3 %collective-permute-done.46.refs_2_ = bf16[96,896]{1,0:T(8,128)(2,1)S(1)} collective-permute-done((bf16[96,896]{1,0:T(8,128)(2,1)}, bf16[96,896]{1,0:T(8,128)(2,1)S(1)}, u32[]{:S(2)}, u32[]{:S(2)}) %collective-permute-start.46) | collective-permute-done | bytes 172064 | tf_op jit(solution)/shard_map/tail_sq2/ppermute | solution.py:480
  325.0 2.0 tail_end.1.refs_0_
  326.9 12.7 %collective-permute-start.48 = (bf16[96,896]{1,0:T(8,128)(2,1)}, bf16[96,896]{1,0:T(8,128)(2,1)S(1)}, u32[]{:S(2)}, u32[]{:S(2)}) collective-permute-start(bf16[96,896]{1,0:T(8,128)(2,1)} %tail_end.1.refs_0_), channel_id=1, source_target_pairs={{0,8},{8,0},{16,24},{24,16},{1,9},{9,1},{17,25},{25,17},{2,10},{10... | collective-permute-start | bytes 516104 | tf_op jit(solution)/shard_map/tail_sq1/ppermute | solution.py:480
  339.6 2.4 collective-permute-start.50
  344.8 1.7 collective-permute-start.43
  347.1 11.6 %collective-permute-done.49.refs_2_ = bf16[96,896]{1,0:T(8,128)(2,1)S(1)} collective-permute-done((bf16[96,896]{1,0:T(8,128)(2,1)}, bf16[96,896]{1,0:T(8,128)(2,1)S(1)}, u32[]{:S(2)}, u32[]{:S(2)}) %collective-permute-start.49) | collective-permute-done | bytes 172064 | tf_op jit(solution)/shard_map/tail_sq2/ppermute | solution.py:480
  358.7 2.0 collective-permute-start.52
  360.8 5.6 %collective-permute-done.42 = bf16[128,768]{1,0:T(8,128)(2,1)S(1)} collective-permute-done((bf16[128,768]{1,0:T(8,128)(2,1)S(1)}, bf16[128,768]{1,0:T(8,128)(2,1)S(1)}, u32[]{:S(2)}, u32[]{:S(2)}) %collective-permute-start.42) | collective-permute-done | bytes 196640 | tf_op jit(solution)/shard_map/dtok_sq2/ppermute | solution.py:480
  367.5 1.5 copy.72
  369.1 1.5 copy.73
  370.6 3.4 slice_convert_fusion
  374.0 1.9 copy.60.refs_8_
  376.6 3.6 tail_place.1
  382.5 2.8 copy.61
  (327 shorter events, 56.7 us)
Async XLA Ops:
  7.2 63.3 %copy-start = (s32[4,64,12,3]{1,0,3,2:T(4,128)S(1)}, s32[4,64,12,3]{1,0,3,2:T(4,128)}, u32[]{:S(2)}) copy-start(s32[4,64,12,3]{1,0,3,2:T(4,128)} %param.31) | copy-start | bytes 110596
  7.2 264.1 %reduce-scatter.2.cloned.1.call-start = ((), (), s32[]{:S(2)}) async-start(), calls=%async_computation.1 | async-start | bytes 1474560 | tf_op jit(solution)/shard_map/reduce_scatter | solution.py:1750
  15.4 29.9 %collective-permute-start.4 = (bf16[880,1536]{1,0:T(8,128)(2,1)}, bf16[880,1536]{1,0:T(8,128)(2,1)}, u32[]{:S(2)}, u32[]{:S(2)}) collective-permute-start(bf16[880,1536]{1,0:T(8,128)(2,1)} %get-tuple-element.80.refs_0_.refs_4_), channel_id=1, source_target_pairs={{0,1},{1,0},{2,3},{3,2},{4,5},{5,4},{6,7},{7,6},{8,9},{9,8},{10,11... | collective-permute-start | bytes 8110088 | tf_op jit(solution)/shard_map/weight_hc1/ppermute | solution.py:480
  15.9 29.5 %collective-permute-start.3 = (bf16[384,1536]{1,0:T(8,128)(2,1)}, bf16[384,1536]{1,0:T(8,128)(2,1)}, u32[]{:S(2)}, u32[]{:S(2)}) collective-permute-start(bf16[384,1536]{1,0:T(8,128)(2,1)} %get-tuple-element.86), channel_id=1, source_target_pairs={{0,2},{2,0},{1,3},{3,1},{4,6},{6,4},{5,7},{7,5},{8,10},{10,8},{9,1... | collective-permute-start | bytes 3538952 | tf_op jit(solution)/shard_map/weight_hy1/ppermute | solution.py:480
  21.8 18.9 %collective-permute-start.1 = (bf16[128,768]{1,0:T(8,128)(2,1)}, bf16[128,768]{1,0:T(8,128)(2,1)}, u32[]{:S(2)}, u32[]{:S(2)}) collective-permute-start(bf16[128,768]{1,0:T(8,128)(2,1)} %get-tuple-element.83.refs_1_), channel_id=1, source_target_pairs={{0,8},{8,0},{16,24},{24,16},{1,9},{9,1},{17,25},{25,17},{2,10},{10... | collective-permute-start | bytes 589832 | tf_op jit(solution)/shard_map/tok_sq1/ppermute | solution.py:480
  23.4 17.3 %collective-permute-start.2 = (bf16[128,768]{1,0:T(8,128)(2,1)}, bf16[128,768]{1,0:T(8,128)(2,1)}, u32[]{:S(2)}, u32[]{:S(2)}) collective-permute-start(bf16[128,768]{1,0:T(8,128)(2,1)} %get-tuple-element.84.refs_3_), channel_id=1, source_target_pairs={{0,24},{8,16},{16,8},{24,0},{1,25},{9,17},{17,9},{25,1},{2,26},{10... | collective-permute-start | bytes 589832 | tf_op jit(solution)/shard_map/tok_sq3/ppermute | solution.py:480
  25.9 18.1 %collective-permute-start = (bf16[128,768]{1,0:T(8,128)(2,1)}, bf16[128,768]{1,0:T(8,128)(2,1)}, u32[]{:S(2)}, u32[]{:S(2)}) collective-permute-start(bf16[128,768]{1,0:T(8,128)(2,1)} %get-tuple-element.82.refs_2_), channel_id=1, source_target_pairs={{0,16},{8,24},{16,0},{24,8},{1,17},{9,25},{17,1},{25,9},{2,18},{10... | collective-permute-start | bytes 589832 | tf_op jit(solution)/shard_map/tok_sq2/ppermute | solution.py:480
  45.4 12.3 %collective-permute-start.6 = (bf16[256,768]{1,0:T(8,128)(2,1)}, bf16[256,768]{1,0:T(8,128)(2,1)S(1)}, u32[]{:S(2)}, u32[]{:S(2)}) collective-permute-start(bf16[256,768]{1,0:T(8,128)(2,1)} %after.11.refs_1_.refs_13_), channel_id=1, source_target_pairs={{0,2},{2,0},{1,3},{3,1},{4,6},{6,4},{5,7},{7,5},{8,10},{10,8},{9,1... | collective-permute-start | bytes 1179656 | tf_op jit(solution)/shard_map/tok_hy1/ppermute | solution.py:480
  48.9 10.7 %collective-permute-start.5 = (bf16[256,768]{1,0:T(8,128)(2,1)}, bf16[256,768]{1,0:T(8,128)(2,1)S(1)}, u32[]{:S(2)}, u32[]{:S(2)}) collective-permute-start(bf16[256,768]{1,0:T(8,128)(2,1)} %after.10.refs_12_), channel_id=1, source_target_pairs={{0,4},{4,0},{1,5},{5,1},{2,6},{6,2},{3,7},{7,3},{8,12},{12,8},{9,1... | collective-permute-start | bytes 1179656 | tf_op jit(solution)/shard_map/tok_part1/ppermute | solution.py:480
  50.4 13.6 %collective-permute-start.7 = (bf16[112,1536]{1,0:T(8,128)(2,1)}, bf16[112,1536]{1,0:T(8,128)(2,1)S(1)}, u32[]{:S(2)}, u32[]{:S(2)}) collective-permute-start(bf16[112,1536]{1,0:T(8,128)(2,1)} %after.12), channel_id=1, source_target_pairs={{0,2},{2,0},{1,3},{3,1},{4,6},{6,4},{5,7},{7,5},{8,10},{10,8},{9,1... | collective-permute-start | bytes 1032200 | tf_op jit(solution)/shard_map/weight_hy1/ppermute | solution.py:480
  60.4 22.3 %collective-permute-start.14 = (bf16[512,768]{1,0:T(8,128)(2,1)}, bf16[512,768]{1,0:T(8,128)(2,1)}, u32[]{:S(2)}, u32[]{:S(2)}) collective-permute-start(bf16[512,768]{1,0:T(8,128)(2,1)} %after.15.refs_4_), channel_id=1, source_target_pairs={{0,4},{4,0},{1,5},{5,1},{2,6},{6,2},{3,7},{7,3},{8,12},{12,8},{9,1... | collective-permute-start | bytes 2359304 | tf_op jit(solution)/shard_map/tok_part1/ppermute | solution.py:480
  64.7 18.7 %collective-permute-start.8 = (bf16[512,768]{1,0:T(8,128)(2,1)}, bf16[512,768]{1,0:T(8,128)(2,1)S(1)}, u32[]{:S(2)}, u32[]{:S(2)}) collective-permute-start(bf16[512,768]{1,0:T(8,128)(2,1)} %after.13.refs_0_), channel_id=1, source_target_pairs={{0,2},{2,0},{1,3},{3,1},{4,6},{6,4},{5,7},{7,5},{8,10},{10,8},{9,1... | collective-permute-start | bytes 2359304 | tf_op jit(solution)/shard_map/tok_hy1/ppermute | solution.py:480
  66.3 15.9 %collective-permute-start.10 = (bf16[128,768]{1,0:T(8,128)(2,1)S(1)}, bf16[128,768]{1,0:T(8,128)(2,1)S(1)}, u32[]{:S(2)}, u32[]{:S(2)}) collective-permute-start(bf16[128,768]{1,0:T(8,128)(2,1)S(1)} %copy-done.15), channel_id=1, source_target_pairs={{0,16},{8,24},{16,0},{24,8},{1,17},{9,25},{17,1},{25,9},{2,18},{10... | collective-permute-start | bytes 589832 | tf_op jit(solution)/shard_map/dres_sq2/ppermute | solution.py:480
  68.9 13.3 %collective-permute-start.11 = (bf16[128,768]{1,0:T(8,128)(2,1)S(1)}, bf16[128,768]{1,0:T(8,128)(2,1)S(1)}, u32[]{:S(2)}, u32[]{:S(2)}) collective-permute-start(bf16[128,768]{1,0:T(8,128)(2,1)S(1)} %copy-done.13), channel_id=1, source_target_pairs={{0,24},{8,16},{16,8},{24,0},{1,25},{9,17},{17,9},{25,1},{2,26},{10... | collective-permute-start | bytes 589832 | tf_op jit(solution)/shard_map/dres_sq3/ppermute | solution.py:480
  70.2 12.5 %collective-permute-start.9 = (bf16[128,768]{1,0:T(8,128)(2,1)S(1)}, bf16[128,768]{1,0:T(8,128)(2,1)S(1)}, u32[]{:S(2)}, u32[]{:S(2)}) collective-permute-start(bf16[128,768]{1,0:T(8,128)(2,1)S(1)} %copy-done.11), channel_id=1, source_target_pairs={{0,8},{8,0},{16,24},{24,16},{1,9},{9,1},{17,25},{25,17},{2,10},{10... | collective-permute-start | bytes 589832 | tf_op jit(solution)/shard_map/dres_sq1/ppermute | solution.py:480
  82.2 4.1 %collective-permute-start.15 = (bf16[512,768]{1,0:T(8,128)(2,1)S(1)}, bf16[512,768]{1,0:T(8,128)(2,1)}, u32[]{:S(2)}, u32[]{:S(2)}) collective-permute-start(bf16[512,768]{1,0:T(8,128)(2,1)S(1)} %copy-done.32), channel_id=1, source_target_pairs={{0,1},{1,0},{2,3},{3,2},{4,5},{5,4},{6,7},{7,6},{8,9},{9,8},{10,11... | collective-permute-start | bytes 2359304 | tf_op jit(solution)/shard_map/tok_hc1/ppermute | solution.py:480
  82.2 4.1 %collective-permute-start.12 = (bf16[512,768]{1,0:T(8,128)(2,1)}, bf16[512,768]{1,0:T(8,128)(2,1)}, u32[]{:S(2)}, u32[]{:S(2)}) collective-permute-start(bf16[512,768]{1,0:T(8,128)(2,1)} %after.13.refs_0_), channel_id=1, source_target_pairs={{0,1},{1,0},{2,3},{3,2},{4,5},{5,4},{6,7},{7,6},{8,9},{9,8},{10,11... | collective-permute-start | bytes 2359304 | tf_op jit(solution)/shard_map/tok_hc1/ppermute | solution.py:480
  82.7 5.5 %collective-permute-start.16 = (bf16[512,768]{1,0:T(8,128)(2,1)}, bf16[512,768]{1,0:T(8,128)(2,1)}, u32[]{:S(2)}, u32[]{:S(2)}) collective-permute-start(bf16[512,768]{1,0:T(8,128)(2,1)} %collective-permute-done.14.refs_5_), channel_id=1, source_target_pairs={{0,1},{1,0},{2,3},{3,2},{4,5},{5,4},{6,7},{7,6},{8,9},{9,8},{10,11... | collective-permute-start | bytes 2359304 | tf_op jit(solution)/shard_map/tok_hc1/ppermute | solution.py:480
  84.4 3.8 collective-permute-start.13
  84.8 29.2 %collective-permute-start.20 = (bf16[384,1536]{1,0:T(8,128)(2,1)}, bf16[384,1536]{1,0:T(8,128)(2,1)S(1)}, u32[]{:S(2)}, u32[]{:S(2)}) collective-permute-start(bf16[384,1536]{1,0:T(8,128)(2,1)} %collective-permute-done.3.refs_6_.refs_7_), channel_id=1, source_target_pairs={{0,4},{4,0},{1,5},{5,1},{2,6},{6,2},{3,7},{7,3},{8,12},{12,8},{9,1... | collective-permute-start | bytes 3538952 | tf_op jit(solution)/shard_map/weight_part1/ppermute | solution.py:480
  113.4 1.6 collective-permute-start.17
  113.6 17.3 %collective-permute-start.22 = (bf16[384,1536]{1,0:T(8,128)(2,1)}, bf16[384,1536]{1,0:T(8,128)(2,1)}, u32[]{:S(2)}, u32[]{:S(2)}) collective-permute-start(bf16[384,1536]{1,0:T(8,128)(2,1)} %collective-permute-done.3.refs_6_.refs_7_), channel_id=1, source_target_pairs={{0,1},{1,0},{2,3},{3,2},{4,5},{5,4},{6,7},{7,6},{8,9},{9,8},{10,11... | collective-permute-start | bytes 3538952 | tf_op jit(solution)/shard_map/weight_hc1/ppermute | solution.py:480
  115.7 16.0 %collective-permute-start.23 = (bf16[384,1536]{1,0:T(8,128)(2,1)}, bf16[384,1536]{1,0:T(8,128)(2,1)S(1)}, u32[]{:S(2)}, u32[]{:S(2)}) collective-permute-start(bf16[384,1536]{1,0:T(8,128)(2,1)} %after.16.refs_8_), channel_id=1, source_target_pairs={{0,1},{1,0},{2,3},{3,2},{4,5},{5,4},{6,7},{7,6},{8,9},{9,8},{10,11... | collective-permute-start | bytes 3538952 | tf_op jit(solution)/shard_map/weight_hc1/ppermute | solution.py:480
  115.8 14.2 %collective-permute-start.18 = (bf16[1024,192]{1,0:T(8,128)(2,1)S(1)}, bf16[1024,192]{1,0:T(8,128)(2,1)S(1)}, u32[]{:S(2)}, u32[]{:S(2)}) collective-permute-start(bf16[1024,192]{1,0:T(8,128)(2,1)S(1)} %copy-done.83), channel_id=1, source_target_pairs={{0,2},{2,0},{1,3},{3,1},{4,6},{6,4},{5,7},{7,5},{8,10},{10,8},{9,1... | collective-permute-start | bytes 1179656 | tf_op jit(solution)/shard_map/attn_hy1/ppermute | solution.py:480
  116.2 14.7 %collective-permute-start.21 = (bf16[112,1536]{1,0:T(8,128)(2,1)S(1)}, bf16[112,1536]{1,0:T(8,128)(2,1)S(1)}, u32[]{:S(2)}, u32[]{:S(2)}) collective-permute-start(bf16[112,1536]{1,0:T(8,128)(2,1)S(1)} %copy-done.46), channel_id=1, source_target_pairs={{0,1},{1,0},{2,3},{3,2},{4,5},{5,4},{6,7},{7,6},{8,9},{9,8},{10,11... | collective-permute-start | bytes 1032200 | tf_op jit(solution)/shard_map/weight_hc1/ppermute | solution.py:480
  130.1 1.6 collective-permute-start.19
  170.4 16.9 %collective-permute-start.30 = (bf16[20,96,1536]{2,1,0:T(8,128)(2,1)}, bf16[20,96,1536]{2,1,0:T(8,128)(2,1)}, u32[]{:S(2)}, u32[]{:S(2)}) collective-permute-start(bf16[20,96,1536]{2,1,0:T(8,128)(2,1)} %far_grad.1), channel_id=1, source_target_pairs={{0,1},{1,0},{2,3},{3,2},{4,5},{5,4},{6,7},{7,6},{8,9},{9,8},{10,11... | collective-permute-start | bytes 17694728 | tf_op jit(solution)/shard_map/wide_hc1/ppermute | solution.py:480
  170.6 14.2 %collective-permute-start.28 = (bf16[2,512,192]{2,1,0:T(8,128)(2,1)S(1)}, bf16[2,512,192]{2,1,0:T(8,128)(2,1)S(1)}, u32[]{:S(2)}, u32[]{:S(2)}) collective-permute-start(bf16[2,512,192]{2,1,0:T(8,128)(2,1)S(1)} %copy-done.84), channel_id=1, source_target_pairs={{0,2},{2,0},{1,3},{3,1},{4,6},{6,4},{5,7},{7,5},{8,10},{10,8},{9,1... | collective-permute-start | bytes 1179656 | tf_op jit(solution)/shard_map/dattn_hy1/ppermute | solution.py:480
  171.0 16.2 %collective-permute-start.27 = (bf16[512,192]{1,0:T(8,128)(2,1)S(1)}, bf16[512,192]{1,0:T(8,128)(2,1)S(1)}, u32[]{:S(2)}, u32[]{:S(2)}) collective-permute-start(bf16[512,192]{1,0:T(8,128)(2,1)S(1)} %copy-done.88), channel_id=1, source_target_pairs={{0,1},{1,0},{2,3},{3,2},{4,5},{5,4},{6,7},{7,6},{8,9},{9,8},{10,11... | collective-permute-start | bytes 589832 | tf_op jit(solution)/shard_map/dattn_hc1/ppermute | solution.py:480
  171.1 27.1 %collective-permute-start.24 = (bf16[128,768]{1,0:T(8,128)(2,1)S(1)}, bf16[128,768]{1,0:T(8,128)(2,1)S(1)}, u32[]{:S(2)}, u32[]{:S(2)}) collective-permute-start(bf16[128,768]{1,0:T(8,128)(2,1)S(1)} %copy-done.90), channel_id=1, source_target_pairs={{0,8},{8,0},{16,24},{24,16},{1,9},{9,1},{17,25},{25,17},{2,10},{10... | collective-permute-start | bytes 589832 | tf_op jit(solution)/shard_map/result_sq1/ppermute | solution.py:480
  173.9 25.8 %collective-permute-start.25 = (bf16[128,768]{1,0:T(8,128)(2,1)S(1)}, bf16[128,768]{1,0:T(8,128)(2,1)S(1)}, u32[]{:S(2)}, u32[]{:S(2)}) collective-permute-start(bf16[128,768]{1,0:T(8,128)(2,1)S(1)} %copy-done.89), channel_id=1, source_target_pairs={{0,16},{8,24},{16,0},{24,8},{1,17},{9,25},{17,1},{25,9},{2,18},{10... | collective-permute-start | bytes 589832 | tf_op jit(solution)/shard_map/result_sq2/ppermute | solution.py:480
  184.8 16.5 %collective-permute-start.26 = (bf16[128,768]{1,0:T(8,128)(2,1)}, bf16[128,768]{1,0:T(8,128)(2,1)S(1)}, u32[]{:S(2)}, u32[]{:S(2)}) collective-permute-start(bf16[128,768]{1,0:T(8,128)(2,1)} %get-tuple-element.100), channel_id=1, source_target_pairs={{0,24},{8,16},{16,8},{24,0},{1,25},{9,17},{17,9},{25,1},{2,26},{10... | collective-permute-start | bytes 589832 | tf_op jit(solution)/shard_map/result_sq3/ppermute | solution.py:480
  187.2 15.0 %collective-permute-start.29 = (bf16[512,192]{1,0:T(8,128)(2,1)S(1)}, bf16[512,192]{1,0:T(8,128)(2,1)}, u32[]{:S(2)}, u32[]{:S(2)}) collective-permute-start(bf16[512,192]{1,0:T(8,128)(2,1)S(1)} %slice_bitcast_fusion), channel_id=1, source_target_pairs={{0,1},{1,0},{2,3},{3,2},{4,5},{5,4},{6,7},{7,6},{8,9},{9,8},{10,11... | collective-permute-start | bytes 589832 | tf_op jit(solution)/shard_map/dattn_hc1/ppermute | solution.py:480
  196.6 41.1 %collective-permute-start.31 = (bf16[496,1536]{1,0:T(8,128)(2,1)}, bf16[496,1536]{1,0:T(8,128)(2,1)S(1)}, u32[]{:S(2)}, u32[]{:S(2)}) collective-permute-start(bf16[496,1536]{1,0:T(8,128)(2,1)} %get-tuple-element.115.refs_11_), channel_id=1, source_target_pairs={{0,2},{2,0},{1,3},{3,1},{4,6},{6,4},{5,7},{7,5},{8,10},{10,8},{9,1... | collective-permute-start | bytes 4571144 | tf_op jit(solution)/shard_map/wide_hy1/ppermute | solution.py:480
  198.2 39.5 %collective-permute-start.32 = (bf16[4,96,1536]{2,1,0:T(8,128)(2,1)}, bf16[4,96,1536]{2,1,0:T(8,128)(2,1)S(1)}, u32[]{:S(2)}, u32[]{:S(2)}) collective-permute-start(bf16[4,96,1536]{2,1,0:T(8,128)(2,1)} %get-tuple-element.116.refs_12_), channel_id=1, source_target_pairs={{0,4},{4,0},{1,5},{5,1},{2,6},{6,2},{3,7},{7,3},{8,12},{12,8},{9,1... | collective-permute-start | bytes 3538952 | tf_op jit(solution)/shard_map/wide_part1/ppermute | solution.py:480
  199.7 37.9 %collective-permute-start.33 = (bf16[96,1536]{1,0:T(8,128)(2,1)}, bf16[96,1536]{1,0:T(8,128)(2,1)S(1)}, u32[]{:S(2)}, u32[]{:S(2)}) collective-permute-start(bf16[96,1536]{1,0:T(8,128)(2,1)} %get-tuple-element.119.refs_15_), channel_id=1, source_target_pairs={{0,8},{8,0},{16,24},{24,16},{1,9},{9,1},{17,25},{25,17},{2,10},{10... | collective-permute-start | bytes 884744 | tf_op jit(solution)/shard_map/wide_sq1/ppermute | solution.py:480
  202.0 35.6 %collective-permute-start.34 = (bf16[96,1536]{1,0:T(8,128)(2,1)}, bf16[96,1536]{1,0:T(8,128)(2,1)S(1)}, u32[]{:S(2)}, u32[]{:S(2)}) collective-permute-start(bf16[96,1536]{1,0:T(8,128)(2,1)} %get-tuple-element.118.refs_14_), channel_id=1, source_target_pairs={{0,16},{8,24},{16,0},{24,8},{1,17},{9,25},{17,1},{25,9},{2,18},{10... | collective-permute-start | bytes 884744 | tf_op jit(solution)/shard_map/wide_sq2/ppermute | solution.py:480
  202.3 35.3 %collective-permute-start.35 = (bf16[96,1536]{1,0:T(8,128)(2,1)}, bf16[96,1536]{1,0:T(8,128)(2,1)S(1)}, u32[]{:S(2)}, u32[]{:S(2)}) collective-permute-start(bf16[96,1536]{1,0:T(8,128)(2,1)} %get-tuple-element.120.refs_16_), channel_id=1, source_target_pairs={{0,24},{8,16},{16,8},{24,0},{1,25},{9,17},{17,9},{25,1},{2,26},{10... | collective-permute-start | bytes 884744 | tf_op jit(solution)/shard_map/wide_sq3/ppermute | solution.py:480
  239.5 7.1 %collective-permute-start.36 = (bf16[2,1024,768]{2,1,0:T(8,128)(2,1)}, bf16[2,1024,768]{2,1,0:T(8,128)(2,1)S(1)}, u32[]{:S(2)}, u32[]{:S(2)}) collective-permute-start(bf16[2,1024,768]{2,1,0:T(8,128)(2,1)} %after.17), channel_id=1, source_target_pairs={{0,1},{1,0},{2,3},{3,2},{4,5},{5,4},{6,7},{7,6},{8,9},{9,8},{10,11... | collective-permute-start | bytes 9437192 | tf_op jit(solution)/shard_map/dtok_hc1/ppermute | solution.py:480
  244.0 126.6 %all-gather.2.cloned.1.call-start = ((), (), s32[]{:S(2)}) async-start(), calls=%async_computation.2 | async-start | bytes 2654208 | tf_op jit(solution)/shard_map/all_gather | solution.py:1763
  244.6 20.1 %collective-permute-start.57 = (bf16[48,1536]{1,0:T(8,128)(2,1)}, bf16[48,1536]{1,0:T(8,128)(2,1)S(1)}, u32[]{:S(2)}, u32[]{:S(2)}) collective-permute-start(bf16[48,1536]{1,0:T(8,128)(2,1)} %get-tuple-element.126.refs_2_), channel_id=1, source_target_pairs={{0,2},{2,0},{1,3},{3,1},{4,6},{6,4},{5,7},{7,5},{8,10},{10,8},{9,1... | collective-permute-start | bytes 442376 | tf_op jit(solution)/shard_map/across_hy1/ppermute | solution.py:480
  246.1 19.8 %collective-permute-start.55 = (bf16[48,1536]{1,0:T(8,128)(2,1)}, bf16[48,1536]{1,0:T(8,128)(2,1)S(1)}, u32[]{:S(2)}, u32[]{:S(2)}) collective-permute-start(bf16[48,1536]{1,0:T(8,128)(2,1)} %get-tuple-element.125.refs_1_), channel_id=1, source_target_pairs={{0,4},{4,0},{1,5},{5,1},{2,6},{6,2},{3,7},{7,3},{8,12},{12,8},{9,1... | collective-permute-start | bytes 442376 | tf_op jit(solution)/shard_map/across_part1/ppermute | solution.py:480
  251.7 23.2 %collective-permute-start.37 = (bf16[512,768]{1,0:T(8,128)(2,1)}, bf16[512,768]{1,0:T(8,128)(2,1)S(1)}, u32[]{:S(2)}, u32[]{:S(2)}) collective-permute-start(bf16[512,768]{1,0:T(8,128)(2,1)} %get-tuple-element.127.refs_8_), channel_id=1, source_target_pairs={{0,2},{2,0},{1,3},{3,1},{4,6},{6,4},{5,7},{7,5},{8,10},{10,8},{9,1... | collective-permute-start | bytes 2359304 | tf_op jit(solution)/shard_map/dtok_hy1/ppermute | solution.py:480
  252.4 22.5 %collective-permute-start.38 = (bf16[512,768]{1,0:T(8,128)(2,1)}, bf16[512,768]{1,0:T(8,128)(2,1)S(1)}, u32[]{:S(2)}, u32[]{:S(2)}) collective-permute-start(bf16[512,768]{1,0:T(8,128)(2,1)} %get-tuple-element.128.refs_9_), channel_id=1, source_target_pairs={{0,4},{4,0},{1,5},{5,1},{2,6},{6,2},{3,7},{7,3},{8,12},{12,8},{9,1... | collective-permute-start | bytes 2359304 | tf_op jit(solution)/shard_map/dtok_part1/ppermute | solution.py:480
  265.4 9.5 %collective-permute-start.58 = (bf16[48,1536]{1,0:T(8,128)(2,1)}, bf16[48,1536]{1,0:T(8,128)(2,1)S(1)}, u32[]{:S(2)}, u32[]{:S(2)}) collective-permute-start(bf16[48,1536]{1,0:T(8,128)(2,1)} %after.19), channel_id=1, source_target_pairs={{0,4},{4,0},{1,5},{5,1},{2,6},{6,2},{3,7},{7,3},{8,12},{12,8},{9,1... | collective-permute-start | bytes 442376 | tf_op jit(solution)/shard_map/across_part1/ppermute | solution.py:480
  266.6 8.3 %collective-permute-start.56 = (bf16[48,1536]{1,0:T(8,128)(2,1)}, bf16[48,1536]{1,0:T(8,128)(2,1)S(1)}, u32[]{:S(2)}, u32[]{:S(2)}) collective-permute-start(bf16[48,1536]{1,0:T(8,128)(2,1)} %after.18), channel_id=1, source_target_pairs={{0,2},{2,0},{1,3},{3,1},{4,6},{6,4},{5,7},{7,5},{8,10},{10,8},{9,1... | collective-permute-start | bytes 442376 | tf_op jit(solution)/shard_map/across_hy1/ppermute | solution.py:480
  278.2 21.6 %collective-permute-start.44 = (bf16[4,96,896]{2,1,0:T(8,128)(2,1)S(1)}, bf16[4,96,896]{2,1,0:T(8,128)(2,1)S(1)}, u32[]{:S(2)}, u32[]{:S(2)}) collective-permute-start(bf16[4,96,896]{2,1,0:T(8,128)(2,1)S(1)} %slice.78), channel_id=1, source_target_pairs={{0,4},{4,0},{1,5},{5,1},{2,6},{6,2},{3,7},{7,3},{8,12},{12,8},{9,1... | collective-permute-start | bytes 2064392 | tf_op jit(solution)/shard_map/tail_part1/ppermute | solution.py:480
  282.4 25.1 %collective-permute-start.39 = (bf16[256,768]{1,0:T(8,128)(2,1)}, bf16[256,768]{1,0:T(8,128)(2,1)S(1)}, u32[]{:S(2)}, u32[]{:S(2)}) collective-permute-start(bf16[256,768]{1,0:T(8,128)(2,1)} %get-tuple-element.132.refs_0_), channel_id=1, source_target_pairs={{0,4},{4,0},{1,5},{5,1},{2,6},{6,2},{3,7},{7,3},{8,12},{12,8},{9,1... | collective-permute-start | bytes 1179656 | tf_op jit(solution)/shard_map/dtok_part1/ppermute | solution.py:480
  282.9 24.6 %collective-permute-start.40 = (bf16[256,768]{1,0:T(8,128)(2,1)}, bf16[256,768]{1,0:T(8,128)(2,1)S(1)}, u32[]{:S(2)}, u32[]{:S(2)}) collective-permute-start(bf16[256,768]{1,0:T(8,128)(2,1)} %get-tuple-element.133.refs_1_), channel_id=1, source_target_pairs={{0,2},{2,0},{1,3},{3,1},{4,6},{6,4},{5,7},{7,5},{8,10},{10,8},{9,1... | collective-permute-start | bytes 1179656 | tf_op jit(solution)/shard_map/dtok_hy1/ppermute | solution.py:480
  303.1 10.8 %collective-permute-start.45 = (bf16[96,896]{1,0:T(8,128)(2,1)}, bf16[96,896]{1,0:T(8,128)(2,1)S(1)}, u32[]{:S(2)}, u32[]{:S(2)}) collective-permute-start(bf16[96,896]{1,0:T(8,128)(2,1)} %get-tuple-element.140), channel_id=1, source_target_pairs={{0,8},{8,0},{16,24},{24,16},{1,9},{9,1},{17,25},{25,17},{2,10},{10... | collective-permute-start | bytes 516104 | tf_op jit(solution)/shard_map/tail_sq1/ppermute | solution.py:480
  303.4 20.9 %collective-permute-start.46 = (bf16[96,896]{1,0:T(8,128)(2,1)}, bf16[96,896]{1,0:T(8,128)(2,1)S(1)}, u32[]{:S(2)}, u32[]{:S(2)}) collective-permute-start(bf16[96,896]{1,0:T(8,128)(2,1)} %get-tuple-element.141), channel_id=1, source_target_pairs={{0,16},{8,24},{16,0},{24,8},{1,17},{9,25},{17,1},{25,9},{2,18},{10... | collective-permute-start | bytes 516104 | tf_op jit(solution)/shard_map/tail_sq2/ppermute | solution.py:480
  304.5 19.7 %collective-permute-start.47 = (bf16[96,896]{1,0:T(8,128)(2,1)}, bf16[96,896]{1,0:T(8,128)(2,1)S(1)}, u32[]{:S(2)}, u32[]{:S(2)}) collective-permute-start(bf16[96,896]{1,0:T(8,128)(2,1)} %get-tuple-element.142), channel_id=1, source_target_pairs={{0,24},{8,16},{16,8},{24,0},{1,25},{9,17},{17,9},{25,1},{2,26},{10... | collective-permute-start | bytes 516104 | tf_op jit(solution)/shard_map/tail_sq3/ppermute | solution.py:480
  311.8 35.2 %copy-start.48 = (bf16[128,768]{1,0:T(8,128)(2,1)S(1)}, bf16[128,768]{1,0:T(8,128)(2,1)}, u32[]{:S(2)}) copy-start(bf16[128,768]{1,0:T(8,128)(2,1)} %get-tuple-element.97) | copy-start | bytes 589828
  325.0 41.9 %copy-start.39 = (bf16[128,768]{1,0:T(8,128)(2,1)S(1)}, bf16[128,768]{1,0:T(8,128)(2,1)}, u32[]{:S(2)}) copy-start(bf16[128,768]{1,0:T(8,128)(2,1)} %get-tuple-element.135.refs_4_) | copy-start | bytes 589828
  326.9 17.8 %collective-permute-start.48 = (bf16[96,896]{1,0:T(8,128)(2,1)}, bf16[96,896]{1,0:T(8,128)(2,1)S(1)}, u32[]{:S(2)}, u32[]{:S(2)}) collective-permute-start(bf16[96,896]{1,0:T(8,128)(2,1)} %tail_end.1.refs_0_), channel_id=1, source_target_pairs={{0,8},{8,0},{16,24},{24,16},{1,9},{9,1},{17,25},{25,17},{2,10},{10... | collective-permute-start | bytes 516104 | tf_op jit(solution)/shard_map/tail_sq1/ppermute | solution.py:480
  339.6 19.1 %collective-permute-start.49 = (bf16[96,896]{1,0:T(8,128)(2,1)}, bf16[96,896]{1,0:T(8,128)(2,1)S(1)}, u32[]{:S(2)}, u32[]{:S(2)}) collective-permute-start(bf16[96,896]{1,0:T(8,128)(2,1)} %tail_end.1.refs_0_), channel_id=1, source_target_pairs={{0,16},{8,24},{16,0},{24,8},{1,17},{9,25},{17,1},{25,9},{2,18},{10... | collective-permute-start | bytes 516104 | tf_op jit(solution)/shard_map/tail_sq2/ppermute | solution.py:480
  339.6 19.1 %collective-permute-start.50 = (bf16[96,896]{1,0:T(8,128)(2,1)}, bf16[96,896]{1,0:T(8,128)(2,1)S(1)}, u32[]{:S(2)}, u32[]{:S(2)}) collective-permute-start(bf16[96,896]{1,0:T(8,128)(2,1)} %tail_end.1.refs_0_), channel_id=1, source_target_pairs={{0,24},{8,16},{16,8},{24,0},{1,25},{9,17},{17,9},{25,1},{2,26},{10... | collective-permute-start | bytes 516104 | tf_op jit(solution)/shard_map/tail_sq3/ppermute | solution.py:480
  342.0 18.8 %collective-permute-start.41 = (bf16[128,768]{1,0:T(8,128)(2,1)S(1)}, bf16[128,768]{1,0:T(8,128)(2,1)S(1)}, u32[]{:S(2)}, u32[]{:S(2)}) collective-permute-start(bf16[128,768]{1,0:T(8,128)(2,1)S(1)} %copy-done.60), channel_id=1, source_target_pairs={{0,8},{8,0},{16,24},{24,16},{1,9},{9,1},{17,25},{25,17},{2,10},{10... | collective-permute-start | bytes 589832 | tf_op jit(solution)/shard_map/dtok_sq1/ppermute | solution.py:480
  343.1 23.3 %collective-permute-start.42 = (bf16[128,768]{1,0:T(8,128)(2,1)S(1)}, bf16[128,768]{1,0:T(8,128)(2,1)S(1)}, u32[]{:S(2)}, u32[]{:S(2)}) collective-permute-start(bf16[128,768]{1,0:T(8,128)(2,1)S(1)} %copy-done.59), channel_id=1, source_target_pairs={{0,16},{8,24},{16,0},{24,8},{1,17},{9,25},{17,1},{25,9},{2,18},{10... | collective-permute-start | bytes 589832 | tf_op jit(solution)/shard_map/dtok_sq2/ppermute | solution.py:480
  344.8 22.1 %collective-permute-start.43 = (bf16[128,768]{1,0:T(8,128)(2,1)S(1)}, bf16[128,768]{1,0:T(8,128)(2,1)S(1)}, u32[]{:S(2)}, u32[]{:S(2)}) collective-permute-start(bf16[128,768]{1,0:T(8,128)(2,1)S(1)} %copy-done.58), channel_id=1, source_target_pairs={{0,24},{8,16},{16,8},{24,0},{1,25},{9,17},{17,9},{25,1},{2,26},{10... | collective-permute-start | bytes 589832 | tf_op jit(solution)/shard_map/dtok_sq3/ppermute | solution.py:480
  358.7 17.2 %collective-permute-start.51 = (bf16[96,896]{1,0:T(8,128)(2,1)S(1)}, bf16[96,896]{1,0:T(8,128)(2,1)S(1)}, u32[]{:S(2)}, u32[]{:S(2)}) collective-permute-start(bf16[96,896]{1,0:T(8,128)(2,1)S(1)} %copy-done.41), channel_id=1, source_target_pairs={{0,4},{4,0},{1,5},{5,1},{2,6},{6,2},{3,7},{7,3},{8,12},{12,8},{9,1... | collective-permute-start | bytes 516104 | tf_op jit(solution)/shard_map/tail_part1/ppermute | solution.py:480
  358.7 17.2 %collective-permute-start.52 = (bf16[96,896]{1,0:T(8,128)(2,1)S(1)}, bf16[96,896]{1,0:T(8,128)(2,1)S(1)}, u32[]{:S(2)}, u32[]{:S(2)}) collective-permute-start(bf16[96,896]{1,0:T(8,128)(2,1)S(1)} %collective-permute-done.48.refs_1_), channel_id=1, source_target_pairs={{0,4},{4,0},{1,5},{5,1},{2,6},{6,2},{3,7},{7,3},{8,12},{12,8},{9,1... | collective-permute-start | bytes 516104 | tf_op jit(solution)/shard_map/tail_part1/ppermute | solution.py:480
  360.7 15.2 %collective-permute-start.53 = (bf16[96,896]{1,0:T(8,128)(2,1)S(1)}, bf16[96,896]{1,0:T(8,128)(2,1)}, u32[]{:S(2)}, u32[]{:S(2)}) collective-permute-start(bf16[96,896]{1,0:T(8,128)(2,1)S(1)} %collective-permute-done.49.refs_2_), channel_id=1, source_target_pairs={{0,4},{4,0},{1,5},{5,1},{2,6},{6,2},{3,7},{7,3},{8,12},{12,8},{9,1... | collective-permute-start | bytes 516104 | tf_op jit(solution)/shard_map/tail_part1/ppermute | solution.py:480
  366.4 9.6 %collective-permute-start.54 = (bf16[96,896]{1,0:T(8,128)(2,1)S(1)}, bf16[96,896]{1,0:T(8,128)(2,1)}, u32[]{:S(2)}, u32[]{:S(2)}) collective-permute-start(bf16[96,896]{1,0:T(8,128)(2,1)S(1)} %collective-permute-done.50.refs_3_), channel_id=1, source_target_pairs={{0,4},{4,0},{1,5},{5,1},{2,6},{6,2},{3,7},{7,3},{8,12},{12,8},{9,1... | collective-permute-start | bytes 516104 | tf_op jit(solution)/shard_map/tail_part1/ppermute | solution.py:480
  (88 other events, 601.8 us)
Sparse Core Ops, SparseCore 0:
  244.1 27.1 reduce-scatter.1
  278.3 66.5 all-gather.1

commit v4 on v3

--- a/solution.py
+++ b/solution.py
@@ -489,6 +489,12 @@
     value = value.reshape((2, 2) + shape[1:])
     value = flipped(flipped(value, place // 2, 0), place % 2, 1)
     return value.reshape(shape)
+
+
+def swap_both(value, name):
+    order = [(i, i ^ 3) for i in range(4)]
+    with jax.named_scope(name + "_both"):
+        return lax.ppermute(value, ("part", "hy"), order)
 
 
 ANY_SPEC = pl.BlockSpec(memory_space=pl.ANY)
@@ -952,11 +958,11 @@
 
 
 def qkv_grad_kernel(span, spot_ref, coord_ref, dq_ref, dkv_ref, keep_ref, got_ref, small_ref, *refs):
-    x_refs, out_ref = refs[:8], refs[-1]
+    x_refs, (keep_out, send_out, held_ref) = refs[:8], refs[-3:]
     piece = 4 * span
     n_kv = dkv_ref.shape[1]
     n_q = dq_ref.shape[1]
-    rows, width = out_ref.shape[1], x_refs[0].shape[1]
+    rows, width = held_ref.shape[1], x_refs[0].shape[1]
     acc = jnp.zeros((n_kv, width), f32)
     acc_q = jnp.zeros((n_q, width), f32)
     for n, x_ref in enumerate(x_refs):
@@ -964,7 +970,7 @@
     pair = 2 * span
     for at, n, src in query_pieces(pair):
         acc_q = acc_q + dot_tn(dq_ref[at : at + pair, :], x_refs[n][src : src + pair, :])
-    out_ref[...] = jnp.zeros_like(out_ref)
+    held_ref[...] = jnp.zeros_like(held_ref)
     both = jnp.concatenate([acc, acc_q], axis=0)
     octets = [both[o * rows : (o + 1) * rows] for o in range(6)]
     w_out = keep_ref[4].astype(f32) + got_ref[4 * rows : 5 * rows, :].astype(f32)
@@ -997,8 +1003,10 @@
     vectors = [lanes_down(small[i : i + 1]) for i in range(6)] + [lanes_down(b_in), sums]
     for o in range(8):
         spot = spot_ref[o]
-        out_ref[spot, :, :width] = octets[o].astype(bf16)
-        out_ref[spot, :16, width:] = split_low(vectors[o])
+        held_ref[spot, :, :width] = octets[o].astype(bf16)
+        held_ref[spot, :16, width:] = split_low(vectors[o])
+    keep_out[...] = held_ref[0:4]
+    send_out[...] = held_ref[4:8]
 
 
 def qkv_grad(span, spots, coords, dq, dkv, keep, got, small, xs, orders):
@@ -1006,9 +1014,10 @@
     rows = (dq.shape[1] + dkv.shape[1]) // 6
     return pl.pallas_call(
         functools.partial(qkv_grad_kernel, span),
-        out_shape=jax.ShapeDtypeStruct((8, rows, width + 128), bf16),
+        out_shape=(jax.ShapeDtypeStruct((4, rows, width + 128), bf16),) * 2,
         in_specs=[SMEM_SPEC] * 2 + [VMEM_SPEC] * 13 + [ANY_SPEC] * len(orders),
-        out_specs=VMEM_SPEC,
+        out_specs=(VMEM_SPEC,) * 2,
+        scratch_shapes=[pltpu.VMEM((8, rows, width + 128), bf16)],
         compiler_params=params(60),
         cost_estimate=pl.CostEstimate(
             flops=14 << 30, bytes_accessed=12 << 20, transcendentals=0
@@ -1017,108 +1026,155 @@
     )(spots, coords, dq, dkv, keep, got, small, *xs, *orders)
 
 
-def wide_sum_kernel(order_ref, keep_ref, y_ref, x_ref, a_ref, b_ref, c_ref, d_ref, out_ref, top_ref, low_ref):
+def across_sum_kernel(a_ref, b_ref, c_ref, d_ref, out_ref):
+    out_ref[...] = sum(r[...].astype(f32) for r in (a_ref, b_ref, c_ref, d_ref)).astype(bf16)
+
+
+def across_sum(parts):
+    return pl.pallas_call(
+        across_sum_kernel,
+        out_shape=jax.ShapeDtypeStruct(parts[0].shape, bf16),
+        in_specs=[VMEM_SPEC] * 4,
+        out_specs=VMEM_SPEC,
+        compiler_params=params(60),
+        cost_estimate=pl.CostEstimate(flops=1 << 24, bytes_accessed=1 << 20, transcendentals=0),
+        name="across_sum",
+    )(*parts)
+
+
+def wide_sum_kernel(order_ref, keep_ref, y_ref, x_ref, *refs):
+    out_ref = refs[-1]
     rows = keep_ref.shape[1]
-    half = rows // 2
-    for i, out in enumerate((top_ref, low_ref)):
-        of = slice(i * half, (i + 1) * half)
-        out[...] = sum(r[of, :].astype(f32) for r in (a_ref, b_ref, c_ref, d_ref)).astype(bf16)
     for k in range(4):
         of = slice(k * rows, (k + 1) * rows)
         out_ref[order_ref[k]] = (keep_ref[k].astype(f32) + y_ref[of, :].astype(f32) + x_ref[k].astype(f32)).astype(bf16)
 
 
-def wide_sum(order, keep, y_got, x_got, across):
+def wide_sum(order, keep, y_got, x_got, orders):
     _, rows, cols = keep.shape
     four = pl.BlockSpec((4, rows, cols), lambda i: (0, 0, 0))
-    octet = pl.BlockSpec((rows, cols), lambda i: (0, 0))
-    half = pl.BlockSpec((rows // 2, cols), lambda i: (0, 0))
     return pl.pallas_call(
         wide_sum_kernel,
         grid=(1,),
-        in_specs=[SMEM_SPEC, four, pl.BlockSpec((4 * rows, cols), lambda i: (0, 0)), four] + [octet] * 4,
-        out_specs=(four, half, half),
-        out_shape=(
-            jax.ShapeDtypeStruct((4, rows, cols), bf16),
-            jax.ShapeDtypeStruct((rows // 2, cols), bf16),
-            jax.ShapeDtypeStruct((rows // 2, cols), bf16),
-        ),
+        in_specs=[SMEM_SPEC, four, pl.BlockSpec((4 * rows, cols), lambda i: (0, 0)), four] + [ANY_SPEC] * len(orders),
+        out_specs=four,
+        out_shape=jax.ShapeDtypeStruct((4, rows, cols), bf16),
         compiler_params=params(60),
-        cost_estimate=pl.CostEstimate(flops=1 << 28, bytes_accessed=6 << 20, transcendentals=0),
+        cost_estimate=pl.CostEstimate(flops=4 << 30, bytes_accessed=6 << 20, transcendentals=0),
         name="wide_sum",
-    )(order, keep, y_got, x_got, *across)
-
-
-def tail_sum_kernel(n_orders, tail_ref, got_ref, *refs):
-    out_refs = refs[n_orders:]
-    thin = tail_ref.shape[2] - 128
+    )(order, keep, y_got, x_got, *orders)
+
+
+def low_sum(out_ref, at, refs):
+    rows, cols = out_ref.shape[1:]
+    thin = cols - 128
+    out_ref[at, :, :thin] = sum(ref[k, :, :thin].astype(f32) for ref, k in refs).astype(bf16)
+    out_ref[at, :, thin:] = jnp.zeros((rows, 128), bf16)
+    out_ref[at, :16, thin:] = split_low(sum(joined(ref[k, :16, thin:]) for ref, k in refs))
+
+
+def tail_sum_kernel(tail_ref, got_ref, *refs):
+    keep_ref, send_ref = refs[-2:]
     for k in range(4):
-        out_refs[k][:, :thin] = (tail_ref[k, :, :thin].astype(f32) + got_ref[k, :, :thin].astype(f32)).astype(bf16)
-        out_refs[k][:, thin:] = jnp.zeros((tail_ref.shape[1], 128), bf16)
-        out_refs[k][:16, thin:] = split_low(joined(tail_ref[k, :16, thin:]) + joined(got_ref[k, :16, thin:]))
-
-
-def tail_sum(tail, tail_got, orders):
+        low_sum(keep_ref if k < 2 else send_ref, k % 2, [(tail_ref, k), (got_ref, k)])
+
+
+def tail_sum(tail, got, orders):
     _, rows, cols = tail.shape
     return pl.pallas_call(
-        functools.partial(tail_sum_kernel, len(orders)),
-        out_shape=(jax.ShapeDtypeStruct((rows, cols), bf16),) * 4,
+        tail_sum_kernel,
+        out_shape=(jax.ShapeDtypeStruct((2, rows, cols), bf16),) * 2,
         in_specs=[VMEM_SPEC] * 2 + [ANY_SPEC] * len(orders),
-        out_specs=(VMEM_SPEC,) * 4,
+        out_specs=(VMEM_SPEC,) * 2,
         compiler_params=params(60),
         cost_estimate=pl.CostEstimate(flops=1 << 28, bytes_accessed=2 << 20, transcendentals=0),
         name="tail_sum",
-    )(tail, tail_got, *orders)
-
-
-def wide_end_kernel(wide_ref, top_ref, low_ref, *refs):
-    out_ref = refs[-1]
-    half = top_ref.shape[0]
-    for i, more_ref in enumerate((top_ref, low_ref)):
-        of = slice(i * half, (i + 1) * half)
-        out_ref[of, :] = (wide_ref[of, :].astype(f32) + more_ref[...].astype(f32)).astype(bf16)
-
-
-def wide_end(wide, top, low, orders):
+    )(tail, got, *orders)
+
+
+def tail_mid_kernel(keep_ref, got_ref, own_ref, send_ref):
+    low_sum(own_ref, 0, [(keep_ref, 0), (got_ref, 0)])
+    low_sum(send_ref, 0, [(keep_ref, 1), (got_ref, 1)])
+
+
+def tail_mid(keep, got):
+    _, rows, cols = keep.shape
+    return pl.pallas_call(
+        tail_mid_kernel,
+        out_shape=(jax.ShapeDtypeStruct((1, rows, cols), bf16),) * 2,
+        in_specs=[VMEM_SPEC] * 2,
+        out_specs=(VMEM_SPEC,) * 2,
+        compiler_params=params(60),
+        cost_estimate=pl.CostEstimate(flops=1 << 28, bytes_accessed=2 << 20, transcendentals=0),
+        name="tail_mid",
+    )(keep, got)
+
+
+def wide_end_kernel(wide_ref, across_ref, *refs):
+    refs[-1][...] = (wide_ref[...].astype(f32) + across_ref[...].astype(f32)).astype(bf16)
+
+
+def wide_end(wide, across, orders):
     return pl.pallas_call(
         wide_end_kernel,
         out_shape=jax.ShapeDtypeStruct(wide.shape, bf16),
-        in_specs=[VMEM_SPEC] * 3 + [ANY_SPEC] * len(orders),
+        in_specs=[VMEM_SPEC] * 2 + [ANY_SPEC] * len(orders),
         out_specs=VMEM_SPEC,
         compiler_params=params(60),
         cost_estimate=pl.CostEstimate(flops=1 << 28, bytes_accessed=3 << 20, transcendentals=0),
         name="wide_end",
-    )(wide, top, low, *orders)
-
-
-def tail_end_kernel(*refs):
-    thin_refs, out_ref = refs[:4], refs[-1]
-    thin = out_ref.shape[1] - 128
-    out_ref[:, :thin] = sum(r[:, :thin].astype(f32) for r in thin_refs).astype(bf16)
-    out_ref[:, thin:] = jnp.zeros((out_ref.shape[0], 128), bf16)
-    out_ref[:16, thin:] = split_low(sum(joined(r[:16, thin:]) for r in thin_refs))
-
-
-def tail_end(thins, orders):
+    )(wide, across, *orders)
+
+
+def tail_end_kernel(own_ref, got_ref, *refs):
+    low_sum(refs[-1], 0, [(own_ref, 0), (got_ref, 0)])
+
+
+def tail_end(own, got, orders):
     return pl.pallas_call(
         tail_end_kernel,
-        out_shape=jax.ShapeDtypeStruct(thins[0].shape, bf16),
-        in_specs=[VMEM_SPEC] * 4 + [ANY_SPEC] * len(orders),
+        out_shape=jax.ShapeDtypeStruct(own.shape, bf16),
+        in_specs=[VMEM_SPEC] * 2 + [ANY_SPEC] * len(orders),
         out_specs=VMEM_SPEC,
         compiler_params=params(60),
         cost_estimate=pl.CostEstimate(flops=1 << 28, bytes_accessed=3 << 20, transcendentals=0),
         name="tail_end",
-    )(*thins, *orders)
+    )(own, got, *orders)
+
+
+def wide_place_kernel(spot_ref, *refs):
+    ins, (in_ref, back_ref, held_ref) = refs[:8], refs[-3:]
+    rows, width = ins[0].shape[0], back_ref.shape[1]
+    for n in range(8):
+        to = pl.ds(pl.multiple_of(spot_ref[n] * rows, 16), rows)
+        held_ref[to, :] = ins[n][:, :width].astype(f32)
+        back_ref[to, :] = ins[n][:, width:].astype(f32)
+    in_ref[...] = held_ref[...].T
+
+
+def wide_place(spots, parts, orders):
+    rows, cols = parts[0].shape
+    width = cols // 2
+    return pl.pallas_call(
+        wide_place_kernel,
+        out_shape=(jax.ShapeDtypeStruct((width, 8 * rows), f32), jax.ShapeDtypeStruct((8 * rows, width), f32)),
+        in_specs=[SMEM_SPEC] + [VMEM_SPEC] * 8 + [ANY_SPEC] * len(orders),
+        out_specs=(VMEM_SPEC,) * 2,
+        scratch_shapes=[pltpu.VMEM((8 * rows, width), f32)],
+        compiler_params=params(60),
+        cost_estimate=pl.CostEstimate(flops=1 << 28, bytes_accessed=3 << 20, transcendentals=0),
+        name="wide_place",
+    )(spots, *parts, *orders)
 
 
 def tail_place_kernel(n_qkv, heads, spot_ref, *refs):
     ins, (qkv_ref, w_out_ref, small_ref, held_ref) = refs[:8], refs[-4:]
-    rows = ins[0].shape[0]
+    rows = ins[0].shape[1]
     cols = held_ref.shape[1]
     for n in range(8):
         spot = spot_ref[n]
-        held_ref[pl.ds(pl.multiple_of(spot * rows, 16), rows), :] = ins[n][:, :cols].astype(f32)
-        small_ref[spot] = joined(ins[n][:16, cols:])
+        held_ref[pl.ds(pl.multiple_of(spot * rows, 16), rows), :] = ins[n][0, :, :cols].astype(f32)
+        small_ref[spot] = joined(ins[n][0, :16, cols:])
     w_out_ref[...] = held_ref[n_qkv:, :]
     hd = n_qkv // 3 // heads
     parts = []
@@ -1129,7 +1185,7 @@
 
 
 def tail_place(spots, parts, n_qkv, heads, orders):
-    rows, cols = parts[0].shape
+    _, rows, cols = parts[0].shape
     width = cols - 128
     return pl.pallas_call(
         functools.partial(tail_place_kernel, n_qkv, heads),
@@ -1539,84 +1595,128 @@
     return out[0] if kc else out
 
 
-def row_sum_one_kernel(near_ref, got_ref, *refs):
-    for i, out in enumerate(refs[-2:]):
-
-        @pl.when(pl.program_id(0) == i)
-        def _(out=out):
-            out[...] = (near_ref[0].astype(f32) + got_ref[0].astype(f32)).astype(bf16)
+def row_sum_one_kernel(n_orders, near_from, got_from, *refs):
+    outs, (near_ref, got_ref, in_sems, out_sems) = refs[n_orders : n_orders + 2], refs[n_orders + 2 :]
+    rows = near_ref.shape[1]
+    far = pl.ds(rows, rows)
+    arriving, leaving = [], []
+    for i in range(2):
+        for j, (src, dst) in enumerate(((near_from, near_ref), (got_from, got_ref))):
+            arriving.append(pltpu.make_async_copy(src.at[i, far], dst.at[i], in_sems.at[i, j]))
+            arriving[-1].start()
+    for i in range(2):
+        arriving[2 * i].wait()
+        arriving[2 * i + 1].wait()
+        near_ref[i] = (near_ref[i].astype(f32) + got_ref[i].astype(f32)).astype(bf16)
+        leaving.append(pltpu.make_async_copy(near_ref.at[i], outs[i], out_sems.at[i]))
+        leaving[-1].start()
+    for copy in leaving:
+        copy.wait()
 
 
 def row_sum_one(near, got, orders):
     _, rows, width = near.shape
-    far = pl.BlockSpec((1, rows // 2, width), lambda i: (i, 1, 0))
-    return pl.pallas_call(
-        row_sum_one_kernel,
-        grid=(2,),
-        out_shape=(jax.ShapeDtypeStruct((rows // 2, width), bf16),) * 2,
-        in_specs=[far] * 2 + [ANY_SPEC] * len(orders),
-        out_specs=(pl.BlockSpec((rows // 2, width), lambda i: (0, 0)),) * 2,
+    half = (2, rows // 2, width)
+    return pl.pallas_call(
+        functools.partial(row_sum_one_kernel, len(orders)),
+        out_shape=(jax.ShapeDtypeStruct(half[1:], bf16),) * 2,
+        in_specs=[ANY_SPEC] * (2 + len(orders)),
+        out_specs=(ANY_SPEC,) * 2,
+        scratch_shapes=[
+            pltpu.VMEM(half, bf16),
+            pltpu.VMEM(half, bf16),
+            pltpu.SemaphoreType.DMA((2, 2)),
+            pltpu.SemaphoreType.DMA((2,)),
+        ],
         compiler_params=params(60),
         cost_estimate=pl.CostEstimate(flops=1 << 28, bytes_accessed=6 << 20, transcendentals=0),
         name="row_sum_one",
     )(near, got, *orders)
 
 
-def row_sum_two_kernel(near_ref, got_ref, even_ref, odd_ref, *refs):
-    for i, (src, out) in enumerate(zip((even_ref, odd_ref), refs[-2:])):
-
-        @pl.when(pl.program_id(0) == i)
-        def _(src=src, out=out):
-            out[...] = (near_ref[0].astype(f32) + got_ref[0].astype(f32) + src[...].astype(f32)).astype(bf16)
+def row_sum_two_kernel(n_orders, near_from, got_from, even_from, odd_from, *refs):
+    outs, (near_ref, got_ref, more_ref, in_sems, out_sems) = refs[n_orders : n_orders + 2], refs[n_orders + 2 :]
+    rows = near_ref.shape[1]
+    part = pl.ds(rows, rows)
+    arriving, leaving = [], []
+    for i, more_from in enumerate((even_from, odd_from)):
+        pairs = (
+            (near_from.at[i, part], near_ref.at[i]),
+            (got_from.at[i, part], got_ref.at[i]),
+            (more_from.at[part], more_ref.at[i]),
+        )
+        for j, (src, dst) in enumerate(pairs):
+            arriving.append(pltpu.make_async_copy(src, dst, in_sems.at[i, j]))
+            arriving[-1].start()
+    for i in range(2):
+        for copy in arriving[3 * i : 3 * i + 3]:
+            copy.wait()
+        near_ref[i] = (near_ref[i].astype(f32) + got_ref[i].astype(f32) + more_ref[i].astype(f32)).astype(bf16)
+        leaving.append(pltpu.make_async_copy(near_ref.at[i], outs[i], out_sems.at[i]))
+        leaving[-1].start()
+    for copy in leaving:
+        copy.wait()
 
 
 def row_sum_two(near, got, even, odd, orders):
     quarter, width = near.shape[1] // 4, near.shape[2]
-    part = pl.BlockSpec((1, quarter, width), lambda i: (i, 1, 0))
-    return pl.pallas_call(
-        row_sum_two_kernel,
-        grid=(2,),
+    two = pltpu.VMEM((2, quarter, width), bf16)
+    return pl.pallas_call(
+        functools.partial(row_sum_two_kernel, len(orders)),
         out_shape=(jax.ShapeDtypeStruct((quarter, width), bf16),) * 2,
-        in_specs=[part] * 2 + [pl.BlockSpec((quarter, width), lambda i: (1, 0))] * 2 + [ANY_SPEC] * len(orders),
-        out_specs=(pl.BlockSpec((quarter, width), lambda i: (0, 0)),) * 2,
+        in_specs=[ANY_SPEC] * (4 + len(orders)),
+        out_specs=(ANY_SPEC,) * 2,
+        scratch_shapes=[two, two, two, pltpu.SemaphoreType.DMA((2, 3)), pltpu.SemaphoreType.DMA((2,))],
         compiler_params=params(60),
         cost_estimate=pl.CostEstimate(flops=1 << 28, bytes_accessed=4 << 20, transcendentals=0),
         name="row_sum_two",
     )(near, got, even, odd, *orders)
 
 
-def row_sum_three_kernel(near_ref, got_ref, even_ref, odd_ref, even_got, odd_got, done_ref, *out_refs):
+def row_sum_three_kernel(n_orders, near_from, got_from, even_from, odd_from, even_got, odd_got, done_from, *refs):
+    refs = refs[n_orders:]
+    outs, (near_ref, got_ref, one_ref, two_ref, done_ref, in_sems, out_sems) = refs[:4], refs[4:]
     rows = near_ref.shape[1]
-    for i, (one, two) in enumerate(((even_ref, even_got), (odd_ref, odd_got))):
-
-        @pl.when(pl.program_id(0) == i)
-        def _(i=i, one=one, two=two):
-            total = (
-                near_ref[0].astype(f32)
-                + got_ref[0].astype(f32)
-                + one[:rows, :].astype(f32)
-                + two[:rows, :].astype(f32)
-                + done_ref[...]
-            ).astype(bf16)
-            out_refs[i][...] = total[: rows // 2]
-            out_refs[i + 2][...] = total[rows // 2 :]
-
-
-def row_sum_three(near, got, even, odd, even_got, odd_got, d_one):
+    part = pl.ds(0, rows)
+    arriving, leaving = [], []
+    for i, (one, two) in enumerate(((even_from, even_got), (odd_from, odd_got))):
+        pairs = (
+            (near_from.at[i, part], near_ref.at[i]),
+            (got_from.at[i, part], got_ref.at[i]),
+            (one.at[part], one_ref.at[i]),
+            (two, two_ref.at[i]),
+            (done_from.at[pl.ds(i * rows, rows)], done_ref.at[i]),
+        )
+        for j, (src, dst) in enumerate(pairs):
+            arriving.append(pltpu.make_async_copy(src, dst, in_sems.at[i, j]))
+            arriving[-1].start()
+    for i in range(2):
+        for copy in arriving[5 * i : 5 * i + 5]:
+            copy.wait()
+        total = near_ref[i].astype(f32) + got_ref[i].astype(f32) + one_ref[i].astype(f32) + two_ref[i].astype(f32)
+        near_ref[i] = (total + done_ref[i]).astype(bf16)
+        for k in range(2):
+            src = near_ref.at[i, pl.ds(k * (rows // 2), rows // 2)]
+            leaving.append(pltpu.make_async_copy(src, outs[i + 2 * k], out_sems.at[i, k]))
+            leaving[-1].start()
+    for copy in leaving:
+        copy.wait()
+
+
+def row_sum_three(near, got, even, odd, even_got, odd_got, d_one, orders):
     quarter, width = near.shape[1] // 4, near.shape[2]
-    part = pl.BlockSpec((1, quarter, width), lambda i: (i, 0, 0))
-    first = pl.BlockSpec((quarter, width), lambda i: (0, 0))
-    out = pl.BlockSpec((quarter // 2, width), lambda i: (0, 0))
-    return pl.pallas_call(
-        row_sum_three_kernel,
-        grid=(2,),
+    two = pltpu.VMEM((2, quarter, width), bf16)
+    return pl.pallas_call(
+        functools.partial(row_sum_three_kernel, len(orders)),
         out_shape=(jax.ShapeDtypeStruct((quarter // 2, width), bf16),) * 4,
-        in_specs=[part] * 2 + [first] * 4 + [pl.BlockSpec((quarter, width), lambda i: (i, 0))],
-        out_specs=(out,) * 4,
+        in_specs=[ANY_SPEC] * (7 + len(orders)),
+        out_specs=(ANY_SPEC,) * 4,
+        scratch_shapes=[two, two, two, two, pltpu.VMEM((2, quarter, width), f32)]
+        + [pltpu.SemaphoreType.DMA((2, 5)), pltpu.SemaphoreType.DMA((2, 2))],
         compiler_params=params(60),
         cost_estimate=pl.CostEstimate(flops=1 << 28, bytes_accessed=4 << 20, transcendentals=0),
         name="row_sum_three",
-    )(near, got, even, odd, even_got, odd_got, d_one)
+    )(near, got, even, odd, even_got, odd_got, d_one, *orders)
 
 
 def plane_layer(
@@ -1743,36 +1843,36 @@
 
     dx_got = swap(dx_far, "hc", name="dtok")
     octets = octet[:4]
-    wide, top, low = wide_sum(
-        ((octets // 2 + octets % 2 * 2) ^ z).astype(jnp.int32), keep, y_got, x_got, [across[0]] + across_got
-    )
-    sent = row_sum_one(dx, dx_got, [wide, top, low])
-    wide = lax.psum_scatter(wide, "sq", scatter_dimension=0, tiled=True)[0]
-    top, low = swap(top, "part", name="across"), swap(low, "hy", name="across")
-    even_got, odd_got = swap(sent[0], "hy", name="dtok"), swap(sent[1], "part", name="dtok")
-
+    beyond = across_sum([across[0]] + across_got)
+    wide = wide_sum(((octets // 2 + octets % 2 * 2) ^ z).astype(jnp.int32), keep, y_got, x_got, [beyond])
+    beyond = swap_both(beyond, "across")
     zq, xq = octet // 2, octet % 2
     zd = zq ^ z
     spots = ((xq ^ px) * 4 + (zd % 2) * 2 + zd // 2).astype(jnp.int32)
-    tail = qkv_grad(span, spots, coords, dq, dkv, keep, y_got, small, xs, [*sent])
-    top, low = after(top, tail), after(low, tail)
-    top, low = swap(top, "hy", name="across"), swap(low, "part", name="across")
-    tail_got = swap(tail[4:], "part", name="tail")
-    wide = wide_end(wide, top, low, [tail, even_got, odd_got])
-    sent_two = row_sum_two(dx, dx_got, even_got, odd_got, [tail])
-    wide = lax.all_gather(wide, SEQ, axis=0, tiled=True)
+    tail, tail_got = qkv_grad(span, spots, coords, dq, dkv, keep, y_got, small, xs, [wide])
+    wide = lax.psum_scatter(wide, "sq", scatter_dimension=0, tiled=True)[0]
+    tail_got = swap(tail_got, "part", name="tail")
+    sent = row_sum_one(dx, dx_got, [tail])
+    even_got, odd_got = swap(sent[0], "hy", name="dtok"), swap(sent[1], "part", name="dtok")
+    keep, send = tail_sum(tail, tail_got, [*sent])
+    wide = wide_end(wide, beyond, [*sent, keep])
+    wide_two = swap(wide, "sq", 2, name="wide")
+    wide = [wide, swap(wide, "sq", 1, name="wide")]
+    own, send = tail_mid(keep, swap(send, "sq", 1, name="tail"))
+    back_spots = (((octet % 4) ^ z) * 2 + ((octet // 4) ^ px)).astype(jnp.int32)
+    sent_two = row_sum_two(dx, dx_got, even_got, odd_got, [send])
+    wide[1], wide_two = after(wide[1], send), after(wide_two, send)
+    wide += [wide_two, swap(wide_two, "sq", 1, name="wide")]
+    wide += [swap(a, "part", name="wide") for a in wide]
+    own = tail_end(own, swap(send, "sq", 2, name="tail"), [*sent_two])
     even_got2, odd_got2 = swap(sent_two[0], "part", name="dtok"), swap(sent_two[1], "hy", name="dtok")
-    thins = tail_sum(tail, tail_got, [*sent_two])
-    thins = [thins[0]] + [swap(thins[p], "sq", k, name="tail") for p, k in ((2, 1), (1, 2), (3, 3))]
-    back_sent = row_sum_three(dx, dx_got, even_got, odd_got, even_got2, odd_got2, d_one)
+    back_sent = row_sum_three(dx, dx_got, even_got, odd_got, even_got2, odd_got2, d_one, [own])
     back = [back_sent[0]] + [swap(back_sent[k], "sq", k, name="dtok") for k in range(1, 4)]
 
-    back_spots = (((octet % 4) ^ z) * 2 + ((octet // 4) ^ px)).astype(jnp.int32)
-    thin_held = tail_end(thins, [*back_sent])
-    thin_held = [thin_held] + [swap(thin_held, "sq", k, name="tail") for k in range(1, 4)]
+    beyond = swap(own, "sq", 2, name="tail")
+    thin_held = [own, swap(own, "sq", 1, name="tail"), beyond, swap(beyond, "sq", 1, name="tail")]
     thin_held += [swap(a, "part", name="tail") for a in thin_held]
-    grad_w_in = jnp.transpose(wide[:, :width]).astype(f32)
-    grad_w_back = wide[:, width:].astype(f32)
+    grad_w_in, grad_w_back = wide_place(back_spots, wide, [*back_sent])
     thin, grad_w_out, small = tail_place(
         back_spots, thin_held, n_o + n_kv, heads, [grad_w_in, grad_w_back]
     )

time: 397 us -> 375 us (0.945)
  waiting for transfers between devices: 99.1 us -> 86.3 us
  starting transfers between devices: 73.3 us -> 62 us
  Pallas kernels: 148 us -> 155 us
  local copies, waits for them, and re-layouts: 42.8 us -> 38.7 us
    ppermute x59 -> x61, starting transfers between devices: 73.2 us -> 59.7 us  [swap(): return lax.ppermute(value, axis, [(i, i ^ step) for i in range(size)])]
    ppermute x59 -> x61, waiting for transfers between devices: 95.8 us -> 82.3 us  [swap(): return lax.ppermute(value, axis, [(i, i ^ step) for i in range(size)])]
    pallas_call x6 -> x9, Pallas kernels: 24.6 us -> 32.6 us  [the longest x1 11.1 us: qkv_grad(): pl.pallas_call(functools.partial(qkv_grad_kernel, span), out_shape=(jax.S...]
    ppermute x0 -> x1, waiting for transfers between devices: none -> 3.99 us  [swap_both(): return lax.ppermute(value, ('part', 'hy'), order)]
    unnamed x186 -> x178, local copies, waits for them, and re-layouts: 30.4 us -> 28.3 us
  transfers between devices with their start and end apart: 61 -> 63, of which waited for: 20 -> 20; matrix products, arithmetic and copies ran while one was open for 7% -> 6% of each run, Pallas kernels for 26% -> 31%
where the time goes in v4:
time: 375 us; the launch traced here: 369 us
  Pallas kernels  155 us (41%)
  waiting for transfers between devices  86.3 us (23%)
  starting transfers between devices  62 us (17%)
  local copies, waits for them, and re-layouts  38.7 us (10%)
  between operations  15.2 us (4%)
  other arithmetic  11.6 us (3%)
    ppermute x61, waiting for transfers between devices, swap(): return lax.ppermute(value, axis, [(i, i ^ step) for i in range(size)])  82.3 us
    ppermute x61, starting transfers between devices, swap(): return lax.ppermute(value, axis, [(i, i ^ step) for i in range(size)])  59.7 us
    pallas_call x1, Pallas kernels, attend_back(): pl.pallas_call(functools.partial(attend_back_kernel, heads, hd, span, len...  32.2 us
    pallas_call x1, Pallas kernels, rows_work(): pl.pallas_call(functools.partial(rows_kernel, width, cols, first_rows), g...  29.6 us
    unnamed x178, local copies, waits for them, and re-layouts  28.3 us
    pallas_call x1, Pallas kernels, project_and_attend(): pl.pallas_call(functools.partial(project_and_attend_kernel, heads, hd, sp...  23.2 us
    pallas_call x2, Pallas kernels, rows_grad(): pl.pallas_call(functools.partial(rows_grad_kernel, kc, len(orders)), out_...  16.2 us
    pallas_call x1, Pallas kernels, qkv_grad(): pl.pallas_call(functools.partial(qkv_grad_kernel, span), out_shape=(jax.S...  11.1 us
  transfers between devices with their start and end apart: 63, of which 20 were waited for; matrix products, arithmetic and copies ran while one was open for 6% of the time, Pallas kernels for 31%

profile of v4, /device:TPU:0, one launch (start us, length us, event | category | flops | bytes accessed | tf_op | source)
XLA Modules:
  0.0 369.0 jit_solution(9380251417395774215)
XLA Ops:
  11.7 3.0 pack.1
  15.9 2.5 collective-permute-start.3
  18.5 3.3 split.2
  21.8 1.6 collective-permute-start.1
  23.4 2.5 collective-permute-start.2
  26.0 4.2 %copy.53.w_ref = bf16[768,3,3,64]{3,2,1,0:T(4,128)(2,1)S(1)} copy(bf16[768,3,3,64]{0,3,2,1:T(8,128)(2,1)} %param.17) | data formatting | bytes 1769472 | tf_op args[1]
  30.2 3.3 split.3
  36.2 2.9 qkv_weights.1
  40.8 2.0 pad_maximum_fusion.5.refs_0_
  45.4 1.8 collective-permute-start.6
  47.2 1.7 pad_maximum_fusion.4.refs_0_
  48.9 1.5 collective-permute-start.5
  51.3 6.4 %collective-permute-done.6.refs_1_ = bf16[256,768]{1,0:T(8,128)(2,1)S(1)} collective-permute-done((bf16[256,768]{1,0:T(8,128)(2,1)}, bf16[256,768]{1,0:T(8,128)(2,1)S(1)}, u32[]{:S(2)}, u32[]{:S(2)}) %collective-permute-start.6) | collective-permute-done | bytes 393248 | tf_op jit(solution)/shard_map/tok_hy1/ppermute | solution.py:480
  60.4 1.6 collective-permute-start.14
  61.9 1.9 pad_maximum_fusion.refs_0_
  64.7 1.5 collective-permute-start.8
  66.3 2.6 collective-permute-start.10
  73.1 9.0 %collective-permute-done.10.refs_4_.refs_16_ = bf16[128,768]{1,0:T(8,128)(2,1)S(1)} collective-permute-done((bf16[128,768]{1,0:T(8,128)(2,1)S(1)}, bf16[128,768]{1,0:T(8,128)(2,1)S(1)}, u32[]{:S(2)}, u32[]{:S(2)}) %collective-permute-start.10) | collective-permute-done | bytes 196640 | tf_op jit(solution)/shard_map/dres_sq2/ppermute | solution.py:480
  84.7 1.5 collective-permute-start.20
  86.2 1.9 collective-permute-done.16.refs_7_
  89.0 23.2 %project_and_attend.1 = (bf16[1024,192]{1,0:T(8,128)(2,1)}, bf16[1024,192]{1,0:T(8,128)(2,1)}, f32[2048,128]{1,0:T(8,128)}, bf16[4096,384]{1,0:T(8,128)(2,1)}, bf16[2048,384]{1,0:T(8,128)(2,1)}) custom-call(s32[4]{0:T(128)} %copy-done.18, s32[576]{0:T(1024)} %reshape.65.refs_2_.rand_ref, bf16[512,768]{1,0:T(8,128)(2,1)} %after.13.refs_0_, ...), custom_call_target="tpu_custom_call" | custom-call | flops 42949672960 | bytes 16777216 | tf_op jit(solution)/shard_map/project_and_attend/pallas_call | solution.py:736
  116.3 13.7 %collective-permute-done.18.refs_2_.refs_6_ = bf16[1024,192]{1,0:T(8,128)(2,1)S(1)} collective-permute-done((bf16[1024,192]{1,0:T(8,128)(2,1)S(1)}, bf16[1024,192]{1,0:T(8,128)(2,1)S(1)}, u32[]{:S(2)}, u32[]{:S(2)}) %collective-permute-start.18) | collective-permute-done | bytes 393248 | tf_op jit(solution)/shard_map/attn_hy1/ppermute | solution.py:480
  133.3 29.6 %rows_work.1 = (bf16[128,768]{1,0:T(8,128)(2,1)}, bf16[128,768]{1,0:T(8,128)(2,1)}, bf16[128,768]{1,0:T(8,128)(2,1)}, bf16[128,768]{1,0:T(8,128)(2,1)}, f32[512,...) custom-call(bf16[1024,192]{1,0:T(8,128)(2,1)} %get-tuple-element.96., ...), custom_call_target="tpu_custom_call" | custom-call | flops 53687091200 | bytes 31457280 | tf_op jit(solution)/shard_map/rows_work/pallas_call | solution.py:1414
  163.0 7.6 %far_grad.1 = bf16[20,96,1536]{2,1,0:T(8,128)(2,1)} custom-call(bf16[512,768]{1,0:T(8,128)(2,1)} %get-tuple-element.109.refs_0_, bf16[512,3072]{1,0:T(8,128)(2,1)} %get-tuple-element.110.refs_1_, bf16[512,3072]{1,0:T(8,128)(2,1)} %get-tuple-element.111.refs_2_, bf16[512,768]{1,0:T(8,128)(2,1)} %get-tuple-element.112.refs_3_, ...), custom_call_target="tpu_custom_call" | custom-call | flops 8589934592 | bytes 16777216 | tf_op jit(solution)/shard_map/far_grad/pallas_call | solution.py:1571
  171.2 2.8 collective-permute-start.24
  174.0 1.9 collective-permute-start.25
  175.9 9.0 %collective-permute-done.28.refs_10_.refs_2_ = bf16[2,512,192]{2,1,0:T(8,128)(2,1)S(1)} collective-permute-done((bf16[2,512,192]{2,1,0:T(8,128)(2,1)S(1)}, bf16[2,512,192]{2,1,0:T(8,128)(2,1)S(1)}, u32[]{:S(2)}, u32[]{:S(2)}) %collective-permute-start.28) | collective-permute-done | bytes 393248 | tf_op jit(solution)/shard_map/dattn_hy1/ppermute | solution.py:480
  185.0 2.4 collective-permute-start.26
  188.1 8.6 %near_grad.1 = (bf16[5,96,1536]{2,1,0:T(8,128)(2,1)}, bf16[496,1536]{1,0:T(8,128)(2,1)}, bf16[4,96,1536]{2,1,0:T(8,128)(2,1)}, bf16[96,1536]{1,0:T(8,128)(2,1)},...) custom-call(bf16[512,768]{1,0:T(8,128)(2,1)} %get-tuple-element.109.refs_0_, ...), custom_call_target="tpu_custom_call" | custom-call | flops 8589934592 | bytes 16777216 | tf_op jit(solution)/shard_map/near_grad/pallas_call | solution.py:1571
  196.7 2.7 collective-permute-start.33
  200.1 1.9 collective-permute-start.35
  204.2 1.5 collective-permute-start.32
  205.6 32.2 %attend_back.1 = (bf16[2048,192]{1,0:T(8,128)(2,1)}, bf16[4096,384]{1,0:T(8,128)(2,1)}, bf16[2,1024,768]{2,1,0:T(8,128)(2,1)}, bf16[2,1024,768]{2,1,0:T(8,128)(2,1)}) custom-call(s32[4]{0:T(128)} %copy-done.18, s32[576]{0:T(1024)} %reshape.65.refs_2_.rand_ref, bf16[2048,384]{1,0:T(8,128)(2,1)} %get-tuple-element.102.q_from, ...), custom_call_target="tpu_custom_call" | custom-call | flops 64424509440 | bytes 25165824 | tf_op jit(solution)/shard_map/attend_back/pallas_call | solution.py:917
  240.4 2.1 across_sum.1.refs_0_
  242.4 3.4 wide_sum.1.refs_8_
  246.4 11.1 %qkv_grad.1 = (bf16[4,96,896]{2,1,0:T(8,128)(2,1)}, bf16[4,96,896]{2,1,0:T(8,128)(2,1)}) custom-call(s32[8]{0:T(128)} %fusion.9.spot_ref, s32[4]{0:T(128)} %copy-done.18, bf16[2048,192]{1,0:T(8,128)(2,1)} %get-tuple-element.124.dq_ref, bf16[4096,384]{1,0:T(8,128)(2,1)} %get-tuple-element.125.dkv_ref, bf16[5,96,1536]{2,1,0:T(8,128)(2,1)} %get-tuple-element.126.keep_ref, ...), custom_call_target="tpu_custom_call" | custom-call | flops 15032385536 | bytes 12582912 | tf_op jit(solution)/shard_map/qkv_grad/pallas_call | solution.py:1015
  257.8 2.3 collective-permute-start.54
  260.1 1.7 copy-done.24
  261.8 3.0 row_sum_one.1
  266.0 10.0 %collective-permute-done.39.got_ref = bf16[4,96,896]{2,1,0:T(8,128)(2,1)} collective-permute-done((bf16[4,96,896]{2,1,0:T(8,128)(2,1)}, bf16[4,96,896]{2,1,0:T(8,128)(2,1)}, u32[]{:S(2)}, u32[]{:S(2)}) %collective-permute-start.39) | collective-permute-done | bytes 688160 | tf_op jit(solution)/shard_map/tail_part1/ppermute | solution.py:480
  276.0 2.2 tail_sum.1
  278.9 4.0 %collective-permute-done.54.across_ref = bf16[96,1536]{1,0:T(8,128)(2,1)S(1)} collective-permute-done((bf16[96,1536]{1,0:T(8,128)(2,1)S(1)}, bf16[96,1536]{1,0:T(8,128)(2,1)S(1)}, u32[]{:S(2)}, u32[]{:S(2)}) %collective-permute-start.54) | collective-permute-done | bytes 294944 | tf_op jit(solution)/shard_map/across_both/ppermute | solution.py:497
  283.6 1.9 wide_end.1.refs_0_
  286.5 1.4 collective-permute-start.55
  288.6 1.9 tail_mid.1
  290.5 10.9 %collective-permute-done.56.refs_0_ = bf16[96,1536]{1,0:T(8,128)(2,1)S(1)} collective-permute-done((bf16[96,1536]{1,0:T(8,128)(2,1)}, bf16[96,1536]{1,0:T(8,128)(2,1)S(1)}, u32[]{:S(2)}, u32[]{:S(2)}) %collective-permute-start.56) | collective-permute-done | bytes 294944 | tf_op jit(solution)/shard_map/wide_sq2/ppermute | solution.py:480
  302.1 2.3 collective-permute-start.43
  305.0 1.8 collective-permute-start.59
  306.8 2.5 row_sum_two.1
  310.0 2.7 collective-permute-done.43.got_ref
  313.3 1.7 tail_end.1.refs_0_
  315.1 3.4 collective-permute-start.48
  318.5 7.6 %collective-permute-done.48.refs_2_ = bf16[1,96,896]{2,1,0:T(8,128)(2,1)S(1)} collective-permute-done((bf16[1,96,896]{2,1,0:T(8,128)(2,1)}, bf16[1,96,896]{2,1,0:T(8,128)(2,1)S(1)}, u32[]{:S(2)}, u32[]{:S(2)}) %collective-permute-start.48) | collective-permute-done | bytes 172064 | tf_op jit(solution)/shard_map/tail_sq2/ppermute | solution.py:480
  326.8 1.8 collective-permute-start.50
  328.7 2.9 collective-permute-done.49.refs_3_
  331.7 1.8 collective-permute-start.51
  334.8 3.4 row_sum_three.1
  339.0 4.7 %wide_place.1 = (f32[768,768]{1,0:T(8,128)}, f32[768,768]{1,0:T(8,128)}) custom-call(s32[8]{0:T(128)} %fusion.5.spot_ref, bf16[96,1536]{1,0:T(8,128)(2,1)} %wide_end.1.refs_0_, bf16[96,1536]{1,0:T(8,128)(2,1)} %after.18.refs_1_, bf16[96,1536]{1,0:T(8,128)(2,1)} %after.19.refs_2_, bf16[96,1536]{1,0:T(8,128)(2,1)} %copy-done.47, bf16[96,1536]{1,0:T(8,128)(2,1)} %copy-done.46, ...), custom_call_target="tpu_custom_call" | custom-call | flops 268435456 | bytes 3145728 | tf_op jit(solution)/shard_map/wide_place/pallas_call | solution.py:1158
  343.8 1.8 collective-permute-start.45
  347.0 2.0 collective-permute-start.46
  349.0 3.6 tail_place.1
  354.2 2.8 copy.56
  358.8 1.5 copy.66
  360.4 1.5 copy.67
  (322 shorter events, 54.5 us)
Async XLA Ops:
  7.2 63.3 %copy-start = (s32[4,64,12,3]{1,0,3,2:T(4,128)S(1)}, s32[4,64,12,3]{1,0,3,2:T(4,128)}, u32[]{:S(2)}) copy-start(s32[4,64,12,3]{1,0,3,2:T(4,128)} %param.31) | copy-start | bytes 110596
  7.2 275.7 %reduce-scatter.2.cloned.1.call-start = ((), (), s32[]{:S(2)}) async-start(), calls=%async_computation.1 | async-start | bytes 1474560 | tf_op jit(solution)/shard_map/reduce_scatter | solution.py:1853
  15.4 29.9 %collective-permute-start.4 = (bf16[880,1536]{1,0:T(8,128)(2,1)}, bf16[880,1536]{1,0:T(8,128)(2,1)}, u32[]{:S(2)}, u32[]{:S(2)}) collective-permute-start(bf16[880,1536]{1,0:T(8,128)(2,1)} %get-tuple-element.81.refs_0_.refs_4_), channel_id=1, source_target_pairs={{0,1},{1,0},{2,3},{3,2},{4,5},{5,4},{6,7},{7,6},{8,9},{9,8},{10,11... | collective-permute-start | bytes 8110088 | tf_op jit(solution)/shard_map/weight_hc1/ppermute | solution.py:480
  15.9 29.5 %collective-permute-start.3 = (bf16[384,1536]{1,0:T(8,128)(2,1)}, bf16[384,1536]{1,0:T(8,128)(2,1)}, u32[]{:S(2)}, u32[]{:S(2)}) collective-permute-start(bf16[384,1536]{1,0:T(8,128)(2,1)} %get-tuple-element.87), channel_id=1, source_target_pairs={{0,2},{2,0},{1,3},{3,1},{4,6},{6,4},{5,7},{7,5},{8,10},{10,8},{9,1... | collective-permute-start | bytes 3538952 | tf_op jit(solution)/shard_map/weight_hy1/ppermute | solution.py:480
  21.8 19.0 %collective-permute-start.1 = (bf16[128,768]{1,0:T(8,128)(2,1)}, bf16[128,768]{1,0:T(8,128)(2,1)}, u32[]{:S(2)}, u32[]{:S(2)}) collective-permute-start(bf16[128,768]{1,0:T(8,128)(2,1)} %get-tuple-element.84.refs_1_), channel_id=1, source_target_pairs={{0,8},{8,0},{16,24},{24,16},{1,9},{9,1},{17,25},{25,17},{2,10},{10... | collective-permute-start | bytes 589832 | tf_op jit(solution)/shard_map/tok_sq1/ppermute | solution.py:480
  23.4 17.3 %collective-permute-start.2 = (bf16[128,768]{1,0:T(8,128)(2,1)}, bf16[128,768]{1,0:T(8,128)(2,1)}, u32[]{:S(2)}, u32[]{:S(2)}) collective-permute-start(bf16[128,768]{1,0:T(8,128)(2,1)} %get-tuple-element.85.refs_3_), channel_id=1, source_target_pairs={{0,24},{8,16},{16,8},{24,0},{1,25},{9,17},{17,9},{25,1},{2,26},{10... | collective-permute-start | bytes 589832 | tf_op jit(solution)/shard_map/tok_sq3/ppermute | solution.py:480
  25.9 18.1 %collective-permute-start = (bf16[128,768]{1,0:T(8,128)(2,1)}, bf16[128,768]{1,0:T(8,128)(2,1)}, u32[]{:S(2)}, u32[]{:S(2)}) collective-permute-start(bf16[128,768]{1,0:T(8,128)(2,1)} %get-tuple-element.83.refs_2_), channel_id=1, source_target_pairs={{0,16},{8,24},{16,0},{24,8},{1,17},{9,25},{17,1},{25,9},{2,18},{10... | collective-permute-start | bytes 589832 | tf_op jit(solution)/shard_map/tok_sq2/ppermute | solution.py:480
  45.4 12.3 %collective-permute-start.6 = (bf16[256,768]{1,0:T(8,128)(2,1)}, bf16[256,768]{1,0:T(8,128)(2,1)S(1)}, u32[]{:S(2)}, u32[]{:S(2)}) collective-permute-start(bf16[256,768]{1,0:T(8,128)(2,1)} %after.11.refs_1_.refs_13_), channel_id=1, source_target_pairs={{0,2},{2,0},{1,3},{3,1},{4,6},{6,4},{5,7},{7,5},{8,10},{10,8},{9,1... | collective-permute-start | bytes 1179656 | tf_op jit(solution)/shard_map/tok_hy1/ppermute | solution.py:480
  48.9 10.7 %collective-permute-start.5 = (bf16[256,768]{1,0:T(8,128)(2,1)}, bf16[256,768]{1,0:T(8,128)(2,1)S(1)}, u32[]{:S(2)}, u32[]{:S(2)}) collective-permute-start(bf16[256,768]{1,0:T(8,128)(2,1)} %after.10.refs_12_), channel_id=1, source_target_pairs={{0,4},{4,0},{1,5},{5,1},{2,6},{6,2},{3,7},{7,3},{8,12},{12,8},{9,1... | collective-permute-start | bytes 1179656 | tf_op jit(solution)/shard_map/tok_part1/ppermute | solution.py:480
  50.4 13.6 %collective-permute-start.7 = (bf16[112,1536]{1,0:T(8,128)(2,1)}, bf16[112,1536]{1,0:T(8,128)(2,1)S(1)}, u32[]{:S(2)}, u32[]{:S(2)}) collective-permute-start(bf16[112,1536]{1,0:T(8,128)(2,1)} %after.12), channel_id=1, source_target_pairs={{0,2},{2,0},{1,3},{3,1},{4,6},{6,4},{5,7},{7,5},{8,10},{10,8},{9,1... | collective-permute-start | bytes 1032200 | tf_op jit(solution)/shard_map/weight_hy1/ppermute | solution.py:480
  60.4 22.3 %collective-permute-start.14 = (bf16[512,768]{1,0:T(8,128)(2,1)}, bf16[512,768]{1,0:T(8,128)(2,1)}, u32[]{:S(2)}, u32[]{:S(2)}) collective-permute-start(bf16[512,768]{1,0:T(8,128)(2,1)} %after.15.refs_4_), channel_id=1, source_target_pairs={{0,4},{4,0},{1,5},{5,1},{2,6},{6,2},{3,7},{7,3},{8,12},{12,8},{9,1... | collective-permute-start | bytes 2359304 | tf_op jit(solution)/shard_map/tok_part1/ppermute | solution.py:480
  64.7 18.7 %collective-permute-start.8 = (bf16[512,768]{1,0:T(8,128)(2,1)}, bf16[512,768]{1,0:T(8,128)(2,1)S(1)}, u32[]{:S(2)}, u32[]{:S(2)}) collective-permute-start(bf16[512,768]{1,0:T(8,128)(2,1)} %after.13.refs_0_), channel_id=1, source_target_pairs={{0,2},{2,0},{1,3},{3,1},{4,6},{6,4},{5,7},{7,5},{8,10},{10,8},{9,1... | collective-permute-start | bytes 2359304 | tf_op jit(solution)/shard_map/tok_hy1/ppermute | solution.py:480
  66.3 15.9 %collective-permute-start.10 = (bf16[128,768]{1,0:T(8,128)(2,1)S(1)}, bf16[128,768]{1,0:T(8,128)(2,1)S(1)}, u32[]{:S(2)}, u32[]{:S(2)}) collective-permute-start(bf16[128,768]{1,0:T(8,128)(2,1)S(1)} %copy-done.15), channel_id=1, source_target_pairs={{0,16},{8,24},{16,0},{24,8},{1,17},{9,25},{17,1},{25,9},{2,18},{10... | collective-permute-start | bytes 589832 | tf_op jit(solution)/shard_map/dres_sq2/ppermute | solution.py:480
  68.9 13.3 %collective-permute-start.11 = (bf16[128,768]{1,0:T(8,128)(2,1)S(1)}, bf16[128,768]{1,0:T(8,128)(2,1)S(1)}, u32[]{:S(2)}, u32[]{:S(2)}) collective-permute-start(bf16[128,768]{1,0:T(8,128)(2,1)S(1)} %copy-done.13), channel_id=1, source_target_pairs={{0,24},{8,16},{16,8},{24,0},{1,25},{9,17},{17,9},{25,1},{2,26},{10... | collective-permute-start | bytes 589832 | tf_op jit(solution)/shard_map/dres_sq3/ppermute | solution.py:480
  70.2 12.5 %collective-permute-start.9 = (bf16[128,768]{1,0:T(8,128)(2,1)S(1)}, bf16[128,768]{1,0:T(8,128)(2,1)S(1)}, u32[]{:S(2)}, u32[]{:S(2)}) collective-permute-start(bf16[128,768]{1,0:T(8,128)(2,1)S(1)} %copy-done.11), channel_id=1, source_target_pairs={{0,8},{8,0},{16,24},{24,16},{1,9},{9,1},{17,25},{25,17},{2,10},{10... | collective-permute-start | bytes 589832 | tf_op jit(solution)/shard_map/dres_sq1/ppermute | solution.py:480
  82.1 4.1 %collective-permute-start.15 = (bf16[512,768]{1,0:T(8,128)(2,1)S(1)}, bf16[512,768]{1,0:T(8,128)(2,1)}, u32[]{:S(2)}, u32[]{:S(2)}) collective-permute-start(bf16[512,768]{1,0:T(8,128)(2,1)S(1)} %copy-done.29), channel_id=1, source_target_pairs={{0,1},{1,0},{2,3},{3,2},{4,5},{5,4},{6,7},{7,6},{8,9},{9,8},{10,11... | collective-permute-start | bytes 2359304 | tf_op jit(solution)/shard_map/tok_hc1/ppermute | solution.py:480
  82.2 4.1 %collective-permute-start.12 = (bf16[512,768]{1,0:T(8,128)(2,1)}, bf16[512,768]{1,0:T(8,128)(2,1)}, u32[]{:S(2)}, u32[]{:S(2)}) collective-permute-start(bf16[512,768]{1,0:T(8,128)(2,1)} %after.13.refs_0_), channel_id=1, source_target_pairs={{0,1},{1,0},{2,3},{3,2},{4,5},{5,4},{6,7},{7,6},{8,9},{9,8},{10,11... | collective-permute-start | bytes 2359304 | tf_op jit(solution)/shard_map/tok_hc1/ppermute | solution.py:480
  82.7 5.5 %collective-permute-start.16 = (bf16[512,768]{1,0:T(8,128)(2,1)}, bf16[512,768]{1,0:T(8,128)(2,1)}, u32[]{:S(2)}, u32[]{:S(2)}) collective-permute-start(bf16[512,768]{1,0:T(8,128)(2,1)} %collective-permute-done.14.refs_5_), channel_id=1, source_target_pairs={{0,1},{1,0},{2,3},{3,2},{4,5},{5,4},{6,7},{7,6},{8,9},{9,8},{10,11... | collective-permute-start | bytes 2359304 | tf_op jit(solution)/shard_map/tok_hc1/ppermute | solution.py:480
  84.3 3.8 %collective-permute-start.13 = (bf16[512,768]{1,0:T(8,128)(2,1)}, bf16[512,768]{1,0:T(8,128)(2,1)S(1)}, u32[]{:S(2)}, u32[]{:S(2)}) collective-permute-start(bf16[512,768]{1,0:T(8,128)(2,1)} %after.14.refs_1_), channel_id=1, source_target_pairs={{0,1},{1,0},{2,3},{3,2},{4,5},{5,4},{6,7},{7,6},{8,9},{9,8},{10,11... | collective-permute-start | bytes 2359304 | tf_op jit(solution)/shard_map/tok_hc1/ppermute | solution.py:480
  84.7 29.2 %collective-permute-start.20 = (bf16[384,1536]{1,0:T(8,128)(2,1)}, bf16[384,1536]{1,0:T(8,128)(2,1)S(1)}, u32[]{:S(2)}, u32[]{:S(2)}) collective-permute-start(bf16[384,1536]{1,0:T(8,128)(2,1)} %collective-permute-done.3.refs_6_.refs_7_), channel_id=1, source_target_pairs={{0,4},{4,0},{1,5},{5,1},{2,6},{6,2},{3,7},{7,3},{8,12},{12,8},{9,1... | collective-permute-start | bytes 3538952 | tf_op jit(solution)/shard_map/weight_part1/ppermute | solution.py:480
  113.4 1.6 collective-permute-start.17
  113.6 17.3 %collective-permute-start.22 = (bf16[384,1536]{1,0:T(8,128)(2,1)}, bf16[384,1536]{1,0:T(8,128)(2,1)}, u32[]{:S(2)}, u32[]{:S(2)}) collective-permute-start(bf16[384,1536]{1,0:T(8,128)(2,1)} %collective-permute-done.3.refs_6_.refs_7_), channel_id=1, source_target_pairs={{0,1},{1,0},{2,3},{3,2},{4,5},{5,4},{6,7},{7,6},{8,9},{9,8},{10,11... | collective-permute-start | bytes 3538952 | tf_op jit(solution)/shard_map/weight_hc1/ppermute | solution.py:480
  115.7 16.0 %collective-permute-start.23 = (bf16[384,1536]{1,0:T(8,128)(2,1)}, bf16[384,1536]{1,0:T(8,128)(2,1)S(1)}, u32[]{:S(2)}, u32[]{:S(2)}) collective-permute-start(bf16[384,1536]{1,0:T(8,128)(2,1)} %after.16.refs_8_), channel_id=1, source_target_pairs={{0,1},{1,0},{2,3},{3,2},{4,5},{5,4},{6,7},{7,6},{8,9},{9,8},{10,11... | collective-permute-start | bytes 3538952 | tf_op jit(solution)/shard_map/weight_hc1/ppermute | solution.py:480
  115.8 14.2 %collective-permute-start.18 = (bf16[1024,192]{1,0:T(8,128)(2,1)S(1)}, bf16[1024,192]{1,0:T(8,128)(2,1)S(1)}, u32[]{:S(2)}, u32[]{:S(2)}) collective-permute-start(bf16[1024,192]{1,0:T(8,128)(2,1)S(1)} %copy-done.76), channel_id=1, source_target_pairs={{0,2},{2,0},{1,3},{3,1},{4,6},{6,4},{5,7},{7,5},{8,10},{10,8},{9,1... | collective-permute-start | bytes 1179656 | tf_op jit(solution)/shard_map/attn_hy1/ppermute | solution.py:480
  116.2 14.7 %collective-permute-start.21 = (bf16[112,1536]{1,0:T(8,128)(2,1)S(1)}, bf16[112,1536]{1,0:T(8,128)(2,1)S(1)}, u32[]{:S(2)}, u32[]{:S(2)}) collective-permute-start(bf16[112,1536]{1,0:T(8,128)(2,1)S(1)} %copy-done.45), channel_id=1, source_target_pairs={{0,1},{1,0},{2,3},{3,2},{4,5},{5,4},{6,7},{7,6},{8,9},{9,8},{10,11... | collective-permute-start | bytes 1032200 | tf_op jit(solution)/shard_map/weight_hc1/ppermute | solution.py:480
  130.0 1.6 collective-permute-start.19
  170.6 16.9 %collective-permute-start.30 = (bf16[20,96,1536]{2,1,0:T(8,128)(2,1)}, bf16[20,96,1536]{2,1,0:T(8,128)(2,1)}, u32[]{:S(2)}, u32[]{:S(2)}) collective-permute-start(bf16[20,96,1536]{2,1,0:T(8,128)(2,1)} %far_grad.1), channel_id=1, source_target_pairs={{0,1},{1,0},{2,3},{3,2},{4,5},{5,4},{6,7},{7,6},{8,9},{9,8},{10,11... | collective-permute-start | bytes 17694728 | tf_op jit(solution)/shard_map/wide_hc1/ppermute | solution.py:480
  170.8 14.2 %collective-permute-start.28 = (bf16[2,512,192]{2,1,0:T(8,128)(2,1)S(1)}, bf16[2,512,192]{2,1,0:T(8,128)(2,1)S(1)}, u32[]{:S(2)}, u32[]{:S(2)}) collective-permute-start(bf16[2,512,192]{2,1,0:T(8,128)(2,1)S(1)} %copy-done.77), channel_id=1, source_target_pairs={{0,2},{2,0},{1,3},{3,1},{4,6},{6,4},{5,7},{7,5},{8,10},{10,8},{9,1... | collective-permute-start | bytes 1179656 | tf_op jit(solution)/shard_map/dattn_hy1/ppermute | solution.py:480
  171.2 16.2 %collective-permute-start.27 = (bf16[512,192]{1,0:T(8,128)(2,1)S(1)}, bf16[512,192]{1,0:T(8,128)(2,1)S(1)}, u32[]{:S(2)}, u32[]{:S(2)}) collective-permute-start(bf16[512,192]{1,0:T(8,128)(2,1)S(1)} %copy-done.83), channel_id=1, source_target_pairs={{0,1},{1,0},{2,3},{3,2},{4,5},{5,4},{6,7},{7,6},{8,9},{9,8},{10,11... | collective-permute-start | bytes 589832 | tf_op jit(solution)/shard_map/dattn_hc1/ppermute | solution.py:480
  171.2 28.2 %collective-permute-start.24 = (bf16[128,768]{1,0:T(8,128)(2,1)S(1)}, bf16[128,768]{1,0:T(8,128)(2,1)S(1)}, u32[]{:S(2)}, u32[]{:S(2)}) collective-permute-start(bf16[128,768]{1,0:T(8,128)(2,1)S(1)} %copy-done.86), channel_id=1, source_target_pairs={{0,8},{8,0},{16,24},{24,16},{1,9},{9,1},{17,25},{25,17},{2,10},{10... | collective-permute-start | bytes 589832 | tf_op jit(solution)/shard_map/result_sq1/ppermute | solution.py:480
  174.0 25.4 %collective-permute-start.25 = (bf16[128,768]{1,0:T(8,128)(2,1)S(1)}, bf16[128,768]{1,0:T(8,128)(2,1)S(1)}, u32[]{:S(2)}, u32[]{:S(2)}) collective-permute-start(bf16[128,768]{1,0:T(8,128)(2,1)S(1)} %copy-done.85), channel_id=1, source_target_pairs={{0,16},{8,24},{16,0},{24,8},{1,17},{9,25},{17,1},{25,9},{2,18},{10... | collective-permute-start | bytes 589832 | tf_op jit(solution)/shard_map/result_sq2/ppermute | solution.py:480
  185.0 17.0 %collective-permute-start.26 = (bf16[128,768]{1,0:T(8,128)(2,1)S(1)}, bf16[128,768]{1,0:T(8,128)(2,1)S(1)}, u32[]{:S(2)}, u32[]{:S(2)}) collective-permute-start(bf16[128,768]{1,0:T(8,128)(2,1)S(1)} %copy-done.84), channel_id=1, source_target_pairs={{0,24},{8,16},{16,8},{24,0},{1,25},{9,17},{17,9},{25,1},{2,26},{10... | collective-permute-start | bytes 589832 | tf_op jit(solution)/shard_map/result_sq3/ppermute | solution.py:480
  187.4 16.1 %collective-permute-start.29 = (bf16[512,192]{1,0:T(8,128)(2,1)S(1)}, bf16[512,192]{1,0:T(8,128)(2,1)S(1)}, u32[]{:S(2)}, u32[]{:S(2)}) collective-permute-start(bf16[512,192]{1,0:T(8,128)(2,1)S(1)} %slice_bitcast_fusion), channel_id=1, source_target_pairs={{0,1},{1,0},{2,3},{3,2},{4,5},{5,4},{6,7},{7,6},{8,9},{9,8},{10,11... | collective-permute-start | bytes 589832 | tf_op jit(solution)/shard_map/dattn_hc1/ppermute | solution.py:480
  196.7 41.2 %collective-permute-start.33 = (bf16[96,1536]{1,0:T(8,128)(2,1)}, bf16[96,1536]{1,0:T(8,128)(2,1)S(1)}, u32[]{:S(2)}, u32[]{:S(2)}) collective-permute-start(bf16[96,1536]{1,0:T(8,128)(2,1)} %get-tuple-element.120.refs_15_), channel_id=1, source_target_pairs={{0,8},{8,0},{16,24},{24,16},{1,9},{9,1},{17,25},{25,17},{2,10},{10... | collective-permute-start | bytes 884744 | tf_op jit(solution)/shard_map/wide_sq1/ppermute | solution.py:480
  199.5 38.5 %collective-permute-start.34 = (bf16[96,1536]{1,0:T(8,128)(2,1)}, bf16[96,1536]{1,0:T(8,128)(2,1)S(1)}, u32[]{:S(2)}, u32[]{:S(2)}) collective-permute-start(bf16[96,1536]{1,0:T(8,128)(2,1)} %get-tuple-element.119.refs_14_), channel_id=1, source_target_pairs={{0,16},{8,24},{16,0},{24,8},{1,17},{9,25},{17,1},{25,9},{2,18},{10... | collective-permute-start | bytes 884744 | tf_op jit(solution)/shard_map/wide_sq2/ppermute | solution.py:480
  200.1 37.8 %collective-permute-start.35 = (bf16[96,1536]{1,0:T(8,128)(2,1)}, bf16[96,1536]{1,0:T(8,128)(2,1)S(1)}, u32[]{:S(2)}, u32[]{:S(2)}) collective-permute-start(bf16[96,1536]{1,0:T(8,128)(2,1)} %get-tuple-element.121.refs_16_), channel_id=1, source_target_pairs={{0,24},{8,16},{16,8},{24,0},{1,25},{9,17},{17,9},{25,1},{2,26},{10... | collective-permute-start | bytes 884744 | tf_op jit(solution)/shard_map/wide_sq3/ppermute | solution.py:480
  202.7 35.3 %collective-permute-start.31 = (bf16[496,1536]{1,0:T(8,128)(2,1)}, bf16[496,1536]{1,0:T(8,128)(2,1)S(1)}, u32[]{:S(2)}, u32[]{:S(2)}) collective-permute-start(bf16[496,1536]{1,0:T(8,128)(2,1)} %get-tuple-element.116.refs_11_), channel_id=1, source_target_pairs={{0,2},{2,0},{1,3},{3,1},{4,6},{6,4},{5,7},{7,5},{8,10},{10,8},{9,1... | collective-permute-start | bytes 4571144 | tf_op jit(solution)/shard_map/wide_hy1/ppermute | solution.py:480
  204.2 33.8 %collective-permute-start.32 = (bf16[4,96,1536]{2,1,0:T(8,128)(2,1)}, bf16[4,96,1536]{2,1,0:T(8,128)(2,1)S(1)}, u32[]{:S(2)}, u32[]{:S(2)}) collective-permute-start(bf16[4,96,1536]{2,1,0:T(8,128)(2,1)} %get-tuple-element.117.refs_12_), channel_id=1, source_target_pairs={{0,4},{4,0},{1,5},{5,1},{2,6},{6,2},{3,7},{7,3},{8,12},{12,8},{9,1... | collective-permute-start | bytes 3538952 | tf_op jit(solution)/shard_map/wide_part1/ppermute | solution.py:480
  239.8 20.3 %collective-permute-start.36 = (bf16[2,1024,768]{2,1,0:T(8,128)(2,1)}, bf16[2,1024,768]{2,1,0:T(8,128)(2,1)S(1)}, u32[]{:S(2)}, u32[]{:S(2)}) collective-permute-start(bf16[2,1024,768]{2,1,0:T(8,128)(2,1)} %after.17), channel_id=1, source_target_pairs={{0,1},{1,0},{2,3},{3,2},{4,5},{5,4},{6,7},{7,6},{8,9},{9,8},{10,11... | collective-permute-start | bytes 9437192 | tf_op jit(solution)/shard_map/dtok_hc1/ppermute | solution.py:480
  257.5 18.5 %collective-permute-start.39 = (bf16[4,96,896]{2,1,0:T(8,128)(2,1)}, bf16[4,96,896]{2,1,0:T(8,128)(2,1)}, u32[]{:S(2)}, u32[]{:S(2)}) collective-permute-start(bf16[4,96,896]{2,1,0:T(8,128)(2,1)} %get-tuple-element.131), channel_id=1, source_target_pairs={{0,4},{4,0},{1,5},{5,1},{2,6},{6,2},{3,7},{7,3},{8,12},{12,8},{9,1... | collective-permute-start | bytes 2064392 | tf_op jit(solution)/shard_map/tail_part1/ppermute | solution.py:480
  257.8 25.0 %collective-permute-start.54 = (bf16[96,1536]{1,0:T(8,128)(2,1)S(1)}, bf16[96,1536]{1,0:T(8,128)(2,1)S(1)}, u32[]{:S(2)}, u32[]{:S(2)}) collective-permute-start(bf16[96,1536]{1,0:T(8,128)(2,1)S(1)} %copy-done.50), channel_id=1, source_target_pairs={{0,6},{2,4},{4,2},{6,0},{1,7},{3,5},{5,3},{7,1},{8,14},{10,12},{12... | collective-permute-start | bytes 884744 | tf_op jit(solution)/shard_map/across_both/ppermute | solution.py:497
  264.7 39.7 %collective-permute-start.37 = (bf16[512,768]{1,0:T(8,128)(2,1)}, bf16[512,768]{1,0:T(8,128)(2,1)S(1)}, u32[]{:S(2)}, u32[]{:S(2)}) collective-permute-start(bf16[512,768]{1,0:T(8,128)(2,1)} %get-tuple-element.129.refs_0_), channel_id=1, source_target_pairs={{0,2},{2,0},{1,3},{3,1},{4,6},{6,4},{5,7},{7,5},{8,10},{10,8},{9,1... | collective-permute-start | bytes 2359304 | tf_op jit(solution)/shard_map/dtok_hy1/ppermute | solution.py:480
  265.7 39.3 %collective-permute-start.38 = (bf16[512,768]{1,0:T(8,128)(2,1)}, bf16[512,768]{1,0:T(8,128)(2,1)S(1)}, u32[]{:S(2)}, u32[]{:S(2)}) collective-permute-start(bf16[512,768]{1,0:T(8,128)(2,1)} %get-tuple-element.130.refs_1_), channel_id=1, source_target_pairs={{0,4},{4,0},{1,5},{5,1},{2,6},{6,2},{3,7},{7,3},{8,12},{12,8},{9,1... | collective-permute-start | bytes 2359304 | tf_op jit(solution)/shard_map/dtok_part1/ppermute | solution.py:480
  278.3 9.7 %collective-permute-start.40 = (bf16[2,96,896]{2,1,0:T(8,128)(2,1)}, bf16[2,96,896]{2,1,0:T(8,128)(2,1)S(1)}, u32[]{:S(2)}, u32[]{:S(2)}) collective-permute-start(bf16[2,96,896]{2,1,0:T(8,128)(2,1)} %get-tuple-element.133), channel_id=1, source_target_pairs={{0,8},{8,0},{16,24},{24,16},{1,9},{9,1},{17,25},{25,17},{2,10},{10... | collective-permute-start | bytes 1032200 | tf_op jit(solution)/shard_map/tail_sq1/ppermute | solution.py:480
  285.5 15.9 %collective-permute-start.56 = (bf16[96,1536]{1,0:T(8,128)(2,1)}, bf16[96,1536]{1,0:T(8,128)(2,1)S(1)}, u32[]{:S(2)}, u32[]{:S(2)}) collective-permute-start(bf16[96,1536]{1,0:T(8,128)(2,1)} %wide_end.1.refs_0_), channel_id=1, source_target_pairs={{0,16},{8,24},{16,0},{24,8},{1,17},{9,25},{17,1},{25,9},{2,18},{10... | collective-permute-start | bytes 884744 | tf_op jit(solution)/shard_map/wide_sq2/ppermute | solution.py:480
  286.5 15.7 %collective-permute-start.55 = (bf16[96,1536]{1,0:T(8,128)(2,1)}, bf16[96,1536]{1,0:T(8,128)(2,1)S(1)}, u32[]{:S(2)}, u32[]{:S(2)}) collective-permute-start(bf16[96,1536]{1,0:T(8,128)(2,1)} %wide_end.1.refs_0_), channel_id=1, source_target_pairs={{0,8},{8,0},{16,24},{24,16},{1,9},{9,1},{17,25},{25,17},{2,10},{10... | collective-permute-start | bytes 884744 | tf_op jit(solution)/shard_map/wide_sq1/ppermute | solution.py:480
  287.9 21.4 %collective-permute-start.58 = (bf16[96,1536]{1,0:T(8,128)(2,1)}, bf16[96,1536]{1,0:T(8,128)(2,1)S(1)}, u32[]{:S(2)}, u32[]{:S(2)}) collective-permute-start(bf16[96,1536]{1,0:T(8,128)(2,1)} %wide_end.1.refs_0_), channel_id=1, source_target_pairs={{0,4},{4,0},{1,5},{5,1},{2,6},{6,2},{3,7},{7,3},{8,12},{12,8},{9,1... | collective-permute-start | bytes 884744 | tf_op jit(solution)/shard_map/wide_part1/ppermute | solution.py:480
  302.1 13.0 %collective-permute-start.57 = (bf16[96,1536]{1,0:T(8,128)(2,1)}, bf16[96,1536]{1,0:T(8,128)(2,1)S(1)}, u32[]{:S(2)}, u32[]{:S(2)}) collective-permute-start(bf16[96,1536]{1,0:T(8,128)(2,1)} %after.19.refs_2_), channel_id=1, source_target_pairs={{0,8},{8,0},{16,24},{24,16},{1,9},{9,1},{17,25},{25,17},{2,10},{10... | collective-permute-start | bytes 884744 | tf_op jit(solution)/shard_map/wide_sq1/ppermute | solution.py:480
  302.1 10.5 %collective-permute-start.43 = (bf16[1,96,896]{2,1,0:T(8,128)(2,1)}, bf16[1,96,896]{2,1,0:T(8,128)(2,1)}, u32[]{:S(2)}, u32[]{:S(2)}) collective-permute-start(bf16[1,96,896]{2,1,0:T(8,128)(2,1)} %get-tuple-element.134.refs_0_.refs_1_), channel_id=1, source_target_pairs={{0,16},{8,24},{16,0},{24,8},{1,17},{9,25},{17,1},{25,9},{2,18},{10... | collective-permute-start | bytes 516104 | tf_op jit(solution)/shard_map/tail_sq2/ppermute | solution.py:480
  304.4 14.0 %collective-permute-start.60 = (bf16[96,1536]{1,0:T(8,128)(2,1)}, bf16[96,1536]{1,0:T(8,128)(2,1)S(1)}, u32[]{:S(2)}, u32[]{:S(2)}) collective-permute-start(bf16[96,1536]{1,0:T(8,128)(2,1)} %after.19.refs_2_), channel_id=1, source_target_pairs={{0,4},{4,0},{1,5},{5,1},{2,6},{6,2},{3,7},{7,3},{8,12},{12,8},{9,1... | collective-permute-start | bytes 884744 | tf_op jit(solution)/shard_map/wide_part1/ppermute | solution.py:480
  305.0 21.1 %collective-permute-start.59 = (bf16[96,1536]{1,0:T(8,128)(2,1)}, bf16[96,1536]{1,0:T(8,128)(2,1)S(1)}, u32[]{:S(2)}, u32[]{:S(2)}) collective-permute-start(bf16[96,1536]{1,0:T(8,128)(2,1)} %after.18.refs_1_), channel_id=1, source_target_pairs={{0,4},{4,0},{1,5},{5,1},{2,6},{6,2},{3,7},{7,3},{8,12},{12,8},{9,1... | collective-permute-start | bytes 884744 | tf_op jit(solution)/shard_map/wide_part1/ppermute | solution.py:480
  309.3 22.4 %collective-permute-start.41 = (bf16[256,768]{1,0:T(8,128)(2,1)}, bf16[256,768]{1,0:T(8,128)(2,1)S(1)}, u32[]{:S(2)}, u32[]{:S(2)}) collective-permute-start(bf16[256,768]{1,0:T(8,128)(2,1)} %get-tuple-element.135.refs_0_), channel_id=1, source_target_pairs={{0,4},{4,0},{1,5},{5,1},{2,6},{6,2},{3,7},{7,3},{8,12},{12,8},{9,1... | collective-permute-start | bytes 1179656 | tf_op jit(solution)/shard_map/dtok_part1/ppermute | solution.py:480
  312.6 20.9 %collective-permute-start.42 = (bf16[256,768]{1,0:T(8,128)(2,1)}, bf16[256,768]{1,0:T(8,128)(2,1)S(1)}, u32[]{:S(2)}, u32[]{:S(2)}) collective-permute-start(bf16[256,768]{1,0:T(8,128)(2,1)} %get-tuple-element.136.refs_1_), channel_id=1, source_target_pairs={{0,2},{2,0},{1,3},{3,1},{4,6},{6,4},{5,7},{7,5},{8,10},{10,8},{9,1... | collective-permute-start | bytes 1179656 | tf_op jit(solution)/shard_map/dtok_hy1/ppermute | solution.py:480
  315.1 11.0 %collective-permute-start.48 = (bf16[1,96,896]{2,1,0:T(8,128)(2,1)}, bf16[1,96,896]{2,1,0:T(8,128)(2,1)S(1)}, u32[]{:S(2)}, u32[]{:S(2)}) collective-permute-start(bf16[1,96,896]{2,1,0:T(8,128)(2,1)} %tail_end.1.refs_0_), channel_id=1, source_target_pairs={{0,16},{8,24},{16,0},{24,8},{1,17},{9,25},{17,1},{25,9},{2,18},{10... | collective-permute-start | bytes 516104 | tf_op jit(solution)/shard_map/tail_sq2/ppermute | solution.py:480
  318.5 8.4 %collective-permute-start.47 = (bf16[1,96,896]{2,1,0:T(8,128)(2,1)}, bf16[1,96,896]{2,1,0:T(8,128)(2,1)}, u32[]{:S(2)}, u32[]{:S(2)}) collective-permute-start(bf16[1,96,896]{2,1,0:T(8,128)(2,1)} %tail_end.1.refs_0_), channel_id=1, source_target_pairs={{0,8},{8,0},{16,24},{24,16},{1,9},{9,1},{17,25},{25,17},{2,10},{10... | collective-permute-start | bytes 516104 | tf_op jit(solution)/shard_map/tail_sq1/ppermute | solution.py:480
  326.0 5.5 %collective-permute-start.49 = (bf16[1,96,896]{2,1,0:T(8,128)(2,1)S(1)}, bf16[1,96,896]{2,1,0:T(8,128)(2,1)}, u32[]{:S(2)}, u32[]{:S(2)}) collective-permute-start(bf16[1,96,896]{2,1,0:T(8,128)(2,1)S(1)} %collective-permute-done.48.refs_2_), channel_id=1, source_target_pairs={{0,8},{8,0},{16,24},{24,16},{1,9},{9,1},{17,25},{25,17},{2,10},{10... | collective-permute-start | bytes 516104 | tf_op jit(solution)/shard_map/tail_sq1/ppermute | solution.py:480
  326.1 12.2 %collective-permute-start.61 = (bf16[96,1536]{1,0:T(8,128)(2,1)S(1)}, bf16[96,1536]{1,0:T(8,128)(2,1)S(1)}, u32[]{:S(2)}, u32[]{:S(2)}) collective-permute-start(bf16[96,1536]{1,0:T(8,128)(2,1)S(1)} %collective-permute-done.57.refs_3_), channel_id=1, source_target_pairs={{0,4},{4,0},{1,5},{5,1},{2,6},{6,2},{3,7},{7,3},{8,12},{12,8},{9,1... | collective-permute-start | bytes 884744 | tf_op jit(solution)/shard_map/wide_part1/ppermute | solution.py:480
  326.8 16.9 %collective-permute-start.50 = (bf16[1,96,896]{2,1,0:T(8,128)(2,1)}, bf16[1,96,896]{2,1,0:T(8,128)(2,1)}, u32[]{:S(2)}, u32[]{:S(2)}) collective-permute-start(bf16[1,96,896]{2,1,0:T(8,128)(2,1)} %tail_end.1.refs_0_), channel_id=1, source_target_pairs={{0,4},{4,0},{1,5},{5,1},{2,6},{6,2},{3,7},{7,3},{8,12},{12,8},{9,1... | collective-permute-start | bytes 516104 | tf_op jit(solution)/shard_map/tail_part1/ppermute | solution.py:480
  331.6 17.4 %collective-permute-start.52 = (bf16[1,96,896]{2,1,0:T(8,128)(2,1)S(1)}, bf16[1,96,896]{2,1,0:T(8,128)(2,1)}, u32[]{:S(2)}, u32[]{:S(2)}) collective-permute-start(bf16[1,96,896]{2,1,0:T(8,128)(2,1)S(1)} %collective-permute-done.48.refs_2_), channel_id=1, source_target_pairs={{0,4},{4,0},{1,5},{5,1},{2,6},{6,2},{3,7},{7,3},{8,12},{12,8},{9,1... | collective-permute-start | bytes 516104 | tf_op jit(solution)/shard_map/tail_part1/ppermute | solution.py:480
  331.7 15.2 %collective-permute-start.51 = (bf16[1,96,896]{2,1,0:T(8,128)(2,1)}, bf16[1,96,896]{2,1,0:T(8,128)(2,1)}, u32[]{:S(2)}, u32[]{:S(2)}) collective-permute-start(bf16[1,96,896]{2,1,0:T(8,128)(2,1)} %collective-permute-done.47.refs_1_), channel_id=1, source_target_pairs={{0,4},{4,0},{1,5},{5,1},{2,6},{6,2},{3,7},{7,3},{8,12},{12,8},{9,1... | collective-permute-start | bytes 516104 | tf_op jit(solution)/shard_map/tail_part1/ppermute | solution.py:480
  333.6 15.4 %collective-permute-start.53 = (bf16[1,96,896]{2,1,0:T(8,128)(2,1)}, bf16[1,96,896]{2,1,0:T(8,128)(2,1)}, u32[]{:S(2)}, u32[]{:S(2)}) collective-permute-start(bf16[1,96,896]{2,1,0:T(8,128)(2,1)} %collective-permute-done.49.refs_3_), channel_id=1, source_target_pairs={{0,4},{4,0},{1,5},{5,1},{2,6},{6,2},{3,7},{7,3},{8,12},{12,8},{9,1... | collective-permute-start | bytes 516104 | tf_op jit(solution)/shard_map/tail_part1/ppermute | solution.py:480
  338.3 19.3 %collective-permute-start.44 = (bf16[128,768]{1,0:T(8,128)(2,1)}, bf16[128,768]{1,0:T(8,128)(2,1)S(1)}, u32[]{:S(2)}, u32[]{:S(2)}) collective-permute-start(bf16[128,768]{1,0:T(8,128)(2,1)} %get-tuple-element.140.refs_9_), channel_id=1, source_target_pairs={{0,8},{8,0},{16,24},{24,16},{1,9},{9,1},{17,25},{25,17},{2,10},{10... | collective-permute-start | bytes 589832 | tf_op jit(solution)/shard_map/dtok_sq1/ppermute | solution.py:480
  343.8 14.5 %collective-permute-start.45 = (bf16[128,768]{1,0:T(8,128)(2,1)S(1)}, bf16[128,768]{1,0:T(8,128)(2,1)S(1)}, u32[]{:S(2)}, u32[]{:S(2)}) collective-permute-start(bf16[128,768]{1,0:T(8,128)(2,1)S(1)} %copy-done.64), channel_id=1, source_target_pairs={{0,16},{8,24},{16,0},{24,8},{1,17},{9,25},{17,1},{25,9},{2,18},{10... | collective-permute-start | bytes 589832 | tf_op jit(solution)/shard_map/dtok_sq2/ppermute | solution.py:480
  347.0 11.3 %collective-permute-start.46 = (bf16[128,768]{1,0:T(8,128)(2,1)S(1)}, bf16[128,768]{1,0:T(8,128)(2,1)S(1)}, u32[]{:S(2)}, u32[]{:S(2)}) collective-permute-start(bf16[128,768]{1,0:T(8,128)(2,1)S(1)} %copy-done.63), channel_id=1, source_target_pairs={{0,24},{8,16},{16,8},{24,0},{1,25},{9,17},{17,9},{25,1},{2,26},{10... | collective-permute-start | bytes 589832 | tf_op jit(solution)/shard_map/dtok_sq3/ppermute | solution.py:480
  (86 other events, 549.0 us)
Sparse Core Ops, SparseCore 0:
  246.0 27.7 reduce-scatter.1

commit v5 on v4

--- a/solution.py
+++ b/solution.py
@@ -1866,7 +1866,7 @@
     wide += [swap(a, "part", name="wide") for a in wide]
     own = tail_end(own, swap(send, "sq", 2, name="tail"), [*sent_two])
     even_got2, odd_got2 = swap(sent_two[0], "part", name="dtok"), swap(sent_two[1], "hy", name="dtok")
-    back_sent = row_sum_three(dx, dx_got, even_got, odd_got, even_got2, odd_got2, d_one, [own])
+    back_sent = row_sum_three(dx, dx_got, even_got, odd_got, even_got2, odd_got2, d_one, [])
     back = [back_sent[0]] + [swap(back_sent[k], "sq", k, name="dtok") for k in range(1, 4)]
 
     beyond = swap(own, "sq", 2, name="tail")

time: 375 us -> 375 us (level)
  transfers between devices with their start and end apart: 63 -> 63, of which waited for: 20 -> 21; matrix products, arithmetic and copies ran while one was open for 6% -> 6% of each run, Pallas kernels for 31% -> 31%
where the time goes in v5:
time: 375 us; the launch traced here: 369 us
  Pallas kernels  155 us (41%)
  waiting for transfers between devices  86.3 us (23%)
  starting transfers between devices  62 us (17%)
  local copies, waits for them, and re-layouts  38.7 us (10%)
  between operations  15.2 us (4%)
  other arithmetic  11.7 us (3%)
    ppermute x61, waiting for transfers between devices, swap(): return lax.ppermute(value, axis, [(i, i ^ step) for i in range(size)])  82.2 us
    ppermute x61, starting transfers between devices, swap(): return lax.ppermute(value, axis, [(i, i ^ step) for i in range(size)])  59.7 us
    pallas_call x1, Pallas kernels, attend_back(): pl.pallas_call(functools.partial(attend_back_kernel, heads, hd, span, len...  32.2 us
    pallas_call x1, Pallas kernels, rows_work(): pl.pallas_call(functools.partial(rows_kernel, width, cols, first_rows), g...  29.6 us
    unnamed x178, local copies, waits for them, and re-layouts  28.3 us
    pallas_call x1, Pallas kernels, project_and_attend(): pl.pallas_call(functools.partial(project_and_attend_kernel, heads, hd, sp...  23.2 us
    pallas_call x2, Pallas kernels, rows_grad(): pl.pallas_call(functools.partial(rows_grad_kernel, kc, len(orders)), out_...  16.2 us
    pallas_call x1, Pallas kernels, qkv_grad(): pl.pallas_call(functools.partial(qkv_grad_kernel, span), out_shape=(jax.S...  11.1 us
  transfers between devices with their start and end apart: 63, of which 21 were waited for; matrix products, arithmetic and copies ran while one was open for 6% of the time, Pallas kernels for 31%

profile of v5, /device:TPU:0, one launch (start us, length us, event | category | flops | bytes accessed | tf_op | source)
XLA Modules:
  0.0 369.0 jit_solution(2695510320385935342)
XLA Ops:
  11.7 3.0 pack.1
  15.9 2.5 collective-permute-start.3
  18.5 3.3 split.2
  21.8 1.6 collective-permute-start.1
  23.4 2.5 collective-permute-start.2
  26.0 4.2 %copy.53.w_ref = bf16[768,3,3,64]{3,2,1,0:T(4,128)(2,1)S(1)} copy(bf16[768,3,3,64]{0,3,2,1:T(8,128)(2,1)} %param.17) | data formatting | bytes 1769472 | tf_op args[1]
  30.2 3.3 split.3
  36.2 2.9 qkv_weights.1
  40.8 2.0 pad_maximum_fusion.5.refs_0_
  45.4 1.8 collective-permute-start.6
  47.2 1.7 pad_maximum_fusion.4.refs_0_
  48.9 1.5 collective-permute-start.5
  51.3 6.4 %collective-permute-done.6.refs_1_ = bf16[256,768]{1,0:T(8,128)(2,1)S(1)} collective-permute-done((bf16[256,768]{1,0:T(8,128)(2,1)}, bf16[256,768]{1,0:T(8,128)(2,1)S(1)}, u32[]{:S(2)}, u32[]{:S(2)}) %collective-permute-start.6) | collective-permute-done | bytes 393248 | tf_op jit(solution)/shard_map/tok_hy1/ppermute | solution.py:480
  60.4 1.6 collective-permute-start.14
  61.9 1.9 pad_maximum_fusion.refs_0_
  64.7 1.5 collective-permute-start.8
  66.3 2.6 collective-permute-start.10
  73.1 9.0 %collective-permute-done.10.refs_4_.refs_16_ = bf16[128,768]{1,0:T(8,128)(2,1)S(1)} collective-permute-done((bf16[128,768]{1,0:T(8,128)(2,1)S(1)}, bf16[128,768]{1,0:T(8,128)(2,1)S(1)}, u32[]{:S(2)}, u32[]{:S(2)}) %collective-permute-start.10) | collective-permute-done | bytes 196640 | tf_op jit(solution)/shard_map/dres_sq2/ppermute | solution.py:480
  84.7 1.5 collective-permute-start.20
  86.2 1.9 collective-permute-done.16.refs_7_
  89.0 23.2 %project_and_attend.1 = (bf16[1024,192]{1,0:T(8,128)(2,1)}, bf16[1024,192]{1,0:T(8,128)(2,1)}, f32[2048,128]{1,0:T(8,128)}, bf16[4096,384]{1,0:T(8,128)(2,1)}, bf16[2048,384]{1,0:T(8,128)(2,1)}) custom-call(s32[4]{0:T(128)} %copy-done.18, s32[576]{0:T(1024)} %reshape.65.refs_2_.rand_ref, bf16[512,768]{1,0:T(8,128)(2,1)} %after.13.refs_0_, ...), custom_call_target="tpu_custom_call" | custom-call | flops 42949672960 | bytes 16777216 | tf_op jit(solution)/shard_map/project_and_attend/pallas_call | solution.py:736
  116.3 13.7 %collective-permute-done.18.refs_2_.refs_6_ = bf16[1024,192]{1,0:T(8,128)(2,1)S(1)} collective-permute-done((bf16[1024,192]{1,0:T(8,128)(2,1)S(1)}, bf16[1024,192]{1,0:T(8,128)(2,1)S(1)}, u32[]{:S(2)}, u32[]{:S(2)}) %collective-permute-start.18) | collective-permute-done | bytes 393248 | tf_op jit(solution)/shard_map/attn_hy1/ppermute | solution.py:480
  133.3 29.6 %rows_work.1 = (bf16[128,768]{1,0:T(8,128)(2,1)}, bf16[128,768]{1,0:T(8,128)(2,1)}, bf16[128,768]{1,0:T(8,128)(2,1)}, bf16[128,768]{1,0:T(8,128)(2,1)}, f32[512,...) custom-call(bf16[1024,192]{1,0:T(8,128)(2,1)} %get-tuple-element.96., ...), custom_call_target="tpu_custom_call" | custom-call | flops 53687091200 | bytes 31457280 | tf_op jit(solution)/shard_map/rows_work/pallas_call | solution.py:1414
  163.0 7.6 %far_grad.1 = bf16[20,96,1536]{2,1,0:T(8,128)(2,1)} custom-call(bf16[512,768]{1,0:T(8,128)(2,1)} %get-tuple-element.109.refs_0_, bf16[512,3072]{1,0:T(8,128)(2,1)} %get-tuple-element.110.refs_1_, bf16[512,3072]{1,0:T(8,128)(2,1)} %get-tuple-element.111.refs_2_, bf16[512,768]{1,0:T(8,128)(2,1)} %get-tuple-element.112.refs_3_, ...), custom_call_target="tpu_custom_call" | custom-call | flops 8589934592 | bytes 16777216 | tf_op jit(solution)/shard_map/far_grad/pallas_call | solution.py:1571
  171.2 2.8 collective-permute-start.24
  174.0 1.9 collective-permute-start.25
  175.9 9.0 %collective-permute-done.28.refs_10_.refs_2_ = bf16[2,512,192]{2,1,0:T(8,128)(2,1)S(1)} collective-permute-done((bf16[2,512,192]{2,1,0:T(8,128)(2,1)S(1)}, bf16[2,512,192]{2,1,0:T(8,128)(2,1)S(1)}, u32[]{:S(2)}, u32[]{:S(2)}) %collective-permute-start.28) | collective-permute-done | bytes 393248 | tf_op jit(solution)/shard_map/dattn_hy1/ppermute | solution.py:480
  185.0 2.4 collective-permute-start.26
  188.1 8.6 %near_grad.1 = (bf16[5,96,1536]{2,1,0:T(8,128)(2,1)}, bf16[496,1536]{1,0:T(8,128)(2,1)}, bf16[4,96,1536]{2,1,0:T(8,128)(2,1)}, bf16[96,1536]{1,0:T(8,128)(2,1)},...) custom-call(bf16[512,768]{1,0:T(8,128)(2,1)} %get-tuple-element.109.refs_0_, ...), custom_call_target="tpu_custom_call" | custom-call | flops 8589934592 | bytes 16777216 | tf_op jit(solution)/shard_map/near_grad/pallas_call | solution.py:1571
  196.7 2.7 collective-permute-start.33
  200.1 1.9 collective-permute-start.35
  204.2 1.5 collective-permute-start.32
  205.6 32.2 %attend_back.1 = (bf16[2048,192]{1,0:T(8,128)(2,1)}, bf16[4096,384]{1,0:T(8,128)(2,1)}, bf16[2,1024,768]{2,1,0:T(8,128)(2,1)}, bf16[2,1024,768]{2,1,0:T(8,128)(2,1)}) custom-call(s32[4]{0:T(128)} %copy-done.18, s32[576]{0:T(1024)} %reshape.65.refs_2_.rand_ref, bf16[2048,384]{1,0:T(8,128)(2,1)} %get-tuple-element.102.q_from, ...), custom_call_target="tpu_custom_call" | custom-call | flops 64424509440 | bytes 25165824 | tf_op jit(solution)/shard_map/attend_back/pallas_call | solution.py:917
  240.4 2.1 across_sum.1.refs_0_
  242.4 3.4 wide_sum.1.refs_8_
  246.4 11.1 %qkv_grad.1 = (bf16[4,96,896]{2,1,0:T(8,128)(2,1)}, bf16[4,96,896]{2,1,0:T(8,128)(2,1)}) custom-call(s32[8]{0:T(128)} %fusion.9.spot_ref, s32[4]{0:T(128)} %copy-done.18, bf16[2048,192]{1,0:T(8,128)(2,1)} %get-tuple-element.124.dq_ref, bf16[4096,384]{1,0:T(8,128)(2,1)} %get-tuple-element.125.dkv_ref, bf16[5,96,1536]{2,1,0:T(8,128)(2,1)} %get-tuple-element.126.keep_ref, ...), custom_call_target="tpu_custom_call" | custom-call | flops 15032385536 | bytes 12582912 | tf_op jit(solution)/shard_map/qkv_grad/pallas_call | solution.py:1015
  257.8 2.2 collective-permute-start.54
  260.0 1.7 copy-done.24
  261.7 3.0 row_sum_one.1
  266.0 10.0 %collective-permute-done.39.got_ref = bf16[4,96,896]{2,1,0:T(8,128)(2,1)} collective-permute-done((bf16[4,96,896]{2,1,0:T(8,128)(2,1)}, bf16[4,96,896]{2,1,0:T(8,128)(2,1)}, u32[]{:S(2)}, u32[]{:S(2)}) %collective-permute-start.39) | collective-permute-done | bytes 688160 | tf_op jit(solution)/shard_map/tail_part1/ppermute | solution.py:480
  276.0 2.2 tail_sum.1
  278.8 4.0 %collective-permute-done.54.across_ref = bf16[96,1536]{1,0:T(8,128)(2,1)S(1)} collective-permute-done((bf16[96,1536]{1,0:T(8,128)(2,1)S(1)}, bf16[96,1536]{1,0:T(8,128)(2,1)S(1)}, u32[]{:S(2)}, u32[]{:S(2)}) %collective-permute-start.54) | collective-permute-done | bytes 294944 | tf_op jit(solution)/shard_map/across_both/ppermute | solution.py:497
  283.6 1.9 wide_end.1.refs_0_
  286.4 1.5 collective-permute-start.55
  288.7 1.9 tail_mid.1
  290.5 10.7 %collective-permute-done.56.refs_0_ = bf16[96,1536]{1,0:T(8,128)(2,1)S(1)} collective-permute-done((bf16[96,1536]{1,0:T(8,128)(2,1)}, bf16[96,1536]{1,0:T(8,128)(2,1)S(1)}, u32[]{:S(2)}, u32[]{:S(2)}) %collective-permute-start.56) | collective-permute-done | bytes 294944 | tf_op jit(solution)/shard_map/wide_sq2/ppermute | solution.py:480
  302.0 2.4 collective-permute-start.46
  305.0 1.8 collective-permute-start.59
  306.8 2.5 row_sum_two.1
  310.0 2.4 collective-permute-done.46.got_ref
  313.4 1.7 tail_end.1.refs_0_
  315.1 3.4 collective-permute-start.48
  318.5 7.6 %collective-permute-done.48.refs_2_ = bf16[1,96,896]{2,1,0:T(8,128)(2,1)S(1)} collective-permute-done((bf16[1,96,896]{2,1,0:T(8,128)(2,1)}, bf16[1,96,896]{2,1,0:T(8,128)(2,1)S(1)}, u32[]{:S(2)}, u32[]{:S(2)}) %collective-permute-start.48) | collective-permute-done | bytes 172064 | tf_op jit(solution)/shard_map/tail_sq2/ppermute | solution.py:480
  326.8 2.0 collective-permute-start.50
  328.8 2.9 collective-permute-done.49.refs_3_
  331.7 2.0 collective-permute-start.51
  334.9 3.4 row_sum_three.1
  339.1 4.7 %wide_place.1 = (f32[768,768]{1,0:T(8,128)}, f32[768,768]{1,0:T(8,128)}) custom-call(s32[8]{0:T(128)} %fusion.5.spot_ref, bf16[96,1536]{1,0:T(8,128)(2,1)} %wide_end.1.refs_0_, bf16[96,1536]{1,0:T(8,128)(2,1)} %after.18.refs_1_, bf16[96,1536]{1,0:T(8,128)(2,1)} %after.19.refs_2_, bf16[96,1536]{1,0:T(8,128)(2,1)} %copy-done.47, bf16[96,1536]{1,0:T(8,128)(2,1)} %copy-done.46, ...), custom_call_target="tpu_custom_call" | custom-call | flops 268435456 | bytes 3145728 | tf_op jit(solution)/shard_map/wide_place/pallas_call | solution.py:1158
  343.8 1.7 collective-permute-start.44
  347.0 1.7 collective-permute-start.45
  348.9 3.6 tail_place.1
  354.1 2.8 copy.56
  358.8 1.5 copy.66
  360.4 1.5 copy.67
  (322 shorter events, 54.9 us)
Async XLA Ops:
  7.2 63.3 %copy-start = (s32[4,64,12,3]{1,0,3,2:T(4,128)S(1)}, s32[4,64,12,3]{1,0,3,2:T(4,128)}, u32[]{:S(2)}) copy-start(s32[4,64,12,3]{1,0,3,2:T(4,128)} %param.31) | copy-start | bytes 110596
  7.2 275.7 %reduce-scatter.2.cloned.1.call-start = ((), (), s32[]{:S(2)}) async-start(), calls=%async_computation.1 | async-start | bytes 1474560 | tf_op jit(solution)/shard_map/reduce_scatter | solution.py:1853
  15.4 29.9 %collective-permute-start.4 = (bf16[880,1536]{1,0:T(8,128)(2,1)}, bf16[880,1536]{1,0:T(8,128)(2,1)}, u32[]{:S(2)}, u32[]{:S(2)}) collective-permute-start(bf16[880,1536]{1,0:T(8,128)(2,1)} %get-tuple-element.81.refs_0_.refs_4_), channel_id=1, source_target_pairs={{0,1},{1,0},{2,3},{3,2},{4,5},{5,4},{6,7},{7,6},{8,9},{9,8},{10,11... | collective-permute-start | bytes 8110088 | tf_op jit(solution)/shard_map/weight_hc1/ppermute | solution.py:480
  15.9 29.5 %collective-permute-start.3 = (bf16[384,1536]{1,0:T(8,128)(2,1)}, bf16[384,1536]{1,0:T(8,128)(2,1)}, u32[]{:S(2)}, u32[]{:S(2)}) collective-permute-start(bf16[384,1536]{1,0:T(8,128)(2,1)} %get-tuple-element.87), channel_id=1, source_target_pairs={{0,2},{2,0},{1,3},{3,1},{4,6},{6,4},{5,7},{7,5},{8,10},{10,8},{9,1... | collective-permute-start | bytes 3538952 | tf_op jit(solution)/shard_map/weight_hy1/ppermute | solution.py:480
  21.8 19.0 %collective-permute-start.1 = (bf16[128,768]{1,0:T(8,128)(2,1)}, bf16[128,768]{1,0:T(8,128)(2,1)}, u32[]{:S(2)}, u32[]{:S(2)}) collective-permute-start(bf16[128,768]{1,0:T(8,128)(2,1)} %get-tuple-element.84.refs_1_), channel_id=1, source_target_pairs={{0,8},{8,0},{16,24},{24,16},{1,9},{9,1},{17,25},{25,17},{2,10},{10... | collective-permute-start | bytes 589832 | tf_op jit(solution)/shard_map/tok_sq1/ppermute | solution.py:480
  23.4 17.3 %collective-permute-start.2 = (bf16[128,768]{1,0:T(8,128)(2,1)}, bf16[128,768]{1,0:T(8,128)(2,1)}, u32[]{:S(2)}, u32[]{:S(2)}) collective-permute-start(bf16[128,768]{1,0:T(8,128)(2,1)} %get-tuple-element.85.refs_3_), channel_id=1, source_target_pairs={{0,24},{8,16},{16,8},{24,0},{1,25},{9,17},{17,9},{25,1},{2,26},{10... | collective-permute-start | bytes 589832 | tf_op jit(solution)/shard_map/tok_sq3/ppermute | solution.py:480
  25.9 18.1 %collective-permute-start = (bf16[128,768]{1,0:T(8,128)(2,1)}, bf16[128,768]{1,0:T(8,128)(2,1)}, u32[]{:S(2)}, u32[]{:S(2)}) collective-permute-start(bf16[128,768]{1,0:T(8,128)(2,1)} %get-tuple-element.83.refs_2_), channel_id=1, source_target_pairs={{0,16},{8,24},{16,0},{24,8},{1,17},{9,25},{17,1},{25,9},{2,18},{10... | collective-permute-start | bytes 589832 | tf_op jit(solution)/shard_map/tok_sq2/ppermute | solution.py:480
  45.4 12.3 %collective-permute-start.6 = (bf16[256,768]{1,0:T(8,128)(2,1)}, bf16[256,768]{1,0:T(8,128)(2,1)S(1)}, u32[]{:S(2)}, u32[]{:S(2)}) collective-permute-start(bf16[256,768]{1,0:T(8,128)(2,1)} %after.11.refs_1_.refs_13_), channel_id=1, source_target_pairs={{0,2},{2,0},{1,3},{3,1},{4,6},{6,4},{5,7},{7,5},{8,10},{10,8},{9,1... | collective-permute-start | bytes 1179656 | tf_op jit(solution)/shard_map/tok_hy1/ppermute | solution.py:480
  48.9 10.7 %collective-permute-start.5 = (bf16[256,768]{1,0:T(8,128)(2,1)}, bf16[256,768]{1,0:T(8,128)(2,1)S(1)}, u32[]{:S(2)}, u32[]{:S(2)}) collective-permute-start(bf16[256,768]{1,0:T(8,128)(2,1)} %after.10.refs_12_), channel_id=1, source_target_pairs={{0,4},{4,0},{1,5},{5,1},{2,6},{6,2},{3,7},{7,3},{8,12},{12,8},{9,1... | collective-permute-start | bytes 1179656 | tf_op jit(solution)/shard_map/tok_part1/ppermute | solution.py:480
  50.4 13.6 %collective-permute-start.7 = (bf16[112,1536]{1,0:T(8,128)(2,1)}, bf16[112,1536]{1,0:T(8,128)(2,1)S(1)}, u32[]{:S(2)}, u32[]{:S(2)}) collective-permute-start(bf16[112,1536]{1,0:T(8,128)(2,1)} %after.12), channel_id=1, source_target_pairs={{0,2},{2,0},{1,3},{3,1},{4,6},{6,4},{5,7},{7,5},{8,10},{10,8},{9,1... | collective-permute-start | bytes 1032200 | tf_op jit(solution)/shard_map/weight_hy1/ppermute | solution.py:480
  60.4 22.3 %collective-permute-start.14 = (bf16[512,768]{1,0:T(8,128)(2,1)}, bf16[512,768]{1,0:T(8,128)(2,1)}, u32[]{:S(2)}, u32[]{:S(2)}) collective-permute-start(bf16[512,768]{1,0:T(8,128)(2,1)} %after.15.refs_4_), channel_id=1, source_target_pairs={{0,4},{4,0},{1,5},{5,1},{2,6},{6,2},{3,7},{7,3},{8,12},{12,8},{9,1... | collective-permute-start | bytes 2359304 | tf_op jit(solution)/shard_map/tok_part1/ppermute | solution.py:480
  64.7 18.7 %collective-permute-start.8 = (bf16[512,768]{1,0:T(8,128)(2,1)}, bf16[512,768]{1,0:T(8,128)(2,1)S(1)}, u32[]{:S(2)}, u32[]{:S(2)}) collective-permute-start(bf16[512,768]{1,0:T(8,128)(2,1)} %after.13.refs_0_), channel_id=1, source_target_pairs={{0,2},{2,0},{1,3},{3,1},{4,6},{6,4},{5,7},{7,5},{8,10},{10,8},{9,1... | collective-permute-start | bytes 2359304 | tf_op jit(solution)/shard_map/tok_hy1/ppermute | solution.py:480
  66.3 15.9 %collective-permute-start.10 = (bf16[128,768]{1,0:T(8,128)(2,1)S(1)}, bf16[128,768]{1,0:T(8,128)(2,1)S(1)}, u32[]{:S(2)}, u32[]{:S(2)}) collective-permute-start(bf16[128,768]{1,0:T(8,128)(2,1)S(1)} %copy-done.15), channel_id=1, source_target_pairs={{0,16},{8,24},{16,0},{24,8},{1,17},{9,25},{17,1},{25,9},{2,18},{10... | collective-permute-start | bytes 589832 | tf_op jit(solution)/shard_map/dres_sq2/ppermute | solution.py:480
  68.9 13.3 %collective-permute-start.11 = (bf16[128,768]{1,0:T(8,128)(2,1)S(1)}, bf16[128,768]{1,0:T(8,128)(2,1)S(1)}, u32[]{:S(2)}, u32[]{:S(2)}) collective-permute-start(bf16[128,768]{1,0:T(8,128)(2,1)S(1)} %copy-done.13), channel_id=1, source_target_pairs={{0,24},{8,16},{16,8},{24,0},{1,25},{9,17},{17,9},{25,1},{2,26},{10... | collective-permute-start | bytes 589832 | tf_op jit(solution)/shard_map/dres_sq3/ppermute | solution.py:480
  70.2 12.5 %collective-permute-start.9 = (bf16[128,768]{1,0:T(8,128)(2,1)S(1)}, bf16[128,768]{1,0:T(8,128)(2,1)S(1)}, u32[]{:S(2)}, u32[]{:S(2)}) collective-permute-start(bf16[128,768]{1,0:T(8,128)(2,1)S(1)} %copy-done.11), channel_id=1, source_target_pairs={{0,8},{8,0},{16,24},{24,16},{1,9},{9,1},{17,25},{25,17},{2,10},{10... | collective-permute-start | bytes 589832 | tf_op jit(solution)/shard_map/dres_sq1/ppermute | solution.py:480
  82.1 4.1 %collective-permute-start.15 = (bf16[512,768]{1,0:T(8,128)(2,1)S(1)}, bf16[512,768]{1,0:T(8,128)(2,1)}, u32[]{:S(2)}, u32[]{:S(2)}) collective-permute-start(bf16[512,768]{1,0:T(8,128)(2,1)S(1)} %copy-done.29), channel_id=1, source_target_pairs={{0,1},{1,0},{2,3},{3,2},{4,5},{5,4},{6,7},{7,6},{8,9},{9,8},{10,11... | collective-permute-start | bytes 2359304 | tf_op jit(solution)/shard_map/tok_hc1/ppermute | solution.py:480
  82.2 4.1 %collective-permute-start.12 = (bf16[512,768]{1,0:T(8,128)(2,1)}, bf16[512,768]{1,0:T(8,128)(2,1)}, u32[]{:S(2)}, u32[]{:S(2)}) collective-permute-start(bf16[512,768]{1,0:T(8,128)(2,1)} %after.13.refs_0_), channel_id=1, source_target_pairs={{0,1},{1,0},{2,3},{3,2},{4,5},{5,4},{6,7},{7,6},{8,9},{9,8},{10,11... | collective-permute-start | bytes 2359304 | tf_op jit(solution)/shard_map/tok_hc1/ppermute | solution.py:480
  82.7 5.5 %collective-permute-start.16 = (bf16[512,768]{1,0:T(8,128)(2,1)}, bf16[512,768]{1,0:T(8,128)(2,1)}, u32[]{:S(2)}, u32[]{:S(2)}) collective-permute-start(bf16[512,768]{1,0:T(8,128)(2,1)} %collective-permute-done.14.refs_5_), channel_id=1, source_target_pairs={{0,1},{1,0},{2,3},{3,2},{4,5},{5,4},{6,7},{7,6},{8,9},{9,8},{10,11... | collective-permute-start | bytes 2359304 | tf_op jit(solution)/shard_map/tok_hc1/ppermute | solution.py:480
  84.3 3.8 %collective-permute-start.13 = (bf16[512,768]{1,0:T(8,128)(2,1)}, bf16[512,768]{1,0:T(8,128)(2,1)S(1)}, u32[]{:S(2)}, u32[]{:S(2)}) collective-permute-start(bf16[512,768]{1,0:T(8,128)(2,1)} %after.14.refs_1_), channel_id=1, source_target_pairs={{0,1},{1,0},{2,3},{3,2},{4,5},{5,4},{6,7},{7,6},{8,9},{9,8},{10,11... | collective-permute-start | bytes 2359304 | tf_op jit(solution)/shard_map/tok_hc1/ppermute | solution.py:480
  84.7 29.2 %collective-permute-start.20 = (bf16[384,1536]{1,0:T(8,128)(2,1)}, bf16[384,1536]{1,0:T(8,128)(2,1)S(1)}, u32[]{:S(2)}, u32[]{:S(2)}) collective-permute-start(bf16[384,1536]{1,0:T(8,128)(2,1)} %collective-permute-done.3.refs_6_.refs_7_), channel_id=1, source_target_pairs={{0,4},{4,0},{1,5},{5,1},{2,6},{6,2},{3,7},{7,3},{8,12},{12,8},{9,1... | collective-permute-start | bytes 3538952 | tf_op jit(solution)/shard_map/weight_part1/ppermute | solution.py:480
  113.4 1.6 collective-permute-start.17
  113.6 17.3 %collective-permute-start.22 = (bf16[384,1536]{1,0:T(8,128)(2,1)}, bf16[384,1536]{1,0:T(8,128)(2,1)}, u32[]{:S(2)}, u32[]{:S(2)}) collective-permute-start(bf16[384,1536]{1,0:T(8,128)(2,1)} %collective-permute-done.3.refs_6_.refs_7_), channel_id=1, source_target_pairs={{0,1},{1,0},{2,3},{3,2},{4,5},{5,4},{6,7},{7,6},{8,9},{9,8},{10,11... | collective-permute-start | bytes 3538952 | tf_op jit(solution)/shard_map/weight_hc1/ppermute | solution.py:480
  115.7 16.0 %collective-permute-start.23 = (bf16[384,1536]{1,0:T(8,128)(2,1)}, bf16[384,1536]{1,0:T(8,128)(2,1)S(1)}, u32[]{:S(2)}, u32[]{:S(2)}) collective-permute-start(bf16[384,1536]{1,0:T(8,128)(2,1)} %after.16.refs_8_), channel_id=1, source_target_pairs={{0,1},{1,0},{2,3},{3,2},{4,5},{5,4},{6,7},{7,6},{8,9},{9,8},{10,11... | collective-permute-start | bytes 3538952 | tf_op jit(solution)/shard_map/weight_hc1/ppermute | solution.py:480
  115.8 14.2 %collective-permute-start.18 = (bf16[1024,192]{1,0:T(8,128)(2,1)S(1)}, bf16[1024,192]{1,0:T(8,128)(2,1)S(1)}, u32[]{:S(2)}, u32[]{:S(2)}) collective-permute-start(bf16[1024,192]{1,0:T(8,128)(2,1)S(1)} %copy-done.76), channel_id=1, source_target_pairs={{0,2},{2,0},{1,3},{3,1},{4,6},{6,4},{5,7},{7,5},{8,10},{10,8},{9,1... | collective-permute-start | bytes 1179656 | tf_op jit(solution)/shard_map/attn_hy1/ppermute | solution.py:480
  116.2 14.7 %collective-permute-start.21 = (bf16[112,1536]{1,0:T(8,128)(2,1)S(1)}, bf16[112,1536]{1,0:T(8,128)(2,1)S(1)}, u32[]{:S(2)}, u32[]{:S(2)}) collective-permute-start(bf16[112,1536]{1,0:T(8,128)(2,1)S(1)} %copy-done.45), channel_id=1, source_target_pairs={{0,1},{1,0},{2,3},{3,2},{4,5},{5,4},{6,7},{7,6},{8,9},{9,8},{10,11... | collective-permute-start | bytes 1032200 | tf_op jit(solution)/shard_map/weight_hc1/ppermute | solution.py:480
  130.0 1.6 collective-permute-start.19
  170.6 16.9 %collective-permute-start.30 = (bf16[20,96,1536]{2,1,0:T(8,128)(2,1)}, bf16[20,96,1536]{2,1,0:T(8,128)(2,1)}, u32[]{:S(2)}, u32[]{:S(2)}) collective-permute-start(bf16[20,96,1536]{2,1,0:T(8,128)(2,1)} %far_grad.1), channel_id=1, source_target_pairs={{0,1},{1,0},{2,3},{3,2},{4,5},{5,4},{6,7},{7,6},{8,9},{9,8},{10,11... | collective-permute-start | bytes 17694728 | tf_op jit(solution)/shard_map/wide_hc1/ppermute | solution.py:480
  170.8 14.2 %collective-permute-start.28 = (bf16[2,512,192]{2,1,0:T(8,128)(2,1)S(1)}, bf16[2,512,192]{2,1,0:T(8,128)(2,1)S(1)}, u32[]{:S(2)}, u32[]{:S(2)}) collective-permute-start(bf16[2,512,192]{2,1,0:T(8,128)(2,1)S(1)} %copy-done.77), channel_id=1, source_target_pairs={{0,2},{2,0},{1,3},{3,1},{4,6},{6,4},{5,7},{7,5},{8,10},{10,8},{9,1... | collective-permute-start | bytes 1179656 | tf_op jit(solution)/shard_map/dattn_hy1/ppermute | solution.py:480
  171.2 16.2 %collective-permute-start.27 = (bf16[512,192]{1,0:T(8,128)(2,1)S(1)}, bf16[512,192]{1,0:T(8,128)(2,1)S(1)}, u32[]{:S(2)}, u32[]{:S(2)}) collective-permute-start(bf16[512,192]{1,0:T(8,128)(2,1)S(1)} %copy-done.83), channel_id=1, source_target_pairs={{0,1},{1,0},{2,3},{3,2},{4,5},{5,4},{6,7},{7,6},{8,9},{9,8},{10,11... | collective-permute-start | bytes 589832 | tf_op jit(solution)/shard_map/dattn_hc1/ppermute | solution.py:480
  171.2 28.2 %collective-permute-start.24 = (bf16[128,768]{1,0:T(8,128)(2,1)S(1)}, bf16[128,768]{1,0:T(8,128)(2,1)S(1)}, u32[]{:S(2)}, u32[]{:S(2)}) collective-permute-start(bf16[128,768]{1,0:T(8,128)(2,1)S(1)} %copy-done.86), channel_id=1, source_target_pairs={{0,8},{8,0},{16,24},{24,16},{1,9},{9,1},{17,25},{25,17},{2,10},{10... | collective-permute-start | bytes 589832 | tf_op jit(solution)/shard_map/result_sq1/ppermute | solution.py:480
  174.0 25.4 %collective-permute-start.25 = (bf16[128,768]{1,0:T(8,128)(2,1)S(1)}, bf16[128,768]{1,0:T(8,128)(2,1)S(1)}, u32[]{:S(2)}, u32[]{:S(2)}) collective-permute-start(bf16[128,768]{1,0:T(8,128)(2,1)S(1)} %copy-done.85), channel_id=1, source_target_pairs={{0,16},{8,24},{16,0},{24,8},{1,17},{9,25},{17,1},{25,9},{2,18},{10... | collective-permute-start | bytes 589832 | tf_op jit(solution)/shard_map/result_sq2/ppermute | solution.py:480
  185.0 17.0 %collective-permute-start.26 = (bf16[128,768]{1,0:T(8,128)(2,1)S(1)}, bf16[128,768]{1,0:T(8,128)(2,1)S(1)}, u32[]{:S(2)}, u32[]{:S(2)}) collective-permute-start(bf16[128,768]{1,0:T(8,128)(2,1)S(1)} %copy-done.84), channel_id=1, source_target_pairs={{0,24},{8,16},{16,8},{24,0},{1,25},{9,17},{17,9},{25,1},{2,26},{10... | collective-permute-start | bytes 589832 | tf_op jit(solution)/shard_map/result_sq3/ppermute | solution.py:480
  187.4 16.1 %collective-permute-start.29 = (bf16[512,192]{1,0:T(8,128)(2,1)S(1)}, bf16[512,192]{1,0:T(8,128)(2,1)S(1)}, u32[]{:S(2)}, u32[]{:S(2)}) collective-permute-start(bf16[512,192]{1,0:T(8,128)(2,1)S(1)} %slice_bitcast_fusion), channel_id=1, source_target_pairs={{0,1},{1,0},{2,3},{3,2},{4,5},{5,4},{6,7},{7,6},{8,9},{9,8},{10,11... | collective-permute-start | bytes 589832 | tf_op jit(solution)/shard_map/dattn_hc1/ppermute | solution.py:480
  196.7 41.2 %collective-permute-start.33 = (bf16[96,1536]{1,0:T(8,128)(2,1)}, bf16[96,1536]{1,0:T(8,128)(2,1)S(1)}, u32[]{:S(2)}, u32[]{:S(2)}) collective-permute-start(bf16[96,1536]{1,0:T(8,128)(2,1)} %get-tuple-element.120.refs_15_), channel_id=1, source_target_pairs={{0,8},{8,0},{16,24},{24,16},{1,9},{9,1},{17,25},{25,17},{2,10},{10... | collective-permute-start | bytes 884744 | tf_op jit(solution)/shard_map/wide_sq1/ppermute | solution.py:480
  199.5 38.5 %collective-permute-start.34 = (bf16[96,1536]{1,0:T(8,128)(2,1)}, bf16[96,1536]{1,0:T(8,128)(2,1)S(1)}, u32[]{:S(2)}, u32[]{:S(2)}) collective-permute-start(bf16[96,1536]{1,0:T(8,128)(2,1)} %get-tuple-element.119.refs_14_), channel_id=1, source_target_pairs={{0,16},{8,24},{16,0},{24,8},{1,17},{9,25},{17,1},{25,9},{2,18},{10... | collective-permute-start | bytes 884744 | tf_op jit(solution)/shard_map/wide_sq2/ppermute | solution.py:480
  200.1 37.8 %collective-permute-start.35 = (bf16[96,1536]{1,0:T(8,128)(2,1)}, bf16[96,1536]{1,0:T(8,128)(2,1)S(1)}, u32[]{:S(2)}, u32[]{:S(2)}) collective-permute-start(bf16[96,1536]{1,0:T(8,128)(2,1)} %get-tuple-element.121.refs_16_), channel_id=1, source_target_pairs={{0,24},{8,16},{16,8},{24,0},{1,25},{9,17},{17,9},{25,1},{2,26},{10... | collective-permute-start | bytes 884744 | tf_op jit(solution)/shard_map/wide_sq3/ppermute | solution.py:480
  202.7 35.3 %collective-permute-start.31 = (bf16[496,1536]{1,0:T(8,128)(2,1)}, bf16[496,1536]{1,0:T(8,128)(2,1)S(1)}, u32[]{:S(2)}, u32[]{:S(2)}) collective-permute-start(bf16[496,1536]{1,0:T(8,128)(2,1)} %get-tuple-element.116.refs_11_), channel_id=1, source_target_pairs={{0,2},{2,0},{1,3},{3,1},{4,6},{6,4},{5,7},{7,5},{8,10},{10,8},{9,1... | collective-permute-start | bytes 4571144 | tf_op jit(solution)/shard_map/wide_hy1/ppermute | solution.py:480
  204.2 33.8 %collective-permute-start.32 = (bf16[4,96,1536]{2,1,0:T(8,128)(2,1)}, bf16[4,96,1536]{2,1,0:T(8,128)(2,1)S(1)}, u32[]{:S(2)}, u32[]{:S(2)}) collective-permute-start(bf16[4,96,1536]{2,1,0:T(8,128)(2,1)} %get-tuple-element.117.refs_12_), channel_id=1, source_target_pairs={{0,4},{4,0},{1,5},{5,1},{2,6},{6,2},{3,7},{7,3},{8,12},{12,8},{9,1... | collective-permute-start | bytes 3538952 | tf_op jit(solution)/shard_map/wide_part1/ppermute | solution.py:480
  239.8 20.2 %collective-permute-start.36 = (bf16[2,1024,768]{2,1,0:T(8,128)(2,1)}, bf16[2,1024,768]{2,1,0:T(8,128)(2,1)S(1)}, u32[]{:S(2)}, u32[]{:S(2)}) collective-permute-start(bf16[2,1024,768]{2,1,0:T(8,128)(2,1)} %after.17), channel_id=1, source_target_pairs={{0,1},{1,0},{2,3},{3,2},{4,5},{5,4},{6,7},{7,6},{8,9},{9,8},{10,11... | collective-permute-start | bytes 9437192 | tf_op jit(solution)/shard_map/dtok_hc1/ppermute | solution.py:480
  257.5 18.5 %collective-permute-start.39 = (bf16[4,96,896]{2,1,0:T(8,128)(2,1)}, bf16[4,96,896]{2,1,0:T(8,128)(2,1)}, u32[]{:S(2)}, u32[]{:S(2)}) collective-permute-start(bf16[4,96,896]{2,1,0:T(8,128)(2,1)} %get-tuple-element.131), channel_id=1, source_target_pairs={{0,4},{4,0},{1,5},{5,1},{2,6},{6,2},{3,7},{7,3},{8,12},{12,8},{9,1... | collective-permute-start | bytes 2064392 | tf_op jit(solution)/shard_map/tail_part1/ppermute | solution.py:480
  257.8 25.1 %collective-permute-start.54 = (bf16[96,1536]{1,0:T(8,128)(2,1)S(1)}, bf16[96,1536]{1,0:T(8,128)(2,1)S(1)}, u32[]{:S(2)}, u32[]{:S(2)}) collective-permute-start(bf16[96,1536]{1,0:T(8,128)(2,1)S(1)} %copy-done.50), channel_id=1, source_target_pairs={{0,6},{2,4},{4,2},{6,0},{1,7},{3,5},{5,3},{7,1},{8,14},{10,12},{12... | collective-permute-start | bytes 884744 | tf_op jit(solution)/shard_map/across_both/ppermute | solution.py:497
  264.7 39.8 %collective-permute-start.37 = (bf16[512,768]{1,0:T(8,128)(2,1)}, bf16[512,768]{1,0:T(8,128)(2,1)S(1)}, u32[]{:S(2)}, u32[]{:S(2)}) collective-permute-start(bf16[512,768]{1,0:T(8,128)(2,1)} %get-tuple-element.129.refs_0_), channel_id=1, source_target_pairs={{0,2},{2,0},{1,3},{3,1},{4,6},{6,4},{5,7},{7,5},{8,10},{10,8},{9,1... | collective-permute-start | bytes 2359304 | tf_op jit(solution)/shard_map/dtok_hy1/ppermute | solution.py:480
  265.7 39.3 %collective-permute-start.38 = (bf16[512,768]{1,0:T(8,128)(2,1)}, bf16[512,768]{1,0:T(8,128)(2,1)S(1)}, u32[]{:S(2)}, u32[]{:S(2)}) collective-permute-start(bf16[512,768]{1,0:T(8,128)(2,1)} %get-tuple-element.130.refs_1_), channel_id=1, source_target_pairs={{0,4},{4,0},{1,5},{5,1},{2,6},{6,2},{3,7},{7,3},{8,12},{12,8},{9,1... | collective-permute-start | bytes 2359304 | tf_op jit(solution)/shard_map/dtok_part1/ppermute | solution.py:480
  278.2 9.7 %collective-permute-start.40 = (bf16[2,96,896]{2,1,0:T(8,128)(2,1)}, bf16[2,96,896]{2,1,0:T(8,128)(2,1)S(1)}, u32[]{:S(2)}, u32[]{:S(2)}) collective-permute-start(bf16[2,96,896]{2,1,0:T(8,128)(2,1)} %get-tuple-element.133), channel_id=1, source_target_pairs={{0,8},{8,0},{16,24},{24,16},{1,9},{9,1},{17,25},{25,17},{2,10},{10... | collective-permute-start | bytes 1032200 | tf_op jit(solution)/shard_map/tail_sq1/ppermute | solution.py:480
  285.5 15.8 %collective-permute-start.56 = (bf16[96,1536]{1,0:T(8,128)(2,1)}, bf16[96,1536]{1,0:T(8,128)(2,1)S(1)}, u32[]{:S(2)}, u32[]{:S(2)}) collective-permute-start(bf16[96,1536]{1,0:T(8,128)(2,1)} %wide_end.1.refs_0_), channel_id=1, source_target_pairs={{0,16},{8,24},{16,0},{24,8},{1,17},{9,25},{17,1},{25,9},{2,18},{10... | collective-permute-start | bytes 884744 | tf_op jit(solution)/shard_map/wide_sq2/ppermute | solution.py:480
  286.4 15.5 %collective-permute-start.55 = (bf16[96,1536]{1,0:T(8,128)(2,1)}, bf16[96,1536]{1,0:T(8,128)(2,1)S(1)}, u32[]{:S(2)}, u32[]{:S(2)}) collective-permute-start(bf16[96,1536]{1,0:T(8,128)(2,1)} %wide_end.1.refs_0_), channel_id=1, source_target_pairs={{0,8},{8,0},{16,24},{24,16},{1,9},{9,1},{17,25},{25,17},{2,10},{10... | collective-permute-start | bytes 884744 | tf_op jit(solution)/shard_map/wide_sq1/ppermute | solution.py:480
  287.9 21.4 %collective-permute-start.58 = (bf16[96,1536]{1,0:T(8,128)(2,1)}, bf16[96,1536]{1,0:T(8,128)(2,1)S(1)}, u32[]{:S(2)}, u32[]{:S(2)}) collective-permute-start(bf16[96,1536]{1,0:T(8,128)(2,1)} %wide_end.1.refs_0_), channel_id=1, source_target_pairs={{0,4},{4,0},{1,5},{5,1},{2,6},{6,2},{3,7},{7,3},{8,12},{12,8},{9,1... | collective-permute-start | bytes 884744 | tf_op jit(solution)/shard_map/wide_part1/ppermute | solution.py:480
  302.0 13.1 %collective-permute-start.57 = (bf16[96,1536]{1,0:T(8,128)(2,1)}, bf16[96,1536]{1,0:T(8,128)(2,1)S(1)}, u32[]{:S(2)}, u32[]{:S(2)}) collective-permute-start(bf16[96,1536]{1,0:T(8,128)(2,1)} %after.19.refs_2_), channel_id=1, source_target_pairs={{0,8},{8,0},{16,24},{24,16},{1,9},{9,1},{17,25},{25,17},{2,10},{10... | collective-permute-start | bytes 884744 | tf_op jit(solution)/shard_map/wide_sq1/ppermute | solution.py:480
  302.0 10.4 %collective-permute-start.46 = (bf16[1,96,896]{2,1,0:T(8,128)(2,1)}, bf16[1,96,896]{2,1,0:T(8,128)(2,1)}, u32[]{:S(2)}, u32[]{:S(2)}) collective-permute-start(bf16[1,96,896]{2,1,0:T(8,128)(2,1)} %get-tuple-element.134.refs_0_.refs_1_), channel_id=1, source_target_pairs={{0,16},{8,24},{16,0},{24,8},{1,17},{9,25},{17,1},{25,9},{2,18},{10... | collective-permute-start | bytes 516104 | tf_op jit(solution)/shard_map/tail_sq2/ppermute | solution.py:480
  304.4 14.1 %collective-permute-start.60 = (bf16[96,1536]{1,0:T(8,128)(2,1)}, bf16[96,1536]{1,0:T(8,128)(2,1)S(1)}, u32[]{:S(2)}, u32[]{:S(2)}) collective-permute-start(bf16[96,1536]{1,0:T(8,128)(2,1)} %after.19.refs_2_), channel_id=1, source_target_pairs={{0,4},{4,0},{1,5},{5,1},{2,6},{6,2},{3,7},{7,3},{8,12},{12,8},{9,1... | collective-permute-start | bytes 884744 | tf_op jit(solution)/shard_map/wide_part1/ppermute | solution.py:480
  305.0 21.2 %collective-permute-start.59 = (bf16[96,1536]{1,0:T(8,128)(2,1)}, bf16[96,1536]{1,0:T(8,128)(2,1)S(1)}, u32[]{:S(2)}, u32[]{:S(2)}) collective-permute-start(bf16[96,1536]{1,0:T(8,128)(2,1)} %after.18.refs_1_), channel_id=1, source_target_pairs={{0,4},{4,0},{1,5},{5,1},{2,6},{6,2},{3,7},{7,3},{8,12},{12,8},{9,1... | collective-permute-start | bytes 884744 | tf_op jit(solution)/shard_map/wide_part1/ppermute | solution.py:480
  309.4 22.4 %collective-permute-start.41 = (bf16[256,768]{1,0:T(8,128)(2,1)}, bf16[256,768]{1,0:T(8,128)(2,1)S(1)}, u32[]{:S(2)}, u32[]{:S(2)}) collective-permute-start(bf16[256,768]{1,0:T(8,128)(2,1)} %get-tuple-element.135.refs_0_), channel_id=1, source_target_pairs={{0,4},{4,0},{1,5},{5,1},{2,6},{6,2},{3,7},{7,3},{8,12},{12,8},{9,1... | collective-permute-start | bytes 1179656 | tf_op jit(solution)/shard_map/dtok_part1/ppermute | solution.py:480
  312.4 21.3 %collective-permute-start.42 = (bf16[256,768]{1,0:T(8,128)(2,1)}, bf16[256,768]{1,0:T(8,128)(2,1)S(1)}, u32[]{:S(2)}, u32[]{:S(2)}) collective-permute-start(bf16[256,768]{1,0:T(8,128)(2,1)} %get-tuple-element.136.refs_1_), channel_id=1, source_target_pairs={{0,2},{2,0},{1,3},{3,1},{4,6},{6,4},{5,7},{7,5},{8,10},{10,8},{9,1... | collective-permute-start | bytes 1179656 | tf_op jit(solution)/shard_map/dtok_hy1/ppermute | solution.py:480
  315.1 11.0 %collective-permute-start.48 = (bf16[1,96,896]{2,1,0:T(8,128)(2,1)}, bf16[1,96,896]{2,1,0:T(8,128)(2,1)S(1)}, u32[]{:S(2)}, u32[]{:S(2)}) collective-permute-start(bf16[1,96,896]{2,1,0:T(8,128)(2,1)} %tail_end.1.refs_0_), channel_id=1, source_target_pairs={{0,16},{8,24},{16,0},{24,8},{1,17},{9,25},{17,1},{25,9},{2,18},{10... | collective-permute-start | bytes 516104 | tf_op jit(solution)/shard_map/tail_sq2/ppermute | solution.py:480
  318.5 8.3 %collective-permute-start.47 = (bf16[1,96,896]{2,1,0:T(8,128)(2,1)}, bf16[1,96,896]{2,1,0:T(8,128)(2,1)}, u32[]{:S(2)}, u32[]{:S(2)}) collective-permute-start(bf16[1,96,896]{2,1,0:T(8,128)(2,1)} %tail_end.1.refs_0_), channel_id=1, source_target_pairs={{0,8},{8,0},{16,24},{24,16},{1,9},{9,1},{17,25},{25,17},{2,10},{10... | collective-permute-start | bytes 516104 | tf_op jit(solution)/shard_map/tail_sq1/ppermute | solution.py:480
  326.1 5.5 %collective-permute-start.49 = (bf16[1,96,896]{2,1,0:T(8,128)(2,1)S(1)}, bf16[1,96,896]{2,1,0:T(8,128)(2,1)}, u32[]{:S(2)}, u32[]{:S(2)}) collective-permute-start(bf16[1,96,896]{2,1,0:T(8,128)(2,1)S(1)} %collective-permute-done.48.refs_2_), channel_id=1, source_target_pairs={{0,8},{8,0},{16,24},{24,16},{1,9},{9,1},{17,25},{25,17},{2,10},{10... | collective-permute-start | bytes 516104 | tf_op jit(solution)/shard_map/tail_sq1/ppermute | solution.py:480
  326.2 12.2 %collective-permute-start.61 = (bf16[96,1536]{1,0:T(8,128)(2,1)S(1)}, bf16[96,1536]{1,0:T(8,128)(2,1)S(1)}, u32[]{:S(2)}, u32[]{:S(2)}) collective-permute-start(bf16[96,1536]{1,0:T(8,128)(2,1)S(1)} %collective-permute-done.57.refs_3_), channel_id=1, source_target_pairs={{0,4},{4,0},{1,5},{5,1},{2,6},{6,2},{3,7},{7,3},{8,12},{12,8},{9,1... | collective-permute-start | bytes 884744 | tf_op jit(solution)/shard_map/wide_part1/ppermute | solution.py:480
  326.8 17.0 %collective-permute-start.50 = (bf16[1,96,896]{2,1,0:T(8,128)(2,1)}, bf16[1,96,896]{2,1,0:T(8,128)(2,1)}, u32[]{:S(2)}, u32[]{:S(2)}) collective-permute-start(bf16[1,96,896]{2,1,0:T(8,128)(2,1)} %tail_end.1.refs_0_), channel_id=1, source_target_pairs={{0,4},{4,0},{1,5},{5,1},{2,6},{6,2},{3,7},{7,3},{8,12},{12,8},{9,1... | collective-permute-start | bytes 516104 | tf_op jit(solution)/shard_map/tail_part1/ppermute | solution.py:480
  331.7 17.0 %collective-permute-start.52 = (bf16[1,96,896]{2,1,0:T(8,128)(2,1)S(1)}, bf16[1,96,896]{2,1,0:T(8,128)(2,1)}, u32[]{:S(2)}, u32[]{:S(2)}) collective-permute-start(bf16[1,96,896]{2,1,0:T(8,128)(2,1)S(1)} %collective-permute-done.48.refs_2_), channel_id=1, source_target_pairs={{0,4},{4,0},{1,5},{5,1},{2,6},{6,2},{3,7},{7,3},{8,12},{12,8},{9,1... | collective-permute-start | bytes 516104 | tf_op jit(solution)/shard_map/tail_part1/ppermute | solution.py:480
  331.7 15.3 %collective-permute-start.51 = (bf16[1,96,896]{2,1,0:T(8,128)(2,1)}, bf16[1,96,896]{2,1,0:T(8,128)(2,1)}, u32[]{:S(2)}, u32[]{:S(2)}) collective-permute-start(bf16[1,96,896]{2,1,0:T(8,128)(2,1)} %collective-permute-done.47.refs_1_), channel_id=1, source_target_pairs={{0,4},{4,0},{1,5},{5,1},{2,6},{6,2},{3,7},{7,3},{8,12},{12,8},{9,1... | collective-permute-start | bytes 516104 | tf_op jit(solution)/shard_map/tail_part1/ppermute | solution.py:480
  333.7 15.2 %collective-permute-start.53 = (bf16[1,96,896]{2,1,0:T(8,128)(2,1)}, bf16[1,96,896]{2,1,0:T(8,128)(2,1)}, u32[]{:S(2)}, u32[]{:S(2)}) collective-permute-start(bf16[1,96,896]{2,1,0:T(8,128)(2,1)} %collective-permute-done.49.refs_3_), channel_id=1, source_target_pairs={{0,4},{4,0},{1,5},{5,1},{2,6},{6,2},{3,7},{7,3},{8,12},{12,8},{9,1... | collective-permute-start | bytes 516104 | tf_op jit(solution)/shard_map/tail_part1/ppermute | solution.py:480
  338.4 19.1 %collective-permute-start.43 = (bf16[128,768]{1,0:T(8,128)(2,1)}, bf16[128,768]{1,0:T(8,128)(2,1)S(1)}, u32[]{:S(2)}, u32[]{:S(2)}) collective-permute-start(bf16[128,768]{1,0:T(8,128)(2,1)} %get-tuple-element.139.refs_9_), channel_id=1, source_target_pairs={{0,8},{8,0},{16,24},{24,16},{1,9},{9,1},{17,25},{25,17},{2,10},{10... | collective-permute-start | bytes 589832 | tf_op jit(solution)/shard_map/dtok_sq1/ppermute | solution.py:480
  343.8 14.4 %collective-permute-start.44 = (bf16[128,768]{1,0:T(8,128)(2,1)S(1)}, bf16[128,768]{1,0:T(8,128)(2,1)S(1)}, u32[]{:S(2)}, u32[]{:S(2)}) collective-permute-start(bf16[128,768]{1,0:T(8,128)(2,1)S(1)} %copy-done.64), channel_id=1, source_target_pairs={{0,16},{8,24},{16,0},{24,8},{1,17},{9,25},{17,1},{25,9},{2,18},{10... | collective-permute-start | bytes 589832 | tf_op jit(solution)/shard_map/dtok_sq2/ppermute | solution.py:480
  347.0 11.2 %collective-permute-start.45 = (bf16[128,768]{1,0:T(8,128)(2,1)S(1)}, bf16[128,768]{1,0:T(8,128)(2,1)S(1)}, u32[]{:S(2)}, u32[]{:S(2)}) collective-permute-start(bf16[128,768]{1,0:T(8,128)(2,1)S(1)} %copy-done.63), channel_id=1, source_target_pairs={{0,24},{8,16},{16,8},{24,0},{1,25},{9,17},{17,9},{25,1},{2,26},{10... | collective-permute-start | bytes 589832 | tf_op jit(solution)/shard_map/dtok_sq3/ppermute | solution.py:480
  (86 other events, 549.3 us)
Sparse Core Ops, SparseCore 0:
  246.0 27.7 reduce-scatter.1
